TPU v7x, 32 devices: a whole 2x2x4 slice. The times are simulated.
32 devices in a mesh: seq: 8 (over z, x), batch: 4 (over y, core).
Axes of the slice: x: 2, y: 2, z: 4, core: 2. Of those that a mesh axis runs over, the one named last changes fastest.
Arguments:
- inputs: float32 [8, 2048, 256], P('batch', 'seq'), may hold values from -6 to 6
- guess_path: float32 [8, 2048, 128], P('batch', 'seq'), may hold values from -3 to 3
- recur_weight: float32 [128, 128], replicated, may hold values from -0.09 to 0.09
- damping: float32 [128], replicated, may hold values from 0.001953125 to 2.5
- in_weight: float32 [256, 128], replicated, may hold values from -0.375 to 0.375
- bias_term: float32 [128], replicated, may hold values from -3 to 3
- targets: float32 [8, 16, 128], P('batch', 'seq'), may hold values from -6 to 6
- target_steps: int32 [8, 16], P('batch', 'seq'), may hold values from 0 to 127
Outputs:
- trajectory: float32 [8, 2048, 128], P('batch', 'seq')
- grad_recur: float32 [128, 128], replicated
- grad_in: float32 [256, 128], replicated
All inputs are finite; a program needn't handle non-finite values.
Results may differ from a plain program's by a relative error of at most 0.0003.
Values sent between devices are 32-bit elements; how exact they have to be, the bound alone decides.
No kernel may reach another device: no remote copies, remote signals or barrier semaphores. Data moves between devices by JAX's collectives and lax.ppermute only.
A program may use at most 64 MiB of HBM per device.

v0:
```python
import jax
import jax.numpy as jnp
from jax import lax
from jax.sharding import PartitionSpec as P

BLK = 16
TBLK = 128


euler_step = 0.02


def shifted(block, axis, distance):
    devices = range(lax.axis_size(axis))
    route = [(i - distance, i) for i in devices if i - distance in devices]
    return lax.ppermute(block, axis, route)


def entering(value, axis, join, neutral, backward):
    count, mine = (lax.axis_size(axis), lax.axis_index(axis))
    pieces = jax.tree.map(lambda part: lax.all_gather(part, axis), value)
    if backward:
        pieces = jax.tree.map(lambda part: part[::-1], pieces)
        mine = count - 1 - mine
    subtotal = jax.tree.map(
        lambda part, zero: jnp.full_like(part, 0) + jnp.asarray(zero, part.dtype), value, neutral
    )

    def hop(position, subtotal):
        longer = join(subtotal, jax.tree.map(lambda part: part[position], pieces))
        return jax.tree.map(lambda new, old: jnp.where(position < mine, new, old), longer, subtotal)

    return lax.fori_loop(0, count - 1, hop, subtotal)


def join_maps(earlier, later):
    highest = lax.Precision.HIGHEST
    matrix = jnp.einsum("isk,ksj->isj", later[0], earlier[0], precision=highest)
    vector = jnp.einsum("isj,sj->si", later[0], earlier[1], precision=highest) + later[1]
    return (matrix, vector)


def apply_map(carry, inputs_now):
    block_map, block_off = inputs_now
    result = jnp.einsum("isj,sj->si", block_map, carry, precision=lax.Precision.HIGHEST) + block_off
    return (result, carry)


def on_device(
    inputs, guess_path, recur_weight, damping, in_weight, bias_term, targets, target_steps
):
    highest = lax.Precision.HIGHEST
    seq_count, step_count, hidden = guess_path.shape
    block_count = step_count // BLK
    lane_count = seq_count * block_count
    skew = recur_weight - recur_weight.T
    skew_t = skew.T
    edge = shifted(guess_path[:, step_count - 1, :], "seq", 1)
    prev = jnp.concatenate([edge[:, None, :], guess_path[:, :-1, :]], axis=1)
    drive = jnp.dot(
        inputs.reshape(seq_count * step_count, -1), in_weight, precision=highest
    ).reshape(seq_count, step_count, hidden)
    preact = jnp.dot(prev.reshape(-1, hidden), skew_t, precision=highest).reshape(
        seq_count, step_count, hidden
    )
    preact = preact - damping * prev + drive + bias_term
    activation = jnp.tanh(preact)
    gain = euler_step * (1.0 - activation * activation)
    resid = prev + euler_step * activation - guess_path

    def by_step(values):
        return (
            values.reshape(seq_count, block_count, BLK, hidden)
            .transpose(2, 0, 1, 3)
            .reshape(BLK, lane_count, hidden)
        )

    def from_step(values):
        return (
            values.reshape(BLK, seq_count, block_count, hidden)
            .transpose(1, 2, 0, 3)
            .reshape(seq_count, step_count, hidden)
        )

    gain_steps = by_step(gain)
    resid_steps = by_step(resid)

    def advance(state, gain_now, resid_now):
        moved = jnp.dot(state, skew_t, precision=highest) - damping * state
        return state + gain_now * moved + resid_now

    def compose(carry, inputs_now):
        maps, offsets = carry
        gain_now, resid_now = inputs_now
        turned = jnp.dot(
            skew, maps.reshape(hidden, lane_count * hidden), precision=highest
        ).reshape(hidden, lane_count, hidden)
        turned = turned - damping[:, None, None] * maps
        maps = maps + gain_now.T[:, :, None] * turned
        offsets = advance(offsets, gain_now, resid_now)
        return ((maps, offsets), None)

    unit_map = jnp.eye(hidden, dtype=jnp.float32)
    lane_zero = jnp.zeros((lane_count, hidden), jnp.float32)
    start_maps = jnp.broadcast_to(unit_map[:, None, :], (hidden, lane_count, hidden))
    (block_maps, block_offs), _ = lax.scan(
        compose, (start_maps, lane_zero), (gain_steps, resid_steps)
    )
    blocks = block_maps.reshape(hidden, seq_count, block_count, hidden).transpose(2, 0, 1, 3)
    offsets = block_offs.reshape(seq_count, block_count, hidden).transpose(1, 0, 2)

    def chain(carry, inputs_now):
        total, offset = carry
        block_map, block_off = inputs_now
        total = jnp.einsum("isk,ksj->isj", block_map, total, precision=highest)
        offset = jnp.einsum("isj,sj->si", block_map, offset, precision=highest) + block_off
        return ((total, offset), None)

    seq_zero = jnp.zeros((seq_count, hidden), jnp.float32)
    unit_stack = jnp.broadcast_to(unit_map[:, None, :], (hidden, seq_count, hidden))
    (dev_map, dev_off), _ = lax.scan(chain, (unit_stack, seq_zero), (blocks, offsets))
    _, delta_in = entering((dev_map, dev_off), "seq", join_maps, (unit_stack, seq_zero), False)
    _, starts = lax.scan(apply_map, delta_in, (blocks, offsets))
    starts = starts.transpose(1, 0, 2).reshape(lane_count, hidden)

    def forward(state, inputs_now):
        state = advance(state, inputs_now[0], inputs_now[1])
        return (state, state)

    _, deltas = lax.scan(forward, starts, (gain_steps, resid_steps))
    trajectory = guess_path + from_step(deltas)
    total_seqs = seq_count * lax.axis_size("batch")
    target_blocks = step_count // TBLK
    target_hit = (jnp.arange(TBLK)[None, None, :] == target_steps[:, :, None]).astype(jnp.float32)
    miss = trajectory.reshape(seq_count, target_blocks, TBLK, hidden) - targets[:, :, None, :]
    source = (target_hit[..., None] * miss / total_seqs).reshape(seq_count, step_count, hidden)
    source_steps = by_step(source)

    def retreat(carry, inputs_now):
        gain_now, source_now = inputs_now
        adjoint = source_now + carry
        scaled = gain_now * adjoint
        carry = adjoint + jnp.dot(scaled, skew, precision=highest) - damping * scaled
        return (carry, adjoint)

    outflow, _ = lax.scan(retreat, lane_zero, (gain_steps, source_steps), reverse=True)
    outflow = outflow.reshape(seq_count, block_count, hidden).transpose(1, 0, 2)
    flipped = blocks.transpose(0, 3, 2, 1)
    adjoint_off, _ = lax.scan(apply_map, seq_zero, (flipped, outflow), reverse=True)
    dev_flipped = dev_map.transpose(2, 1, 0)
    _, adjoint_in = entering(
        (dev_flipped, adjoint_off), "seq", join_maps, (unit_stack, seq_zero), True
    )
    _, block_ends = lax.scan(apply_map, adjoint_in, (flipped, outflow), reverse=True)
    block_ends = block_ends.transpose(1, 0, 2).reshape(lane_count, hidden)
    _, adjoints = lax.scan(retreat, block_ends, (gain_steps, source_steps), reverse=True)
    grad_pre = gain * from_step(adjoints)
    flat_pre = grad_pre.reshape(-1, hidden)
    recur_sum = jnp.dot(flat_pre.T, prev.reshape(-1, hidden), precision=highest)
    input_sum = jnp.dot(inputs.reshape(seq_count * step_count, -1).T, flat_pre, precision=highest)
    recur_sum, input_sum = lax.psum((recur_sum, input_sum), ("seq", "batch"))
    return (trajectory, recur_sum - recur_sum.T, input_sum)


def solution(mesh):
    placed = (
        P("batch", "seq", None),
        P("batch", "seq", None),
        P(),
        P(),
        P(),
        P(),
        P("batch", "seq", None),
        P("batch", "seq"),
    )
    return jax.shard_map(
        on_device,
        mesh=mesh,
        in_specs=placed,
        out_specs=(P("batch", "seq", None), P(), P()),
        check_vma=False,
    )
```

profile of v0, /device:TPU:0, one launch (start us, length us, event | category | flops | bytes accessed | tf_op | source)
XLA Modules:
  0.0 475.6 jit_solution(12140832158586609956)
XLA Ops:
  8.0 4.8 %collective-permute-start = (f32[2,128]{1,0:T(2,128)S(1)}, f32[2,128]{1,0:T(2,128)S(1)}, u32[]{:S(2)}, u32[]{:S(2)}) collective-permute-start(f32[2,128]{1,0:T(2,128)S(1)} %bitcast.367), channel_id=1, source_target_pairs={{0,4},{4,8},{8,12},{12,16},{16,20},{20,24},{24,28},{1,5},{5,9},{9,... | collective-permute-start | bytes 3080 | tf_op jit(solution)/shard_map/ppermute | solution.py:16
  14.6 1.5 fusion.47
  16.3 2.4 add_subtract_fusion
  19.1 95.0 %while.144 = (s32[]{:T(128)}, f32[128,32,128]{2,0,1:T(8,128)S(1)}, f32[32,128]{1,0:T(8,128)S(1)}, f32[16,32,128]{2,1,0:T(8,128)S(1)}, f32[128,128]{1,0:T(8,128)S...) while((s32[]{:T(128)}, f32[128,32,128]{2,0,1:T(8,128)S(1)}, ...), condition=%wide.region_1.2_spmd.clone, body=%wide.region_0.1_spmd.clone.sunk | while | flops 813723648 | bytes 10782838 | solution.py:106
  19.3 1.8 copy.132
  21.1 3.9 multiply_add_fusion.3
  25.2 1.8 copy.132
  27.1 3.9 multiply_add_fusion.3
  31.2 1.8 copy.132
  33.0 3.9 multiply_add_fusion.3
  37.1 1.8 copy.132
  38.9 3.9 multiply_add_fusion.3
  43.0 1.8 copy.132
  44.9 3.9 multiply_add_fusion.3
  49.0 1.8 copy.132
  50.8 3.9 multiply_add_fusion.3
  54.9 1.8 copy.132
  56.7 3.9 multiply_add_fusion.3
  60.8 1.8 copy.132
  62.7 3.9 multiply_add_fusion.3
  66.8 1.8 copy.132
  68.6 3.9 multiply_add_fusion.3
  72.7 1.8 copy.132
  74.6 3.9 multiply_add_fusion.3
  78.7 1.8 copy.132
  80.5 3.9 multiply_add_fusion.3
  84.6 1.8 copy.132
  86.4 3.9 multiply_add_fusion.3
  90.5 1.8 copy.132
  92.4 3.9 multiply_add_fusion.3
  96.5 1.8 copy.132
  98.3 3.9 multiply_add_fusion.3
  102.4 1.8 copy.132
  104.2 3.9 multiply_add_fusion.3
  108.3 1.8 copy.132
  110.2 3.9 multiply_add_fusion.3
  114.1 29.5 %while.145 = (s32[]{:T(128)}, f32[128,2,128]{2,0,1:T(8,128)S(1)}, f32[2,128]{1,0:T(2,128)}, f32[16,128,2,128]{3,1,0,2:T(8,128)S(1)}, f32[16,2,128]{2,1,0:T(2,128)S(1)}, /*index=5*/s32[]{:T(128)}, s32[]{:T(128)}) while((s32[]{:T(128)}, f32[128,2,128]{2,0,1:T(8,128)S(1)}, f32[2,128]{1,0:T(2,128)}, f32[16,128,2,128]{3,1,0,2:T(8,128)S(1)}, ...), condition=%wide.region_3.4_spmd.clone, body=%wide.region_2.3_spmd.clone.sunk | while | flops 50725376 | bytes 793699 | solution.py:121
  145.2 1.3 broadcast_bitcast_fusion
  147.2 2.3 copy.74
  149.5 19.7 %all-gather.4 = f32[8,2,128]{2,1,0:T(2,128)S(1)} all-gather(f32[1,2,128]{2,1,0:T(2,128)} %bitcast.38), channel_id=3, replica_groups=mesh['seq'=8,'batch'=4] {'seq'}, dimensions={0}, use_global_device_ids=true | all-gather | bytes 9216 | tf_op jit(solution)/shard_map/all_gather | solution.py:21
  169.2 15.7 %all-gather.9.cloned.1.call-done = f32[1024,2,128]{2,0,1:T(8,128)} async-done(((f32[128,2,128]{2,0,1:T(8,128)}), f32[1024,2,128]{2,0,1:T(8,128)}) %all-gather.9.cloned.1.call-update) | async-done | bytes 1048592 | tf_op jit(solution)/shard_map/all_gather | solution.py:21
  185.0 3.1 copy.66
  188.0 8.8 %while.146 = (s32[]{:T(128)}, f32[2,128]{1,0:T(2,128)S(1)}, s32[]{:T(128)}, f32[8,128,2,128]{3,2,1,0:T(2,128)}, f32[8,2,128]{2,1,0:T(2,128)S(1)}, /*index=5*/s32[]{:T(128)}, s32[]{:T(128)}) while((s32[]{:T(128)}, f32[2,128]{1,0:T(2,128)S(1)}, s32[]{:T(128)}, f32[8,128,2,128]{3,2,1,0:T(2,128)}, f32[8,2,128]{2,1,0:T(2,128)S(1)}, ...), condition=%wide.region_5.6_spmd.clone, body=%wide.region_4.5_spmd.clone.sunk | while | flops 394244 | bytes 401514 | solution.py:33
  197.5 58.3 %while.140 = (s32[]{:T(128)}, f32[2,128]{1,0:T(2,128)}, f32[16,2,128]{2,1,0:T(2,128)}, f32[16,128,2,128]{3,1,0,2:T(8,128)S(1)}, f32[16,2,128]{2,1,0:T(2,128)}, /*index=5*/s32[]{:T(128)}) while((s32[]{:T(128)}, f32[2,128]{1,0:T(2,128)}, f32[16,2,128]{2,1,0:T(2,128)}, f32[16,128,2,128]{3,1,0,2:T(8,128)S(1)}, f32[16,2,128]{2,1,0:T(2,128)}, ...), condition=%wide.region_7.8_spmd, body=%wide.region_6.7_spmd.sunk | while | flops 393474 | bytes 663117 | solution.py:123
  199.9 1.3 bitcast_add_fusion.15
  203.5 1.3 bitcast_add_fusion.15
  207.1 1.3 bitcast_add_fusion.15
  210.8 1.3 bitcast_add_fusion.15
  214.4 1.3 bitcast_add_fusion.15
  218.1 1.3 bitcast_add_fusion.15
  221.7 1.3 bitcast_add_fusion.15
  225.4 1.3 bitcast_add_fusion.15
  256.5 13.9 %while.141 = (s32[]{:T(128)}, f32[32,128]{1,0:T(8,128)S(1)}, f32[16,32,128]{2,1,0:T(8,128)S(1)}, f32[16,32,128]{2,1,0:T(8,128)S(1)}, f32[128,128]{1,0:T(8,128)S(...) while((s32[]{:T(128)}, f32[32,128]{1,0:T(8,128)S(1)}, f32[16,32,128]{2,1,0:T(8,128)S(1)}, ...), condition=%wide.region_9.10_spmd, body=%wide.region_8.9_spmd.sunk | while | flops 6311938 | bytes 197209 | solution.py:130
  271.4 3.4 while.147
  274.8 20.2 %while.148 = (s32[]{:T(128)}, f32[2,128]{1,0:T(2,128)S(1)}, f32[16,128,2,128]{3,2,1,0:T(2,128)}, f32[16,2,128]{2,1,0:T(2,128)S(1)}, s32[]{:T(128)}, /*index=5*/s32[]{:T(128)}, s32[]{:T(128)}) while((s32[]{:T(128)}, f32[2,128]{1,0:T(2,128)S(1)}, f32[16,128,2,128]{3,2,1,0:T(2,128)}, f32[16,2,128]{2,1,0:T(2,128)S(1)}, s32[]{:T(128)}, ...), condition=%wide.region_13.14_spmd.clone, body=%wide.region_12.13_spmd.clone.sunk | while | flops 393732 | bytes 400491 | solution.py:149
  295.1 18.3 %all-gather.5 = f32[8,2,128]{2,1,0:T(2,128)S(1)} all-gather(f32[1,2,128]{2,1,0:T(2,128)S(1)} %bitcast.364), channel_id=5, replica_groups=mesh['seq'=8,'batch'=4] {'seq'}, dimensions={0}, use_global_device_ids=true | all-gather | bytes 9216 | tf_op jit(solution)/shard_map/all_gather | solution.py:21
  313.4 1.5 copy.72
  315.0 2.6 while.149
  317.6 20.1 %while.142 = (s32[]{:T(128)}, f32[2,128]{1,0:T(2,128)S(1)}, f32[16,2,128]{2,1,0:T(2,128)S(1)}, f32[16,128,2,128]{3,2,1,0:T(2,128)}, f32[16,2,128]{2,1,0:T(2,128)S(1)}, /*index=5*/s32[]{:T(128)}, s32[]{:T(128)}) while((s32[]{:T(128)}, f32[2,128]{1,0:T(2,128)S(1)}, f32[16,2,128]{2,1,0:T(2,128)S(1)}, f32[16,128,2,128]{3,2,1,0:T(2,128)}, ...), condition=%wide.region_17.18_spmd, body=%wide.region_16.17_spmd.sunk | while | flops 393475 | bytes 400485 | solution.py:154
  337.8 3.7 while.143
  341.7 1.3 convolution_bitcast_fusion.1
  344.2 120.7 %all-reduce.3.cloned.1.call-done = (f32[128,128]{1,0:T(8,128)}, f32[256,128]{0,1:T(8,128)}) async-done(((f32[128,128]{1,0:T(8,128)}, f32[256,128]{0,1:T(8,128)}), (f32[128,128]{1,0:T(8,128)}, f32[256,128]{0,1:T(8,128)})) %all-reduce.3.cloned.1.call-update) | async-done | bytes 196624 | tf_op jit(solution)/shard_map/psum | solution.py:161
  465.9 1.5 bitcast_subtract_fusion
  467.4 1.7 copy.83
  (572 shorter events, 160.5 us)
Async XLA Ops:
  7.2 7.4 %copy-start = (f32[2,256,256]{2,1,0:T(8,128)S(1)}, f32[2,256,256]{2,1,0:T(8,128)}, u32[]{:S(2)}) copy-start(f32[2,256,256]{2,1,0:T(8,128)} %param.28) | copy-start | bytes 1572868
  7.2 177.8 %all-gather.9.cloned.1.call-start = ((), (), s32[]{:S(2)}) async-start(), calls=%async_computation | async-start | bytes 1179648 | tf_op jit(solution)/shard_map/all_gather | solution.py:21
  8.0 8.3 %collective-permute-start = (f32[2,128]{1,0:T(2,128)S(1)}, f32[2,128]{1,0:T(2,128)S(1)}, u32[]{:S(2)}, u32[]{:S(2)}) collective-permute-start(f32[2,128]{1,0:T(2,128)S(1)} %bitcast.367), channel_id=1, source_target_pairs={{0,4},{4,8},{8,12},{12,16},{16,20},{20,24},{24,28},{1,5},{5,9},{9,... | collective-permute-start | bytes 3080 | tf_op jit(solution)/shard_map/ppermute | solution.py:16
  16.2 2.8 copy-start.13
  16.3 2.8 copy-start.7
  143.6 0.7 copy-start.1
  143.6 0.7 copy-start.11
  144.3 169.1 %all-gather.11.cloned.1.call-start = ((), (), s32[]{:S(2)}) async-start(), calls=%async_computation.1 | async-start | bytes 1179648 | tf_op jit(solution)/shard_map/all_gather | solution.py:21
  169.2 295.8 %all-reduce.3.cloned.1.call-start = ((), (), s32[]{:S(2)}) async-start(), calls=%async_computation.2 | async-start | bytes 393216 | tf_op jit(solution)/shard_map/psum | solution.py:161
  196.9 0.6 copy-start.6
  197.5 73.2 %copy-start.2 = (f32[2,256,128]{2,1,0:T(8,128)S(1)}, f32[2,256,128]{2,1,0:T(8,128)}, u32[]{:S(2)}) copy-start(f32[2,256,128]{2,1,0:T(8,128)} %param.29) | copy-start | bytes 786436
  255.8 14.9 %copy-start.9 = (f32[2,16,128]{2,1,0:T(8,128)S(1)}, f32[2,16,128]{2,1,0:T(8,128)}, u32[]{:S(2)}) copy-start(f32[2,16,128]{2,1,0:T(8,128)} %broadcast_bitcast_fusion) | copy-start | bytes 49156
  255.8 15.0 %copy-start.10 = (f32[2,16,16]{2,1,0:T(8,128)S(1)}, f32[2,16,16]{2,1,0:T(8,128)}, u32[]{:S(2)}) copy-start(f32[2,16,16]{2,1,0:T(8,128)} %compare_convert_fusion) | copy-start | bytes 6148
  256.5 18.3 %copy-start.12 = (f32[2,128]{1,0:T(2,128)S(1)}, f32[2,128]{1,0:T(2,128)}, u32[]{:S(2)}) copy-start(f32[2,128]{1,0:T(2,128)} %custom-call.4) | copy-start | bytes 3076
  270.5 0.7 copy-start.8
  270.7 0.7 copy-start.3
  313.4 1.6 copy-start.5
  317.6 24.0 %copy-start.4 = (f32[2,256,128]{2,1,0:T(8,128)S(1)}, f32[2,256,128]{2,1,0:T(8,128)}, u32[]{:S(2)}) copy-start(f32[2,256,128]{2,1,0:T(8,128)} %get-tuple-element.1127) | copy-start | bytes 786436
  337.7 5.2 %copy-start.14 = (f32[2,128]{1,0:T(2,128)S(1)}, f32[2,128]{1,0:T(2,128)}, u32[]{:S(2)}) copy-start(f32[2,128]{1,0:T(2,128)} %copy-done.13) | copy-start | bytes 3076
Sparse Core Ops, SparseCore 0:
  144.4 40.5 all-gather.8
  187.6 38.9 all-gather.10
  344.4 120.5 all-reduce.2
where the time goes:
time: 479 us; the launch traced here: 476 us
  waiting for transfers between devices  137 us (29%)
  matrix products  129 us (27%)
  local copies, waits for them, and re-layouts  105 us (22%)
  other arithmetic  44 us (9%)
  blocking collectives  38 us (8%)
  between operations  14.2 us (3%)
  starting transfers between devices  4.95 us (1%)
    psum x1, waiting for transfers between devices, on_device(): recur_sum, input_sum = lax.psum((recur_sum, input_sum), ('seq', 'batch'))  121 us
    dot_general x16, matrix products, compose(): jnp.dot(skew, maps.reshape(hidden, lane_count * hidden), precision=highest)  61.7 us
    all_gather x2, blocking collectives, entering(): pieces = jax.tree.map(lambda part: lax.all_gather(part, axis), value)  38 us
    while x96, local copies, waits for them, and re-layouts  29.8 us
    squeeze x32, local copies, waits for them, and re-layouts, on_device(): lax.scan(chain, (unit_stack, seq_zero), (blocks, offsets))  29.7 us
    dot_general x48, matrix products, apply_map(): jnp.einsum('isj,sj->si', block_map, carry, precision=lax.Precision.HIGHEST)  25.6 us
    add x48, other arithmetic, apply_map(): jnp.einsum('isj,sj->si', block_map, carry, precision=lax.Precision.HIGHEST)  20.5 us
    dynamic_update_slice x32, local copies, waits for them, and re-layouts, on_device(): _, starts = lax.scan(apply_map, delta_in, (blocks, offsets))  20.3 us
  transfers between devices with their start and end apart: 4, of which 2 were waited for; matrix products, arithmetic and copies ran while one was open for 24% of the time, Pallas kernels for 0%

commit v1 on v0

v1 whole, which is shorter than its diff:
```python
import functools

import jax
import jax.numpy as jnp
from jax import lax
from jax.experimental import pallas as pl
from jax.experimental.pallas import tpu as pltpu
from jax.sharding import PartitionSpec as P

LANE = 16
MIB = 1 << 20
F32 = jnp.float32
BF16 = jnp.bfloat16
SMEM = pl.BlockSpec(memory_space=pltpu.SMEM)
VMEM = pl.BlockSpec(memory_space=pltpu.VMEM)

euler_step = 0.02


def split(value):
    high = value.astype(BF16)
    return high, (value - high.astype(F32)).astype(BF16)


def left(value):
    return jnp.concatenate(split(value), axis=1)


def right(weight):
    row = jnp.concatenate(split(weight), axis=1)
    return jnp.concatenate([row, row], axis=0)


def right_t(weight):
    high, low = split(weight)
    return jnp.concatenate(
        [jnp.concatenate([high, high], axis=1), jnp.concatenate([low, low], axis=1)], axis=0
    )


def halves(wide):
    hidden = wide.shape[1] // 2
    return wide[:, :hidden] + wide[:, hidden:]


def mul(x, packed):
    return halves(jnp.dot(left(x), packed, preferred_element_type=F32))


def mul_t(x, packed):
    return halves(
        lax.dot_general(left(x), packed, (((1,), (1,)), ((), ())), preferred_element_type=F32)
    )


def mm(x, weight):
    return mul(x, right(weight))


def mm_t(x, weight):
    return mul_t(x, right_t(weight))


def eight(row):
    return jnp.broadcast_to(row, (8, row.shape[1]))


def identity(hidden):
    rows = lax.broadcasted_iota(jnp.int32, (hidden, hidden), 0)
    return (rows == lax.broadcasted_iota(jnp.int32, (hidden, hidden), 1)).astype(F32)


def drift_t(recur_ref, damping_ref):
    weight = recur_ref[...]
    return weight.T - weight - identity(weight.shape[0]) * damping_ref[...]


def compose_kernel(
    seqs, blocks, total_seqs, steps_ref, x_ref, guess_ref, edge_ref, recur_ref, damping_ref,
    in_ref, bias_ref, targets_ref,
    message_ref, maps_ref, before_ref, start_ref, hit_ref, reach_ref, reach_off_ref, gain_ref,
    resid_ref, prev_ref,
    off_ref, hit_off_ref,
):
    rows, hidden = guess_ref.shape
    count = rows // seqs
    chunks = count // LANE
    lanes = seqs * chunks
    block = count // blocks
    drift = drift_t(recur_ref, damping_ref)
    drift_w = right(drift)

    guess = guess_ref[...]
    prev_ref[pl.ds(1, rows - 1), :] = guess_ref[pl.ds(0, rows - 1), :]
    for s in range(seqs):
        prev_ref[pl.ds(s * count, 1), :] = edge_ref[pl.ds(s, 1), :]
    prev = prev_ref[...]
    x_high, x_low = split(x_ref[...])
    in_w = jnp.concatenate(split(in_ref[...]), axis=1)
    drive = halves(
        jnp.dot(x_high, in_w, preferred_element_type=F32)
        + jnp.dot(x_low, in_w, preferred_element_type=F32)
    )
    activation = jnp.tanh(mul(prev, drift_w) + drive + bias_ref[...])
    gain_ref[...] = euler_step * (1.0 - activation * activation)
    resid_ref[...] = prev + euler_step * activation - guess

    unit = identity(hidden)
    for lane in range(lanes):
        maps_ref[lane] = unit + drift * gain_ref[pl.ds(lane * LANE, 1), :]
    off_ref[...] = resid_ref[pl.ds(0, lanes, stride=LANE), :]

    def place(j):
        step = (j % blocks) * block + steps_ref[j // blocks, j % blocks]
        return (j // blocks) * chunks + step // LANE, step % LANE, (j // blocks) * count + step

    def capture(now):
        for j in range(seqs * blocks):
            lane, at, _ = place(j)

            @pl.when(at == now)
            def _():
                hit_ref[j] = maps_ref[lane]
                hit_off_ref[pl.ds(j, 1), :] = off_ref[pl.ds(lane, 1), :]

    capture(0)

    def advance(now, _):
        for lane in range(0, lanes, 2):
            pair = maps_ref[lane : lane + 2].reshape(2 * hidden, hidden)
            moved = mul(pair, drift_w)
            for k in range(2):
                gain_now = gain_ref[pl.ds((lane + k) * LANE + now, 1), :]
                part = slice(k * hidden, (k + 1) * hidden)
                maps_ref[lane + k] = pair[part] + gain_now * moved[part]
        off = off_ref[...]
        off_ref[...] = (
            off
            + gain_ref[pl.ds(now, lanes, stride=LANE), :] * mul(off, drift_w)
            + resid_ref[pl.ds(now, lanes, stride=LANE), :]
        )
        capture(now)
        return 0

    lax.fori_loop(1, LANE, advance, 0)

    running = [unit] * seqs
    offset = [jnp.zeros((8, hidden), F32)] * seqs
    for chunk in range(chunks):
        for s in range(seqs):
            lane = s * chunks + chunk
            before_ref[lane] = running[s]
            start_ref[pl.ds(lane, 1), :] = offset[s][:1]
            this, this_off = maps_ref[lane], off_ref[pl.ds(lane, 1), :]
            if chunk == 0:
                running[s], offset[s] = this, eight(this_off)
            else:
                packed = right(this)
                running[s] = mul(running[s], packed)
                offset[s] = mul(offset[s], packed) + this_off

    for s in range(seqs):
        message_ref[s, pl.ds(0, hidden), :] = running[s]
        total = jnp.zeros((hidden, hidden), F32)
        total_off = jnp.zeros((8, hidden), F32)
        for k in range(blocks):
            j = s * blocks + k
            lane, _, row = place(j)
            packed = right(hit_ref[j])
            reach = mul(before_ref[lane], packed)
            reach_off = mul(eight(start_ref[pl.ds(lane, 1), :]), packed) + hit_off_ref[pl.ds(j, 1), :]
            reach_ref[j] = reach
            miss = reach_off + guess_ref[pl.ds(row, 1), :] - targets_ref[pl.ds(j, 1), :]
            reach_off_ref[pl.ds(j, 1), :] = miss[:1]
            reach_t = right_t(reach)
            total = total + mul_t(reach, reach_t)
            total_off = total_off + mul_t(miss, reach_t)
        message_ref[s, pl.ds(hidden, hidden), :] = total / total_seqs
        message_ref[s, pl.ds(2 * hidden, 8), :] = jnp.concatenate(
            [offset[s][:1], total_off[:1] / total_seqs, jnp.zeros((6, hidden), F32)], axis=0
        )


def join(first, second, hidden, with_map):
    map_1, curve_1, off_1, adj_1 = first
    map_2, curve_2, off_2, adj_2 = second
    curve_w = right(curve_2)
    map_1_t = right_t(map_1)
    curve = curve_1 + mul_t(mul(map_1, curve_w), map_1_t)
    adj = adj_1 + mul_t(mul(off_1, curve_w) + adj_2, map_1_t)
    map_w = right(map_2)
    off = mul(off_1, map_w) + off_2
    return (mul(map_1, map_w) if with_map else None), curve, off, adj


def opened(ref, s, hidden):
    return (
        ref[s, pl.ds(0, hidden), :],
        ref[s, pl.ds(hidden, hidden), :],
        eight(ref[s, pl.ds(2 * hidden, 1), :]),
        eight(ref[s, pl.ds(2 * hidden + 1, 1), :]),
    )


def pick(flag, one, other):
    return tuple(jnp.where(flag, a, b) for a, b in zip(one, other))


def vector_rows(off, adj):
    return jnp.concatenate([off[:1], adj[:1], jnp.zeros((6, off.shape[1]), F32)], axis=0)


def join_kernel(level, with_map, place_ref, mine_ref, other_ref, out_ref):
    seqs, hidden = mine_ref.shape[0], mine_ref.shape[2]
    upper = (place_ref[0] >> level) & 1 == 1
    for s in range(seqs):
        mine, other = opened(mine_ref, s, hidden), opened(other_ref, s, hidden)
        result = join(pick(upper, other, mine), pick(upper, mine, other), hidden, with_map)
        at = 0
        if with_map:
            out_ref[s, pl.ds(0, hidden), :] = result[0]
            at = hidden
        out_ref[s, pl.ds(at, hidden), :] = result[1]
        out_ref[s, pl.ds(at + hidden, 8), :] = vector_rows(result[2], result[3])


def sides_kernel(levels, place_ref, *refs):
    received, (before_ref, after_ref) = refs[:levels], refs[levels:]
    seqs, hidden = before_ref.shape[0], before_ref.shape[2]
    for s in range(seqs):
        zero = jnp.zeros((8, hidden), F32)
        unit = identity(hidden)
        blank = jnp.zeros((hidden, hidden), F32)
        before = (unit, zero)
        after = (unit, blank, zero, zero)
        for level in range(levels):
            upper = (place_ref[0] >> level) & 1 == 1
            other = opened(received[level], s, hidden)
            if level == 0:
                longer, extended = (other[0], other[2]), other
            else:
                packed = right(before[0])
                longer = (mul(other[0], packed), mul(other[2], packed) + before[1])
                extended = join(after, other, hidden, True)
            before = pick(upper, longer, before)
            after = pick(upper, after, extended)
        before_ref[s, pl.ds(0, hidden), :] = before[0]
        before_ref[s, pl.ds(hidden, 8), :] = vector_rows(before[1], zero)
        after_ref[s, pl.ds(0, hidden), :] = after[0]
        after_ref[s, pl.ds(hidden, hidden), :] = after[1]
        after_ref[s, pl.ds(2 * hidden, 8), :] = vector_rows(after[2], after[3])


def solve_kernel(
    seqs, blocks, total_seqs, level, place_ref, steps_ref, message_ref, mine_ref, other_ref,
    sides_before_ref, sides_after_ref, maps_ref, before_ref, start_ref, hit_ref, reach_ref,
    reach_off_ref, gain_ref, resid_ref, prev_ref, guess_ref, x_ref, recur_ref, damping_ref,
    path_ref, grads_ref,
    state_ref, carry_ref, source_ref, pre_ref,
):
    rows, hidden = guess_ref.shape
    count = rows // seqs
    chunks = count // LANE
    lanes = seqs * chunks
    block = count // blocks
    upper = (place_ref[0] >> level) & 1 == 1
    drift = drift_t(recur_ref, damping_ref)
    drift_w = right(drift)
    drift_wt = right_t(drift)
    source_ref[...] = jnp.zeros_like(source_ref)

    entry, tail, pulls = [], [], []
    for s in range(seqs):
        mine_off = eight(mine_ref[s, pl.ds(hidden, 1), :])
        other_off = eight(other_ref[s, pl.ds(hidden, 1), :])
        lead, lead_off = sides_before_ref[s, pl.ds(0, hidden), :], eight(sides_before_ref[s, pl.ds(hidden, 1), :])
        state = jnp.where(upper, mm(other_off, lead) + lead_off, lead_off)
        entry.append(state)
        beyond = mm(mine_off, other_ref[s, pl.ds(0, hidden), :]) + other_ref[s, pl.ds(hidden + 1, 1), :]
        beyond = jnp.where(upper, jnp.zeros_like(beyond), beyond)
        dev_map, _, dev_off, _ = opened(message_ref, s, hidden)
        leaving = mm(state, dev_map) + dev_off
        after_map, after_curve, _, after_adj = opened(sides_after_ref, s, hidden)
        tail.append(mm(leaving, after_curve) + after_adj + mm_t(beyond, after_map))

    for s in range(seqs):
        for k in range(blocks):
            j = s * blocks + k
            step = k * block + steps_ref[s, k]
            miss = (mm(entry[s], reach_ref[j]) + reach_off_ref[pl.ds(j, 1), :]) / total_seqs
            source_ref[pl.ds(s * count + step, 1), :] = miss[:1]
            pulls.append((s, step // LANE, mm_t(miss, hit_ref[j])))
        for chunk in range(chunks):
            lane = s * chunks + chunk
            if chunk == 0:
                state_ref[pl.ds(lane, 1), :] = entry[s][:1]
            else:
                state_ref[pl.ds(lane, 1), :] = (
                    mm(entry[s], before_ref[lane])[:1] + start_ref[pl.ds(lane, 1), :]
                )
    state = state_ref[...]
    for now in range(LANE):
        at = pl.ds(now, lanes, stride=LANE)
        state = state + gain_ref[at, :] * mul(state, drift_w) + resid_ref[at, :]
        path_ref[at, :] = guess_ref[at, :] + state

    for chunk in reversed(range(chunks)):
        for s in range(seqs):
            lane = s * chunks + chunk
            carry_ref[pl.ds(lane, 1), :] = tail[s][:1]
            if chunk:
                carry = mm_t(tail[s], maps_ref[lane])
                for owner, at, pull in pulls:
                    if owner == s:
                        carry = carry + jnp.where(at == chunk, pull, jnp.zeros_like(pull))
                tail[s] = carry
    carry = carry_ref[...]
    for now in reversed(range(LANE)):
        at = pl.ds(now, lanes, stride=LANE)
        adjoint = source_ref[at, :] + carry
        scaled = gain_ref[at, :] * adjoint
        pre_ref[at, :] = scaled
        if now:
            carry = adjoint + mul_t(scaled, drift_wt)

    pre_high, pre_low = split(pre_ref[...])

    def gathered(value):
        high, low = split(value)
        flat = (((0,), (0,)), ((), ()))
        return (
            lax.dot_general(high, pre_high, flat, preferred_element_type=F32)
            + lax.dot_general(high, pre_low, flat, preferred_element_type=F32)
            + lax.dot_general(low, pre_high, flat, preferred_element_type=F32)
        )

    recur = gathered(prev_ref[...])
    recur = recur.T - recur
    half = hidden // 2
    row = lax.broadcasted_iota(jnp.int32, (half, half), 0)
    col = lax.broadcasted_iota(jnp.int32, (half, half), 1)
    folded = jnp.where(col > row, recur[:half, :half], recur[half:, half:])
    grads_ref[pl.ds(0, half), :] = jnp.concatenate([folded, recur[:half, half:]], axis=1)
    grads_ref[pl.ds(half, x_ref.shape[1]), :] = gathered(x_ref[...])


def unfold_kernel(place_ref, mine_ref, other_ref, recur_ref, in_ref):
    hidden = recur_ref.shape[0]
    half = hidden // 2
    odd = place_ref[1] & 1 == 1
    mine, other = mine_ref[...], other_ref[...]
    whole = jnp.concatenate([jnp.where(odd, other, mine), jnp.where(odd, mine, other)], axis=0)
    in_ref[...] = whole[half:]
    row = lax.broadcasted_iota(jnp.int32, (half, half), 0)
    col = lax.broadcasted_iota(jnp.int32, (half, half), 1)
    folded, corner = whole[:half, :half], whole[:half, half:]
    first = jnp.where(col > row, folded, 0.0)
    last = jnp.where(col < row, folded, 0.0)
    recur_ref[pl.ds(0, half), :] = jnp.concatenate([first - first.T, corner], axis=1)
    recur_ref[pl.ds(half, half), :] = jnp.concatenate([-corner.T, last - last.T], axis=1)


def call(kernel, shapes, specs, scratch=(), flops=0, room=24):
    return pl.pallas_call(
        kernel,
        out_shape=[jax.ShapeDtypeStruct(shape, F32) for shape in shapes],
        in_specs=specs,
        out_specs=[VMEM] * len(shapes),
        scratch_shapes=[pltpu.VMEM(shape, F32) for shape in scratch],
        compiler_params=pltpu.CompilerParams(vmem_limit_bytes=room * MIB),
        cost_estimate=pl.CostEstimate(flops=flops, bytes_accessed=1 << 20, transcendentals=0),
    )


def swapped(value, axis, distance):
    return lax.ppermute(value, axis, [(i, i ^ distance) for i in range(lax.axis_size(axis))])


def levels_of(axis):
    return lax.axis_size(axis).bit_length() - 1


def on_device(
    inputs, guess_path, recur_weight, damping, in_weight, bias_term, targets, target_steps
):
    seqs, count, hidden = guess_path.shape
    blocks = targets.shape[1]
    features = inputs.shape[2]
    rows = seqs * count
    lanes = rows // LANE
    hits = seqs * blocks
    total_seqs = seqs * lax.axis_size("batch")
    place = jnp.stack([lax.axis_index("seq"), lax.axis_index("batch")]).astype(jnp.int32)
    route = [(i, i + 1) for i in range(lax.axis_size("seq") - 1)]
    edge = lax.ppermute(guess_path[:, count - 1, :], "seq", route)
    x = inputs.reshape(rows, features)
    guess = guess_path.reshape(rows, hidden)
    damping = damping.reshape(1, hidden)

    message, maps, before, start, hit, reach, reach_off, gain, resid, prev = call(
        functools.partial(compose_kernel, seqs, blocks, total_seqs),
        [
            (seqs, 2 * hidden + 8, hidden),
            (lanes, hidden, hidden),
            (lanes, hidden, hidden),
            (lanes, hidden),
            (hits, hidden, hidden),
            (hits, hidden, hidden),
            (hits, hidden),
            (rows, hidden),
            (rows, hidden),
            (rows, hidden),
        ],
        [SMEM] + [VMEM] * 8,
        [(lanes, hidden), (hits, hidden)],
    )(target_steps, x, guess, edge, recur_weight, damping, in_weight, bias_term.reshape(1, hidden),
      targets.reshape(hits, hidden))

    levels = levels_of("seq")
    group, received = message, []
    for level in range(levels - 1):
        other = swapped(group, "seq", 1 << level)
        received.append(other)
        with_map = level < levels - 2
        height = (2 if with_map else 1) * hidden + 8
        (group,) = call(
            functools.partial(join_kernel, level, with_map),
            [(seqs, height, hidden)],
            [SMEM, VMEM, VMEM],
        )(place, group, other)
    other = swapped(group, "seq", 1 << (levels - 1))
    sides_before, sides_after = call(
        functools.partial(sides_kernel, levels - 1),
        [(seqs, hidden + 8, hidden), (seqs, 2 * hidden + 8, hidden)],
        [SMEM] + [VMEM] * (levels - 1),
        flops=1 << 30,
    )(place, *received)

    path, grads = call(
        functools.partial(solve_kernel, seqs, blocks, total_seqs, levels - 1),
        [(rows, hidden), (hidden // 2 + features, hidden)],
        [SMEM, SMEM] + [VMEM] * 18,
        [(lanes, hidden), (lanes, hidden), (rows, hidden), (rows, hidden)],
    )(place, target_steps, message, group, other, sides_before, sides_after, maps, before, start,
      hit, reach, reach_off, gain, resid, prev, guess, x, recur_weight, damping)

    middle = grads.shape[0] // 2
    odd = place[1] & 1 == 1
    kept = jnp.where(odd, grads[middle:], grads[:middle])
    given = jnp.where(odd, grads[:middle], grads[middle:])
    kept = kept + swapped(given, "batch", 1)
    for level in range(1, levels_of("batch")):
        kept = kept + swapped(kept, "batch", 1 << level)
    for level in range(levels):
        kept = kept + swapped(kept, "seq", 1 << level)
    grad_recur, grad_in = call(
        unfold_kernel,
        [(hidden, hidden), (features, hidden)],
        [SMEM, VMEM, VMEM],
    )(place, kept, swapped(kept, "batch", 1))
    return (path.reshape(seqs, count, hidden), grad_recur, grad_in)


def solution(mesh):
    placed = (
        P("batch", "seq", None),
        P("batch", "seq", None),
        P(),
        P(),
        P(),
        P(),
        P("batch", "seq", None),
        P("batch", "seq"),
    )
    return jax.shard_map(
        on_device,
        mesh=mesh,
        in_specs=placed,
        out_specs=(P("batch", "seq", None), P(), P()),
        check_vma=False,
    )
```

time: 479 us -> 92 us (0.19)
  matrix products: 129 us -> 0 us
  waiting for transfers between devices: 137 us -> 27.8 us
  local copies, waits for them, and re-layouts: 105 us -> 14.9 us
  other arithmetic: 44 us -> 0.15 us
  blocking collectives: 38 us -> 0 us
  Pallas kernels: 0 us -> 28.6 us
  starting transfers between devices: 4.95 us -> 19.2 us
  between operations: 14.2 us -> 0.87 us
    dot_general x178 -> x0, matrix products: 129 us -> none  [the longest x16 61.7 us: compose(): jnp.dot(skew, maps.reshape(hidden, lane_count * hidden), precision=highest)]
    psum x1 -> x0, waiting for transfers between devices: 121 us -> none  [on_device(): recur_sum, input_sum = lax.psum((recur_sum, input_sum), ('seq', 'batch'))]
    all_gather x2 -> x0, blocking collectives: 38 us -> none  [entering(): pieces = jax.tree.map(lambda part: lax.all_gather(part, axis), value)]
    squeeze x46 -> x0, local copies, waits for them, and re-layouts: 36.3 us -> none  [the longest x32 29.7 us: on_device(): lax.scan(chain, (unit_stack, seq_zero), (blocks, offsets))]
    add x65 -> x5, other arithmetic: 29.9 us -> 0.06 us  [the longest x3 0.03 us: on_device(): kept = kept + swapped(kept, 'seq', 1 << level)]
    while x96 -> x0, local copies, waits for them, and re-layouts: 29.8 us -> none
    pallas_call x0 -> x6, Pallas kernels: none -> 28.6 us  [the longest x1 15.7 us: on_device(): call(functools.partial(compose_kernel, seqs, blocks, total_seqs), [(seqs,...]
    ppermute x1 -> x10, waiting for transfers between devices: 0.01 us -> 27.8 us  [the longest x9 26.5 us: swapped(): lax.ppermute(value, axis, [(i, i ^ distance) for i in range(lax.axis_size...]
  transfers between devices with their start and end apart: 4 -> 10, of which waited for: 2 -> 10; matrix products, arithmetic and copies ran while one was open for 24% -> 0% of each run, Pallas kernels for 0% -> 1%
where the time goes in v1:
time: 92 us; the launch traced here: 91.5 us
  Pallas kernels  28.6 us (31%)
  waiting for transfers between devices  27.8 us (30%)
  starting transfers between devices  19.2 us (21%)
  local copies, waits for them, and re-layouts  14.9 us (16%)
    ppermute x9, waiting for transfers between devices, swapped(): lax.ppermute(value, axis, [(i, i ^ distance) for i in range(lax.axis_size...  26.5 us
    pallas_call x1, Pallas kernels, on_device(): call(functools.partial(compose_kernel, seqs, blocks, total_seqs), [(seqs,...  15.7 us
    ppermute x9, starting transfers between devices, swapped(): lax.ppermute(value, axis, [(i, i ^ distance) for i in range(lax.axis_size...  14.4 us
    unnamed x58, local copies, waits for them, and re-layouts  14.2 us
    pallas_call x1, Pallas kernels, on_device(): call(functools.partial(solve_kernel, seqs, blocks, total_seqs, levels - 1...  8.12 us
    ppermute x1, starting transfers between devices, on_device(): edge = lax.ppermute(guess_path[:, count - 1, :], 'seq', route)  4.83 us
    pallas_call x2, Pallas kernels, on_device(): call(functools.partial(join_kernel, level, with_map), [(seqs, height, hid...  2.19 us
  transfers between devices with their start and end apart: 10, of which 10 were waited for; matrix products, arithmetic and copies ran while one was open for 0% of the time, Pallas kernels for 1%

profile of v1, /device:TPU:0, one launch (start us, length us, event | category | flops | bytes accessed | tf_op | source)
XLA Modules:
  0.0 91.5 jit_solution(3309702944373789657)
XLA Ops:
  0.6 0.7 slice.11
  1.3 4.8 %collective-permute-start = (f32[2,128]{1,0:T(2,128)S(1)}, f32[2,128]{1,0:T(2,128)S(1)}, u32[]{:S(2)}, u32[]{:S(2)}) collective-permute-start(f32[2,128]{1,0:T(2,128)S(1)} %bitcast.19), channel_id=1, source_target_pairs={{0,4},{4,8},{8,12},{12,16},{16,20},{20,24},{24,28},{1,5},{5,9},{9,... | collective-permute-start | bytes 3080 | tf_op jit(solution)/shard_map/ppermute | solution.py:395
  6.2 1.3 %collective-permute-done.edge_ref = f32[2,128]{1,0:T(2,128)S(1)} collective-permute-done((f32[2,128]{1,0:T(2,128)S(1)}, f32[2,128]{1,0:T(2,128)S(1)}, u32[]{:S(2)}, u32[]{:S(2)}) %collective-permute-start) | collective-permute-done | bytes 1056 | tf_op jit(solution)/shard_map/ppermute | solution.py:395
  7.5 0.0 copy-start.2
  7.5 1.0 %copy-done.2 = f32[2,256,256]{2,1,0:T(8,128)S(1)} copy-done((f32[2,256,256]{2,1,0:T(8,128)S(1)}, f32[2,256,256]{2,1,0:T(8,128)}, u32[]{:S(2)}) %copy-start.2) | copy-done | bytes 524312
  8.5 0.9 %copy-done.4 = f32[2,256,128]{2,1,0:T(8,128)S(1)} copy-done((f32[2,256,128]{2,1,0:T(8,128)S(1)}, f32[2,256,128]{2,1,0:T(8,128)}, u32[]{:S(2)}) %copy-start.4) | copy-done | bytes 262168
  9.4 0.8 copy-done.10
  10.3 0.9 copy-done.22
  11.2 0.7 copy-done.23
  11.9 0.7 copy-done.25
  12.6 0.7 copy-done.26
  13.2 0.7 copy-done.28
  13.9 15.7 %shard_map.103 = (f32[2,264,128]{2,1,0:T(8,128)S(1)}, f32[32,128,128]{2,1,0:T(8,128)S(1)}, f32[32,128,128]{2,1,0:T(8,128)S(1)}, f32[32,128]{1,0:T(8,128)S(1)}, f...) custom-call(s32[2,2]{1,0:T(2,128)S(1)} %copy-done.23, ...), custom_call_target="tpu_custom_call" | custom-call | bytes 1048576 | tf_op jit(solution)/shard_map/pallas_call | solution.py:400
  29.6 0.0 copy-start
  29.6 1.4 %copy-done = f32[32,128,128]{2,1,0:T(8,128)} copy-done((f32[32,128,128]{2,1,0:T(8,128)}, f32[32,128,128]{2,1,0:T(8,128)S(1)}, u32[]{:S(2)}) %copy-start) | copy-done | bytes 2097176
  31.0 0.7 copy-done.12
  31.7 0.7 copy-done.14
  32.4 0.7 copy-done.16
  33.1 0.7 copy-done.18
  33.8 0.7 copy-done.20
  34.5 2.3 %collective-permute-start.1 = (f32[2,264,128]{2,1,0:T(8,128)S(1)}, f32[2,264,128]{2,1,0:T(8,128)S(1)}, u32[]{:S(2)}, u32[]{:S(2)}) collective-permute-start(f32[2,264,128]{2,1,0:T(8,128)S(1)} %get-tuple-element.19.mine_ref.message_ref), channel_id=1, source_target_pairs={{0,4},{4,0},{8,12},{12,8},{16,20},{20,16},{24,28},{28,24},{1,5},{5... | collective-permute-start | bytes 811016 | tf_op jit(solution)/shard_map/ppermute | solution.py:376
  36.7 0.1 pad_add_fusion.place_ref
  36.8 5.3 %collective-permute-done.1.other_ref.refs_0_ = f32[2,264,128]{2,1,0:T(8,128)S(1)} collective-permute-done((f32[2,264,128]{2,1,0:T(8,128)S(1)}, f32[2,264,128]{2,1,0:T(8,128)S(1)}, u32[]{:S(2)}, u32[]{:S(2)}) %collective-permute-start.1) | collective-permute-done | bytes 270368 | tf_op jit(solution)/shard_map/ppermute | solution.py:376
  42.1 1.1 %shard_map.104.mine_ref = f32[2,264,128]{2,1,0:T(8,128)S(1)} custom-call(s32[2]{0:T(128)S(1)} %pad_add_fusion.place_ref, f32[2,264,128]{2,1,0:T(8,128)S(1)} %get-tuple-element.19.mine_ref.message_ref, f32[2,264,128]{2,1,0:T(8,128)S(1)} %collective-permute-done.1.other_ref.refs_0_), custom_call_target="tpu_custom_call" | custom-call | bytes 1048576 | tf_op jit(solution)/shard_map/pallas_call | solution.py:426
  43.2 2.8 %collective-permute-start.2 = (f32[2,264,128]{2,1,0:T(8,128)S(1)}, f32[2,264,128]{2,1,0:T(8,128)S(1)}, u32[]{:S(2)}, u32[]{:S(2)}) collective-permute-start(f32[2,264,128]{2,1,0:T(8,128)S(1)} %shard_map.104.mine_ref), channel_id=1, source_target_pairs={{0,8},{4,12},{8,0},{12,4},{16,24},{20,28},{24,16},{28,20},{1,9},{5... | collective-permute-start | bytes 811016 | tf_op jit(solution)/shard_map/ppermute | solution.py:376
  46.0 4.4 %collective-permute-done.2.other_ref.refs_1_ = f32[2,264,128]{2,1,0:T(8,128)S(1)} collective-permute-done((f32[2,264,128]{2,1,0:T(8,128)S(1)}, f32[2,264,128]{2,1,0:T(8,128)S(1)}, u32[]{:S(2)}, u32[]{:S(2)}) %collective-permute-start.2) | collective-permute-done | bytes 270368 | tf_op jit(solution)/shard_map/ppermute | solution.py:376
  50.5 0.0 copy-done.8
  50.5 0.0 copy-start.27
  50.5 1.1 %shard_map.105.mine_ref = f32[2,136,128]{2,1,0:T(8,128)S(1)} custom-call(s32[2]{0:T(128)S(1)} %pad_add_fusion.place_ref, f32[2,264,128]{2,1,0:T(8,128)S(1)} %shard_map.104.mine_ref, f32[2,264,128]{2,1,0:T(8,128)S(1)} %collective-permute-done.2.other_ref.refs_1_), custom_call_target="tpu_custom_call" | custom-call | bytes 1048576 | tf_op jit(solution)/shard_map/pallas_call | solution.py:426
  51.6 0.0 copy-done.6
  51.6 0.0 copy-start.3
  51.6 0.0 copy-start.5
  51.6 3.1 %collective-permute-start.3 = (f32[2,136,128]{2,1,0:T(8,128)S(1)}, f32[2,136,128]{2,1,0:T(8,128)S(1)}, u32[]{:S(2)}, u32[]{:S(2)}) collective-permute-start(f32[2,136,128]{2,1,0:T(8,128)S(1)} %shard_map.105.mine_ref), channel_id=1, source_target_pairs={{0,16},{4,20},{8,24},{12,28},{16,0},{20,4},{24,8},{28,12},{1,17},{... | collective-permute-start | bytes 417800 | tf_op jit(solution)/shard_map/ppermute | solution.py:376
  54.7 1.0 %copy-done.7 = f32[2,264,128]{2,1,0:T(8,128)S(1)} copy-done((f32[2,264,128]{2,1,0:T(8,128)S(1)}, f32[2,264,128]{2,1,0:T(8,128)}, u32[]{:S(2)}) %copy-start.7) | copy-done | bytes 270360
  55.6 1.0 %copy-done.9 = f32[2,264,128]{2,1,0:T(8,128)S(1)} copy-done((f32[2,264,128]{2,1,0:T(8,128)S(1)}, f32[2,264,128]{2,1,0:T(8,128)}, u32[]{:S(2)}) %copy-start.9) | copy-done | bytes 270360
  56.6 0.0 copy-start.19
  56.6 1.2 %shard_map.106 = (f32[2,136,128]{2,1,0:T(8,128)S(1)}, f32[2,264,128]{2,1,0:T(8,128)S(1)}) custom-call(s32[2]{0:T(128)S(1)} %pad_add_fusion.place_ref, f32[2,264,128]{2,1,0:T(8,128)S(1)} %copy-done.9, f32[2,264,128]{2,1,0:T(8,128)S(1)} %copy-done.7), custom_call_target="tpu_custom_call" | custom-call | flops 1073741824 | bytes 1048576 | tf_op jit(solution)/shard_map/pallas_call | solution.py:432
  57.8 1.4 %collective-permute-done.3.other_ref = f32[2,136,128]{2,1,0:T(8,128)S(1)} collective-permute-done((f32[2,136,128]{2,1,0:T(8,128)S(1)}, f32[2,136,128]{2,1,0:T(8,128)S(1)}, u32[]{:S(2)}, u32[]{:S(2)}) %collective-permute-start.3) | collective-permute-done | bytes 139296 | tf_op jit(solution)/shard_map/ppermute | solution.py:376
  59.2 0.0 copy-done.11
  59.2 0.0 copy-done.24
  59.2 0.0 copy-done.27
  59.2 0.0 copy-done.3
  59.2 0.0 copy-done.5
  59.2 0.0 copy-done.1
  59.2 0.0 copy-done.13
  59.3 0.0 copy-done.15
  59.3 0.0 copy-done.17
  59.3 0.0 copy-done.19
  59.3 0.0 copy-start.21
  59.3 0.9 %copy-done.21 = f32[512,128]{1,0:T(8,128)S(1)} copy-done((f32[512,128]{1,0:T(8,128)S(1)}, f32[512,128]{1,0:T(8,128)}, u32[]{:S(2)}) %copy-start.21) | copy-done | bytes 262168
  60.2 8.1 %shard_map.107 = (f32[512,128]{1,0:T(8,128)}, f32[320,128]{1,0:T(8,128)S(1)}) custom-call(s32[2]{0:T(128)S(1)} %pad_add_fusion.place_ref, s32[2,2]{1,0:T(2,128)S(1)} %copy-done.24, f32[2,264,128]{2,1,0:T(8,128)S(1)} %get-tuple-element.19.mine_ref.message_ref, f32[2,136,128]{2,1,0:T(8,128)S(1)} %shard_map.105.mine_ref, ...), custom_call_target="tpu_custom_call" | custom-call | bytes 1048576 | tf_op jit(solution)/shard_map/pallas_call | solution.py:439
  68.4 0.1 collective-permute-start.4
  68.5 1.3 %collective-permute-done.4 = f32[160,128]{1,0:T(8,128)S(1)} collective-permute-done((f32[160,128]{1,0:T(8,128)S(1)}, f32[160,128]{1,0:T(8,128)S(1)}, u32[]{:S(2)}, u32[]{:S(2)}) %collective-permute-start.4) | collective-permute-done | bytes 81952 | tf_op jit(solution)/shard_map/ppermute | solution.py:376
  69.8 1.6 %collective-permute-start.5 = (f32[160,128]{1,0:T(8,128)S(1)}, f32[160,128]{1,0:T(8,128)S(1)}, u32[]{:S(2)}, u32[]{:S(2)}) collective-permute-start(f32[160,128]{1,0:T(8,128)S(1)} %select_add_fusion), channel_id=1, source_target_pairs={{0,2},{1,3},{2,0},{3,1},{4,6},{5,7},{6,4},{7,5},{8,10},{9,11},{10,... | collective-permute-start | bytes 245768 | tf_op jit(solution)/shard_map/ppermute | solution.py:376
  71.3 3.0 %collective-permute-done.5 = f32[160,128]{1,0:T(8,128)S(1)} collective-permute-done((f32[160,128]{1,0:T(8,128)S(1)}, f32[160,128]{1,0:T(8,128)S(1)}, u32[]{:S(2)}, u32[]{:S(2)}) %collective-permute-start.5) | collective-permute-done | bytes 81952 | tf_op jit(solution)/shard_map/ppermute | solution.py:376
  74.3 1.0 %collective-permute-start.6 = (f32[160,128]{1,0:T(8,128)S(1)}, f32[160,128]{1,0:T(8,128)S(1)}, u32[]{:S(2)}, u32[]{:S(2)}) collective-permute-start(f32[160,128]{1,0:T(8,128)S(1)} %add.16), channel_id=1, source_target_pairs={{0,4},{4,0},{8,12},{12,8},{16,20},{20,16},{24,28},{28,24},{1,5},{5... | collective-permute-start | bytes 245768 | tf_op jit(solution)/shard_map/ppermute | solution.py:376
  75.3 3.5 %collective-permute-done.6 = f32[160,128]{1,0:T(8,128)S(1)} collective-permute-done((f32[160,128]{1,0:T(8,128)S(1)}, f32[160,128]{1,0:T(8,128)S(1)}, u32[]{:S(2)}, u32[]{:S(2)}) %collective-permute-start.6) | collective-permute-done | bytes 81952 | tf_op jit(solution)/shard_map/ppermute | solution.py:376
  78.9 1.1 %collective-permute-start.7 = (f32[160,128]{1,0:T(8,128)S(1)}, f32[160,128]{1,0:T(8,128)S(1)}, u32[]{:S(2)}, u32[]{:S(2)}) collective-permute-start(f32[160,128]{1,0:T(8,128)S(1)} %add.17), channel_id=1, source_target_pairs={{0,8},{4,12},{8,0},{12,4},{16,24},{20,28},{24,16},{28,20},{1,9},{5... | collective-permute-start | bytes 245768 | tf_op jit(solution)/shard_map/ppermute | solution.py:376
  79.9 3.4 %collective-permute-done.7 = f32[160,128]{1,0:T(8,128)S(1)} collective-permute-done((f32[160,128]{1,0:T(8,128)S(1)}, f32[160,128]{1,0:T(8,128)S(1)}, u32[]{:S(2)}, u32[]{:S(2)}) %collective-permute-start.7) | collective-permute-done | bytes 81952 | tf_op jit(solution)/shard_map/ppermute | solution.py:376
  83.4 2.5 %collective-permute-start.8 = (f32[160,128]{1,0:T(8,128)S(1)}, f32[160,128]{1,0:T(8,128)S(1)}, u32[]{:S(2)}, u32[]{:S(2)}) collective-permute-start(f32[160,128]{1,0:T(8,128)S(1)} %add.18), channel_id=1, source_target_pairs={{0,16},{4,20},{8,24},{12,28},{16,0},{20,4},{24,8},{28,12},{1,17},{... | collective-permute-start | bytes 245768 | tf_op jit(solution)/shard_map/ppermute | solution.py:376
  85.8 2.9 %collective-permute-done.8 = f32[160,128]{1,0:T(8,128)S(1)} collective-permute-done((f32[160,128]{1,0:T(8,128)S(1)}, f32[160,128]{1,0:T(8,128)S(1)}, u32[]{:S(2)}, u32[]{:S(2)}) %collective-permute-start.8) | collective-permute-done | bytes 81952 | tf_op jit(solution)/shard_map/ppermute | solution.py:376
  88.8 0.1 collective-permute-start.9
  88.9 1.3 %collective-permute-done.9.other_ref = f32[160,128]{1,0:T(8,128)S(1)} collective-permute-done((f32[160,128]{1,0:T(8,128)S(1)}, f32[160,128]{1,0:T(8,128)S(1)}, u32[]{:S(2)}, u32[]{:S(2)}) %collective-permute-start.9) | collective-permute-done | bytes 81952 | tf_op jit(solution)/shard_map/ppermute | solution.py:376
  90.1 1.4 %shard_map.108 = (f32[128,128]{1,0:T(8,128)}, f32[256,128]{1,0:T(8,128)}) custom-call(s32[2]{0:T(128)S(1)} %pad_add_fusion.place_ref, f32[160,128]{1,0:T(8,128)S(1)} %add.19.mine_ref, f32[160,128]{1,0:T(8,128)S(1)} %collective-permute-done.9.other_ref), custom_call_target="tpu_custom_call" | custom-call | bytes 1048576 | tf_op jit(solution)/shard_map/pallas_call | solution.py:456
  (28 shorter events, 0.1 us)
Async XLA Ops:
  1.3 6.1 %collective-permute-start = (f32[2,128]{1,0:T(2,128)S(1)}, f32[2,128]{1,0:T(2,128)S(1)}, u32[]{:S(2)}, u32[]{:S(2)}) collective-permute-start(f32[2,128]{1,0:T(2,128)S(1)} %bitcast.19), channel_id=1, source_target_pairs={{0,4},{4,8},{8,12},{12,16},{16,20},{20,24},{24,28},{1,5},{5,9},{9,... | collective-permute-start | bytes 3080 | tf_op jit(solution)/shard_map/ppermute | solution.py:395
  7.5 1.0 %copy-start.2 = (f32[2,256,256]{2,1,0:T(8,128)S(1)}, f32[2,256,256]{2,1,0:T(8,128)}, u32[]{:S(2)}) copy-start(f32[2,256,256]{2,1,0:T(8,128)} %param.8) | copy-start | bytes 1572868
  8.5 0.9 %copy-start.4 = (f32[2,256,128]{2,1,0:T(8,128)S(1)}, f32[2,256,128]{2,1,0:T(8,128)}, u32[]{:S(2)}) copy-start(f32[2,256,128]{2,1,0:T(8,128)} %param.9) | copy-start | bytes 786436
  9.4 0.8 copy-start.10
  10.3 0.9 copy-start.22
  11.2 0.7 copy-start.23
  11.9 0.7 copy-start.25
  12.6 0.7 copy-start.26
  13.2 0.7 copy-start.28
  29.6 1.4 %copy-start = (f32[32,128,128]{2,1,0:T(8,128)}, f32[32,128,128]{2,1,0:T(8,128)S(1)}, u32[]{:S(2)}) copy-start(f32[32,128,128]{2,1,0:T(8,128)S(1)} %get-tuple-element.23.before_ref) | copy-start | bytes 6291460
  31.0 0.7 copy-start.12
  31.7 0.7 copy-start.14
  32.4 0.7 copy-start.16
  33.1 0.7 copy-start.18
  33.8 0.7 copy-start.20
  34.5 7.6 %collective-permute-start.1 = (f32[2,264,128]{2,1,0:T(8,128)S(1)}, f32[2,264,128]{2,1,0:T(8,128)S(1)}, u32[]{:S(2)}, u32[]{:S(2)}) collective-permute-start(f32[2,264,128]{2,1,0:T(8,128)S(1)} %get-tuple-element.19.mine_ref.message_ref), channel_id=1, source_target_pairs={{0,4},{4,0},{8,12},{12,8},{16,20},{20,16},{24,28},{28,24},{1,5},{5... | collective-permute-start | bytes 811016 | tf_op jit(solution)/shard_map/ppermute | solution.py:376
  42.1 8.4 %copy-start.8 = (f32[2,264,128]{2,1,0:T(8,128)}, f32[2,264,128]{2,1,0:T(8,128)S(1)}, u32[]{:S(2)}) copy-start(f32[2,264,128]{2,1,0:T(8,128)S(1)} %collective-permute-done.1.other_ref.refs_0_) | copy-start | bytes 811012
  43.2 7.3 %collective-permute-start.2 = (f32[2,264,128]{2,1,0:T(8,128)S(1)}, f32[2,264,128]{2,1,0:T(8,128)S(1)}, u32[]{:S(2)}, u32[]{:S(2)}) collective-permute-start(f32[2,264,128]{2,1,0:T(8,128)S(1)} %shard_map.104.mine_ref), channel_id=1, source_target_pairs={{0,8},{4,12},{8,0},{12,4},{16,24},{20,28},{24,16},{28,20},{1,9},{5... | collective-permute-start | bytes 811016 | tf_op jit(solution)/shard_map/ppermute | solution.py:376
  50.5 1.1 %copy-start.6 = (f32[2,264,128]{2,1,0:T(8,128)}, f32[2,264,128]{2,1,0:T(8,128)S(1)}, u32[]{:S(2)}) copy-start(f32[2,264,128]{2,1,0:T(8,128)S(1)} %collective-permute-done.2.other_ref.refs_1_) | copy-start | bytes 811012
  50.5 8.7 %copy-start.11 = (f32[128,128]{1,0:T(8,128)S(1)}, f32[128,128]{1,0:T(8,128)}, u32[]{:S(2)}) copy-start(f32[128,128]{1,0:T(8,128)} %recur_ref.3) | copy-start | bytes 196612
  50.5 8.7 %copy-start.24 = (s32[2,2]{1,0:T(2,128)S(1)}, s32[2,2]{1,0:T(2,128)}, u32[]{:S(2)}) copy-start(s32[2,2]{1,0:T(2,128)} %steps_ref.3) | copy-start | bytes 52
  50.5 8.7 %copy-start.27 = (f32[128]{0:T(128)S(1)}, f32[128]{0:T(128)}, u32[]{:S(2)}) copy-start(f32[128]{0:T(128)} %param.11) | copy-start | bytes 1540
  51.6 7.7 %copy-start.3 = (f32[2,256,256]{2,1,0:T(8,128)S(1)}, f32[2,256,256]{2,1,0:T(8,128)}, u32[]{:S(2)}) copy-start(f32[2,256,256]{2,1,0:T(8,128)} %param.8) | copy-start | bytes 1572868
  51.6 7.7 %copy-start.5 = (f32[2,256,128]{2,1,0:T(8,128)S(1)}, f32[2,256,128]{2,1,0:T(8,128)}, u32[]{:S(2)}) copy-start(f32[2,256,128]{2,1,0:T(8,128)} %param.9) | copy-start | bytes 786436
  51.6 7.6 %collective-permute-start.3 = (f32[2,136,128]{2,1,0:T(8,128)S(1)}, f32[2,136,128]{2,1,0:T(8,128)S(1)}, u32[]{:S(2)}, u32[]{:S(2)}) collective-permute-start(f32[2,136,128]{2,1,0:T(8,128)S(1)} %shard_map.105.mine_ref), channel_id=1, source_target_pairs={{0,16},{4,20},{8,24},{12,28},{16,0},{20,4},{24,8},{28,12},{1,17},{... | collective-permute-start | bytes 417800 | tf_op jit(solution)/shard_map/ppermute | solution.py:376
  54.7 1.0 %copy-start.7 = (f32[2,264,128]{2,1,0:T(8,128)S(1)}, f32[2,264,128]{2,1,0:T(8,128)}, u32[]{:S(2)}) copy-start(f32[2,264,128]{2,1,0:T(8,128)} %copy-done.6) | copy-start | bytes 811012
  55.6 1.0 %copy-start.9 = (f32[2,264,128]{2,1,0:T(8,128)S(1)}, f32[2,264,128]{2,1,0:T(8,128)}, u32[]{:S(2)}) copy-start(f32[2,264,128]{2,1,0:T(8,128)} %copy-done.8) | copy-start | bytes 811012
  56.6 2.7 %copy-start.1 = (f32[32,128,128]{2,1,0:T(8,128)S(1)}, f32[32,128,128]{2,1,0:T(8,128)}, u32[]{:S(2)}) copy-start(f32[32,128,128]{2,1,0:T(8,128)} %copy-done) | copy-start | bytes 6291460
  56.6 2.7 %copy-start.13 = (f32[4,128,128]{2,1,0:T(8,128)S(1)}, f32[4,128,128]{2,1,0:T(8,128)}, u32[]{:S(2)}) copy-start(f32[4,128,128]{2,1,0:T(8,128)} %copy-done.12) | copy-start | bytes 786436
  56.6 2.7 %copy-start.15 = (f32[4,128,128]{2,1,0:T(8,128)S(1)}, f32[4,128,128]{2,1,0:T(8,128)}, u32[]{:S(2)}) copy-start(f32[4,128,128]{2,1,0:T(8,128)} %copy-done.14) | copy-start | bytes 786436
  56.6 2.7 %copy-start.17 = (f32[512,128]{1,0:T(8,128)S(1)}, f32[512,128]{1,0:T(8,128)}, u32[]{:S(2)}) copy-start(f32[512,128]{1,0:T(8,128)} %copy-done.16) | copy-start | bytes 786436
  56.6 2.7 %copy-start.19 = (f32[512,128]{1,0:T(8,128)S(1)}, f32[512,128]{1,0:T(8,128)}, u32[]{:S(2)}) copy-start(f32[512,128]{1,0:T(8,128)} %copy-done.18) | copy-start | bytes 786436
  59.3 1.0 %copy-start.21 = (f32[512,128]{1,0:T(8,128)S(1)}, f32[512,128]{1,0:T(8,128)}, u32[]{:S(2)}) copy-start(f32[512,128]{1,0:T(8,128)} %copy-done.20) | copy-start | bytes 786436
  68.4 1.3 %collective-permute-start.4 = (f32[160,128]{1,0:T(8,128)S(1)}, f32[160,128]{1,0:T(8,128)S(1)}, u32[]{:S(2)}, u32[]{:S(2)}) collective-permute-start(f32[160,128]{1,0:T(8,128)S(1)} %slice_select_fusion), channel_id=1, source_target_pairs={{0,1},{1,0},{2,3},{3,2},{4,5},{5,4},{6,7},{7,6},{8,9},{9,8},{10,11... | collective-permute-start | bytes 245768 | tf_op jit(solution)/shard_map/ppermute | solution.py:376
  69.8 4.6 %collective-permute-start.5 = (f32[160,128]{1,0:T(8,128)S(1)}, f32[160,128]{1,0:T(8,128)S(1)}, u32[]{:S(2)}, u32[]{:S(2)}) collective-permute-start(f32[160,128]{1,0:T(8,128)S(1)} %select_add_fusion), channel_id=1, source_target_pairs={{0,2},{1,3},{2,0},{3,1},{4,6},{5,7},{6,4},{7,5},{8,10},{9,11},{10,... | collective-permute-start | bytes 245768 | tf_op jit(solution)/shard_map/ppermute | solution.py:376
  74.3 4.5 %collective-permute-start.6 = (f32[160,128]{1,0:T(8,128)S(1)}, f32[160,128]{1,0:T(8,128)S(1)}, u32[]{:S(2)}, u32[]{:S(2)}) collective-permute-start(f32[160,128]{1,0:T(8,128)S(1)} %add.16), channel_id=1, source_target_pairs={{0,4},{4,0},{8,12},{12,8},{16,20},{20,16},{24,28},{28,24},{1,5},{5... | collective-permute-start | bytes 245768 | tf_op jit(solution)/shard_map/ppermute | solution.py:376
  78.9 4.5 %collective-permute-start.7 = (f32[160,128]{1,0:T(8,128)S(1)}, f32[160,128]{1,0:T(8,128)S(1)}, u32[]{:S(2)}, u32[]{:S(2)}) collective-permute-start(f32[160,128]{1,0:T(8,128)S(1)} %add.17), channel_id=1, source_target_pairs={{0,8},{4,12},{8,0},{12,4},{16,24},{20,28},{24,16},{28,20},{1,9},{5... | collective-permute-start | bytes 245768 | tf_op jit(solution)/shard_map/ppermute | solution.py:376
  83.4 5.4 %collective-permute-start.8 = (f32[160,128]{1,0:T(8,128)S(1)}, f32[160,128]{1,0:T(8,128)S(1)}, u32[]{:S(2)}, u32[]{:S(2)}) collective-permute-start(f32[160,128]{1,0:T(8,128)S(1)} %add.18), channel_id=1, source_target_pairs={{0,16},{4,20},{8,24},{12,28},{16,0},{20,4},{24,8},{28,12},{1,17},{... | collective-permute-start | bytes 245768 | tf_op jit(solution)/shard_map/ppermute | solution.py:376
  88.8 1.3 %collective-permute-start.9 = (f32[160,128]{1,0:T(8,128)S(1)}, f32[160,128]{1,0:T(8,128)S(1)}, u32[]{:S(2)}, u32[]{:S(2)}) collective-permute-start(f32[160,128]{1,0:T(8,128)S(1)} %add.19.mine_ref), channel_id=1, source_target_pairs={{0,1},{1,0},{2,3},{3,2},{4,5},{5,4},{6,7},{7,6},{8,9},{9,8},{10,11... | collective-permute-start | bytes 245768 | tf_op jit(solution)/shard_map/ppermute | solution.py:376

commit v2 on v1

v2 whole, which is shorter than its diff:
```python
import functools

import jax
import jax.numpy as jnp
from jax import lax
from jax.experimental import pallas as pl
from jax.experimental.pallas import tpu as pltpu
from jax.sharding import PartitionSpec as P

LANE = 16
MIB = 1 << 20
UNROLL = 3
KEEP = 36 * MIB
F32 = jnp.float32
BF16 = jnp.bfloat16
SMEM = pl.BlockSpec(memory_space=pltpu.SMEM)
VMEM = pl.BlockSpec(memory_space=pltpu.VMEM)
ANY = pl.BlockSpec(memory_space=pl.ANY)

euler_step = 0.02


def split(value):
    high = value.astype(BF16)
    return high, (value - high.astype(F32)).astype(BF16)


def left(value):
    return jnp.concatenate(split(value), axis=1)


def right(weight):
    row = jnp.concatenate(split(weight), axis=1)
    return jnp.concatenate([row, row], axis=0)


def right_t(weight):
    high, low = split(weight)
    return jnp.concatenate(
        [jnp.concatenate([high, high], axis=1), jnp.concatenate([low, low], axis=1)], axis=0
    )


def halves(wide):
    hidden = wide.shape[1] // 2
    return wide[:, :hidden] + wide[:, hidden:]


def mul(x, packed):
    return halves(jnp.dot(left(x), packed, preferred_element_type=F32))


def mul_t(x, packed):
    return halves(
        lax.dot_general(left(x), packed, (((1,), (1,)), ((), ())), preferred_element_type=F32)
    )


def mm(x, weight):
    return mul(x, right(weight))


def mm_t(x, weight):
    return mul_t(x, right_t(weight))


def eight(row):
    return jnp.broadcast_to(row, (8, row.shape[1]))


def identity(hidden):
    rows = lax.broadcasted_iota(jnp.int32, (hidden, hidden), 0)
    return (rows == lax.broadcasted_iota(jnp.int32, (hidden, hidden), 1)).astype(F32)


def drift_t(recur_ref, damping_ref):
    weight = recur_ref[...]
    return weight.T - weight - identity(weight.shape[0]) * damping_ref[...]


def column(row, unit):
    return jnp.broadcast_to(jnp.sum(unit * row, axis=1, keepdims=True), unit.shape)


def along(col, weight):
    return jnp.sum(col * weight, axis=0, keepdims=True)


OFFSET, ADJOINT, DRIVE, FIRST, LAST = range(5)


def vectors(*rows):
    hidden = rows[0].shape[1]
    blank = jnp.zeros((8 - len(rows), hidden), F32)
    return jnp.concatenate([row[:1] for row in rows] + [blank], axis=0)


def compose_kernel(
    seqs, blocks, total_seqs, keep, place_ref, steps_ref, x_ref, guess_ref, recur_ref, damping_ref,
    in_ref, bias_ref, targets_ref,
    message_ref, maps_out, before_out, start_ref, hit_ref, reach_ref, reach_off_ref, gain_ref,
    resid_ref, drift_ref,
    partial_ref, before_ref, off_ref, hit_off_ref, prev_ref, maps_sem, before_sem,
):
    rows, hidden = guess_ref.shape
    count = rows // seqs
    chunks = count // LANE
    lanes = seqs * chunks
    block = count // blocks
    drift = drift_t(recur_ref, damping_ref)
    drift_ref[...] = drift
    drift_w = right(drift)

    guess = guess_ref[...]
    prev_ref[pl.ds(1, rows - 1), :] = guess_ref[pl.ds(0, rows - 1), :]
    for s in range(seqs):
        prev_ref[pl.ds(s * count, 1), :] = jnp.zeros((1, hidden), F32)
    prev = prev_ref[...]
    x_high, x_low = split(x_ref[...])
    in_w = jnp.concatenate(split(in_ref[...]), axis=1)
    drive = bias_ref[...] + halves(
        jnp.dot(x_high, in_w, preferred_element_type=F32)
        + jnp.dot(x_low, in_w, preferred_element_type=F32)
    )
    activation = jnp.tanh(mul(prev, drift_w) + drive)
    gain_ref[...] = euler_step * (1.0 - activation * activation)
    resid_ref[...] = prev + euler_step * activation - guess
    own = (place_ref[0] == 0).astype(F32)
    for s in range(seqs):
        edge = pl.ds(s * count, 1)
        gain_ref[edge, :] = gain_ref[edge, :] * own
        resid_ref[edge, :] = resid_ref[edge, :] * own

    unit = identity(hidden)
    for lane in range(lanes):
        partial_ref[0, lane] = unit + drift * gain_ref[pl.ds(lane * LANE, 1), :]
    off_ref[0] = resid_ref[pl.ds(0, lanes, stride=LANE), :]

    def place(j):
        step = (j % blocks) * block + steps_ref[j // blocks, j % blocks]
        return (j // blocks) * chunks + step // LANE, step % LANE, (j // blocks) * count + step

    def slot(now):
        return now if keep else 0

    def capture(now):
        for j in range(seqs * blocks):
            lane, at, _ = place(j)

            @pl.when(at == now)
            def _():
                hit_ref[j] = partial_ref[0, lane]
                hit_off_ref[pl.ds(j, 1), :] = off_ref[0, pl.ds(lane, 1), :]

    def advance(now, _):
        off = off_ref[slot(now - 1)]
        off_ref[slot(now)] = (
            off
            + gain_ref[pl.ds(now, lanes, stride=LANE), :] * mul(off, drift_w)
            + resid_ref[pl.ds(now, lanes, stride=LANE), :]
        )
        for lane in range(0, lanes, 2):
            pair = partial_ref[slot(now - 1), lane : lane + 2].reshape(2 * hidden, hidden)
            moved = mul(pair, drift_w)
            for k in range(2):
                gain_now = gain_ref[pl.ds((lane + k) * LANE + now, 1), :]
                part = slice(k * hidden, (k + 1) * hidden)
                partial_ref[slot(now), lane + k] = pair[part] + gain_now * moved[part]
        if not keep:
            capture(now)
        return 0

    if keep:
        lax.fori_loop(1, LANE, advance, 0, unroll=UNROLL)
        for j in range(seqs * blocks):
            lane, at, _ = place(j)
            hit_ref[j] = partial_ref[at, lane]
            hit_off_ref[pl.ds(j, 1), :] = off_ref[at, pl.ds(lane, 1), :]
    else:
        capture(0)
        lax.fori_loop(1, LANE, advance, 0)
    last = slot(LANE - 1)
    maps_copy = pltpu.make_async_copy(partial_ref.at[last], maps_out, maps_sem)
    maps_copy.start()

    running = [unit] * seqs
    offset = [jnp.zeros((8, hidden), F32)] * seqs
    for chunk in range(chunks):
        for s in range(seqs):
            lane = s * chunks + chunk
            before_ref[lane] = running[s]
            start_ref[pl.ds(lane, 1), :] = offset[s][:1]
            this, this_off = partial_ref[last, lane], off_ref[last, pl.ds(lane, 1), :]
            if chunk == 0:
                running[s], offset[s] = this, eight(this_off)
            else:
                packed = right(this)
                running[s] = mul(running[s], packed)
                offset[s] = mul(offset[s], packed) + this_off
    before_copy = pltpu.make_async_copy(before_ref, before_out, before_sem)
    before_copy.start()

    for s in range(seqs):
        message_ref[s, pl.ds(0, hidden), :] = running[s]
        total = jnp.zeros((hidden, hidden), F32)
        total_off = jnp.zeros((8, hidden), F32)
        for k in range(blocks):
            j = s * blocks + k
            lane, _, row = place(j)
            packed = right(hit_ref[j])
            reach = mul(before_ref[lane], packed)
            reach_off = mul(eight(start_ref[pl.ds(lane, 1), :]), packed) + hit_off_ref[pl.ds(j, 1), :]
            reach_ref[j] = reach
            miss = reach_off + guess_ref[pl.ds(row, 1), :] - targets_ref[pl.ds(j, 1), :]
            reach_off_ref[pl.ds(j, 1), :] = miss[:1]
            reach_t = right_t(reach)
            total = total + mul_t(reach, reach_t)
            total_off = total_off + mul_t(miss, reach_t)
        message_ref[s, pl.ds(hidden, hidden), :] = total / total_seqs
        message_ref[s, pl.ds(2 * hidden, 8), :] = vectors(
            offset[s], total_off / total_seqs, drive[s * count : s * count + 1],
            guess_ref[pl.ds(s * count, 1), :], guess_ref[pl.ds((s + 1) * count - 1, 1), :],
        )
    maps_copy.wait()
    before_copy.wait()


def opened(ref, s, with_map=True):
    hidden = ref.shape[2]
    at = hidden if with_map else 0
    rows = [eight(ref[s, pl.ds(at + hidden + k, 1), :]) for k in range(5)]
    return (ref[s, pl.ds(0, hidden), :] if with_map else None, ref[s, pl.ds(at, hidden), :], rows)


def pick(flag, one, other):
    return jax.tree.map(lambda a, b: jnp.where(flag, a, b), one, other)


def crossing(last, drive, first, drift_w):
    activation = jnp.tanh(mul(last, drift_w) + drive)
    return euler_step * (1.0 - activation * activation), last + euler_step * activation - first


def join(one, two, drift_w, with_map=True):
    map_1, curve_1, rows_1 = one
    map_2, curve_2, rows_2 = two
    gain, resid = crossing(rows_1[LAST], rows_2[DRIVE], rows_2[FIRST], drift_w)
    map_1 = map_1 + mul(map_1, drift_w) * gain[:1]
    off_1 = rows_1[OFFSET] + mul(rows_1[OFFSET], drift_w) * gain + resid
    curve_w, map_w, map_1_t = right(curve_2), right(map_2), right_t(map_1)
    curve = curve_1 + mul_t(mul(map_1, curve_w), map_1_t)
    adjoint = rows_1[ADJOINT] + mul_t(mul(off_1, curve_w) + rows_2[ADJOINT], map_1_t)
    rows = [mul(off_1, map_w) + rows_2[OFFSET], adjoint, rows_1[DRIVE], rows_1[FIRST], rows_2[LAST]]
    return (mul(map_1, map_w) if with_map else None), curve, rows


def join_kernel(level, with_map, place_ref, drift_ref, mine_ref, other_ref, out_ref):
    seqs, hidden = mine_ref.shape[0], mine_ref.shape[2]
    upper = (place_ref[0] >> level) & 1 == 1
    drift_w = right(drift_ref[...])
    for s in range(seqs):
        mine, other = opened(mine_ref, s), opened(other_ref, s)
        whole, curve, rows = join(pick(upper, other, mine), pick(upper, mine, other), drift_w, with_map)
        at = 0
        if with_map:
            out_ref[s, pl.ds(0, hidden), :] = whole
            at = hidden
        out_ref[s, pl.ds(at, hidden), :] = curve
        out_ref[s, pl.ds(at + hidden, 8), :] = vectors(*rows)


def sides_kernel(levels, place_ref, drift_ref, *refs):
    mines, others = refs[:levels], refs[levels : 2 * levels]
    entry_ref, tail_ref, back_ref, rows_ref = refs[2 * levels :]
    seqs, hidden = entry_ref.shape[0], entry_ref.shape[1]
    drift_w = right(drift_ref[...])
    unit = identity(hidden)
    for s in range(seqs):
        zero = jnp.zeros((8, hidden), F32)
        lead, lead_off = unit, zero
        after = (unit, jnp.zeros((hidden, hidden), F32), [zero] * 5)
        edge, edge_gain = zero, zero
        fresh = place_ref[0] >= 0
        for level in range(levels):
            upper = (place_ref[0] >> level) & 1 == 1
            mine, other = opened(mines[level], s), opened(others[level], s)
            gain, resid = crossing(other[2][LAST], mine[2][DRIVE], mine[2][FIRST], drift_w)
            far = other[0] + mul(other[0], drift_w) * gain[:1]
            far_off = other[2][OFFSET] + mul(other[2][OFFSET], drift_w) * gain + resid
            lead_w = right(lead)
            longer = (mul(far, lead_w), mul(far_off, lead_w) + lead_off)
            known = jnp.logical_and(upper, fresh)
            edge, edge_gain = pick(known, (other[2][LAST], gain), (edge, edge_gain))
            fresh = jnp.logical_and(fresh, jnp.logical_not(upper))
            after[2][LAST] = mine[2][LAST]
            extended = join(after, other, drift_w)
            lead, lead_off = pick(upper, longer, (lead, lead_off))
            after = pick(upper, after, extended)
        own_map, _, own_rows = opened(mines[0], s)
        own_w, curve_w = right(own_map), right(after[1])
        entry_ref[s] = lead
        tail_ref[s] = mul(mul(lead, own_w), curve_w)
        back_ref[s] = after[0].T
        leaving = mul(lead_off, own_w) + own_rows[OFFSET]
        tail_off = mul(leaving, curve_w) + after[2][ADJOINT]
        rows_ref[pl.ds(8 * s, 8), :] = vectors(lead_off, tail_off, edge, edge_gain)


def prepare_kernel(
    seqs, blocks, steps_ref, maps_ref, hit_ref, x_ref, guess_ref,
    home_ref, pull_ref, high_ref, low_ref,
    prev_ref,
):
    rows, hidden = guess_ref.shape
    count = rows // seqs
    chunks = count // LANE
    per_block = chunks // blocks
    unit = identity(hidden)
    blank = jnp.zeros((hidden, hidden), F32)
    prev_ref[pl.ds(1, rows - 1), :] = guess_ref[pl.ds(0, rows - 1), :]
    for s in range(seqs):
        prev_ref[pl.ds(s * count, 1), :] = jnp.zeros((1, hidden), F32)
    high_ref[pl.ds(0, hidden), :], low_ref[pl.ds(0, hidden), :] = split(prev_ref[...].T)
    high_ref[pl.ds(hidden, x_ref.shape[1]), :], low_ref[pl.ds(hidden, x_ref.shape[1]), :] = split(
        x_ref[...].T
    )
    home = [unit] * seqs
    pulls = [[blank] * blocks for _ in range(seqs)]
    for chunk in reversed(range(chunks)):
        for s in range(seqs):
            lane = s * chunks + chunk
            home_ref[lane] = home[s]
            active = [k for k in range(blocks) if chunk < (k + 1) * per_block]
            for k in active:
                pull_ref[s * blocks + k, chunk] = pulls[s][k]
            if chunk:
                stack = jnp.concatenate([home[s]] + [pulls[s][k] for k in active], axis=0)
                stack = mul_t(stack, right_t(maps_ref[lane]))
                home[s] = stack[:hidden]
                for i, k in enumerate(active):
                    owner = (k * (count // blocks) + steps_ref[s, k]) // LANE
                    part = stack[(i + 1) * hidden : (i + 2) * hidden]
                    pulls[s][k] = jnp.where(owner == chunk, hit_ref[s * blocks + k].T, part)


def solve_kernel(
    seqs, blocks, total_seqs, level, place_ref, steps_ref, drift_ref, mine_ref, other_ref,
    entry_ref, tail_ref, back_ref, sides_ref, before_ref, start_ref, home_ref, pull_ref, reach_ref,
    reach_off_ref, gain_ref, resid_ref, guess_ref, high_ref, low_ref,
    path_ref, grads_ref,
    state_ref, carry_ref, source_ref, pre_ref, gain_back_ref,
):
    rows, hidden = guess_ref.shape
    count = rows // seqs
    chunks = count // LANE
    lanes = seqs * chunks
    block = count // blocks
    per_block = chunks // blocks
    upper = (place_ref[0] >> level) & 1 == 1
    lowest = (place_ref[0] & ((1 << level) - 1)) == 0
    drift = drift_ref[...]
    drift_w = right(drift)
    drift_wt = right_t(drift)
    unit = identity(hidden)
    source_ref[...] = jnp.zeros_like(source_ref)
    gain_back_ref[...] = gain_ref[...]

    entries, tails, sources, edges = [], [], [], []
    for s in range(seqs):
        mine, other = opened(mine_ref, s, False), opened(other_ref, s, False)
        last, middle = pick(upper, (other[2][LAST], other[2][OFFSET]), (mine[2][LAST], mine[2][OFFSET]))
        drive, first = pick(upper, (mine[2][DRIVE], mine[2][FIRST]), (other[2][DRIVE], other[2][FIRST]))
        gain, resid = crossing(last, drive, first, drift_w)
        middle = middle + mul(middle, drift_w) * gain + resid
        middle_col = column(middle[:1], unit)
        row = along(middle_col, jnp.where(upper, entry_ref[s], other[1]))
        lead_off, tail_off, edge, edge_gain = [sides_ref[pl.ds(8 * s + k, 1), :] for k in range(4)]
        beyond = eight(row) + other[2][ADJOINT]
        beyond = beyond + mul_t(beyond * gain, drift_wt)
        entries.append(column(jnp.where(upper, row, 0.0) + lead_off, unit))
        tail = jnp.where(
            upper, along(middle_col, tail_ref[s]), along(column(beyond[:1], unit), back_ref[s])
        )
        tails.append(column(tail + tail_off, unit))
        known = jnp.logical_and(upper, lowest)
        edge = jnp.where(known, last[:1], edge)
        edges.append(edge)
        edge_gain = jnp.where(known, gain[:1], edge_gain)
        at = pl.ds(s * count, 1)
        gain_back_ref[at, :] = gain_ref[at, :] + edge_gain
        here = []
        for k in range(blocks):
            j = s * blocks + k
            miss = (along(entries[s], reach_ref[j]) + reach_off_ref[pl.ds(j, 1), :]) / total_seqs
            source_ref[pl.ds(s * count + k * block + steps_ref[s, k], 1), :] = miss
            here.append(column(miss, unit))
        sources.append(here)

    for part in range(blocks):

        def ends(chunk, _):
            for s in range(seqs):
                lane = s * chunks + chunk
                state_ref[pl.ds(lane, 1), :] = along(entries[s], before_ref[lane]) + start_ref[pl.ds(lane, 1), :]
                sums = tails[s] * home_ref[lane]
                for k in range(part, blocks):
                    sums = sums + sources[s][k] * pull_ref[s * blocks + k, chunk]
                carry_ref[pl.ds(lane, 1), :] = jnp.sum(sums, axis=0, keepdims=True)
            return 0

        lax.fori_loop(part * per_block, (part + 1) * per_block, ends, 0, unroll=2)

    def walk(now, both):
        state, carry = both
        at = pl.ds(now, lanes, stride=LANE)
        back = pl.ds(LANE - 1 - now, lanes, stride=LANE)
        state = state + gain_ref[at, :] * mul(state, drift_w) + resid_ref[at, :]
        path_ref[at, :] = guess_ref[at, :] + state
        adjoint = source_ref[back, :] + carry
        scaled = gain_back_ref[back, :] * adjoint
        pre_ref[back, :] = scaled
        return state, adjoint + mul_t(scaled, drift_wt)

    lax.fori_loop(0, LANE, walk, (state_ref[...], carry_ref[...]), unroll=2)

    pre_high, pre_low = split(pre_ref[...])
    pre_w = jnp.concatenate([pre_high, pre_low], axis=1)
    sums = halves(jnp.dot(high_ref[...], pre_w, preferred_element_type=F32)) + jnp.dot(
        low_ref[...], pre_high, preferred_element_type=F32
    )
    recur = sums[:hidden]
    for s in range(seqs):
        recur = recur + column(edges[s], unit) * pre_ref[pl.ds(s * count, 1), :]
    recur = recur.T - recur
    half = hidden // 2
    row = lax.broadcasted_iota(jnp.int32, (half, half), 0)
    col = lax.broadcasted_iota(jnp.int32, (half, half), 1)
    folded = jnp.where(col > row, recur[:half, :half], recur[half:, half:])
    grads_ref[pl.ds(0, half), :] = jnp.concatenate([folded, recur[:half, half:]], axis=1)
    grads_ref[pl.ds(half, sums.shape[0] - hidden), :] = sums[hidden:]


def unfold_kernel(place_ref, mine_ref, other_ref, recur_ref, in_ref):
    hidden = recur_ref.shape[0]
    half = hidden // 2
    odd = place_ref[1] & 1 == 1
    mine, other = mine_ref[...], other_ref[...]
    whole = jnp.concatenate([jnp.where(odd, other, mine), jnp.where(odd, mine, other)], axis=0)
    in_ref[...] = whole[half:]
    row = lax.broadcasted_iota(jnp.int32, (half, half), 0)
    col = lax.broadcasted_iota(jnp.int32, (half, half), 1)
    folded, corner = whole[:half, :half], whole[:half, half:]
    first = jnp.where(col > row, folded, 0.0)
    last = jnp.where(col < row, folded, 0.0)
    recur_ref[pl.ds(0, half), :] = jnp.concatenate([first - first.T, corner], axis=1)
    recur_ref[pl.ds(half, half), :] = jnp.concatenate([-corner.T, last - last.T], axis=1)


def call(kernel, shapes, in_specs, scratch=(), flops=0, room=24, out_specs=None):
    shapes = [shape if hasattr(shape, "dtype") else jax.ShapeDtypeStruct(shape, F32) for shape in shapes]
    return pl.pallas_call(
        kernel,
        out_shape=shapes,
        in_specs=in_specs,
        out_specs=out_specs or [VMEM] * len(shapes),
        scratch_shapes=[pltpu.VMEM(s, F32) if isinstance(s, tuple) else s for s in scratch],
        compiler_params=pltpu.CompilerParams(vmem_limit_bytes=room * MIB),
        cost_estimate=pl.CostEstimate(flops=flops, bytes_accessed=1 << 20, transcendentals=0),
    )


def swapped(value, axis, distance):
    return lax.ppermute(value, axis, [(i, i ^ distance) for i in range(lax.axis_size(axis))])


def levels_of(axis):
    return lax.axis_size(axis).bit_length() - 1


def on_device(
    inputs, guess_path, recur_weight, damping, in_weight, bias_term, targets, target_steps
):
    seqs, count, hidden = guess_path.shape
    blocks = targets.shape[1]
    features = inputs.shape[2]
    rows = seqs * count
    lanes = rows // LANE
    chunks = lanes // seqs
    hits = seqs * blocks
    total_seqs = seqs * lax.axis_size("batch")
    place = jnp.stack([lax.axis_index("seq"), lax.axis_index("batch")]).astype(jnp.int32)
    x = inputs.reshape(rows, features)
    guess = guess_path.reshape(rows, hidden)
    keep = rows * hidden * hidden * 4 <= KEEP
    depth = LANE if keep else 1

    message, maps, before, start, hit, reach, reach_off, gain, resid, drift = call(
        functools.partial(compose_kernel, seqs, blocks, total_seqs, keep),
        [
            (seqs, 2 * hidden + 8, hidden),
            (lanes, hidden, hidden),
            (lanes, hidden, hidden),
            (lanes, hidden),
            (hits, hidden, hidden),
            (hits, hidden, hidden),
            (hits, hidden),
            (rows, hidden),
            (rows, hidden),
            (hidden, hidden),
        ],
        [SMEM, SMEM] + [VMEM] * 7,
        [
            (depth, lanes, hidden, hidden),
            (lanes, hidden, hidden),
            (depth, lanes, hidden),
            (hits, hidden),
            (rows, hidden),
            pltpu.SemaphoreType.DMA(()),
            pltpu.SemaphoreType.DMA(()),
        ],
        room=56,
        out_specs=[VMEM, ANY, ANY] + [VMEM] * 7,
    )(place, target_steps, x, guess, recur_weight, damping.reshape(1, hidden), in_weight,
      bias_term.reshape(1, hidden), targets.reshape(hits, hidden))

    home, pull, high, low = call(
        functools.partial(prepare_kernel, seqs, blocks),
        [
            (lanes, hidden, hidden),
            (hits, chunks, hidden, hidden),
            jax.ShapeDtypeStruct((hidden + features, rows), BF16),
            jax.ShapeDtypeStruct((hidden + features, rows), BF16),
        ],
        [SMEM] + [VMEM] * 4,
        [(rows, hidden)],
        flops=1 << 32,
    )(target_steps, maps, hit, x, guess)

    levels = levels_of("seq")
    groups, received = [message], []
    for level in range(levels - 1):
        received.append(swapped(groups[-1], "seq", 1 << level))
        with_map = level < levels - 2
        height = (2 if with_map else 1) * hidden + 8
        groups += call(
            functools.partial(join_kernel, level, with_map),
            [(seqs, height, hidden)],
            [SMEM, VMEM, VMEM, VMEM],
        )(place, drift, groups[-1], received[-1])
    other = swapped(groups[-1], "seq", 1 << (levels - 1))
    square = (seqs, hidden, hidden)
    entry, tail, back, sides = call(
        functools.partial(sides_kernel, levels - 1),
        [square, square, square, (8 * seqs, hidden)],
        [SMEM] + [VMEM] * (2 * levels - 1),
        flops=1 << 30,
    )(place, drift, *groups[:-1], *received)

    path, grads = call(
        functools.partial(solve_kernel, seqs, blocks, total_seqs, levels - 1),
        [(rows, hidden), (hidden // 2 + features, hidden)],
        [SMEM, SMEM] + [VMEM] * 18,
        [(lanes, hidden), (lanes, hidden), (rows, hidden), (rows, hidden), (rows, hidden)],
    )(place, target_steps, drift, groups[-1], other, entry, tail, back, sides, before, start, home,
      pull, reach, reach_off, gain, resid, guess, high, low)

    middle = grads.shape[0] // 2
    odd = place[1] & 1 == 1
    kept = jnp.where(odd, grads[middle:], grads[:middle])
    given = jnp.where(odd, grads[:middle], grads[middle:])
    kept = kept + swapped(given, "batch", 1)
    for level in range(1, levels_of("batch")):
        kept = kept + swapped(kept, "batch", 1 << level)
    for level in range(levels):
        kept = kept + swapped(kept, "seq", 1 << level)
    grad_recur, grad_in = call(
        unfold_kernel,
        [(hidden, hidden), (features, hidden)],
        [SMEM, VMEM, VMEM],
    )(place, kept, swapped(kept, "batch", 1))
    return (path.reshape(seqs, count, hidden), grad_recur, grad_in)


def solution(mesh):
    placed = (
        P("batch", "seq", None),
        P("batch", "seq", None),
        P(),
        P(),
        P(),
        P(),
        P("batch", "seq", None),
        P("batch", "seq"),
    )
    return jax.shard_map(
        on_device,
        mesh=mesh,
        in_specs=placed,
        out_specs=(P("batch", "seq", None), P(), P()),
        check_vma=False,
    )
```

time: 92 us -> 128 us (1.39)
  Pallas kernels: 28.6 us -> 69.2 us
  starting transfers between devices: 19.2 us -> 12.9 us
    pallas_call x2 -> x3, Pallas kernels: 16.9 us -> 58.9 us  [the longest x1 53.1 us: on_device(): call(functools.partial(compose_kernel, seqs, blocks, total_seqs, keep), [...]
    ppermute x1 -> x0, starting transfers between devices: 4.83 us -> none  [on_device(): edge = lax.ppermute(guess_path[:, count - 1, :], 'seq', route)]
    ppermute x9, waiting for transfers between devices: 26.5 us -> 28.7 us  [swapped(): lax.ppermute(value, axis, [(i, i ^ distance) for i in range(lax.axis_size...]
    pallas_call x1, Pallas kernels: 8.12 us -> 6.18 us  [on_device(): call(functools.partial(solve_kernel, seqs, blocks, total_seqs, levels - 1...]
    ppermute x9, starting transfers between devices: 14.4 us -> 12.9 us  [swapped(): lax.ppermute(value, axis, [(i, i ^ distance) for i in range(lax.axis_size...]
    ppermute x1 -> x0, waiting for transfers between devices: 1.28 us -> none  [on_device(): edge = lax.ppermute(guess_path[:, count - 1, :], 'seq', route)]
    unnamed x58 -> x54, local copies, waits for them, and re-layouts: 14.2 us -> 15.1 us
  transfers between devices with their start and end apart: 10 -> 9, of which waited for: 10 -> 8; matrix products, arithmetic and copies ran while one was open for 0% -> 0% of each run, Pallas kernels for 1% -> 5%
where the time goes in v2:
time: 128 us; the launch traced here: 127 us
  Pallas kernels  69.2 us (54%)
  waiting for transfers between devices  28.7 us (22%)
  local copies, waits for them, and re-layouts  15.1 us (12%)
  starting transfers between devices  12.9 us (10%)
    pallas_call x1, Pallas kernels, on_device(): call(functools.partial(compose_kernel, seqs, blocks, total_seqs, keep), [...  53.1 us
    ppermute x9, waiting for transfers between devices, swapped(): lax.ppermute(value, axis, [(i, i ^ distance) for i in range(lax.axis_size...  28.7 us
    unnamed x54, local copies, waits for them, and re-layouts  15.1 us
    ppermute x9, starting transfers between devices, swapped(): lax.ppermute(value, axis, [(i, i ^ distance) for i in range(lax.axis_size...  12.9 us
    pallas_call x1, Pallas kernels, on_device(): call(functools.partial(solve_kernel, seqs, blocks, total_seqs, levels - 1...  6.18 us
    pallas_call x1, Pallas kernels, on_device(): call(functools.partial(sides_kernel, levels - 1), [square, square, square...  3.12 us
    pallas_call x2, Pallas kernels, on_device(): call(functools.partial(join_kernel, level, with_map), [(seqs, height, hid...  2.76 us
    pallas_call x1, Pallas kernels, on_device(): call(functools.partial(prepare_kernel, seqs, blocks), [(lanes, hidden, hi...  2.75 us
  transfers between devices with their start and end apart: 9, of which 8 were waited for; matrix products, arithmetic and copies ran while one was open for 0% of the time, Pallas kernels for 5%

profile of v2, /device:TPU:0, one launch (start us, length us, event | category | flops | bytes accessed | tf_op | source)
XLA Modules:
  0.0 127.5 jit_solution(12570041123313384937)
XLA Ops:
  0.6 0.0 copy-start.23
  0.6 0.0 copy-start.5
  0.7 0.0 copy-start.8
  0.7 0.6 pad_add_fusion.place_ref
  1.3 53.1 %shard_map.103 = (f32[2,264,128]{2,1,0:T(8,128)}, f32[32,128,128]{2,1,0:T(8,128)}, f32[32,128,128]{2,1,0:T(8,128)}, f32[32,128]{1,0:T(8,128)}, f32[4,128,128]{2,...) custom-call(s32[2]{0:T(128)} %pad_add_fusion.place_ref, ...), custom_call_target="tpu_custom_call" | custom-call | bytes 1048576 | tf_op jit(solution)/shard_map/pallas_call | solution.py:497
  54.4 3.0 %collective-permute-start = (f32[2,264,128]{2,1,0:T(8,128)}, f32[2,264,128]{2,1,0:T(8,128)S(1)}, u32[]{:S(2)}, u32[]{:S(2)}) collective-permute-start(f32[2,264,128]{2,1,0:T(8,128)} %get-tuple-element.26.mine_ref.refs_0_), channel_id=1, source_target_pairs={{0,4},{4,0},{8,12},{12,8},{16,20},{20,16},{24,28},{28,24},{1,5},{5... | collective-permute-start | bytes 811016 | tf_op jit(solution)/shard_map/ppermute | solution.py:473
  57.4 6.7 %collective-permute-done.other_ref.refs_2_ = f32[2,264,128]{2,1,0:T(8,128)S(1)} collective-permute-done((f32[2,264,128]{2,1,0:T(8,128)}, f32[2,264,128]{2,1,0:T(8,128)S(1)}, u32[]{:S(2)}, u32[]{:S(2)}) %collective-permute-start) | collective-permute-done | bytes 270368 | tf_op jit(solution)/shard_map/ppermute | solution.py:473
  64.1 0.0 copy-start.13
  64.1 0.0 copy-start.6
  64.1 0.9 copy-done.6
  64.9 0.0 copy-start.11
  64.9 1.0 copy-done.11
  65.9 0.6 copy-done.21
  66.5 1.4 %shard_map.104.mine_ref.refs_1_ = f32[2,264,128]{2,1,0:T(8,128)S(1)} custom-call(s32[2]{0:T(128)S(1)} %copy-done.21, f32[128,128]{1,0:T(8,128)S(1)} %copy-done.6, f32[2,264,128]{2,1,0:T(8,128)S(1)} %copy-done.11, f32[2,264,128]{2,1,0:T(8,128)S(1)} %collective-permute-done.other_ref.refs_2_), custom_call_target="tpu_custom_call" | custom-call | bytes 1048576 | tf_op jit(solution)/shard_map/pallas_call | solution.py:545
  68.0 1.9 %collective-permute-start.1 = (f32[2,264,128]{2,1,0:T(8,128)S(1)}, f32[2,264,128]{2,1,0:T(8,128)S(1)}, u32[]{:S(2)}, u32[]{:S(2)}) collective-permute-start(f32[2,264,128]{2,1,0:T(8,128)S(1)} %shard_map.104.mine_ref.refs_1_), channel_id=1, source_target_pairs={{0,8},{4,12},{8,0},{12,4},{16,24},{20,28},{24,16},{28,20},{1,9},{5... | collective-permute-start | bytes 811016 | tf_op jit(solution)/shard_map/ppermute | solution.py:473
  69.9 5.8 %collective-permute-done.1.other_ref.refs_3_ = f32[2,264,128]{2,1,0:T(8,128)S(1)} collective-permute-done((f32[2,264,128]{2,1,0:T(8,128)S(1)}, f32[2,264,128]{2,1,0:T(8,128)S(1)}, u32[]{:S(2)}, u32[]{:S(2)}) %collective-permute-start.1) | collective-permute-done | bytes 270368 | tf_op jit(solution)/shard_map/ppermute | solution.py:473
  75.7 1.3 %shard_map.105.mine_ref = f32[2,136,128]{2,1,0:T(8,128)S(1)} custom-call(s32[2]{0:T(128)S(1)} %copy-done.21, f32[128,128]{1,0:T(8,128)S(1)} %copy-done.6, f32[2,264,128]{2,1,0:T(8,128)S(1)} %shard_map.104.mine_ref.refs_1_, f32[2,264,128]{2,1,0:T(8,128)S(1)} %collective-permute-done.1.other_ref.refs_3_), custom_call_target="tpu_custom_call" | custom-call | bytes 1048576 | tf_op jit(solution)/shard_map/pallas_call | solution.py:545
  77.0 2.6 %collective-permute-start.2 = (f32[2,136,128]{2,1,0:T(8,128)S(1)}, f32[2,136,128]{2,1,0:T(8,128)}, u32[]{:S(2)}, u32[]{:S(2)}) collective-permute-start(f32[2,136,128]{2,1,0:T(8,128)S(1)} %shard_map.105.mine_ref), channel_id=1, source_target_pairs={{0,16},{4,20},{8,24},{12,28},{16,0},{20,4},{24,8},{28,12},{1,17},{... | collective-permute-start | bytes 417800 | tf_op jit(solution)/shard_map/ppermute | solution.py:473
  79.6 0.0 copy-done.15
  79.6 0.0 copy-done.13
  79.6 0.0 copy-done.23
  79.6 0.0 copy-done.5
  79.6 0.0 copy-done.8
  79.6 0.0 copy-start.25
  79.7 1.6 %copy-done.25 = f32[32,128,128]{2,1,0:T(8,128)S(1)} copy-done((f32[32,128,128]{2,1,0:T(8,128)S(1)}, f32[32,128,128]{2,1,0:T(8,128)}, u32[]{:S(2)}) %copy-start.25) | copy-done | bytes 2097176
  81.2 0.9 copy-done.26
  82.2 0.0 copy-start.24
  82.2 2.7 %shard_map.107 = (f32[32,128,128]{2,1,0:T(8,128)S(1)}, f32[4,16,128,128]{3,2,1,0:T(8,128)S(1)}, bf16[384,512]{1,0:T(8,128)(2,1)S(1)}, bf16[384,512]{1,0:T(8,128)(2,1)S(1)}) custom-call(s32[2,2]{1,0:T(2,128)S(1)} %copy-done.23, f32[32,128,128]{2,1,0:T(8,128)S(1)} %copy-done.25, f32[4,128,128]{2,1,0:T(8,128)S(1)} %copy-done.26, f32[512,256]{1,0:T(8,128)S(1)} %bitcast.12, ...), custom_call_target="tpu_custom_call" | custom-call | flops 4294967296 | bytes 1048576 | tf_op jit(solution)/shard_map/pallas_call | solution.py:526
  85.0 0.0 copy-start
  85.0 2.0 %copy-done = f32[4,16,128,128]{3,2,1,0:T(8,128)} copy-done((f32[4,16,128,128]{3,2,1,0:T(8,128)}, f32[4,16,128,128]{3,2,1,0:T(8,128)S(1)}, u32[]{:S(2)}) %copy-start) | copy-done | bytes 4194328
  86.9 1.4 %copy-done.3 = f32[32,128,128]{2,1,0:T(8,128)} copy-done((f32[32,128,128]{2,1,0:T(8,128)}, f32[32,128,128]{2,1,0:T(8,128)S(1)}, u32[]{:S(2)}) %copy-start.3) | copy-done | bytes 2097176
  88.3 0.8 copy-done.9
  89.1 0.0 copy-done.7
  89.1 0.0 copy-done.12
  89.1 0.0 copy-done.22
  89.1 0.0 copy-start.14
  89.2 1.1 copy-done.14
  90.2 1.0 copy-done.16
  91.2 3.1 %shard_map.106 = (f32[2,128,128]{2,1,0:T(8,128)S(1)}, f32[2,128,128]{2,1,0:T(8,128)S(1)}, f32[2,128,128]{2,1,0:T(8,128)S(1)}, f32[16,128]{1,0:T(8,128)S(1)}) custom-call(s32[2]{0:T(128)S(1)} %copy-done.22, f32[128,128]{1,0:T(8,128)S(1)} %copy-done.7, f32[2,264,128]{2,1,0:T(8,128)S(1)} %copy-done.12, f32[2,264,128]{2,1,0:T(8,128)S(1)} %shard_map.104.mine_ref.refs_1_, ...), custom_call_target="tpu_custom_call" | custom-call | flops 1073741824 | bytes 1048576 | tf_op jit(solution)/shard_map/pallas_call | solution.py:552
  94.3 0.0 collective-permute-done.2.other_ref
  94.3 0.0 copy-done.20
  94.4 0.0 copy-done.24
  94.4 0.0 copy-done.2
  94.4 0.0 copy-done.10
  94.4 0.0 copy-done.17
  94.4 0.0 copy-done.18
  94.4 0.0 copy-done.19
  94.4 0.0 copy-start.1
  94.4 2.2 %copy-done.1 = f32[4,16,128,128]{3,2,1,0:T(8,128)S(1)} copy-done((f32[4,16,128,128]{3,2,1,0:T(8,128)S(1)}, f32[4,16,128,128]{3,2,1,0:T(8,128)}, u32[]{:S(2)}) %copy-start.1) | copy-done | bytes 4194328
  96.6 1.6 %copy-done.4 = f32[32,128,128]{2,1,0:T(8,128)S(1)} copy-done((f32[32,128,128]{2,1,0:T(8,128)S(1)}, f32[32,128,128]{2,1,0:T(8,128)}, u32[]{:S(2)}) %copy-start.4) | copy-done | bytes 2097176
  98.2 6.2 %shard_map.108 = (f32[512,128]{1,0:T(8,128)}, f32[320,128]{1,0:T(8,128)S(1)}) custom-call(s32[2]{0:T(128)S(1)} %copy-done.22, s32[2,2]{1,0:T(2,128)S(1)} %copy-done.23, f32[128,128]{1,0:T(8,128)S(1)} %copy-done.7, f32[2,136,128]{2,1,0:T(8,128)S(1)} %shard_map.105.mine_ref, f32[2,136,128]{2,1,0:T(8,128)} %collective-permute-done.2.other_ref, ...), custom_call_target="tpu_custom_call" | custom-call | bytes 1048576 | tf_op jit(solution)/shard_map/pallas_call | solution.py:559
  104.4 0.1 collective-permute-start.3
  104.5 1.3 collective-permute-done.3
  105.8 1.6 %collective-permute-start.4 = (f32[160,128]{1,0:T(8,128)S(1)}, f32[160,128]{1,0:T(8,128)S(1)}, u32[]{:S(2)}, u32[]{:S(2)}) collective-permute-start(f32[160,128]{1,0:T(8,128)S(1)} %select_add_fusion), channel_id=1, source_target_pairs={{0,2},{1,3},{2,0},{3,1},{4,6},{5,7},{6,4},{7,5},{8,10},{9,11},{10,... | collective-permute-start | bytes 245768 | tf_op jit(solution)/shard_map/ppermute | solution.py:473
  107.4 3.0 %collective-permute-done.4 = f32[160,128]{1,0:T(8,128)S(1)} collective-permute-done((f32[160,128]{1,0:T(8,128)S(1)}, f32[160,128]{1,0:T(8,128)S(1)}, u32[]{:S(2)}, u32[]{:S(2)}) %collective-permute-start.4) | collective-permute-done | bytes 81952 | tf_op jit(solution)/shard_map/ppermute | solution.py:473
  110.3 1.6 %collective-permute-start.5 = (f32[160,128]{1,0:T(8,128)S(1)}, f32[160,128]{1,0:T(8,128)S(1)}, u32[]{:S(2)}, u32[]{:S(2)}) collective-permute-start(f32[160,128]{1,0:T(8,128)S(1)} %add.16), channel_id=1, source_target_pairs={{0,4},{4,0},{8,12},{12,8},{16,20},{20,16},{24,28},{28,24},{1,5},{5... | collective-permute-start | bytes 245768 | tf_op jit(solution)/shard_map/ppermute | solution.py:473
  111.9 2.9 %collective-permute-done.5 = f32[160,128]{1,0:T(8,128)S(1)} collective-permute-done((f32[160,128]{1,0:T(8,128)S(1)}, f32[160,128]{1,0:T(8,128)S(1)}, u32[]{:S(2)}, u32[]{:S(2)}) %collective-permute-start.5) | collective-permute-done | bytes 81952 | tf_op jit(solution)/shard_map/ppermute | solution.py:473
  114.9 1.7 %collective-permute-start.6 = (f32[160,128]{1,0:T(8,128)S(1)}, f32[160,128]{1,0:T(8,128)S(1)}, u32[]{:S(2)}, u32[]{:S(2)}) collective-permute-start(f32[160,128]{1,0:T(8,128)S(1)} %add.17), channel_id=1, source_target_pairs={{0,8},{4,12},{8,0},{12,4},{16,24},{20,28},{24,16},{28,20},{1,9},{5... | collective-permute-start | bytes 245768 | tf_op jit(solution)/shard_map/ppermute | solution.py:473
  116.5 2.9 %collective-permute-done.6 = f32[160,128]{1,0:T(8,128)S(1)} collective-permute-done((f32[160,128]{1,0:T(8,128)S(1)}, f32[160,128]{1,0:T(8,128)S(1)}, u32[]{:S(2)}, u32[]{:S(2)}) %collective-permute-start.6) | collective-permute-done | bytes 81952 | tf_op jit(solution)/shard_map/ppermute | solution.py:473
  119.4 0.5 collective-permute-start.7
  119.9 4.9 %collective-permute-done.7 = f32[160,128]{1,0:T(8,128)S(1)} collective-permute-done((f32[160,128]{1,0:T(8,128)S(1)}, f32[160,128]{1,0:T(8,128)S(1)}, u32[]{:S(2)}, u32[]{:S(2)}) %collective-permute-start.7) | collective-permute-done | bytes 81952 | tf_op jit(solution)/shard_map/ppermute | solution.py:473
  124.8 0.1 collective-permute-start.8
  124.9 1.3 collective-permute-done.8.other_ref
  126.1 1.4 %shard_map.109 = (f32[128,128]{1,0:T(8,128)}, f32[256,128]{1,0:T(8,128)}) custom-call(s32[2]{0:T(128)S(1)} %copy-done.22, f32[160,128]{1,0:T(8,128)S(1)} %add.19.mine_ref, f32[160,128]{1,0:T(8,128)S(1)} %collective-permute-done.8.other_ref), custom_call_target="tpu_custom_call" | custom-call | bytes 1048576 | tf_op jit(solution)/shard_map/pallas_call | solution.py:576
  (22 shorter events, 0.1 us)
Async XLA Ops:
  0.6 79.0 %copy-start.23 = (s32[2,2]{1,0:T(2,128)S(1)}, s32[2,2]{1,0:T(2,128)}, u32[]{:S(2)}) copy-start(s32[2,2]{1,0:T(2,128)} %steps_ref.5) | copy-start | bytes 52
  0.6 79.0 %copy-start.5 = (f32[2,256,128]{2,1,0:T(8,128)S(1)}, f32[2,256,128]{2,1,0:T(8,128)}, u32[]{:S(2)}) copy-start(f32[2,256,128]{2,1,0:T(8,128)} %param.9) | copy-start | bytes 786436
  0.7 79.0 %copy-start.8 = (f32[2,256,256]{2,1,0:T(8,128)S(1)}, f32[2,256,256]{2,1,0:T(8,128)}, u32[]{:S(2)}) copy-start(f32[2,256,256]{2,1,0:T(8,128)} %param.8) | copy-start | bytes 1572868
  54.4 9.7 %collective-permute-start = (f32[2,264,128]{2,1,0:T(8,128)}, f32[2,264,128]{2,1,0:T(8,128)S(1)}, u32[]{:S(2)}, u32[]{:S(2)}) collective-permute-start(f32[2,264,128]{2,1,0:T(8,128)} %get-tuple-element.26.mine_ref.refs_0_), channel_id=1, source_target_pairs={{0,4},{4,0},{8,12},{12,8},{16,20},{20,16},{24,28},{28,24},{1,5},{5... | collective-permute-start | bytes 811016 | tf_op jit(solution)/shard_map/ppermute | solution.py:473
  64.1 15.6 %copy-start.13 = (f32[2,264,128]{2,1,0:T(8,128)}, f32[2,264,128]{2,1,0:T(8,128)S(1)}, u32[]{:S(2)}) copy-start(f32[2,264,128]{2,1,0:T(8,128)S(1)} %collective-permute-done.other_ref.refs_2_) | copy-start | bytes 811012
  64.1 0.9 copy-start.6
  64.9 1.0 copy-start.11
  65.9 0.6 copy-start.21
  68.0 7.7 %collective-permute-start.1 = (f32[2,264,128]{2,1,0:T(8,128)S(1)}, f32[2,264,128]{2,1,0:T(8,128)S(1)}, u32[]{:S(2)}, u32[]{:S(2)}) collective-permute-start(f32[2,264,128]{2,1,0:T(8,128)S(1)} %shard_map.104.mine_ref.refs_1_), channel_id=1, source_target_pairs={{0,8},{4,12},{8,0},{12,4},{16,24},{20,28},{24,16},{28,20},{1,9},{5... | collective-permute-start | bytes 811016 | tf_op jit(solution)/shard_map/ppermute | solution.py:473
  75.7 3.9 %copy-start.15 = (f32[2,264,128]{2,1,0:T(8,128)}, f32[2,264,128]{2,1,0:T(8,128)S(1)}, u32[]{:S(2)}) copy-start(f32[2,264,128]{2,1,0:T(8,128)S(1)} %collective-permute-done.1.other_ref.refs_3_) | copy-start | bytes 811012
  77.0 17.3 %collective-permute-start.2 = (f32[2,136,128]{2,1,0:T(8,128)S(1)}, f32[2,136,128]{2,1,0:T(8,128)}, u32[]{:S(2)}, u32[]{:S(2)}) collective-permute-start(f32[2,136,128]{2,1,0:T(8,128)S(1)} %shard_map.105.mine_ref), channel_id=1, source_target_pairs={{0,16},{4,20},{8,24},{12,28},{16,0},{20,4},{24,8},{28,12},{1,17},{... | collective-permute-start | bytes 417800 | tf_op jit(solution)/shard_map/ppermute | solution.py:473
  79.6 1.6 %copy-start.25 = (f32[32,128,128]{2,1,0:T(8,128)S(1)}, f32[32,128,128]{2,1,0:T(8,128)}, u32[]{:S(2)}) copy-start(f32[32,128,128]{2,1,0:T(8,128)} %get-tuple-element.33.maps_ref) | copy-start | bytes 6291460
  81.2 0.9 copy-start.26
  82.2 7.0 %copy-start.7 = (f32[128,128]{1,0:T(8,128)S(1)}, f32[128,128]{1,0:T(8,128)}, u32[]{:S(2)}) copy-start(f32[128,128]{1,0:T(8,128)} %get-tuple-element.25.drift_ref) | copy-start | bytes 196612
  82.2 7.0 %copy-start.12 = (f32[2,264,128]{2,1,0:T(8,128)S(1)}, f32[2,264,128]{2,1,0:T(8,128)}, u32[]{:S(2)}) copy-start(f32[2,264,128]{2,1,0:T(8,128)} %get-tuple-element.26.mine_ref.refs_0_) | copy-start | bytes 811012
  82.2 7.0 %copy-start.22 = (s32[2]{0:T(128)S(1)}, s32[2]{0:T(128)}, u32[]{:S(2)}) copy-start(s32[2]{0:T(128)} %pad_add_fusion.place_ref) | copy-start | bytes 28
  82.2 12.2 %copy-start.20 = (f32[32,128]{1,0:T(8,128)S(1)}, f32[32,128]{1,0:T(8,128)}, u32[]{:S(2)}) copy-start(f32[32,128]{1,0:T(8,128)} %get-tuple-element.32.start_ref) | copy-start | bytes 49156
  82.2 12.2 %copy-start.24 = (f32[4,128]{1,0:T(4,128)S(1)}, f32[4,128]{1,0:T(4,128)}, u32[]{:S(2)}) copy-start(f32[4,128]{1,0:T(4,128)} %get-tuple-element.38.reach_off_ref) | copy-start | bytes 6148
  85.0 2.0 %copy-start = (f32[4,16,128,128]{3,2,1,0:T(8,128)}, f32[4,16,128,128]{3,2,1,0:T(8,128)S(1)}, u32[]{:S(2)}) copy-start(f32[4,16,128,128]{3,2,1,0:T(8,128)S(1)} %get-tuple-element.36.pull_ref) | copy-start | bytes 12582916
  86.9 1.4 %copy-start.3 = (f32[32,128,128]{2,1,0:T(8,128)}, f32[32,128,128]{2,1,0:T(8,128)S(1)}, u32[]{:S(2)}) copy-start(f32[32,128,128]{2,1,0:T(8,128)S(1)} %get-tuple-element.35.home_ref) | copy-start | bytes 6291460
  88.3 0.8 copy-start.9
  89.1 5.2 %copy-start.2 = (f32[32,128,128]{2,1,0:T(8,128)S(1)}, f32[32,128,128]{2,1,0:T(8,128)}, u32[]{:S(2)}) copy-start(f32[32,128,128]{2,1,0:T(8,128)} %get-tuple-element.31.before_ref) | copy-start | bytes 6291460
  89.1 1.1 copy-start.14
  90.2 1.0 copy-start.16
  91.2 3.2 %copy-start.10 = (bf16[384,512]{1,0:T(8,128)(2,1)S(1)}, bf16[384,512]{1,0:T(8,128)(2,1)}, u32[]{:S(2)}) copy-start(bf16[384,512]{1,0:T(8,128)(2,1)} %copy-done.9) | copy-start | bytes 1179652
  91.2 3.2 %copy-start.17 = (f32[4,128,128]{2,1,0:T(8,128)S(1)}, f32[4,128,128]{2,1,0:T(8,128)}, u32[]{:S(2)}) copy-start(f32[4,128,128]{2,1,0:T(8,128)} %get-tuple-element.37.reach_ref) | copy-start | bytes 786436
  91.2 3.2 %copy-start.18 = (f32[512,128]{1,0:T(8,128)S(1)}, f32[512,128]{1,0:T(8,128)}, u32[]{:S(2)}) copy-start(f32[512,128]{1,0:T(8,128)} %get-tuple-element.39.gain_ref) | copy-start | bytes 786436
  91.2 3.2 %copy-start.19 = (f32[512,128]{1,0:T(8,128)S(1)}, f32[512,128]{1,0:T(8,128)}, u32[]{:S(2)}) copy-start(f32[512,128]{1,0:T(8,128)} %get-tuple-element.40.resid_ref) | copy-start | bytes 786436
  94.4 2.2 %copy-start.1 = (f32[4,16,128,128]{3,2,1,0:T(8,128)S(1)}, f32[4,16,128,128]{3,2,1,0:T(8,128)}, u32[]{:S(2)}) copy-start(f32[4,16,128,128]{3,2,1,0:T(8,128)} %copy-done) | copy-start | bytes 12582916
  96.6 1.6 %copy-start.4 = (f32[32,128,128]{2,1,0:T(8,128)S(1)}, f32[32,128,128]{2,1,0:T(8,128)}, u32[]{:S(2)}) copy-start(f32[32,128,128]{2,1,0:T(8,128)} %copy-done.3) | copy-start | bytes 6291460
  104.4 1.3 %collective-permute-start.3 = (f32[160,128]{1,0:T(8,128)S(1)}, f32[160,128]{1,0:T(8,128)S(1)}, u32[]{:S(2)}, u32[]{:S(2)}) collective-permute-start(f32[160,128]{1,0:T(8,128)S(1)} %slice_select_fusion), channel_id=1, source_target_pairs={{0,1},{1,0},{2,3},{3,2},{4,5},{5,4},{6,7},{7,6},{8,9},{9,8},{10,11... | collective-permute-start | bytes 245768 | tf_op jit(solution)/shard_map/ppermute | solution.py:473
  105.8 4.6 %collective-permute-start.4 = (f32[160,128]{1,0:T(8,128)S(1)}, f32[160,128]{1,0:T(8,128)S(1)}, u32[]{:S(2)}, u32[]{:S(2)}) collective-permute-start(f32[160,128]{1,0:T(8,128)S(1)} %select_add_fusion), channel_id=1, source_target_pairs={{0,2},{1,3},{2,0},{3,1},{4,6},{5,7},{6,4},{7,5},{8,10},{9,11},{10,... | collective-permute-start | bytes 245768 | tf_op jit(solution)/shard_map/ppermute | solution.py:473
  110.3 4.5 %collective-permute-start.5 = (f32[160,128]{1,0:T(8,128)S(1)}, f32[160,128]{1,0:T(8,128)S(1)}, u32[]{:S(2)}, u32[]{:S(2)}) collective-permute-start(f32[160,128]{1,0:T(8,128)S(1)} %add.16), channel_id=1, source_target_pairs={{0,4},{4,0},{8,12},{12,8},{16,20},{20,16},{24,28},{28,24},{1,5},{5... | collective-permute-start | bytes 245768 | tf_op jit(solution)/shard_map/ppermute | solution.py:473
  114.9 4.5 %collective-permute-start.6 = (f32[160,128]{1,0:T(8,128)S(1)}, f32[160,128]{1,0:T(8,128)S(1)}, u32[]{:S(2)}, u32[]{:S(2)}) collective-permute-start(f32[160,128]{1,0:T(8,128)S(1)} %add.17), channel_id=1, source_target_pairs={{0,8},{4,12},{8,0},{12,4},{16,24},{20,28},{24,16},{28,20},{1,9},{5... | collective-permute-start | bytes 245768 | tf_op jit(solution)/shard_map/ppermute | solution.py:473
  119.4 5.4 %collective-permute-start.7 = (f32[160,128]{1,0:T(8,128)S(1)}, f32[160,128]{1,0:T(8,128)S(1)}, u32[]{:S(2)}, u32[]{:S(2)}) collective-permute-start(f32[160,128]{1,0:T(8,128)S(1)} %add.18), channel_id=1, source_target_pairs={{0,16},{4,20},{8,24},{12,28},{16,0},{20,4},{24,8},{28,12},{1,17},{... | collective-permute-start | bytes 245768 | tf_op jit(solution)/shard_map/ppermute | solution.py:473
  124.8 1.3 %collective-permute-start.8 = (f32[160,128]{1,0:T(8,128)S(1)}, f32[160,128]{1,0:T(8,128)S(1)}, u32[]{:S(2)}, u32[]{:S(2)}) collective-permute-start(f32[160,128]{1,0:T(8,128)S(1)} %add.19.mine_ref), channel_id=1, source_target_pairs={{0,1},{1,0},{2,3},{3,2},{4,5},{5,4},{6,7},{7,6},{8,9},{9,8},{10,11... | collective-permute-start | bytes 245768 | tf_op jit(solution)/shard_map/ppermute | solution.py:473

commit v3 on v2

--- a/solution.py
+++ b/solution.py
@@ -9,13 +9,22 @@
 
 LANE = 16
 MIB = 1 << 20
-UNROLL = 3
+UNROLL = 5
+ROOM = 41
 KEEP = 36 * MIB
 F32 = jnp.float32
 BF16 = jnp.bfloat16
-SMEM = pl.BlockSpec(memory_space=pltpu.SMEM)
 VMEM = pl.BlockSpec(memory_space=pltpu.VMEM)
-ANY = pl.BlockSpec(memory_space=pl.ANY)
+HBM = pl.BlockSpec(memory_space=pltpu.HBM)
+
+
+def far(shape):
+    return pltpu.HBM(shape, F32)
+
+
+def near(shape):
+    return pltpu.VMEM(shape, F32)
+
 
 euler_step = 0.02
 
@@ -96,12 +105,24 @@
 
 
 def compose_kernel(
-    seqs, blocks, total_seqs, keep, place_ref, steps_ref, x_ref, guess_ref, recur_ref, damping_ref,
-    in_ref, bias_ref, targets_ref,
+    seqs, blocks, total_seqs, keep, steps_in, x_in, guess_in, recur_in, damping_in, in_in, bias_in,
+    targets_in,
     message_ref, maps_out, before_out, start_ref, hit_ref, reach_ref, reach_off_ref, gain_ref,
     resid_ref, drift_ref,
-    partial_ref, before_ref, off_ref, hit_off_ref, prev_ref, maps_sem, before_sem,
+    record_ref, record_off_ref, maps_ref, before_ref, off_ref, hit_off_ref, prev_ref,
+    steps_ref, x_ref, guess_ref, recur_ref, damping_ref, in_ref, bias_ref, targets_ref, sems,
 ):
+    fetches = [
+        pltpu.make_async_copy(source, to, sems.at[i])
+        for i, (source, to) in enumerate([
+            (recur_in, recur_ref), (damping_in, damping_ref), (guess_in, guess_ref), (x_in, x_ref),
+            (in_in, in_ref), (bias_in, bias_ref), (targets_in, targets_ref), (steps_in, steps_ref),
+        ])
+    ]
+    for fetch in fetches:
+        fetch.start()
+    for fetch in fetches[:3]:
+        fetch.wait()
     rows, hidden = guess_ref.shape
     count = rows // seqs
     chunks = count // LANE
@@ -116,6 +137,8 @@
     for s in range(seqs):
         prev_ref[pl.ds(s * count, 1), :] = jnp.zeros((1, hidden), F32)
     prev = prev_ref[...]
+    for fetch in fetches[3:]:
+        fetch.wait()
     x_high, x_low = split(x_ref[...])
     in_w = jnp.concatenate(split(in_ref[...]), axis=1)
     drive = bias_ref[...] + halves(
@@ -125,7 +148,7 @@
     activation = jnp.tanh(mul(prev, drift_w) + drive)
     gain_ref[...] = euler_step * (1.0 - activation * activation)
     resid_ref[...] = prev + euler_step * activation - guess
-    own = (place_ref[0] == 0).astype(F32)
+    own = (lax.axis_index("seq") == 0).astype(F32)
     for s in range(seqs):
         edge = pl.ds(s * count, 1)
         gain_ref[edge, :] = gain_ref[edge, :] * own
@@ -133,39 +156,47 @@
 
     unit = identity(hidden)
     for lane in range(lanes):
-        partial_ref[0, lane] = unit + drift * gain_ref[pl.ds(lane * LANE, 1), :]
-    off_ref[0] = resid_ref[pl.ds(0, lanes, stride=LANE), :]
+        first = unit + drift * gain_ref[pl.ds(lane * LANE, 1), :]
+        maps_ref[lane] = first
+        if keep:
+            record_ref[0, lane] = first
+    off_ref[...] = resid_ref[pl.ds(0, lanes, stride=LANE), :]
+    if keep:
+        record_off_ref[0] = off_ref[...]
 
     def place(j):
         step = (j % blocks) * block + steps_ref[j // blocks, j % blocks]
         return (j // blocks) * chunks + step // LANE, step % LANE, (j // blocks) * count + step
 
-    def slot(now):
-        return now if keep else 0
-
     def capture(now):
         for j in range(seqs * blocks):
             lane, at, _ = place(j)
 
             @pl.when(at == now)
             def _():
-                hit_ref[j] = partial_ref[0, lane]
-                hit_off_ref[pl.ds(j, 1), :] = off_ref[0, pl.ds(lane, 1), :]
+                hit_ref[j] = maps_ref[lane]
+                hit_off_ref[pl.ds(j, 1), :] = off_ref[pl.ds(lane, 1), :]
 
     def advance(now, _):
-        off = off_ref[slot(now - 1)]
-        off_ref[slot(now)] = (
+        off = off_ref[...]
+        off = (
             off
             + gain_ref[pl.ds(now, lanes, stride=LANE), :] * mul(off, drift_w)
             + resid_ref[pl.ds(now, lanes, stride=LANE), :]
         )
+        off_ref[...] = off
+        if keep:
+            record_off_ref[now] = off
         for lane in range(0, lanes, 2):
-            pair = partial_ref[slot(now - 1), lane : lane + 2].reshape(2 * hidden, hidden)
+            pair = maps_ref[lane : lane + 2].reshape(2 * hidden, hidden)
             moved = mul(pair, drift_w)
             for k in range(2):
                 gain_now = gain_ref[pl.ds((lane + k) * LANE + now, 1), :]
                 part = slice(k * hidden, (k + 1) * hidden)
-                partial_ref[slot(now), lane + k] = pair[part] + gain_now * moved[part]
+                longer = pair[part] + gain_now * moved[part]
+                maps_ref[lane + k] = longer
+                if keep:
+                    record_ref[now, lane + k] = longer
         if not keep:
             capture(now)
         return 0
@@ -174,13 +205,12 @@
         lax.fori_loop(1, LANE, advance, 0, unroll=UNROLL)
         for j in range(seqs * blocks):
             lane, at, _ = place(j)
-            hit_ref[j] = partial_ref[at, lane]
-            hit_off_ref[pl.ds(j, 1), :] = off_ref[at, pl.ds(lane, 1), :]
+            hit_ref[j] = record_ref[at, lane]
+            hit_off_ref[pl.ds(j, 1), :] = record_off_ref[at, pl.ds(lane, 1), :]
     else:
         capture(0)
         lax.fori_loop(1, LANE, advance, 0)
-    last = slot(LANE - 1)
-    maps_copy = pltpu.make_async_copy(partial_ref.at[last], maps_out, maps_sem)
+    maps_copy = pltpu.make_async_copy(maps_ref, maps_out, sems.at[8])
     maps_copy.start()
 
     running = [unit] * seqs
@@ -190,14 +220,14 @@
             lane = s * chunks + chunk
             before_ref[lane] = running[s]
             start_ref[pl.ds(lane, 1), :] = offset[s][:1]
-            this, this_off = partial_ref[last, lane], off_ref[last, pl.ds(lane, 1), :]
+            this, this_off = maps_ref[lane], off_ref[pl.ds(lane, 1), :]
             if chunk == 0:
                 running[s], offset[s] = this, eight(this_off)
             else:
                 packed = right(this)
                 running[s] = mul(running[s], packed)
                 offset[s] = mul(offset[s], packed) + this_off
-    before_copy = pltpu.make_async_copy(before_ref, before_out, before_sem)
+    before_copy = pltpu.make_async_copy(before_ref, before_out, sems.at[9])
     before_copy.start()
 
     for s in range(seqs):
@@ -254,9 +284,9 @@
     return (mul(map_1, map_w) if with_map else None), curve, rows
 
 
-def join_kernel(level, with_map, place_ref, drift_ref, mine_ref, other_ref, out_ref):
+def join_kernel(level, with_map, drift_ref, mine_ref, other_ref, _, out_ref):
     seqs, hidden = mine_ref.shape[0], mine_ref.shape[2]
-    upper = (place_ref[0] >> level) & 1 == 1
+    upper = (lax.axis_index("seq") >> level) & 1 == 1
     drift_w = right(drift_ref[...])
     for s in range(seqs):
         mine, other = opened(mine_ref, s), opened(other_ref, s)
@@ -269,7 +299,7 @@
         out_ref[s, pl.ds(at + hidden, 8), :] = vectors(*rows)
 
 
-def sides_kernel(levels, place_ref, drift_ref, *refs):
+def sides_kernel(levels, drift_ref, *refs):
     mines, others = refs[:levels], refs[levels : 2 * levels]
     entry_ref, tail_ref, back_ref, rows_ref = refs[2 * levels :]
     seqs, hidden = entry_ref.shape[0], entry_ref.shape[1]
@@ -280,9 +310,10 @@
         lead, lead_off = unit, zero
         after = (unit, jnp.zeros((hidden, hidden), F32), [zero] * 5)
         edge, edge_gain = zero, zero
-        fresh = place_ref[0] >= 0
+        place = lax.axis_index("seq")
+        fresh = place >= 0
         for level in range(levels):
-            upper = (place_ref[0] >> level) & 1 == 1
+            upper = (place >> level) & 1 == 1
             mine, other = opened(mines[level], s), opened(others[level], s)
             gain, resid = crossing(other[2][LAST], mine[2][DRIVE], mine[2][FIRST], drift_w)
             far = other[0] + mul(other[0], drift_w) * gain[:1]
@@ -307,25 +338,36 @@
 
 
 def prepare_kernel(
-    seqs, blocks, steps_ref, maps_ref, hit_ref, x_ref, guess_ref,
-    home_ref, pull_ref, high_ref, low_ref,
-    prev_ref,
+    seqs, blocks, steps_in, maps_in, x_in, guess_in, hit_ref,
+    home_out, pull_out, high_ref, low_ref, ready_ref,
+    home_ref, pull_ref, prev_ref, steps_ref, maps_ref, x_ref, guess_ref, in_sems, out_sems,
 ):
+    fetches = [
+        pltpu.make_async_copy(source, to, in_sems.at[i])
+        for i, (source, to) in enumerate(
+            [(maps_in, maps_ref), (steps_in, steps_ref), (guess_in, guess_ref), (x_in, x_ref)]
+        )
+    ]
+    for fetch in fetches:
+        fetch.start()
+    ready_ref[...] = jnp.zeros_like(ready_ref)
     rows, hidden = guess_ref.shape
     count = rows // seqs
     chunks = count // LANE
     per_block = chunks // blocks
     unit = identity(hidden)
     blank = jnp.zeros((hidden, hidden), F32)
-    prev_ref[pl.ds(1, rows - 1), :] = guess_ref[pl.ds(0, rows - 1), :]
-    for s in range(seqs):
-        prev_ref[pl.ds(s * count, 1), :] = jnp.zeros((1, hidden), F32)
-    high_ref[pl.ds(0, hidden), :], low_ref[pl.ds(0, hidden), :] = split(prev_ref[...].T)
-    high_ref[pl.ds(hidden, x_ref.shape[1]), :], low_ref[pl.ds(hidden, x_ref.shape[1]), :] = split(
-        x_ref[...].T
-    )
     home = [unit] * seqs
     pulls = [[blank] * blocks for _ in range(seqs)]
+    sends = []
+
+    def send(source, to):
+        copy = pltpu.make_async_copy(source, to, out_sems.at[len(sends)])
+        copy.start()
+        sends.append(copy)
+
+    fetches[0].wait()
+    fetches[1].wait()
     for chunk in reversed(range(chunks)):
         for s in range(seqs):
             lane = s * chunks + chunk
@@ -333,6 +375,12 @@
             active = [k for k in range(blocks) if chunk < (k + 1) * per_block]
             for k in active:
                 pull_ref[s * blocks + k, chunk] = pulls[s][k]
+            if chunk % per_block == 0:
+                for k in active:
+                    part = (s * blocks + k, pl.ds(chunk, per_block))
+                    send(pull_ref.at[part], pull_out.at[part])
+                part = pl.ds(lane, per_block)
+                send(home_ref.at[part], home_out.at[part])
             if chunk:
                 stack = jnp.concatenate([home[s]] + [pulls[s][k] for k in active], axis=0)
                 stack = mul_t(stack, right_t(maps_ref[lane]))
@@ -341,14 +389,25 @@
                     owner = (k * (count // blocks) + steps_ref[s, k]) // LANE
                     part = stack[(i + 1) * hidden : (i + 2) * hidden]
                     pulls[s][k] = jnp.where(owner == chunk, hit_ref[s * blocks + k].T, part)
+    fetches[2].wait()
+    fetches[3].wait()
+    prev_ref[pl.ds(1, rows - 1), :] = guess_ref[pl.ds(0, rows - 1), :]
+    for s in range(seqs):
+        prev_ref[pl.ds(s * count, 1), :] = jnp.zeros((1, hidden), F32)
+    high_ref[pl.ds(0, hidden), :], low_ref[pl.ds(0, hidden), :] = split(prev_ref[...].T)
+    high_ref[pl.ds(hidden, x_ref.shape[1]), :], low_ref[pl.ds(hidden, x_ref.shape[1]), :] = split(
+        x_ref[...].T
+    )
+    for copy in sends:
+        copy.wait()
 
 
 def solve_kernel(
-    seqs, blocks, total_seqs, level, place_ref, steps_ref, drift_ref, mine_ref, other_ref,
-    entry_ref, tail_ref, back_ref, sides_ref, before_ref, start_ref, home_ref, pull_ref, reach_ref,
+    seqs, blocks, total_seqs, level, steps_in, drift_ref, mine_ref, other_ref,
+    home_in, pull_in, entry_ref, tail_ref, back_ref, sides_ref, before_ref, start_ref, reach_ref,
     reach_off_ref, gain_ref, resid_ref, guess_ref, high_ref, low_ref,
-    path_ref, grads_ref,
-    state_ref, carry_ref, source_ref, pre_ref, gain_back_ref,
+    path_out, grads_ref,
+    state_ref, carry_ref, source_ref, pre_ref, gain_back_ref, path_ref, home_ref, pull_ref, steps_ref, sems,
 ):
     rows, hidden = guess_ref.shape
     count = rows // seqs
@@ -356,8 +415,26 @@
     lanes = seqs * chunks
     block = count // blocks
     per_block = chunks // blocks
-    upper = (place_ref[0] >> level) & 1 == 1
-    lowest = (place_ref[0] & ((1 << level) - 1)) == 0
+    fetch_steps = pltpu.make_async_copy(steps_in, steps_ref, sems.at[0])
+    fetch_steps.start()
+    per_block = guess_ref.shape[0] // seqs // LANE // blocks
+    fetches = [[] for _ in range(blocks)]
+
+    def fetch(part, source, to):
+        copy = pltpu.make_async_copy(source, to, sems.at[2 + sum(map(len, fetches))])
+        copy.start()
+        fetches[part].append(copy)
+
+    for part in range(blocks):
+        for s in range(seqs):
+            at = pl.ds((s * blocks + part) * per_block, per_block)
+            fetch(part, home_in.at[at], home_ref.at[at])
+            for k in range(part, blocks):
+                at = (s * blocks + k, pl.ds(part * per_block, per_block))
+                fetch(part, pull_in.at[at], pull_ref.at[at])
+    place = lax.axis_index("seq")
+    upper = (place >> level) & 1 == 1
+    lowest = (place & ((1 << level) - 1)) == 0
     drift = drift_ref[...]
     drift_w = right(drift)
     drift_wt = right_t(drift)
@@ -389,6 +466,8 @@
         at = pl.ds(s * count, 1)
         gain_back_ref[at, :] = gain_ref[at, :] + edge_gain
         here = []
+        if s == 0:
+            fetch_steps.wait()
         for k in range(blocks):
             j = s * blocks + k
             miss = (along(entries[s], reach_ref[j]) + reach_off_ref[pl.ds(j, 1), :]) / total_seqs
@@ -397,6 +476,8 @@
         sources.append(here)
 
     for part in range(blocks):
+        for copy in fetches[part]:
+            copy.wait()
 
         def ends(chunk, _):
             for s in range(seqs):
@@ -422,6 +503,8 @@
         return state, adjoint + mul_t(scaled, drift_wt)
 
     lax.fori_loop(0, LANE, walk, (state_ref[...], carry_ref[...]), unroll=2)
+    path_copy = pltpu.make_async_copy(path_ref, path_out, sems.at[1])
+    path_copy.start()
 
     pre_high, pre_low = split(pre_ref[...])
     pre_w = jnp.concatenate([pre_high, pre_low], axis=1)
@@ -438,12 +521,13 @@
     folded = jnp.where(col > row, recur[:half, :half], recur[half:, half:])
     grads_ref[pl.ds(0, half), :] = jnp.concatenate([folded, recur[:half, half:]], axis=1)
     grads_ref[pl.ds(half, sums.shape[0] - hidden), :] = sums[hidden:]
-
-
-def unfold_kernel(place_ref, mine_ref, other_ref, recur_ref, in_ref):
+    path_copy.wait()
+
+
+def unfold_kernel(mine_ref, other_ref, recur_ref, in_ref):
     hidden = recur_ref.shape[0]
     half = hidden // 2
-    odd = place_ref[1] & 1 == 1
+    odd = lax.axis_index("batch") & 1 == 1
     mine, other = mine_ref[...], other_ref[...]
     whole = jnp.concatenate([jnp.where(odd, other, mine), jnp.where(odd, mine, other)], axis=0)
     in_ref[...] = whole[half:]
@@ -456,17 +540,27 @@
     recur_ref[pl.ds(half, half), :] = jnp.concatenate([-corner.T, last - last.T], axis=1)
 
 
-def call(kernel, shapes, in_specs, scratch=(), flops=0, room=24, out_specs=None):
-    shapes = [shape if hasattr(shape, "dtype") else jax.ShapeDtypeStruct(shape, F32) for shape in shapes]
-    return pl.pallas_call(
+def call(kernel, shapes, in_specs, scratch=(), flops=0, room=14):
+    out_shapes = [jax.ShapeDtypeStruct(s, F32) if isinstance(s, tuple) else s for s in shapes]
+    run = pl.pallas_call(
         kernel,
-        out_shape=shapes,
+        out_shape=out_shapes,
         in_specs=in_specs,
-        out_specs=out_specs or [VMEM] * len(shapes),
+        out_specs=[
+            HBM if getattr(s, "memory_space", None) == pltpu.HBM else VMEM for s in out_shapes
+        ],
         scratch_shapes=[pltpu.VMEM(s, F32) if isinstance(s, tuple) else s for s in scratch],
         compiler_params=pltpu.CompilerParams(vmem_limit_bytes=room * MIB),
         cost_estimate=pl.CostEstimate(flops=flops, bytes_accessed=1 << 20, transcendentals=0),
     )
+
+    def pinned(*operands):
+        return run(*[
+            pltpu.with_memory_space_constraint(x, pltpu.HBM) if spec is HBM else x
+            for x, spec in zip(operands, in_specs, strict=True)
+        ])
+
+    return pinned
 
 
 def swapped(value, axis, distance):
@@ -488,7 +582,6 @@
     chunks = lanes // seqs
     hits = seqs * blocks
     total_seqs = seqs * lax.axis_size("batch")
-    place = jnp.stack([lax.axis_index("seq"), lax.axis_index("batch")]).astype(jnp.int32)
     x = inputs.reshape(rows, features)
     guess = guess_path.reshape(rows, hidden)
     keep = rows * hidden * hidden * 4 <= KEEP
@@ -497,9 +590,9 @@
     message, maps, before, start, hit, reach, reach_off, gain, resid, drift = call(
         functools.partial(compose_kernel, seqs, blocks, total_seqs, keep),
         [
-            (seqs, 2 * hidden + 8, hidden),
-            (lanes, hidden, hidden),
-            (lanes, hidden, hidden),
+            near((seqs, 2 * hidden + 8, hidden)),
+            far((lanes, hidden, hidden)),
+            far((lanes, hidden, hidden)),
             (lanes, hidden),
             (hits, hidden, hidden),
             (hits, hidden, hidden),
@@ -508,33 +601,53 @@
             (rows, hidden),
             (hidden, hidden),
         ],
-        [SMEM, SMEM] + [VMEM] * 7,
+        [HBM] * 8,
         [
-            (depth, lanes, hidden, hidden),
+            (depth, lanes if keep else 1, hidden, hidden),
+            (depth, lanes if keep else 1, hidden),
             (lanes, hidden, hidden),
-            (depth, lanes, hidden),
+            (lanes, hidden, hidden),
+            (lanes, hidden),
             (hits, hidden),
             (rows, hidden),
-            pltpu.SemaphoreType.DMA(()),
-            pltpu.SemaphoreType.DMA(()),
+            pltpu.SMEM((seqs, blocks), jnp.int32),
+            (rows, features),
+            (rows, hidden),
+            (hidden, hidden),
+            (1, hidden),
+            (features, hidden),
+            (1, hidden),
+            (hits, hidden),
+            pltpu.SemaphoreType.DMA((10,)),
         ],
-        room=56,
-        out_specs=[VMEM, ANY, ANY] + [VMEM] * 7,
-    )(place, target_steps, x, guess, recur_weight, damping.reshape(1, hidden), in_weight,
+        room=ROOM,
+    )(target_steps, x, guess, recur_weight, damping.reshape(1, hidden), in_weight,
       bias_term.reshape(1, hidden), targets.reshape(hits, hidden))
 
-    home, pull, high, low = call(
+    home, pull, high, low, ready = call(
         functools.partial(prepare_kernel, seqs, blocks),
+        [
+            far((lanes, hidden, hidden)),
+            far((hits, chunks, hidden, hidden)),
+            jax.ShapeDtypeStruct((hidden + features, rows), BF16),
+            jax.ShapeDtypeStruct((hidden + features, rows), BF16),
+            (8, hidden),
+        ],
+        [HBM, HBM, HBM, HBM, VMEM],
         [
             (lanes, hidden, hidden),
             (hits, chunks, hidden, hidden),
-            jax.ShapeDtypeStruct((hidden + features, rows), BF16),
-            jax.ShapeDtypeStruct((hidden + features, rows), BF16),
+            (rows, hidden),
+            pltpu.SMEM((seqs, blocks), jnp.int32),
+            (lanes, hidden, hidden),
+            (rows, features),
+            (rows, hidden),
+            pltpu.SemaphoreType.DMA((4,)),
+            pltpu.SemaphoreType.DMA((seqs * blocks * (blocks + 3) // 2,)),
         ],
-        [SMEM] + [VMEM] * 4,
-        [(rows, hidden)],
         flops=1 << 32,
-    )(target_steps, maps, hit, x, guess)
+        room=20,
+    )(target_steps, maps, x, guess, hit)
 
     levels = levels_of("seq")
     groups, received = [message], []
@@ -545,27 +658,32 @@
         groups += call(
             functools.partial(join_kernel, level, with_map),
             [(seqs, height, hidden)],
-            [SMEM, VMEM, VMEM, VMEM],
-        )(place, drift, groups[-1], received[-1])
+            [VMEM, VMEM, VMEM, VMEM],
+        )(drift, groups[-1], received[-1], ready)
     other = swapped(groups[-1], "seq", 1 << (levels - 1))
     square = (seqs, hidden, hidden)
     entry, tail, back, sides = call(
         functools.partial(sides_kernel, levels - 1),
         [square, square, square, (8 * seqs, hidden)],
-        [SMEM] + [VMEM] * (2 * levels - 1),
+        [VMEM] * (2 * levels - 1),
         flops=1 << 30,
-    )(place, drift, *groups[:-1], *received)
+    )(drift, *groups[:-1], *received)
 
     path, grads = call(
         functools.partial(solve_kernel, seqs, blocks, total_seqs, levels - 1),
-        [(rows, hidden), (hidden // 2 + features, hidden)],
-        [SMEM, SMEM] + [VMEM] * 18,
-        [(lanes, hidden), (lanes, hidden), (rows, hidden), (rows, hidden), (rows, hidden)],
-    )(place, target_steps, drift, groups[-1], other, entry, tail, back, sides, before, start, home,
-      pull, reach, reach_off, gain, resid, guess, high, low)
+        [far((rows, hidden)), near((hidden // 2 + features, hidden))],
+        [HBM] + [VMEM] * 3 + [HBM] * 2 + [VMEM] * 13,
+        [(lanes, hidden)] * 2 + [(rows, hidden)] * 4 + [
+            (lanes, hidden, hidden),
+            (hits, chunks, hidden, hidden),
+            pltpu.SMEM((seqs, blocks), jnp.int32),
+            pltpu.SemaphoreType.DMA((2 + seqs * blocks * (blocks + 3) // 2,)),
+        ],
+    )(target_steps, drift, groups[-1], other, home, pull, entry, tail, back, sides, before, start,
+      reach, reach_off, gain, resid, guess, high, low)
 
     middle = grads.shape[0] // 2
-    odd = place[1] & 1 == 1
+    odd = lax.axis_index("batch") & 1 == 1
     kept = jnp.where(odd, grads[middle:], grads[:middle])
     given = jnp.where(odd, grads[:middle], grads[middle:])
     kept = kept + swapped(given, "batch", 1)
@@ -576,8 +694,8 @@
     grad_recur, grad_in = call(
         unfold_kernel,
         [(hidden, hidden), (features, hidden)],
-        [SMEM, VMEM, VMEM],
-    )(place, kept, swapped(kept, "batch", 1))
+        [VMEM, VMEM],
+    )(kept, swapped(kept, "batch", 1))
     return (path.reshape(seqs, count, hidden), grad_recur, grad_in)
 
 

time: 128 us -> 74.5 us (0.58)
  Pallas kernels: 69.2 us -> 33.6 us
  local copies, waits for them, and re-layouts: 15.1 us -> 1.96 us
  waiting for transfers between devices: 28.7 us -> 25.3 us
    pallas_call x7, Pallas kernels: 69.2 us -> 33.6 us  [pinned(): run(*[pltpu.with_memory_space_constraint(x, pltpu.HBM) if spec is HBM els...]
    unnamed x54 -> x28, local copies, waits for them, and re-layouts: 15.1 us -> 1.96 us
    ppermute x9, waiting for transfers between devices: 28.7 us -> 25.3 us  [swapped(): lax.ppermute(value, axis, [(i, i ^ distance) for i in range(lax.axis_size...]
  transfers between devices with their start and end apart: 9 -> 9, of which waited for: 8 -> 9; matrix products, arithmetic and copies ran while one was open for 0% -> 0% of each run, Pallas kernels for 5% -> 11%
where the time goes in v3:
time: 74.5 us; the launch traced here: 74.2 us
  Pallas kernels  33.6 us (45%)
  waiting for transfers between devices  25.3 us (34%)
  starting transfers between devices  12.5 us (17%)
  local copies, waits for them, and re-layouts  1.96 us (3%)
  between operations  0.84 us (1%)
    pallas_call x7, Pallas kernels, pinned(): run(*[pltpu.with_memory_space_constraint(x, pltpu.HBM) if spec is HBM els...  33.6 us
    ppermute x9, waiting for transfers between devices, swapped(): lax.ppermute(value, axis, [(i, i ^ distance) for i in range(lax.axis_size...  25.3 us
    ppermute x9, starting transfers between devices, swapped(): lax.ppermute(value, axis, [(i, i ^ distance) for i in range(lax.axis_size...  12.5 us
    unnamed x28, local copies, waits for them, and re-layouts  1.96 us
  transfers between devices with their start and end apart: 9, of which 9 were waited for; matrix products, arithmetic and copies ran while one was open for 0% of the time, Pallas kernels for 11%

profile of v3, /device:TPU:0, one launch (start us, length us, event | category | flops | bytes accessed | tf_op | source)
XLA Modules:
  0.0 74.2 jit_solution(10099532708683734883)
XLA Ops:
  0.6 15.8 %shard_map.103 = (f32[2,264,128]{2,1,0:T(8,128)S(1)}, f32[32,128,128]{2,1,0:T(8,128)}, f32[32,128,128]{2,1,0:T(8,128)}, f32[32,128]{1,0:T(8,128)S(1)}, f32[4,128...) custom-call(s32[2,2]{1,0:T(2,128)} %steps_in.5, ...), custom_call_target="tpu_custom_call" | custom-call | bytes 1048576 | tf_op jit(solution)/shard_map/pallas_call | solution.py:558
  16.4 0.0 copy-start.8
  16.4 0.0 copy-start.10
  16.4 0.0 copy-start.12
  16.4 3.0 %collective-permute-start = (f32[2,264,128]{2,1,0:T(8,128)S(1)}, f32[2,264,128]{2,1,0:T(8,128)S(1)}, u32[]{:S(2)}, u32[]{:S(2)}) collective-permute-start(f32[2,264,128]{2,1,0:T(8,128)S(1)} %get-tuple-element.27.mine_ref.refs_0_), channel_id=1, source_target_pairs={{0,4},{4,0},{8,12},{12,8},{16,20},{20,16},{24,28},{28,24},{1,5},{5... | collective-permute-start | bytes 811016 | tf_op jit(solution)/shard_map/ppermute | solution.py:567
  19.4 5.5 %shard_map.104 = (f32[32,128,128]{2,1,0:T(8,128)}, f32[4,16,128,128]{3,2,1,0:T(8,128)}, bf16[384,512]{1,0:T(8,128)(2,1)S(1)}, bf16[384,512]{1,0:T(8,128)(2,1)S(1)}, f32[8,128]{1,0:T(8,128)S(1)}) custom-call(s32[2,2]{1,0:T(2,128)} %steps_in.5, f32[32,128,128]{2,1,0:T(8,128)} %get-tuple-element.28.maps_in, f32[512,256]{1,0:T(8,128)} %bitcast.10, ...), custom_call_target="tpu_custom_call" | custom-call | flops 4294967296 | bytes 1048576 | tf_op jit(solution)/shard_map/pallas_call | solution.py:558
  24.9 0.0 copy-done.8
  24.9 0.0 copy-done.10
  24.9 0.0 copy-done.12
  24.9 0.0 copy-start.2
  25.0 1.0 %collective-permute-done.other_ref.refs_2_ = f32[2,264,128]{2,1,0:T(8,128)S(1)} collective-permute-done((f32[2,264,128]{2,1,0:T(8,128)S(1)}, f32[2,264,128]{2,1,0:T(8,128)S(1)}, u32[]{:S(2)}, u32[]{:S(2)}) %collective-permute-start) | collective-permute-done | bytes 270368 | tf_op jit(solution)/shard_map/ppermute | solution.py:567
  25.9 0.0 copy-start.4
  25.9 0.9 %shard_map.105.mine_ref.refs_1_ = f32[2,264,128]{2,1,0:T(8,128)S(1)} custom-call(f32[128,128]{1,0:T(8,128)S(1)} %get-tuple-element.26.drift_ref, f32[2,264,128]{2,1,0:T(8,128)S(1)} %get-tuple-element.27.mine_ref.refs_0_, f32[2,264,128]{2,1,0:T(8,128)S(1)} %collective-permute-done.other_ref.refs_2_, f32[8,128]{1,0:T(8,128)S(1)} %get-tuple-element.30._), custom_call_target="tpu_custom_call" | custom-call | bytes 1048576 | tf_op jit(solution)/shard_map/pallas_call | solution.py:558
  26.8 1.9 %collective-permute-start.1 = (f32[2,264,128]{2,1,0:T(8,128)S(1)}, f32[2,264,128]{2,1,0:T(8,128)S(1)}, u32[]{:S(2)}, u32[]{:S(2)}) collective-permute-start(f32[2,264,128]{2,1,0:T(8,128)S(1)} %shard_map.105.mine_ref.refs_1_), channel_id=1, source_target_pairs={{0,8},{4,12},{8,0},{12,4},{16,24},{20,28},{24,16},{28,20},{1,9},{5... | collective-permute-start | bytes 811016 | tf_op jit(solution)/shard_map/ppermute | solution.py:567
  28.7 5.8 %collective-permute-done.1.other_ref.refs_3_ = f32[2,264,128]{2,1,0:T(8,128)S(1)} collective-permute-done((f32[2,264,128]{2,1,0:T(8,128)S(1)}, f32[2,264,128]{2,1,0:T(8,128)S(1)}, u32[]{:S(2)}, u32[]{:S(2)}) %collective-permute-start.1) | collective-permute-done | bytes 270368 | tf_op jit(solution)/shard_map/ppermute | solution.py:567
  34.5 0.0 copy-done.2
  34.5 0.0 copy-start.6
  34.5 0.8 %shard_map.106.mine_ref = f32[2,136,128]{2,1,0:T(8,128)S(1)} custom-call(f32[128,128]{1,0:T(8,128)S(1)} %get-tuple-element.26.drift_ref, f32[2,264,128]{2,1,0:T(8,128)S(1)} %shard_map.105.mine_ref.refs_1_, f32[2,264,128]{2,1,0:T(8,128)S(1)} %collective-permute-done.1.other_ref.refs_3_, f32[8,128]{1,0:T(8,128)S(1)} %get-tuple-element.30._), custom_call_target="tpu_custom_call" | custom-call | bytes 1048576 | tf_op jit(solution)/shard_map/pallas_call | solution.py:558
  35.3 0.0 copy-done.4
  35.4 0.0 copy-start
  35.4 0.0 copy-start.1
  35.4 2.6 %collective-permute-start.2 = (f32[2,136,128]{2,1,0:T(8,128)S(1)}, f32[2,136,128]{2,1,0:T(8,128)}, u32[]{:S(2)}, u32[]{:S(2)}) collective-permute-start(f32[2,136,128]{2,1,0:T(8,128)S(1)} %shard_map.106.mine_ref), channel_id=1, source_target_pairs={{0,16},{4,20},{8,24},{12,28},{16,0},{20,4},{24,8},{28,12},{1,17},{... | collective-permute-start | bytes 417800 | tf_op jit(solution)/shard_map/ppermute | solution.py:567
  37.9 0.0 copy-done.6
  37.9 0.0 copy-start.5
  38.0 1.0 %copy-done.5 = f32[2,264,128]{2,1,0:T(8,128)S(1)} copy-done((f32[2,264,128]{2,1,0:T(8,128)S(1)}, f32[2,264,128]{2,1,0:T(8,128)}, u32[]{:S(2)}) %copy-start.5) | copy-done | bytes 270360
  38.9 0.0 copy-start.7
  38.9 1.0 %copy-done.7 = f32[2,264,128]{2,1,0:T(8,128)S(1)} copy-done((f32[2,264,128]{2,1,0:T(8,128)S(1)}, f32[2,264,128]{2,1,0:T(8,128)}, u32[]{:S(2)}) %copy-start.7) | copy-done | bytes 270360
  39.9 0.0 copy-start.3
  39.9 0.0 copy-start.9
  39.9 0.0 copy-start.11
  39.9 0.0 copy-start.13
  39.9 2.6 %shard_map.107 = (f32[2,128,128]{2,1,0:T(8,128)S(1)}, f32[2,128,128]{2,1,0:T(8,128)S(1)}, f32[2,128,128]{2,1,0:T(8,128)S(1)}, f32[16,128]{1,0:T(8,128)S(1)}) custom-call(f32[128,128]{1,0:T(8,128)S(1)} %get-tuple-element.26.drift_ref, f32[2,264,128]{2,1,0:T(8,128)S(1)} %get-tuple-element.27.mine_ref.refs_0_, f32[2,264,128]{2,1,0:T(8,128)S(1)} %shard_map.105.mine_ref.refs_1_, ...), custom_call_target="tpu_custom_call" | custom-call | flops 1073741824 | bytes 1048576 | tf_op jit(solution)/shard_map/pallas_call | solution.py:558
  42.5 0.9 %collective-permute-done.2.other_ref = f32[2,136,128]{2,1,0:T(8,128)} collective-permute-done((f32[2,136,128]{2,1,0:T(8,128)S(1)}, f32[2,136,128]{2,1,0:T(8,128)}, u32[]{:S(2)}, u32[]{:S(2)}) %collective-permute-start.2) | collective-permute-done | bytes 139296 | tf_op jit(solution)/shard_map/ppermute | solution.py:567
  43.4 0.0 copy-done
  43.4 0.0 copy-done.1
  43.4 0.0 copy-done.3
  43.4 0.0 copy-done.9
  43.4 0.0 copy-done.11
  43.4 0.0 copy-done.13
  43.4 7.3 %shard_map.108 = (f32[512,128]{1,0:T(8,128)}, f32[320,128]{1,0:T(8,128)S(1)}) custom-call(s32[2,2]{1,0:T(2,128)} %steps_in.5, f32[128,128]{1,0:T(8,128)S(1)} %get-tuple-element.26.drift_ref, f32[2,136,128]{2,1,0:T(8,128)S(1)} %shard_map.106.mine_ref, f32[2,136,128]{2,1,0:T(8,128)} %collective-permute-done.2.other_ref, ...), custom_call_target="tpu_custom_call" | custom-call | bytes 1048576 | tf_op jit(solution)/shard_map/pallas_call | solution.py:558
  50.8 0.1 collective-permute-start.3
  50.9 1.3 %collective-permute-done.3 = f32[160,128]{1,0:T(8,128)S(1)} collective-permute-done((f32[160,128]{1,0:T(8,128)S(1)}, f32[160,128]{1,0:T(8,128)S(1)}, u32[]{:S(2)}, u32[]{:S(2)}) %collective-permute-start.3) | collective-permute-done | bytes 81952 | tf_op jit(solution)/shard_map/ppermute | solution.py:567
  52.2 1.2 %collective-permute-start.4 = (f32[160,128]{1,0:T(8,128)S(1)}, f32[160,128]{1,0:T(8,128)S(1)}, u32[]{:S(2)}, u32[]{:S(2)}) collective-permute-start(f32[160,128]{1,0:T(8,128)S(1)} %select_add_fusion), channel_id=1, source_target_pairs={{0,2},{1,3},{2,0},{3,1},{4,6},{5,7},{6,4},{7,5},{8,10},{9,11},{10,... | collective-permute-start | bytes 245768 | tf_op jit(solution)/shard_map/ppermute | solution.py:567
  53.3 3.4 %collective-permute-done.4 = f32[160,128]{1,0:T(8,128)S(1)} collective-permute-done((f32[160,128]{1,0:T(8,128)S(1)}, f32[160,128]{1,0:T(8,128)S(1)}, u32[]{:S(2)}, u32[]{:S(2)}) %collective-permute-start.4) | collective-permute-done | bytes 81952 | tf_op jit(solution)/shard_map/ppermute | solution.py:567
  56.7 1.2 %collective-permute-start.5 = (f32[160,128]{1,0:T(8,128)S(1)}, f32[160,128]{1,0:T(8,128)S(1)}, u32[]{:S(2)}, u32[]{:S(2)}) collective-permute-start(f32[160,128]{1,0:T(8,128)S(1)} %add.16), channel_id=1, source_target_pairs={{0,4},{4,0},{8,12},{12,8},{16,20},{20,16},{24,28},{28,24},{1,5},{5... | collective-permute-start | bytes 245768 | tf_op jit(solution)/shard_map/ppermute | solution.py:567
  57.9 3.3 %collective-permute-done.5 = f32[160,128]{1,0:T(8,128)S(1)} collective-permute-done((f32[160,128]{1,0:T(8,128)S(1)}, f32[160,128]{1,0:T(8,128)S(1)}, u32[]{:S(2)}, u32[]{:S(2)}) %collective-permute-start.5) | collective-permute-done | bytes 81952 | tf_op jit(solution)/shard_map/ppermute | solution.py:567
  61.3 0.8 %collective-permute-start.6 = (f32[160,128]{1,0:T(8,128)S(1)}, f32[160,128]{1,0:T(8,128)S(1)}, u32[]{:S(2)}, u32[]{:S(2)}) collective-permute-start(f32[160,128]{1,0:T(8,128)S(1)} %add.17), channel_id=1, source_target_pairs={{0,8},{4,12},{8,0},{12,4},{16,24},{20,28},{24,16},{28,20},{1,9},{5... | collective-permute-start | bytes 245768 | tf_op jit(solution)/shard_map/ppermute | solution.py:567
  62.0 3.7 %collective-permute-done.6 = f32[160,128]{1,0:T(8,128)S(1)} collective-permute-done((f32[160,128]{1,0:T(8,128)S(1)}, f32[160,128]{1,0:T(8,128)S(1)}, u32[]{:S(2)}, u32[]{:S(2)}) %collective-permute-start.6) | collective-permute-done | bytes 81952 | tf_op jit(solution)/shard_map/ppermute | solution.py:567
  65.8 1.7 %collective-permute-start.7 = (f32[160,128]{1,0:T(8,128)S(1)}, f32[160,128]{1,0:T(8,128)S(1)}, u32[]{:S(2)}, u32[]{:S(2)}) collective-permute-start(f32[160,128]{1,0:T(8,128)S(1)} %add.18), channel_id=1, source_target_pairs={{0,16},{4,20},{8,24},{12,28},{16,0},{20,4},{24,8},{28,12},{1,17},{... | collective-permute-start | bytes 245768 | tf_op jit(solution)/shard_map/ppermute | solution.py:567
  67.5 4.6 %collective-permute-done.7 = f32[160,128]{1,0:T(8,128)S(1)} collective-permute-done((f32[160,128]{1,0:T(8,128)S(1)}, f32[160,128]{1,0:T(8,128)S(1)}, u32[]{:S(2)}, u32[]{:S(2)}) %collective-permute-start.7) | collective-permute-done | bytes 81952 | tf_op jit(solution)/shard_map/ppermute | solution.py:567
  72.1 0.1 collective-permute-start.8
  72.2 1.3 %collective-permute-done.8.other_ref = f32[160,128]{1,0:T(8,128)S(1)} collective-permute-done((f32[160,128]{1,0:T(8,128)S(1)}, f32[160,128]{1,0:T(8,128)S(1)}, u32[]{:S(2)}, u32[]{:S(2)}) %collective-permute-start.8) | collective-permute-done | bytes 81952 | tf_op jit(solution)/shard_map/ppermute | solution.py:567
  73.4 0.8 %shard_map.109 = (f32[128,128]{1,0:T(8,128)}, f32[256,128]{1,0:T(8,128)}) custom-call(f32[160,128]{1,0:T(8,128)S(1)} %add.19.mine_ref, f32[160,128]{1,0:T(8,128)S(1)} %collective-permute-done.8.other_ref), custom_call_target="tpu_custom_call" | custom-call | bytes 1048576 | tf_op jit(solution)/shard_map/pallas_call | solution.py:558
  (6 shorter events, 0.1 us)
Async XLA Ops:
  16.4 8.5 %copy-start.8 = (f32[4,128,128]{2,1,0:T(8,128)}, f32[4,128,128]{2,1,0:T(8,128)S(1)}, u32[]{:S(2)}) copy-start(f32[4,128,128]{2,1,0:T(8,128)S(1)} %get-tuple-element.39.reach_ref) | copy-start | bytes 786436
  16.4 8.5 %copy-start.10 = (f32[512,128]{1,0:T(8,128)}, f32[512,128]{1,0:T(8,128)S(1)}, u32[]{:S(2)}) copy-start(f32[512,128]{1,0:T(8,128)S(1)} %get-tuple-element.41.gain_ref) | copy-start | bytes 786436
  16.4 8.5 %copy-start.12 = (f32[512,128]{1,0:T(8,128)}, f32[512,128]{1,0:T(8,128)S(1)}, u32[]{:S(2)}) copy-start(f32[512,128]{1,0:T(8,128)S(1)} %get-tuple-element.42.resid_ref) | copy-start | bytes 786436
  16.4 9.5 %collective-permute-start = (f32[2,264,128]{2,1,0:T(8,128)S(1)}, f32[2,264,128]{2,1,0:T(8,128)S(1)}, u32[]{:S(2)}, u32[]{:S(2)}) collective-permute-start(f32[2,264,128]{2,1,0:T(8,128)S(1)} %get-tuple-element.27.mine_ref.refs_0_), channel_id=1, source_target_pairs={{0,4},{4,0},{8,12},{12,8},{16,20},{20,16},{24,28},{28,24},{1,5},{5... | collective-permute-start | bytes 811016 | tf_op jit(solution)/shard_map/ppermute | solution.py:567
  24.9 9.6 %copy-start.2 = (bf16[384,512]{1,0:T(8,128)(2,1)}, bf16[384,512]{1,0:T(8,128)(2,1)S(1)}, u32[]{:S(2)}) copy-start(bf16[384,512]{1,0:T(8,128)(2,1)S(1)} %get-tuple-element.44.low_ref) | copy-start | bytes 1179652
  25.9 9.4 %copy-start.4 = (f32[2,264,128]{2,1,0:T(8,128)}, f32[2,264,128]{2,1,0:T(8,128)S(1)}, u32[]{:S(2)}) copy-start(f32[2,264,128]{2,1,0:T(8,128)S(1)} %collective-permute-done.other_ref.refs_2_) | copy-start | bytes 811012
  26.8 7.7 %collective-permute-start.1 = (f32[2,264,128]{2,1,0:T(8,128)S(1)}, f32[2,264,128]{2,1,0:T(8,128)S(1)}, u32[]{:S(2)}, u32[]{:S(2)}) collective-permute-start(f32[2,264,128]{2,1,0:T(8,128)S(1)} %shard_map.105.mine_ref.refs_1_), channel_id=1, source_target_pairs={{0,8},{4,12},{8,0},{12,4},{16,24},{20,28},{24,16},{28,20},{1,9},{5... | collective-permute-start | bytes 811016 | tf_op jit(solution)/shard_map/ppermute | solution.py:567
  34.5 3.4 %copy-start.6 = (f32[2,264,128]{2,1,0:T(8,128)}, f32[2,264,128]{2,1,0:T(8,128)S(1)}, u32[]{:S(2)}) copy-start(f32[2,264,128]{2,1,0:T(8,128)S(1)} %collective-permute-done.1.other_ref.refs_3_) | copy-start | bytes 811012
  35.4 8.0 %copy-start = (f32[32,128,128]{2,1,0:T(8,128)S(1)}, f32[32,128,128]{2,1,0:T(8,128)}, u32[]{:S(2)}) copy-start(f32[32,128,128]{2,1,0:T(8,128)} %get-tuple-element.37.before_ref) | copy-start | bytes 6291460
  35.4 8.0 %copy-start.1 = (f32[2,256,128]{2,1,0:T(8,128)S(1)}, f32[2,256,128]{2,1,0:T(8,128)}, u32[]{:S(2)}) copy-start(f32[2,256,128]{2,1,0:T(8,128)} %param.9) | copy-start | bytes 786436
  35.4 8.0 %collective-permute-start.2 = (f32[2,136,128]{2,1,0:T(8,128)S(1)}, f32[2,136,128]{2,1,0:T(8,128)}, u32[]{:S(2)}, u32[]{:S(2)}) collective-permute-start(f32[2,136,128]{2,1,0:T(8,128)S(1)} %shard_map.106.mine_ref), channel_id=1, source_target_pairs={{0,16},{4,20},{8,24},{12,28},{16,0},{20,4},{24,8},{28,12},{1,17},{... | collective-permute-start | bytes 417800 | tf_op jit(solution)/shard_map/ppermute | solution.py:567
  37.9 1.0 %copy-start.5 = (f32[2,264,128]{2,1,0:T(8,128)S(1)}, f32[2,264,128]{2,1,0:T(8,128)}, u32[]{:S(2)}) copy-start(f32[2,264,128]{2,1,0:T(8,128)} %copy-done.4) | copy-start | bytes 811012
  38.9 1.0 %copy-start.7 = (f32[2,264,128]{2,1,0:T(8,128)S(1)}, f32[2,264,128]{2,1,0:T(8,128)}, u32[]{:S(2)}) copy-start(f32[2,264,128]{2,1,0:T(8,128)} %copy-done.6) | copy-start | bytes 811012
  39.9 3.5 %copy-start.3 = (bf16[384,512]{1,0:T(8,128)(2,1)S(1)}, bf16[384,512]{1,0:T(8,128)(2,1)}, u32[]{:S(2)}) copy-start(bf16[384,512]{1,0:T(8,128)(2,1)} %copy-done.2) | copy-start | bytes 1179652
  39.9 3.5 %copy-start.9 = (f32[4,128,128]{2,1,0:T(8,128)S(1)}, f32[4,128,128]{2,1,0:T(8,128)}, u32[]{:S(2)}) copy-start(f32[4,128,128]{2,1,0:T(8,128)} %copy-done.8) | copy-start | bytes 786436
  39.9 3.5 %copy-start.11 = (f32[512,128]{1,0:T(8,128)S(1)}, f32[512,128]{1,0:T(8,128)}, u32[]{:S(2)}) copy-start(f32[512,128]{1,0:T(8,128)} %copy-done.10) | copy-start | bytes 786436
  39.9 3.5 %copy-start.13 = (f32[512,128]{1,0:T(8,128)S(1)}, f32[512,128]{1,0:T(8,128)}, u32[]{:S(2)}) copy-start(f32[512,128]{1,0:T(8,128)} %copy-done.12) | copy-start | bytes 786436
  50.8 1.3 %collective-permute-start.3 = (f32[160,128]{1,0:T(8,128)S(1)}, f32[160,128]{1,0:T(8,128)S(1)}, u32[]{:S(2)}, u32[]{:S(2)}) collective-permute-start(f32[160,128]{1,0:T(8,128)S(1)} %slice_select_fusion), channel_id=1, source_target_pairs={{0,1},{1,0},{2,3},{3,2},{4,5},{5,4},{6,7},{7,6},{8,9},{9,8},{10,11... | collective-permute-start | bytes 245768 | tf_op jit(solution)/shard_map/ppermute | solution.py:567
  52.2 4.6 %collective-permute-start.4 = (f32[160,128]{1,0:T(8,128)S(1)}, f32[160,128]{1,0:T(8,128)S(1)}, u32[]{:S(2)}, u32[]{:S(2)}) collective-permute-start(f32[160,128]{1,0:T(8,128)S(1)} %select_add_fusion), channel_id=1, source_target_pairs={{0,2},{1,3},{2,0},{3,1},{4,6},{5,7},{6,4},{7,5},{8,10},{9,11},{10,... | collective-permute-start | bytes 245768 | tf_op jit(solution)/shard_map/ppermute | solution.py:567
  56.7 4.5 %collective-permute-start.5 = (f32[160,128]{1,0:T(8,128)S(1)}, f32[160,128]{1,0:T(8,128)S(1)}, u32[]{:S(2)}, u32[]{:S(2)}) collective-permute-start(f32[160,128]{1,0:T(8,128)S(1)} %add.16), channel_id=1, source_target_pairs={{0,4},{4,0},{8,12},{12,8},{16,20},{20,16},{24,28},{28,24},{1,5},{5... | collective-permute-start | bytes 245768 | tf_op jit(solution)/shard_map/ppermute | solution.py:567
  61.3 4.5 %collective-permute-start.6 = (f32[160,128]{1,0:T(8,128)S(1)}, f32[160,128]{1,0:T(8,128)S(1)}, u32[]{:S(2)}, u32[]{:S(2)}) collective-permute-start(f32[160,128]{1,0:T(8,128)S(1)} %add.17), channel_id=1, source_target_pairs={{0,8},{4,12},{8,0},{12,4},{16,24},{20,28},{24,16},{28,20},{1,9},{5... | collective-permute-start | bytes 245768 | tf_op jit(solution)/shard_map/ppermute | solution.py:567
  65.8 6.3 %collective-permute-start.7 = (f32[160,128]{1,0:T(8,128)S(1)}, f32[160,128]{1,0:T(8,128)S(1)}, u32[]{:S(2)}, u32[]{:S(2)}) collective-permute-start(f32[160,128]{1,0:T(8,128)S(1)} %add.18), channel_id=1, source_target_pairs={{0,16},{4,20},{8,24},{12,28},{16,0},{20,4},{24,8},{28,12},{1,17},{... | collective-permute-start | bytes 245768 | tf_op jit(solution)/shard_map/ppermute | solution.py:567
  72.1 1.3 %collective-permute-start.8 = (f32[160,128]{1,0:T(8,128)S(1)}, f32[160,128]{1,0:T(8,128)S(1)}, u32[]{:S(2)}, u32[]{:S(2)}) collective-permute-start(f32[160,128]{1,0:T(8,128)S(1)} %add.19.mine_ref), channel_id=1, source_target_pairs={{0,1},{1,0},{2,3},{3,2},{4,5},{5,4},{6,7},{7,6},{8,9},{9,8},{10,11... | collective-permute-start | bytes 245768 | tf_op jit(solution)/shard_map/ppermute | solution.py:567

commit v4 on v3

--- a/solution.py
+++ b/solution.py
@@ -95,7 +95,30 @@
     return jnp.sum(col * weight, axis=0, keepdims=True)
 
 
-OFFSET, ADJOINT, DRIVE, FIRST, LAST = range(5)
+OFFSET, ADJOINT, DRIVE, FIRST, LAST, DIAGONAL = range(6)
+
+
+def triangles(half):
+    row = lax.broadcasted_iota(jnp.int32, (half, half), 0)
+    col = lax.broadcasted_iota(jnp.int32, (half, half), 1)
+    return col > row, col < row
+
+
+def fold(whole):
+    half = whole.shape[0] // 2
+    above, _ = triangles(half)
+    return jnp.concatenate(
+        [jnp.where(above, whole[:half, :half], whole[half:, half:]), whole[:half, half:]], axis=1
+    )
+
+
+def unfold(folded):
+    half = folded.shape[0]
+    above, below = triangles(half)
+    both = folded[:, :half]
+    upper = jnp.concatenate([jnp.where(above, both, 0.0), folded[:, half:]], axis=1)
+    lower = jnp.concatenate([jnp.zeros((half, half), F32), jnp.where(below, both, 0.0)], axis=1)
+    return jnp.concatenate([upper, lower], axis=0)
 
 
 def vectors(*rows):
@@ -246,10 +269,12 @@
             reach_t = right_t(reach)
             total = total + mul_t(reach, reach_t)
             total_off = total_off + mul_t(miss, reach_t)
-        message_ref[s, pl.ds(hidden, hidden), :] = total / total_seqs
-        message_ref[s, pl.ds(2 * hidden, 8), :] = vectors(
+        total = total / total_seqs
+        message_ref[s, pl.ds(hidden, hidden // 2), :] = fold(total)
+        message_ref[s, pl.ds(hidden + hidden // 2, 8), :] = vectors(
             offset[s], total_off / total_seqs, drive[s * count : s * count + 1],
             guess_ref[pl.ds(s * count, 1), :], guess_ref[pl.ds((s + 1) * count - 1, 1), :],
+            jnp.sum(unit * total, axis=0, keepdims=True),
         )
     maps_copy.wait()
     before_copy.wait()
@@ -258,8 +283,11 @@
 def opened(ref, s, with_map=True):
     hidden = ref.shape[2]
     at = hidden if with_map else 0
-    rows = [eight(ref[s, pl.ds(at + hidden + k, 1), :]) for k in range(5)]
-    return (ref[s, pl.ds(0, hidden), :] if with_map else None, ref[s, pl.ds(at, hidden), :], rows)
+    rows = [eight(ref[s, pl.ds(at + hidden // 2 + k, 1), :]) for k in range(5)]
+    diagonal = ref[s, pl.ds(at + hidden // 2 + DIAGONAL, 1), :]
+    half = unfold(ref[s, pl.ds(at, hidden // 2), :])
+    curve = half + half.T + identity(hidden) * diagonal
+    return (ref[s, pl.ds(0, hidden), :] if with_map else None, curve, rows)
 
 
 def pick(flag, one, other):
@@ -295,8 +323,9 @@
         if with_map:
             out_ref[s, pl.ds(0, hidden), :] = whole
             at = hidden
-        out_ref[s, pl.ds(at, hidden), :] = curve
-        out_ref[s, pl.ds(at + hidden, 8), :] = vectors(*rows)
+        out_ref[s, pl.ds(at, hidden // 2), :] = fold(curve)
+        diagonal = jnp.sum(identity(hidden) * curve, axis=0, keepdims=True)
+        out_ref[s, pl.ds(at + hidden // 2, 8), :] = vectors(*rows, diagonal)
 
 
 def sides_kernel(levels, drift_ref, *refs):
@@ -338,22 +367,19 @@
 
 
 def prepare_kernel(
-    seqs, blocks, steps_in, maps_in, x_in, guess_in, hit_ref,
-    home_out, pull_out, high_ref, low_ref, ready_ref,
-    home_ref, pull_ref, prev_ref, steps_ref, maps_ref, x_ref, guess_ref, in_sems, out_sems,
+    seqs, blocks, steps_in, maps_in, hit_ref, home_out, pull_out, ready_ref,
+    home_ref, pull_ref, steps_ref, maps_ref, in_sems, out_sems,
 ):
     fetches = [
         pltpu.make_async_copy(source, to, in_sems.at[i])
-        for i, (source, to) in enumerate(
-            [(maps_in, maps_ref), (steps_in, steps_ref), (guess_in, guess_ref), (x_in, x_ref)]
-        )
+        for i, (source, to) in enumerate([(maps_in, maps_ref), (steps_in, steps_ref)])
     ]
     for fetch in fetches:
         fetch.start()
     ready_ref[...] = jnp.zeros_like(ready_ref)
-    rows, hidden = guess_ref.shape
-    count = rows // seqs
-    chunks = count // LANE
+    lanes, hidden, _ = maps_ref.shape
+    chunks = lanes // seqs
+    count = chunks * LANE
     per_block = chunks // blocks
     unit = identity(hidden)
     blank = jnp.zeros((hidden, hidden), F32)
@@ -389,17 +415,25 @@
                     owner = (k * (count // blocks) + steps_ref[s, k]) // LANE
                     part = stack[(i + 1) * hidden : (i + 2) * hidden]
                     pulls[s][k] = jnp.where(owner == chunk, hit_ref[s * blocks + k].T, part)
-    fetches[2].wait()
-    fetches[3].wait()
+    for copy in sends:
+        copy.wait()
+
+
+def factors_kernel(seqs, x_in, guess_in, _, high_ref, low_ref, ready_ref, prev_ref, x_ref, guess_ref, sems):
+    fetch_guess = pltpu.make_async_copy(guess_in, guess_ref, sems.at[0])
+    fetch_x = pltpu.make_async_copy(x_in, x_ref, sems.at[1])
+    fetch_guess.start()
+    fetch_x.start()
+    ready_ref[...] = jnp.zeros_like(ready_ref)
+    rows, hidden = guess_ref.shape
+    fetch_guess.wait()
     prev_ref[pl.ds(1, rows - 1), :] = guess_ref[pl.ds(0, rows - 1), :]
     for s in range(seqs):
-        prev_ref[pl.ds(s * count, 1), :] = jnp.zeros((1, hidden), F32)
+        prev_ref[pl.ds(s * (rows // seqs), 1), :] = jnp.zeros((1, hidden), F32)
     high_ref[pl.ds(0, hidden), :], low_ref[pl.ds(0, hidden), :] = split(prev_ref[...].T)
-    high_ref[pl.ds(hidden, x_ref.shape[1]), :], low_ref[pl.ds(hidden, x_ref.shape[1]), :] = split(
-        x_ref[...].T
-    )
-    for copy in sends:
-        copy.wait()
+    fetch_x.wait()
+    rest = pl.ds(hidden, x_ref.shape[1])
+    high_ref[rest, :], low_ref[rest, :] = split(x_ref[...].T)
 
 
 def solve_kernel(
@@ -516,28 +550,20 @@
         recur = recur + column(edges[s], unit) * pre_ref[pl.ds(s * count, 1), :]
     recur = recur.T - recur
     half = hidden // 2
-    row = lax.broadcasted_iota(jnp.int32, (half, half), 0)
-    col = lax.broadcasted_iota(jnp.int32, (half, half), 1)
-    folded = jnp.where(col > row, recur[:half, :half], recur[half:, half:])
-    grads_ref[pl.ds(0, half), :] = jnp.concatenate([folded, recur[:half, half:]], axis=1)
+    grads_ref[pl.ds(0, half), :] = fold(recur)
     grads_ref[pl.ds(half, sums.shape[0] - hidden), :] = sums[hidden:]
     path_copy.wait()
 
 
-def unfold_kernel(mine_ref, other_ref, recur_ref, in_ref):
+def finish_kernel(mine_ref, other_ref, recur_ref, in_ref):
     hidden = recur_ref.shape[0]
     half = hidden // 2
     odd = lax.axis_index("batch") & 1 == 1
     mine, other = mine_ref[...], other_ref[...]
     whole = jnp.concatenate([jnp.where(odd, other, mine), jnp.where(odd, mine, other)], axis=0)
     in_ref[...] = whole[half:]
-    row = lax.broadcasted_iota(jnp.int32, (half, half), 0)
-    col = lax.broadcasted_iota(jnp.int32, (half, half), 1)
-    folded, corner = whole[:half, :half], whole[:half, half:]
-    first = jnp.where(col > row, folded, 0.0)
-    last = jnp.where(col < row, folded, 0.0)
-    recur_ref[pl.ds(0, half), :] = jnp.concatenate([first - first.T, corner], axis=1)
-    recur_ref[pl.ds(half, half), :] = jnp.concatenate([-corner.T, last - last.T], axis=1)
+    upper = unfold(whole[:half])
+    recur_ref[...] = upper - upper.T
 
 
 def call(kernel, shapes, in_specs, scratch=(), flops=0, room=14):
@@ -590,7 +616,7 @@
     message, maps, before, start, hit, reach, reach_off, gain, resid, drift = call(
         functools.partial(compose_kernel, seqs, blocks, total_seqs, keep),
         [
-            near((seqs, 2 * hidden + 8, hidden)),
+            near((seqs, hidden + hidden // 2 + 8, hidden)),
             far((lanes, hidden, hidden)),
             far((lanes, hidden, hidden)),
             (lanes, hidden),
@@ -624,37 +650,40 @@
     )(target_steps, x, guess, recur_weight, damping.reshape(1, hidden), in_weight,
       bias_term.reshape(1, hidden), targets.reshape(hits, hidden))
 
-    home, pull, high, low, ready = call(
+    home, pull, ready = call(
         functools.partial(prepare_kernel, seqs, blocks),
-        [
-            far((lanes, hidden, hidden)),
-            far((hits, chunks, hidden, hidden)),
-            jax.ShapeDtypeStruct((hidden + features, rows), BF16),
-            jax.ShapeDtypeStruct((hidden + features, rows), BF16),
-            (8, hidden),
-        ],
-        [HBM, HBM, HBM, HBM, VMEM],
+        [far((lanes, hidden, hidden)), far((hits, chunks, hidden, hidden)), (8, hidden)],
+        [HBM, HBM, VMEM],
         [
             (lanes, hidden, hidden),
             (hits, chunks, hidden, hidden),
-            (rows, hidden),
             pltpu.SMEM((seqs, blocks), jnp.int32),
             (lanes, hidden, hidden),
-            (rows, features),
-            (rows, hidden),
-            pltpu.SemaphoreType.DMA((4,)),
+            pltpu.SemaphoreType.DMA((2,)),
             pltpu.SemaphoreType.DMA((seqs * blocks * (blocks + 3) // 2,)),
         ],
         flops=1 << 32,
         room=20,
-    )(target_steps, maps, x, guess, hit)
+    )(target_steps, maps, hit)
 
     levels = levels_of("seq")
     groups, received = [message], []
     for level in range(levels - 1):
         received.append(swapped(groups[-1], "seq", 1 << level))
+        if level == 1:
+            high, low, ready = call(
+                functools.partial(factors_kernel, seqs),
+                [
+                    jax.ShapeDtypeStruct((hidden + features, rows), BF16),
+                    jax.ShapeDtypeStruct((hidden + features, rows), BF16),
+                    (8, hidden),
+                ],
+                [HBM, HBM, VMEM],
+                [(rows, hidden), (rows, features), (rows, hidden), pltpu.SemaphoreType.DMA((2,))],
+                flops=1 << 31,
+            )(x, guess, groups[1])
         with_map = level < levels - 2
-        height = (2 if with_map else 1) * hidden + 8
+        height = (hidden if with_map else 0) + hidden // 2 + 8
         groups += call(
             functools.partial(join_kernel, level, with_map),
             [(seqs, height, hidden)],
@@ -687,12 +716,17 @@
     kept = jnp.where(odd, grads[middle:], grads[:middle])
     given = jnp.where(odd, grads[:middle], grads[middle:])
     kept = kept + swapped(given, "batch", 1)
-    for level in range(1, levels_of("batch")):
-        kept = kept + swapped(kept, "batch", 1 << level)
-    for level in range(levels):
-        kept = kept + swapped(kept, "seq", 1 << level)
+    width = lax.axis_size("batch")
+    hops = [(0, 1 << k) for k in range(1, levels_of("batch"))] + [(1 << k, 0) for k in range(levels)]
+    for stage in range(len(hops)):
+        route = []
+        for i in range(lax.axis_size("seq")):
+            for j in range(width):
+                along_seq, along_batch = hops[(stage + (j & 1) * (len(hops) // 2)) % len(hops)]
+                route.append((i * width + j, (i ^ along_seq) * width + (j ^ along_batch)))
+        kept = kept + lax.ppermute(kept, ("seq", "batch"), route)
     grad_recur, grad_in = call(
-        unfold_kernel,
+        finish_kernel,
         [(hidden, hidden), (features, hidden)],
         [VMEM, VMEM],
     )(kept, swapped(kept, "batch", 1))

time: 74.5 us -> 67.8 us (0.910)
  waiting for transfers between devices: 25.3 us -> 18.3 us
  local copies, waits for them, and re-layouts: 1.96 us -> 0.01 us
  starting transfers between devices: 12.5 us -> 14.3 us
    ppermute x9 -> x5, waiting for transfers between devices: 25.3 us -> 6.2 us  [swapped(): lax.ppermute(value, axis, [(i, i ^ distance) for i in range(lax.axis_size...]
    ppermute x0 -> x4, waiting for transfers between devices: none -> 12.1 us  [on_device(): kept = kept + lax.ppermute(kept, ('seq', 'batch'), route)]
    ppermute x0 -> x4, starting transfers between devices: none -> 6.86 us  [on_device(): kept = kept + lax.ppermute(kept, ('seq', 'batch'), route)]
    ppermute x9 -> x5, starting transfers between devices: 12.5 us -> 7.45 us  [swapped(): lax.ppermute(value, axis, [(i, i ^ distance) for i in range(lax.axis_size...]
    unnamed x28 -> x4, local copies, waits for them, and re-layouts: 1.96 us -> 0.01 us
    pallas_call x7 -> x8, Pallas kernels: 33.6 us -> 34.2 us  [pinned(): run(*[pltpu.with_memory_space_constraint(x, pltpu.HBM) if spec is HBM els...]
  transfers between devices with their start and end apart: 9 -> 9, of which waited for: 9 -> 8; matrix products, arithmetic and copies ran while one was open for 0% -> 0% of each run, Pallas kernels for 11% -> 14%
where the time goes in v4:
time: 67.8 us; the launch traced here: 67.6 us
  Pallas kernels  34.2 us (50%)
  waiting for transfers between devices  18.3 us (27%)
  starting transfers between devices  14.3 us (21%)
  between operations  0.76 us (1%)
    pallas_call x8, Pallas kernels, pinned(): run(*[pltpu.with_memory_space_constraint(x, pltpu.HBM) if spec is HBM els...  34.2 us
    ppermute x4, waiting for transfers between devices, on_device(): kept = kept + lax.ppermute(kept, ('seq', 'batch'), route)  12.1 us
    ppermute x5, starting transfers between devices, swapped(): lax.ppermute(value, axis, [(i, i ^ distance) for i in range(lax.axis_size...  7.45 us
    ppermute x4, starting transfers between devices, on_device(): kept = kept + lax.ppermute(kept, ('seq', 'batch'), route)  6.86 us
    ppermute x5, waiting for transfers between devices, swapped(): lax.ppermute(value, axis, [(i, i ^ distance) for i in range(lax.axis_size...  6.2 us
  transfers between devices with their start and end apart: 9, of which 8 were waited for; matrix products, arithmetic and copies ran while one was open for 0% of the time, Pallas kernels for 14%

profile of v4, /device:TPU:0, one launch (start us, length us, event | category | flops | bytes accessed | tf_op | source)
XLA Modules:
  0.0 67.6 jit_solution(11408254786702485386)
XLA Ops:
  0.6 15.7 %shard_map.103 = (f32[2,200,128]{2,1,0:T(8,128)S(1)}, f32[32,128,128]{2,1,0:T(8,128)}, f32[32,128,128]{2,1,0:T(8,128)}, f32[32,128]{1,0:T(8,128)S(1)}, f32[4,128...) custom-call(s32[2,2]{1,0:T(2,128)} %steps_in.5, ...), custom_call_target="tpu_custom_call" | custom-call | bytes 1048576 | tf_op jit(solution)/shard_map/pallas_call | solution.py:584
  16.4 3.0 %collective-permute-start = (f32[2,200,128]{2,1,0:T(8,128)S(1)}, f32[2,200,128]{2,1,0:T(8,128)S(1)}, u32[]{:S(2)}, u32[]{:S(2)}) collective-permute-start(f32[2,200,128]{2,1,0:T(8,128)S(1)} %get-tuple-element.28.mine_ref.refs_0_), channel_id=1, source_target_pairs={{0,4},{4,0},{8,12},{12,8},{16,20},{20,16},{24,28},{28,24},{1,5},{5... | collective-permute-start | bytes 614408 | tf_op jit(solution)/shard_map/ppermute | solution.py:593
  19.4 5.5 %shard_map.104 = (f32[32,128,128]{2,1,0:T(8,128)}, f32[4,16,128,128]{3,2,1,0:T(8,128)}, f32[8,128]{1,0:T(8,128)S(1)}) custom-call(s32[2,2]{1,0:T(2,128)} %steps_in.5, f32[32,128,128]{2,1,0:T(8,128)} %get-tuple-element.29.maps_in, f32[4,128,128]{2,1,0:T(8,128)S(1)} %get-tuple-element.30.hit_ref), custom_call_target="tpu_custom_call" | custom-call | flops 4294967296 | bytes 1048576 | tf_op jit(solution)/shard_map/pallas_call | solution.py:584
  24.9 0.0 collective-permute-done.other_ref.refs_2_
  24.9 0.9 %shard_map.105._.mine_ref.refs_1_ = f32[2,200,128]{2,1,0:T(8,128)S(1)} custom-call(f32[128,128]{1,0:T(8,128)S(1)} %get-tuple-element.27.drift_ref, f32[2,200,128]{2,1,0:T(8,128)S(1)} %get-tuple-element.28.mine_ref.refs_0_, f32[2,200,128]{2,1,0:T(8,128)S(1)} %collective-permute-done.other_ref.refs_2_, f32[8,128]{1,0:T(8,128)S(1)} %get-tuple-element.31._), custom_call_target="tpu_custom_call" | custom-call | bytes 1048576 | tf_op jit(solution)/shard_map/pallas_call | solution.py:584
  25.8 1.6 %collective-permute-start.1 = (f32[2,200,128]{2,1,0:T(8,128)S(1)}, f32[2,200,128]{2,1,0:T(8,128)S(1)}, u32[]{:S(2)}, u32[]{:S(2)}) collective-permute-start(f32[2,200,128]{2,1,0:T(8,128)S(1)} %shard_map.105._.mine_ref.refs_1_), channel_id=1, source_target_pairs={{0,8},{4,12},{8,0},{12,4},{16,24},{20,28},{24,16},{28,20},{1,9},{5... | collective-permute-start | bytes 614408 | tf_op jit(solution)/shard_map/ppermute | solution.py:593
  27.5 1.3 %shard_map.106 = (bf16[384,512]{1,0:T(8,128)(2,1)S(1)}, bf16[384,512]{1,0:T(8,128)(2,1)S(1)}, f32[8,128]{1,0:T(8,128)S(1)}) custom-call(f32[512,256]{1,0:T(8,128)} %bitcast.10, f32[512,128]{1,0:T(8,128)} %bitcast.7, f32[2,200,128]{2,1,0:T(8,128)S(1)} %shard_map.105._.mine_ref.refs_1_), custom_call_target="tpu_custom_call" | custom-call | flops 2147483648 | bytes 1048576 | tf_op jit(solution)/shard_map/pallas_call | solution.py:584
  28.8 3.6 %collective-permute-done.1.other_ref.refs_3_ = f32[2,200,128]{2,1,0:T(8,128)S(1)} collective-permute-done((f32[2,200,128]{2,1,0:T(8,128)S(1)}, f32[2,200,128]{2,1,0:T(8,128)S(1)}, u32[]{:S(2)}, u32[]{:S(2)}) %collective-permute-start.1) | collective-permute-done | bytes 204832 | tf_op jit(solution)/shard_map/ppermute | solution.py:593
  32.4 0.9 %shard_map.107.mine_ref = f32[2,72,128]{2,1,0:T(8,128)S(1)} custom-call(f32[128,128]{1,0:T(8,128)S(1)} %get-tuple-element.27.drift_ref, f32[2,200,128]{2,1,0:T(8,128)S(1)} %shard_map.105._.mine_ref.refs_1_, f32[2,200,128]{2,1,0:T(8,128)S(1)} %collective-permute-done.1.other_ref.refs_3_, f32[8,128]{1,0:T(8,128)S(1)} %get-tuple-element.32._), custom_call_target="tpu_custom_call" | custom-call | bytes 1048576 | tf_op jit(solution)/shard_map/pallas_call | solution.py:584
  33.3 0.0 copy-start
  33.3 0.0 copy-start.1
  33.3 2.7 %collective-permute-start.2 = (f32[2,72,128]{2,1,0:T(8,128)S(1)}, f32[2,72,128]{2,1,0:T(8,128)S(1)}, u32[]{:S(2)}, u32[]{:S(2)}) collective-permute-start(f32[2,72,128]{2,1,0:T(8,128)S(1)} %shard_map.107.mine_ref), channel_id=1, source_target_pairs={{0,16},{4,20},{8,24},{12,28},{16,0},{20,4},{24,8},{28,12},{1,17},{... | collective-permute-start | bytes 221192 | tf_op jit(solution)/shard_map/ppermute | solution.py:593
  36.0 2.6 %shard_map.108 = (f32[2,128,128]{2,1,0:T(8,128)S(1)}, f32[2,128,128]{2,1,0:T(8,128)S(1)}, f32[2,128,128]{2,1,0:T(8,128)S(1)}, f32[16,128]{1,0:T(8,128)S(1)}) custom-call(f32[128,128]{1,0:T(8,128)S(1)} %get-tuple-element.27.drift_ref, f32[2,200,128]{2,1,0:T(8,128)S(1)} %get-tuple-element.28.mine_ref.refs_0_, ...), custom_call_target="tpu_custom_call" | custom-call | flops 1073741824 | bytes 1048576 | tf_op jit(solution)/shard_map/pallas_call | solution.py:584
  38.6 0.1 collective-permute-done.2.other_ref
  38.6 0.0 copy-done
  38.6 0.0 copy-done.1
  38.6 6.5 %shard_map.109 = (f32[512,128]{1,0:T(8,128)}, f32[320,128]{1,0:T(8,128)S(1)}) custom-call(s32[2,2]{1,0:T(2,128)} %steps_in.5, f32[128,128]{1,0:T(8,128)S(1)} %get-tuple-element.27.drift_ref, f32[2,72,128]{2,1,0:T(8,128)S(1)} %shard_map.107.mine_ref, f32[2,72,128]{2,1,0:T(8,128)S(1)} %collective-permute-done.2.other_ref, ...), custom_call_target="tpu_custom_call" | custom-call | bytes 1048576 | tf_op jit(solution)/shard_map/pallas_call | solution.py:584
  45.1 0.1 collective-permute-start.3
  45.2 1.3 %collective-permute-done.3 = f32[160,128]{1,0:T(8,128)S(1)} collective-permute-done((f32[160,128]{1,0:T(8,128)S(1)}, f32[160,128]{1,0:T(8,128)S(1)}, u32[]{:S(2)}, u32[]{:S(2)}) %collective-permute-start.3) | collective-permute-done | bytes 81952 | tf_op jit(solution)/shard_map/ppermute | solution.py:593
  46.5 1.6 %collective-permute-start.4 = (f32[160,128]{1,0:T(8,128)S(1)}, f32[160,128]{1,0:T(8,128)S(1)}, u32[]{:S(2)}, u32[]{:S(2)}) collective-permute-start(f32[160,128]{1,0:T(8,128)S(1)} %select_add_fusion), channel_id=1, source_target_pairs={{0,2},{1,9},{2,0},{3,11},{4,6},{5,13},{6,4},{7,15},{8,10},{9,1},{1... | collective-permute-start | bytes 245768 | tf_op jit(solution)/shard_map/ppermute | solution.py:727
  48.1 2.9 %collective-permute-done.4 = f32[160,128]{1,0:T(8,128)S(1)} collective-permute-done((f32[160,128]{1,0:T(8,128)S(1)}, f32[160,128]{1,0:T(8,128)S(1)}, u32[]{:S(2)}, u32[]{:S(2)}) %collective-permute-start.4) | collective-permute-done | bytes 81952 | tf_op jit(solution)/shard_map/ppermute | solution.py:727
  51.0 0.7 %collective-permute-start.5 = (f32[160,128]{1,0:T(8,128)S(1)}, f32[160,128]{1,0:T(8,128)S(1)}, u32[]{:S(2)}, u32[]{:S(2)}) collective-permute-start(f32[160,128]{1,0:T(8,128)S(1)} %add.16), channel_id=1, source_target_pairs={{0,4},{1,17},{2,6},{3,19},{4,0},{5,21},{6,2},{7,23},{8,12},{9,25},... | collective-permute-start | bytes 245768 | tf_op jit(solution)/shard_map/ppermute | solution.py:727
  51.8 3.8 %collective-permute-done.5 = f32[160,128]{1,0:T(8,128)S(1)} collective-permute-done((f32[160,128]{1,0:T(8,128)S(1)}, f32[160,128]{1,0:T(8,128)S(1)}, u32[]{:S(2)}, u32[]{:S(2)}) %collective-permute-start.5) | collective-permute-done | bytes 81952 | tf_op jit(solution)/shard_map/ppermute | solution.py:727
  55.5 1.6 %collective-permute-start.6 = (f32[160,128]{1,0:T(8,128)S(1)}, f32[160,128]{1,0:T(8,128)S(1)}, u32[]{:S(2)}, u32[]{:S(2)}) collective-permute-start(f32[160,128]{1,0:T(8,128)S(1)} %add.17), channel_id=1, source_target_pairs={{0,8},{1,3},{2,10},{3,1},{4,12},{5,7},{6,14},{7,5},{8,0},{9,11},{1... | collective-permute-start | bytes 245768 | tf_op jit(solution)/shard_map/ppermute | solution.py:727
  57.2 2.9 %collective-permute-done.6 = f32[160,128]{1,0:T(8,128)S(1)} collective-permute-done((f32[160,128]{1,0:T(8,128)S(1)}, f32[160,128]{1,0:T(8,128)S(1)}, u32[]{:S(2)}, u32[]{:S(2)}) %collective-permute-start.6) | collective-permute-done | bytes 81952 | tf_op jit(solution)/shard_map/ppermute | solution.py:727
  60.1 2.9 %collective-permute-start.7 = (f32[160,128]{1,0:T(8,128)S(1)}, f32[160,128]{1,0:T(8,128)S(1)}, u32[]{:S(2)}, u32[]{:S(2)}) collective-permute-start(f32[160,128]{1,0:T(8,128)S(1)} %add.18), channel_id=1, source_target_pairs={{0,16},{1,5},{2,18},{3,7},{4,20},{5,1},{6,22},{7,3},{8,24},{9,13},... | collective-permute-start | bytes 245768 | tf_op jit(solution)/shard_map/ppermute | solution.py:727
  62.9 2.5 %collective-permute-done.7 = f32[160,128]{1,0:T(8,128)S(1)} collective-permute-done((f32[160,128]{1,0:T(8,128)S(1)}, f32[160,128]{1,0:T(8,128)S(1)}, u32[]{:S(2)}, u32[]{:S(2)}) %collective-permute-start.7) | collective-permute-done | bytes 81952 | tf_op jit(solution)/shard_map/ppermute | solution.py:727
  65.5 0.1 collective-permute-start.8
  65.6 1.3 %collective-permute-done.8.other_ref = f32[160,128]{1,0:T(8,128)S(1)} collective-permute-done((f32[160,128]{1,0:T(8,128)S(1)}, f32[160,128]{1,0:T(8,128)S(1)}, u32[]{:S(2)}, u32[]{:S(2)}) %collective-permute-start.8) | collective-permute-done | bytes 81952 | tf_op jit(solution)/shard_map/ppermute | solution.py:593
  66.8 0.8 %shard_map.110 = (f32[128,128]{1,0:T(8,128)}, f32[256,128]{1,0:T(8,128)}) custom-call(f32[160,128]{1,0:T(8,128)S(1)} %add.19.mine_ref, f32[160,128]{1,0:T(8,128)S(1)} %collective-permute-done.8.other_ref), custom_call_target="tpu_custom_call" | custom-call | bytes 1048576 | tf_op jit(solution)/shard_map/pallas_call | solution.py:584
  (6 shorter events, 0.1 us)
Async XLA Ops:
  16.4 8.5 %collective-permute-start = (f32[2,200,128]{2,1,0:T(8,128)S(1)}, f32[2,200,128]{2,1,0:T(8,128)S(1)}, u32[]{:S(2)}, u32[]{:S(2)}) collective-permute-start(f32[2,200,128]{2,1,0:T(8,128)S(1)} %get-tuple-element.28.mine_ref.refs_0_), channel_id=1, source_target_pairs={{0,4},{4,0},{8,12},{12,8},{16,20},{20,16},{24,28},{28,24},{1,5},{5... | collective-permute-start | bytes 614408 | tf_op jit(solution)/shard_map/ppermute | solution.py:593
  25.8 6.6 %collective-permute-start.1 = (f32[2,200,128]{2,1,0:T(8,128)S(1)}, f32[2,200,128]{2,1,0:T(8,128)S(1)}, u32[]{:S(2)}, u32[]{:S(2)}) collective-permute-start(f32[2,200,128]{2,1,0:T(8,128)S(1)} %shard_map.105._.mine_ref.refs_1_), channel_id=1, source_target_pairs={{0,8},{4,12},{8,0},{12,4},{16,24},{20,28},{24,16},{28,20},{1,9},{5... | collective-permute-start | bytes 614408 | tf_op jit(solution)/shard_map/ppermute | solution.py:593
  33.3 5.3 %copy-start = (f32[32,128,128]{2,1,0:T(8,128)S(1)}, f32[32,128,128]{2,1,0:T(8,128)}, u32[]{:S(2)}) copy-start(f32[32,128,128]{2,1,0:T(8,128)} %get-tuple-element.39.before_ref) | copy-start | bytes 6291460
  33.3 5.3 %copy-start.1 = (f32[2,256,128]{2,1,0:T(8,128)S(1)}, f32[2,256,128]{2,1,0:T(8,128)}, u32[]{:S(2)}) copy-start(f32[2,256,128]{2,1,0:T(8,128)} %param.9) | copy-start | bytes 786436
  33.3 5.3 %collective-permute-start.2 = (f32[2,72,128]{2,1,0:T(8,128)S(1)}, f32[2,72,128]{2,1,0:T(8,128)S(1)}, u32[]{:S(2)}, u32[]{:S(2)}) collective-permute-start(f32[2,72,128]{2,1,0:T(8,128)S(1)} %shard_map.107.mine_ref), channel_id=1, source_target_pairs={{0,16},{4,20},{8,24},{12,28},{16,0},{20,4},{24,8},{28,12},{1,17},{... | collective-permute-start | bytes 221192 | tf_op jit(solution)/shard_map/ppermute | solution.py:593
  45.1 1.3 %collective-permute-start.3 = (f32[160,128]{1,0:T(8,128)S(1)}, f32[160,128]{1,0:T(8,128)S(1)}, u32[]{:S(2)}, u32[]{:S(2)}) collective-permute-start(f32[160,128]{1,0:T(8,128)S(1)} %slice_select_fusion), channel_id=1, source_target_pairs={{0,1},{1,0},{2,3},{3,2},{4,5},{5,4},{6,7},{7,6},{8,9},{9,8},{10,11... | collective-permute-start | bytes 245768 | tf_op jit(solution)/shard_map/ppermute | solution.py:593
  46.5 4.5 %collective-permute-start.4 = (f32[160,128]{1,0:T(8,128)S(1)}, f32[160,128]{1,0:T(8,128)S(1)}, u32[]{:S(2)}, u32[]{:S(2)}) collective-permute-start(f32[160,128]{1,0:T(8,128)S(1)} %select_add_fusion), channel_id=1, source_target_pairs={{0,2},{1,9},{2,0},{3,11},{4,6},{5,13},{6,4},{7,15},{8,10},{9,1},{1... | collective-permute-start | bytes 245768 | tf_op jit(solution)/shard_map/ppermute | solution.py:727
  51.0 4.5 %collective-permute-start.5 = (f32[160,128]{1,0:T(8,128)S(1)}, f32[160,128]{1,0:T(8,128)S(1)}, u32[]{:S(2)}, u32[]{:S(2)}) collective-permute-start(f32[160,128]{1,0:T(8,128)S(1)} %add.16), channel_id=1, source_target_pairs={{0,4},{1,17},{2,6},{3,19},{4,0},{5,21},{6,2},{7,23},{8,12},{9,25},... | collective-permute-start | bytes 245768 | tf_op jit(solution)/shard_map/ppermute | solution.py:727
  55.5 4.5 %collective-permute-start.6 = (f32[160,128]{1,0:T(8,128)S(1)}, f32[160,128]{1,0:T(8,128)S(1)}, u32[]{:S(2)}, u32[]{:S(2)}) collective-permute-start(f32[160,128]{1,0:T(8,128)S(1)} %add.17), channel_id=1, source_target_pairs={{0,8},{1,3},{2,10},{3,1},{4,12},{5,7},{6,14},{7,5},{8,0},{9,11},{1... | collective-permute-start | bytes 245768 | tf_op jit(solution)/shard_map/ppermute | solution.py:727
  60.1 5.4 %collective-permute-start.7 = (f32[160,128]{1,0:T(8,128)S(1)}, f32[160,128]{1,0:T(8,128)S(1)}, u32[]{:S(2)}, u32[]{:S(2)}) collective-permute-start(f32[160,128]{1,0:T(8,128)S(1)} %add.18), channel_id=1, source_target_pairs={{0,16},{1,5},{2,18},{3,7},{4,20},{5,1},{6,22},{7,3},{8,24},{9,13},... | collective-permute-start | bytes 245768 | tf_op jit(solution)/shard_map/ppermute | solution.py:727
  65.5 1.3 %collective-permute-start.8 = (f32[160,128]{1,0:T(8,128)S(1)}, f32[160,128]{1,0:T(8,128)S(1)}, u32[]{:S(2)}, u32[]{:S(2)}) collective-permute-start(f32[160,128]{1,0:T(8,128)S(1)} %add.19.mine_ref), channel_id=1, source_target_pairs={{0,1},{1,0},{2,3},{3,2},{4,5},{5,4},{6,7},{7,6},{8,9},{9,8},{10,11... | collective-permute-start | bytes 245768 | tf_op jit(solution)/shard_map/ppermute | solution.py:593

commit v5 on v4

--- a/solution.py
+++ b/solution.py
@@ -130,9 +130,9 @@
 def compose_kernel(
     seqs, blocks, total_seqs, keep, steps_in, x_in, guess_in, recur_in, damping_in, in_in, bias_in,
     targets_in,
-    message_ref, maps_out, before_out, start_ref, hit_ref, reach_ref, reach_off_ref, gain_ref,
+    message_ref, maps_ref, before_out, start_ref, hit_out, reach_ref, reach_off_ref, gain_ref,
     resid_ref, drift_ref,
-    record_ref, record_off_ref, maps_ref, before_ref, off_ref, hit_off_ref, prev_ref,
+    record_ref, record_off_ref, before_ref, off_ref, hit_ref, hit_off_ref, prev_ref,
     steps_ref, x_ref, guess_ref, recur_ref, damping_ref, in_ref, bias_ref, targets_ref, sems,
 ):
     fetches = [
@@ -233,8 +233,8 @@
     else:
         capture(0)
         lax.fori_loop(1, LANE, advance, 0)
-    maps_copy = pltpu.make_async_copy(maps_ref, maps_out, sems.at[8])
-    maps_copy.start()
+    hit_copy = pltpu.make_async_copy(hit_ref, hit_out, sems.at[9])
+    hit_copy.start()
 
     running = [unit] * seqs
     offset = [jnp.zeros((8, hidden), F32)] * seqs
@@ -250,7 +250,7 @@
                 packed = right(this)
                 running[s] = mul(running[s], packed)
                 offset[s] = mul(offset[s], packed) + this_off
-    before_copy = pltpu.make_async_copy(before_ref, before_out, sems.at[9])
+    before_copy = pltpu.make_async_copy(before_ref, before_out, sems.at[8])
     before_copy.start()
 
     for s in range(seqs):
@@ -276,8 +276,8 @@
             guess_ref[pl.ds(s * count, 1), :], guess_ref[pl.ds((s + 1) * count - 1, 1), :],
             jnp.sum(unit * total, axis=0, keepdims=True),
         )
-    maps_copy.wait()
     before_copy.wait()
+    hit_copy.wait()
 
 
 def opened(ref, s, with_map=True):
@@ -367,59 +367,41 @@
 
 
 def prepare_kernel(
-    seqs, blocks, steps_in, maps_in, hit_ref, home_out, pull_out, ready_ref,
-    home_ref, pull_ref, steps_ref, maps_ref, in_sems, out_sems,
+    seq, blocks, steps_in, hit_in, maps_ref, _, home_ref, pull_ref, ready_ref, steps_ref, hit_ref, sems
 ):
-    fetches = [
-        pltpu.make_async_copy(source, to, in_sems.at[i])
-        for i, (source, to) in enumerate([(maps_in, maps_ref), (steps_in, steps_ref)])
-    ]
-    for fetch in fetches:
-        fetch.start()
+    fetch_steps = pltpu.make_async_copy(steps_in, steps_ref, sems.at[0])
+    fetch_hit = pltpu.make_async_copy(hit_in.at[pl.ds(seq * blocks, blocks)], hit_ref, sems.at[1])
+    fetch_steps.start()
+    fetch_hit.start()
     ready_ref[...] = jnp.zeros_like(ready_ref)
-    lanes, hidden, _ = maps_ref.shape
-    chunks = lanes // seqs
-    count = chunks * LANE
+    chunks, hidden = home_ref.shape[:2]
     per_block = chunks // blocks
     unit = identity(hidden)
-    blank = jnp.zeros((hidden, hidden), F32)
-    home = [unit] * seqs
-    pulls = [[blank] * blocks for _ in range(seqs)]
-    sends = []
-
-    def send(source, to):
-        copy = pltpu.make_async_copy(source, to, out_sems.at[len(sends)])
-        copy.start()
-        sends.append(copy)
-
-    fetches[0].wait()
-    fetches[1].wait()
+    home = unit
+    pulls = [jnp.zeros((hidden, hidden), F32)] * blocks
+    fetch_steps.wait()
+    fetch_hit.wait()
     for chunk in reversed(range(chunks)):
-        for s in range(seqs):
-            lane = s * chunks + chunk
-            home_ref[lane] = home[s]
-            active = [k for k in range(blocks) if chunk < (k + 1) * per_block]
-            for k in active:
-                pull_ref[s * blocks + k, chunk] = pulls[s][k]
-            if chunk % per_block == 0:
-                for k in active:
-                    part = (s * blocks + k, pl.ds(chunk, per_block))
-                    send(pull_ref.at[part], pull_out.at[part])
-                part = pl.ds(lane, per_block)
-                send(home_ref.at[part], home_out.at[part])
-            if chunk:
-                stack = jnp.concatenate([home[s]] + [pulls[s][k] for k in active], axis=0)
-                stack = mul_t(stack, right_t(maps_ref[lane]))
-                home[s] = stack[:hidden]
-                for i, k in enumerate(active):
-                    owner = (k * (count // blocks) + steps_ref[s, k]) // LANE
-                    part = stack[(i + 1) * hidden : (i + 2) * hidden]
-                    pulls[s][k] = jnp.where(owner == chunk, hit_ref[s * blocks + k].T, part)
-    for copy in sends:
-        copy.wait()
-
-
-def factors_kernel(seqs, x_in, guess_in, _, high_ref, low_ref, ready_ref, prev_ref, x_ref, guess_ref, sems):
+        home_ref[chunk] = home
+        active = [k for k in range(blocks) if chunk < (k + 1) * per_block]
+        for k in active:
+            pull_ref[k, chunk] = pulls[k]
+        if chunk:
+            stack = jnp.concatenate([home] + [pulls[k] for k in active], axis=0)
+            stack = mul_t(stack, right_t(maps_ref[seq * chunks + chunk]))
+            home = stack[:hidden]
+            for i, k in enumerate(active):
+                owner = (k * per_block * LANE + steps_ref[seq, k]) // LANE
+                part = stack[(i + 1) * hidden : (i + 2) * hidden]
+                pulls[k] = jnp.where(owner == chunk, hit_ref[k].T, part)
+
+
+def factors_kernel(
+    seqs, blocks, steps_in, x_in, guess_in, _, high_ref, low_ref, mark_ref, ready_ref,
+    prev_ref, x_ref, guess_ref, steps_ref, sems,
+):
+    fetch_steps = pltpu.make_async_copy(steps_in, steps_ref, sems.at[2])
+    fetch_steps.start()
     fetch_guess = pltpu.make_async_copy(guess_in, guess_ref, sems.at[0])
     fetch_x = pltpu.make_async_copy(x_in, x_ref, sems.at[1])
     fetch_guess.start()
@@ -434,38 +416,28 @@
     fetch_x.wait()
     rest = pl.ds(hidden, x_ref.shape[1])
     high_ref[rest, :], low_ref[rest, :] = split(x_ref[...].T)
-
-
-def solve_kernel(
-    seqs, blocks, total_seqs, level, steps_in, drift_ref, mine_ref, other_ref,
-    home_in, pull_in, entry_ref, tail_ref, back_ref, sides_ref, before_ref, start_ref, reach_ref,
-    reach_off_ref, gain_ref, resid_ref, guess_ref, high_ref, low_ref,
-    path_out, grads_ref,
-    state_ref, carry_ref, source_ref, pre_ref, gain_back_ref, path_ref, home_ref, pull_ref, steps_ref, sems,
+    fetch_steps.wait()
+    block = rows // (seqs * blocks)
+    row = lax.broadcasted_iota(jnp.int32, (block, hidden), 0)
+    for s in range(seqs):
+        for k in range(blocks):
+            mark_ref[pl.ds((s * blocks + k) * block, block), :] = (row == steps_ref[s, k]).astype(F32)
+
+
+def ends_kernel(
+    seqs, blocks, total_seqs, level, drift_ref, mine_ref, other_ref, *refs
 ):
-    rows, hidden = guess_ref.shape
+    home_refs, pull_refs, refs = refs[:seqs], refs[seqs : 2 * seqs], refs[2 * seqs :]
+    (
+        entry_ref, tail_ref, back_ref, sides_ref, before_ref, start_ref, reach_ref, reach_off_ref,
+        gain_ref, mark_ref,
+        state_ref, carry_ref, source_ref, gain_back_ref, edge_ref,
+    ) = refs
+    rows, hidden = gain_ref.shape
     count = rows // seqs
     chunks = count // LANE
-    lanes = seqs * chunks
     block = count // blocks
     per_block = chunks // blocks
-    fetch_steps = pltpu.make_async_copy(steps_in, steps_ref, sems.at[0])
-    fetch_steps.start()
-    per_block = guess_ref.shape[0] // seqs // LANE // blocks
-    fetches = [[] for _ in range(blocks)]
-
-    def fetch(part, source, to):
-        copy = pltpu.make_async_copy(source, to, sems.at[2 + sum(map(len, fetches))])
-        copy.start()
-        fetches[part].append(copy)
-
-    for part in range(blocks):
-        for s in range(seqs):
-            at = pl.ds((s * blocks + part) * per_block, per_block)
-            fetch(part, home_in.at[at], home_ref.at[at])
-            for k in range(part, blocks):
-                at = (s * blocks + k, pl.ds(part * per_block, per_block))
-                fetch(part, pull_in.at[at], pull_ref.at[at])
     place = lax.axis_index("seq")
     upper = (place >> level) & 1 == 1
     lowest = (place & ((1 << level) - 1)) == 0
@@ -473,10 +445,9 @@
     drift_w = right(drift)
     drift_wt = right_t(drift)
     unit = identity(hidden)
-    source_ref[...] = jnp.zeros_like(source_ref)
     gain_back_ref[...] = gain_ref[...]
 
-    entries, tails, sources, edges = [], [], [], []
+    entries, tails, sources = [], [], []
     for s in range(seqs):
         mine, other = opened(mine_ref, s, False), opened(other_ref, s, False)
         last, middle = pick(upper, (other[2][LAST], other[2][OFFSET]), (mine[2][LAST], mine[2][OFFSET]))
@@ -495,51 +466,71 @@
         tails.append(column(tail + tail_off, unit))
         known = jnp.logical_and(upper, lowest)
         edge = jnp.where(known, last[:1], edge)
-        edges.append(edge)
+        edge_ref[pl.ds(s, 1), :] = edge
         edge_gain = jnp.where(known, gain[:1], edge_gain)
         at = pl.ds(s * count, 1)
         gain_back_ref[at, :] = gain_ref[at, :] + edge_gain
         here = []
-        if s == 0:
-            fetch_steps.wait()
         for k in range(blocks):
             j = s * blocks + k
             miss = (along(entries[s], reach_ref[j]) + reach_off_ref[pl.ds(j, 1), :]) / total_seqs
-            source_ref[pl.ds(s * count + k * block + steps_ref[s, k], 1), :] = miss
+            here_rows = pl.ds(j * block, block)
+            source_ref[here_rows, :] = mark_ref[here_rows, :] * miss
             here.append(column(miss, unit))
         sources.append(here)
 
     for part in range(blocks):
-        for copy in fetches[part]:
-            copy.wait()
 
         def ends(chunk, _):
             for s in range(seqs):
                 lane = s * chunks + chunk
                 state_ref[pl.ds(lane, 1), :] = along(entries[s], before_ref[lane]) + start_ref[pl.ds(lane, 1), :]
-                sums = tails[s] * home_ref[lane]
+                sums = tails[s] * home_refs[s][chunk]
                 for k in range(part, blocks):
-                    sums = sums + sources[s][k] * pull_ref[s * blocks + k, chunk]
+                    sums = sums + sources[s][k] * pull_refs[s][k, chunk]
                 carry_ref[pl.ds(lane, 1), :] = jnp.sum(sums, axis=0, keepdims=True)
             return 0
 
         lax.fori_loop(part * per_block, (part + 1) * per_block, ends, 0, unroll=2)
 
-    def walk(now, both):
-        state, carry = both
-        at = pl.ds(now, lanes, stride=LANE)
-        back = pl.ds(LANE - 1 - now, lanes, stride=LANE)
-        state = state + gain_ref[at, :] * mul(state, drift_w) + resid_ref[at, :]
-        path_ref[at, :] = guess_ref[at, :] + state
-        adjoint = source_ref[back, :] + carry
-        scaled = gain_back_ref[back, :] * adjoint
-        pre_ref[back, :] = scaled
-        return state, adjoint + mul_t(scaled, drift_wt)
-
-    lax.fori_loop(0, LANE, walk, (state_ref[...], carry_ref[...]), unroll=2)
-    path_copy = pltpu.make_async_copy(path_ref, path_out, sems.at[1])
-    path_copy.start()
-
+
+def walk_kernel(
+    drift_ref, state_ref, carry_ref, source_ref, gain_ref, gain_back_ref, resid_ref, guess_ref,
+    path_ref, pre_ref,
+):
+    lanes, hidden = state_ref.shape
+    drift = drift_ref[...]
+
+    def walks(ahead_ref, behind_ref):
+        pltpu.matmul_push_rhs(right(drift), 0, 0)
+        pltpu.matmul_push_rhs(right_t(drift), 0, 1, transpose=True)
+
+        def walk(now, both, staged=None):
+            state, carry = both
+            at = pl.ds(now, lanes, stride=LANE)
+            back = pl.ds(LANE - 1 - now, lanes, stride=LANE)
+            adjoint = source_ref[back, :] + carry
+            scaled = gain_back_ref[back, :] * adjoint
+            pltpu.matmul_acc_lhs(ahead_ref, left(state), staged)
+            pltpu.matmul_acc_lhs(behind_ref, left(scaled), staged)
+            pre_ref[back, :] = scaled
+            rest = state + resid_ref[at, :]
+            state = rest + gain_ref[at, :] * halves(pltpu.matmul_pop(ahead_ref))
+            path_ref[at, :] = guess_ref[at, :] + state
+            return state, adjoint + halves(pltpu.matmul_pop(behind_ref))
+
+        both = walk(0, (state_ref[...], carry_ref[...]), 0)
+        lax.fori_loop(1, LANE, walk, both, unroll=3)
+
+    wide = (lanes, 2 * hidden)
+    pl.run_scoped(walks, pltpu.ACC(0)(wide, F32), pltpu.ACC(1)(wide, F32))
+
+
+def gradients_kernel(edge_ref, pre_ref, high_ref, low_ref, grads_ref):
+    rows, hidden = pre_ref.shape
+    seqs = edge_ref.shape[0]
+    count = rows // seqs
+    unit = identity(hidden)
     pre_high, pre_low = split(pre_ref[...])
     pre_w = jnp.concatenate([pre_high, pre_low], axis=1)
     sums = halves(jnp.dot(high_ref[...], pre_w, preferred_element_type=F32)) + jnp.dot(
@@ -547,12 +538,11 @@
     )
     recur = sums[:hidden]
     for s in range(seqs):
-        recur = recur + column(edges[s], unit) * pre_ref[pl.ds(s * count, 1), :]
+        recur = recur + column(edge_ref[pl.ds(s, 1), :], unit) * pre_ref[pl.ds(s * count, 1), :]
     recur = recur.T - recur
     half = hidden // 2
     grads_ref[pl.ds(0, half), :] = fold(recur)
     grads_ref[pl.ds(half, sums.shape[0] - hidden), :] = sums[hidden:]
-    path_copy.wait()
 
 
 def finish_kernel(mine_ref, other_ref, recur_ref, in_ref):
@@ -617,11 +607,11 @@
         functools.partial(compose_kernel, seqs, blocks, total_seqs, keep),
         [
             near((seqs, hidden + hidden // 2 + 8, hidden)),
-            far((lanes, hidden, hidden)),
+            near((lanes, hidden, hidden)),
             far((lanes, hidden, hidden)),
             (lanes, hidden),
-            (hits, hidden, hidden),
-            (hits, hidden, hidden),
+            far((hits, hidden, hidden)),
+            near((hits, hidden, hidden)),
             (hits, hidden),
             (rows, hidden),
             (rows, hidden),
@@ -632,8 +622,8 @@
             (depth, lanes if keep else 1, hidden, hidden),
             (depth, lanes if keep else 1, hidden),
             (lanes, hidden, hidden),
-            (lanes, hidden, hidden),
             (lanes, hidden),
+            (hits, hidden, hidden),
             (hits, hidden),
             (rows, hidden),
             pltpu.SMEM((seqs, blocks), jnp.int32),
@@ -650,38 +640,49 @@
     )(target_steps, x, guess, recur_weight, damping.reshape(1, hidden), in_weight,
       bias_term.reshape(1, hidden), targets.reshape(hits, hidden))
 
-    home, pull, ready = call(
-        functools.partial(prepare_kernel, seqs, blocks),
-        [far((lanes, hidden, hidden)), far((hits, chunks, hidden, hidden)), (8, hidden)],
-        [HBM, HBM, VMEM],
-        [
-            (lanes, hidden, hidden),
-            (hits, chunks, hidden, hidden),
-            pltpu.SMEM((seqs, blocks), jnp.int32),
-            (lanes, hidden, hidden),
-            pltpu.SemaphoreType.DMA((2,)),
-            pltpu.SemaphoreType.DMA((seqs * blocks * (blocks + 3) // 2,)),
-        ],
-        flops=1 << 32,
-        room=20,
-    )(target_steps, maps, hit)
-
+    def prepare(seq, gate):
+        return call(
+            functools.partial(prepare_kernel, seq, blocks),
+            [
+                near((chunks, hidden, hidden)),
+                near((blocks, chunks, hidden, hidden)),
+                (8, hidden),
+            ],
+            [HBM, HBM, VMEM, VMEM],
+            [
+                pltpu.SMEM((seqs, blocks), jnp.int32),
+                (blocks, hidden, hidden),
+                pltpu.SemaphoreType.DMA((2,)),
+            ],
+            flops=1 << 32,
+        )(target_steps, hit, maps, gate)
+
+    prepared = [prepare(0, drift)]
+    ready = prepared[0][2]
     levels = levels_of("seq")
     groups, received = [message], []
     for level in range(levels - 1):
         received.append(swapped(groups[-1], "seq", 1 << level))
         if level == 1:
-            high, low, ready = call(
-                functools.partial(factors_kernel, seqs),
+            prepared += [prepare(s, groups[1]) for s in range(1, seqs)]
+            high, low, mark, ready = call(
+                functools.partial(factors_kernel, seqs, blocks),
                 [
                     jax.ShapeDtypeStruct((hidden + features, rows), BF16),
                     jax.ShapeDtypeStruct((hidden + features, rows), BF16),
+                    near((rows, hidden)),
                     (8, hidden),
                 ],
-                [HBM, HBM, VMEM],
-                [(rows, hidden), (rows, features), (rows, hidden), pltpu.SemaphoreType.DMA((2,))],
+                [HBM, HBM, HBM, VMEM],
+                [
+                    (rows, hidden),
+                    (rows, features),
+                    (rows, hidden),
+                    pltpu.SMEM((seqs, blocks), jnp.int32),
+                    pltpu.SemaphoreType.DMA((3,)),
+                ],
                 flops=1 << 31,
-            )(x, guess, groups[1])
+            )(target_steps, x, guess, prepared[-1][2])
         with_map = level < levels - 2
         height = (hidden if with_map else 0) + hidden // 2 + 8
         groups += call(
@@ -698,18 +699,26 @@
         flops=1 << 30,
     )(drift, *groups[:-1], *received)
 
-    path, grads = call(
-        functools.partial(solve_kernel, seqs, blocks, total_seqs, levels - 1),
-        [far((rows, hidden)), near((hidden // 2 + features, hidden))],
-        [HBM] + [VMEM] * 3 + [HBM] * 2 + [VMEM] * 13,
-        [(lanes, hidden)] * 2 + [(rows, hidden)] * 4 + [
-            (lanes, hidden, hidden),
-            (hits, chunks, hidden, hidden),
-            pltpu.SMEM((seqs, blocks), jnp.int32),
-            pltpu.SemaphoreType.DMA((2 + seqs * blocks * (blocks + 3) // 2,)),
+    state, carry, source, gain_back, edge = call(
+        functools.partial(ends_kernel, seqs, blocks, total_seqs, levels - 1),
+        [
+            near((lanes, hidden)),
+            near((lanes, hidden)),
+            near((rows, hidden)),
+            near((rows, hidden)),
+            near((seqs, hidden)),
         ],
-    )(target_steps, drift, groups[-1], other, home, pull, entry, tail, back, sides, before, start,
-      reach, reach_off, gain, resid, guess, high, low)
+        [VMEM] * (13 + 2 * seqs),
+    )(drift, groups[-1], other, *[p[0] for p in prepared],
+      *[p[1] for p in prepared], entry, tail, back, sides, before, start, reach, reach_off, gain, mark)
+    path, pre = call(
+        walk_kernel,
+        [near((rows, hidden)), near((rows, hidden))],
+        [VMEM] * 8,
+    )(drift, state, carry, source, gain, gain_back, resid, guess)
+    (grads,) = call(
+        gradients_kernel, [near((hidden // 2 + features, hidden))], [VMEM] * 4
+    )(edge, pre, high, low)
 
     middle = grads.shape[0] // 2
     odd = lax.axis_index("batch") & 1 == 1

time: 67.8 us -> 64.4 us (0.950)
  waiting for transfers between devices: 18.3 us -> 15.8 us
  Pallas kernels: 34.2 us -> 31.9 us
  local copies, waits for them, and re-layouts: 0.01 us -> 0.71 us
  starting transfers between devices: 14.3 us -> 15 us
    pallas_call x8 -> x11, Pallas kernels: 34.2 us -> 31.9 us  [pinned(): run(*[pltpu.with_memory_space_constraint(x, pltpu.HBM) if spec is HBM els...]
    ppermute x5, waiting for transfers between devices: 6.2 us -> 4.24 us  [swapped(): lax.ppermute(value, axis, [(i, i ^ distance) for i in range(lax.axis_size...]
    unnamed x4 -> x5, local copies, waits for them, and re-layouts: 0.01 us -> 0.71 us
  transfers between devices with their start and end apart: 9 -> 9, of which waited for: 8 -> 9; matrix products, arithmetic and copies ran while one was open for 0% -> 1% of each run, Pallas kernels for 14% -> 15%
where the time goes in v5:
time: 64.4 us; the launch traced here: 64.2 us
  Pallas kernels  31.9 us (50%)
  waiting for transfers between devices  15.8 us (25%)
  starting transfers between devices  15 us (23%)
  between operations  0.77 us (1%)
  local copies, waits for them, and re-layouts  0.71 us (1%)
    pallas_call x11, Pallas kernels, pinned(): run(*[pltpu.with_memory_space_constraint(x, pltpu.HBM) if spec is HBM els...  31.9 us
    ppermute x4, waiting for transfers between devices, on_device(): kept = kept + lax.ppermute(kept, ('seq', 'batch'), route)  11.5 us
    ppermute x5, starting transfers between devices, swapped(): lax.ppermute(value, axis, [(i, i ^ distance) for i in range(lax.axis_size...  7.62 us
    ppermute x4, starting transfers between devices, on_device(): kept = kept + lax.ppermute(kept, ('seq', 'batch'), route)  7.38 us
    ppermute x5, waiting for transfers between devices, swapped(): lax.ppermute(value, axis, [(i, i ^ distance) for i in range(lax.axis_size...  4.24 us
  transfers between devices with their start and end apart: 9, of which 9 were waited for; matrix products, arithmetic and copies ran while one was open for 1% of the time, Pallas kernels for 15%

profile of v5, /device:TPU:0, one launch (start us, length us, event | category | flops | bytes accessed | tf_op | source)
XLA Modules:
  0.0 64.2 jit_solution(12282330657092229406)
XLA Ops:
  0.6 15.2 %shard_map.103 = (f32[2,200,128]{2,1,0:T(8,128)S(1)}, f32[32,128,128]{2,1,0:T(8,128)S(1)}, f32[32,128,128]{2,1,0:T(8,128)}, f32[32,128]{1,0:T(8,128)S(1)}, f32[4...) custom-call(s32[2,2]{1,0:T(2,128)} %steps_in.7, ...), custom_call_target="tpu_custom_call" | custom-call | bytes 1048576 | tf_op jit(solution)/shard_map/pallas_call | solution.py:574
  15.8 3.0 %collective-permute-start = (f32[2,200,128]{2,1,0:T(8,128)S(1)}, f32[2,200,128]{2,1,0:T(8,128)S(1)}, u32[]{:S(2)}, u32[]{:S(2)}) collective-permute-start(f32[2,200,128]{2,1,0:T(8,128)S(1)} %get-tuple-element.37.mine_ref.refs_0_), channel_id=1, source_target_pairs={{0,4},{4,0},{8,12},{12,8},{16,20},{20,16},{24,28},{28,24},{1,5},{5... | collective-permute-start | bytes 614408 | tf_op jit(solution)/shard_map/ppermute | solution.py:583
  18.8 2.9 %shard_map.104 = (f32[16,128,128]{2,1,0:T(8,128)S(1)}, f32[2,16,128,128]{3,2,1,0:T(8,128)S(1)}, f32[8,128]{1,0:T(8,128)S(1)}) custom-call(s32[2,2]{1,0:T(2,128)} %steps_in.7, f32[4,128,128]{2,1,0:T(8,128)} %get-tuple-element.38.hit_in, f32[32,128,128]{2,1,0:T(8,128)S(1)} %get-tuple-element.39.maps_ref, f32[128,128]{1,0:T(8,128)S(1)} %get-tuple-element.36._.drift_ref), custom_call_target="tpu_custom_call" | custom-call | flops 4294967296 | bytes 1048576 | tf_op jit(solution)/shard_map/pallas_call | solution.py:574
  21.7 2.2 %collective-permute-done.other_ref.refs_2_ = f32[2,200,128]{2,1,0:T(8,128)S(1)} collective-permute-done((f32[2,200,128]{2,1,0:T(8,128)S(1)}, f32[2,200,128]{2,1,0:T(8,128)S(1)}, u32[]{:S(2)}, u32[]{:S(2)}) %collective-permute-start) | collective-permute-done | bytes 204832 | tf_op jit(solution)/shard_map/ppermute | solution.py:583
  23.9 0.9 %shard_map.105._.mine_ref.refs_1_ = f32[2,200,128]{2,1,0:T(8,128)S(1)} custom-call(f32[128,128]{1,0:T(8,128)S(1)} %get-tuple-element.36._.drift_ref, f32[2,200,128]{2,1,0:T(8,128)S(1)} %get-tuple-element.37.mine_ref.refs_0_, f32[2,200,128]{2,1,0:T(8,128)S(1)} %collective-permute-done.other_ref.refs_2_, f32[8,128]{1,0:T(8,128)S(1)} %get-tuple-element.40._), custom_call_target="tpu_custom_call" | custom-call | bytes 1048576 | tf_op jit(solution)/shard_map/pallas_call | solution.py:574
  24.8 1.9 %collective-permute-start.1 = (f32[2,200,128]{2,1,0:T(8,128)S(1)}, f32[2,200,128]{2,1,0:T(8,128)S(1)}, u32[]{:S(2)}, u32[]{:S(2)}) collective-permute-start(f32[2,200,128]{2,1,0:T(8,128)S(1)} %shard_map.105._.mine_ref.refs_1_), channel_id=1, source_target_pairs={{0,8},{4,12},{8,0},{12,4},{16,24},{20,28},{24,16},{28,20},{1,9},{5... | collective-permute-start | bytes 614408 | tf_op jit(solution)/shard_map/ppermute | solution.py:583
  26.7 2.9 %shard_map.106 = (f32[16,128,128]{2,1,0:T(8,128)S(1)}, f32[2,16,128,128]{3,2,1,0:T(8,128)S(1)}, f32[8,128]{1,0:T(8,128)S(1)}) custom-call(s32[2,2]{1,0:T(2,128)} %steps_in.7, f32[4,128,128]{2,1,0:T(8,128)} %get-tuple-element.38.hit_in, f32[32,128,128]{2,1,0:T(8,128)S(1)} %get-tuple-element.39.maps_ref, f32[2,200,128]{2,1,0:T(8,128)S(1)} %shard_map.105._.mine_ref.refs_1_), custom_call_target="tpu_custom_call" | custom-call | flops 4294967296 | bytes 1048576 | tf_op jit(solution)/shard_map/pallas_call | solution.py:574
  29.6 1.4 %shard_map.107 = (bf16[384,512]{1,0:T(8,128)(2,1)S(1)}, bf16[384,512]{1,0:T(8,128)(2,1)S(1)}, f32[512,128]{1,0:T(8,128)S(1)}, f32[8,128]{1,0:T(8,128)S(1)}) custom-call(s32[2,2]{1,0:T(2,128)} %steps_in.7, f32[512,256]{1,0:T(8,128)} %bitcast.11, f32[512,128]{1,0:T(8,128)} %bitcast.8, f32[8,128]{1,0:T(8,128)S(1)} %get-tuple-element.41._), custom_call_target="tpu_custom_call" | custom-call | flops 2147483648 | bytes 1048576 | tf_op jit(solution)/shard_map/pallas_call | solution.py:574
  31.0 0.1 collective-permute-done.1.other_ref.refs_3_
  31.1 0.9 %shard_map.108.mine_ref = f32[2,72,128]{2,1,0:T(8,128)S(1)} custom-call(f32[128,128]{1,0:T(8,128)S(1)} %get-tuple-element.36._.drift_ref, f32[2,200,128]{2,1,0:T(8,128)S(1)} %shard_map.105._.mine_ref.refs_1_, f32[2,200,128]{2,1,0:T(8,128)S(1)} %collective-permute-done.1.other_ref.refs_3_, f32[8,128]{1,0:T(8,128)S(1)} %get-tuple-element.42._), custom_call_target="tpu_custom_call" | custom-call | bytes 1048576 | tf_op jit(solution)/shard_map/pallas_call | solution.py:574
  32.0 0.0 copy-start
  32.0 2.6 %collective-permute-start.2 = (f32[2,72,128]{2,1,0:T(8,128)S(1)}, f32[2,72,128]{2,1,0:T(8,128)S(1)}, u32[]{:S(2)}, u32[]{:S(2)}) collective-permute-start(f32[2,72,128]{2,1,0:T(8,128)S(1)} %shard_map.108.mine_ref), channel_id=1, source_target_pairs={{0,16},{4,20},{8,24},{12,28},{16,0},{20,4},{24,8},{28,12},{1,17},{... | collective-permute-start | bytes 221192 | tf_op jit(solution)/shard_map/ppermute | solution.py:583
  34.6 2.6 %shard_map.109 = (f32[2,128,128]{2,1,0:T(8,128)S(1)}, f32[2,128,128]{2,1,0:T(8,128)S(1)}, f32[2,128,128]{2,1,0:T(8,128)S(1)}, f32[16,128]{1,0:T(8,128)S(1)}) custom-call(f32[128,128]{1,0:T(8,128)S(1)} %get-tuple-element.36._.drift_ref, f32[2,200,128]{2,1,0:T(8,128)S(1)} %get-tuple-element.37.mine_ref.refs_0_, ...), custom_call_target="tpu_custom_call" | custom-call | flops 1073741824 | bytes 1048576 | tf_op jit(solution)/shard_map/pallas_call | solution.py:574
  37.2 0.2 collective-permute-done.2.other_ref
  37.3 0.0 copy-done
  37.3 0.0 copy-start.1
  37.3 1.8 %shard_map.110 = (f32[32,128]{1,0:T(8,128)S(1)}, f32[32,128]{1,0:T(8,128)S(1)}, f32[512,128]{1,0:T(8,128)S(1)}, f32[512,128]{1,0:T(8,128)S(1)}, f32[2,128]{1,0:T(2,128)S(1)}) custom-call(f32[128,128]{1,0:T(8,128)S(1)} %get-tuple-element.36._.drift_ref, f32[2,72,128]{2,1,0:T(8,128)S(1)} %shard_map.108.mine_ref, ...), custom_call_target="tpu_custom_call" | custom-call | bytes 1048576 | tf_op jit(solution)/shard_map/pallas_call | solution.py:574
  39.1 0.0 copy-done.1
  39.1 2.1 %shard_map.111 = (f32[512,128]{1,0:T(8,128)S(1)}, f32[512,128]{1,0:T(8,128)S(1)}) custom-call(f32[128,128]{1,0:T(8,128)S(1)} %get-tuple-element.36._.drift_ref, f32[32,128]{1,0:T(8,128)S(1)} %get-tuple-element.57.state_ref, f32[32,128]{1,0:T(8,128)S(1)} %get-tuple-element.58.carry_ref, f32[512,128]{1,0:T(8,128)S(1)} %get-tuple-element.59.source_ref, ...), custom_call_target="tpu_custom_call" | custom-call | bytes 1048576 | tf_op jit(solution)/shard_map/pallas_call | solution.py:574
  41.2 0.5 shard_map.112
  41.7 0.1 collective-permute-start.3
  41.8 1.3 %collective-permute-done.3 = f32[160,128]{1,0:T(8,128)S(1)} collective-permute-done((f32[160,128]{1,0:T(8,128)S(1)}, f32[160,128]{1,0:T(8,128)S(1)}, u32[]{:S(2)}, u32[]{:S(2)}) %collective-permute-start.3) | collective-permute-done | bytes 81952 | tf_op jit(solution)/shard_map/ppermute | solution.py:583
  43.1 1.5 %collective-permute-start.4 = (f32[160,128]{1,0:T(8,128)S(1)}, f32[160,128]{1,0:T(8,128)S(1)}, u32[]{:S(2)}, u32[]{:S(2)}) collective-permute-start(f32[160,128]{1,0:T(8,128)S(1)} %select_add_fusion), channel_id=1, source_target_pairs={{0,2},{1,9},{2,0},{3,11},{4,6},{5,13},{6,4},{7,15},{8,10},{9,1},{1... | collective-permute-start | bytes 245768 | tf_op jit(solution)/shard_map/ppermute | solution.py:736
  44.6 3.0 %collective-permute-done.4 = f32[160,128]{1,0:T(8,128)S(1)} collective-permute-done((f32[160,128]{1,0:T(8,128)S(1)}, f32[160,128]{1,0:T(8,128)S(1)}, u32[]{:S(2)}, u32[]{:S(2)}) %collective-permute-start.4) | collective-permute-done | bytes 81952 | tf_op jit(solution)/shard_map/ppermute | solution.py:736
  47.6 1.5 %collective-permute-start.5 = (f32[160,128]{1,0:T(8,128)S(1)}, f32[160,128]{1,0:T(8,128)S(1)}, u32[]{:S(2)}, u32[]{:S(2)}) collective-permute-start(f32[160,128]{1,0:T(8,128)S(1)} %add.16), channel_id=1, source_target_pairs={{0,4},{1,17},{2,6},{3,19},{4,0},{5,21},{6,2},{7,23},{8,12},{9,25},... | collective-permute-start | bytes 245768 | tf_op jit(solution)/shard_map/ppermute | solution.py:736
  49.1 3.0 %collective-permute-done.5 = f32[160,128]{1,0:T(8,128)S(1)} collective-permute-done((f32[160,128]{1,0:T(8,128)S(1)}, f32[160,128]{1,0:T(8,128)S(1)}, u32[]{:S(2)}, u32[]{:S(2)}) %collective-permute-start.5) | collective-permute-done | bytes 81952 | tf_op jit(solution)/shard_map/ppermute | solution.py:736
  52.1 1.6 %collective-permute-start.6 = (f32[160,128]{1,0:T(8,128)S(1)}, f32[160,128]{1,0:T(8,128)S(1)}, u32[]{:S(2)}, u32[]{:S(2)}) collective-permute-start(f32[160,128]{1,0:T(8,128)S(1)} %add.17), channel_id=1, source_target_pairs={{0,8},{1,3},{2,10},{3,1},{4,12},{5,7},{6,14},{7,5},{8,0},{9,11},{1... | collective-permute-start | bytes 245768 | tf_op jit(solution)/shard_map/ppermute | solution.py:736
  53.7 2.9 %collective-permute-done.6 = f32[160,128]{1,0:T(8,128)S(1)} collective-permute-done((f32[160,128]{1,0:T(8,128)S(1)}, f32[160,128]{1,0:T(8,128)S(1)}, u32[]{:S(2)}, u32[]{:S(2)}) %collective-permute-start.6) | collective-permute-done | bytes 81952 | tf_op jit(solution)/shard_map/ppermute | solution.py:736
  56.7 2.8 %collective-permute-start.7 = (f32[160,128]{1,0:T(8,128)S(1)}, f32[160,128]{1,0:T(8,128)S(1)}, u32[]{:S(2)}, u32[]{:S(2)}) collective-permute-start(f32[160,128]{1,0:T(8,128)S(1)} %add.18), channel_id=1, source_target_pairs={{0,16},{1,5},{2,18},{3,7},{4,20},{5,1},{6,22},{7,3},{8,24},{9,13},... | collective-permute-start | bytes 245768 | tf_op jit(solution)/shard_map/ppermute | solution.py:736
  59.5 2.6 %collective-permute-done.7 = f32[160,128]{1,0:T(8,128)S(1)} collective-permute-done((f32[160,128]{1,0:T(8,128)S(1)}, f32[160,128]{1,0:T(8,128)S(1)}, u32[]{:S(2)}, u32[]{:S(2)}) %collective-permute-start.7) | collective-permute-done | bytes 81952 | tf_op jit(solution)/shard_map/ppermute | solution.py:736
  62.1 0.1 collective-permute-start.8
  62.2 0.7 %copy.11 = f32[2,256,128]{2,1,0:T(8,128)} copy(f32[2,256,128]{2,1,0:T(8,128)S(1)} %bitcast.6) | data formatting | bytes 524288
  62.9 0.6 collective-permute-done.8.other_ref
  63.4 0.8 %shard_map.113 = (f32[128,128]{1,0:T(8,128)}, f32[256,128]{1,0:T(8,128)}) custom-call(f32[160,128]{1,0:T(8,128)S(1)} %add.19.mine_ref, f32[160,128]{1,0:T(8,128)S(1)} %collective-permute-done.8.other_ref), custom_call_target="tpu_custom_call" | custom-call | bytes 1048576 | tf_op jit(solution)/shard_map/pallas_call | solution.py:574
  (6 shorter events, 0.1 us)
Async XLA Ops:
  15.8 8.1 %collective-permute-start = (f32[2,200,128]{2,1,0:T(8,128)S(1)}, f32[2,200,128]{2,1,0:T(8,128)S(1)}, u32[]{:S(2)}, u32[]{:S(2)}) collective-permute-start(f32[2,200,128]{2,1,0:T(8,128)S(1)} %get-tuple-element.37.mine_ref.refs_0_), channel_id=1, source_target_pairs={{0,4},{4,0},{8,12},{12,8},{16,20},{20,16},{24,28},{28,24},{1,5},{5... | collective-permute-start | bytes 614408 | tf_op jit(solution)/shard_map/ppermute | solution.py:583
  24.8 6.3 %collective-permute-start.1 = (f32[2,200,128]{2,1,0:T(8,128)S(1)}, f32[2,200,128]{2,1,0:T(8,128)S(1)}, u32[]{:S(2)}, u32[]{:S(2)}) collective-permute-start(f32[2,200,128]{2,1,0:T(8,128)S(1)} %shard_map.105._.mine_ref.refs_1_), channel_id=1, source_target_pairs={{0,8},{4,12},{8,0},{12,4},{16,24},{20,28},{24,16},{28,20},{1,9},{5... | collective-permute-start | bytes 614408 | tf_op jit(solution)/shard_map/ppermute | solution.py:583
  32.0 5.3 %copy-start = (f32[32,128,128]{2,1,0:T(8,128)S(1)}, f32[32,128,128]{2,1,0:T(8,128)}, u32[]{:S(2)}) copy-start(f32[32,128,128]{2,1,0:T(8,128)} %get-tuple-element.51.refs_8_) | copy-start | bytes 6291460
  32.0 5.3 %collective-permute-start.2 = (f32[2,72,128]{2,1,0:T(8,128)S(1)}, f32[2,72,128]{2,1,0:T(8,128)S(1)}, u32[]{:S(2)}, u32[]{:S(2)}) collective-permute-start(f32[2,72,128]{2,1,0:T(8,128)S(1)} %shard_map.108.mine_ref), channel_id=1, source_target_pairs={{0,16},{4,20},{8,24},{12,28},{16,0},{20,4},{24,8},{28,12},{1,17},{... | collective-permute-start | bytes 221192 | tf_op jit(solution)/shard_map/ppermute | solution.py:583
  37.3 1.8 %copy-start.1 = (f32[2,256,128]{2,1,0:T(8,128)S(1)}, f32[2,256,128]{2,1,0:T(8,128)}, u32[]{:S(2)}) copy-start(f32[2,256,128]{2,1,0:T(8,128)} %param.9) | copy-start | bytes 786436
  41.7 1.3 %collective-permute-start.3 = (f32[160,128]{1,0:T(8,128)S(1)}, f32[160,128]{1,0:T(8,128)S(1)}, u32[]{:S(2)}, u32[]{:S(2)}) collective-permute-start(f32[160,128]{1,0:T(8,128)S(1)} %slice_select_fusion), channel_id=1, source_target_pairs={{0,1},{1,0},{2,3},{3,2},{4,5},{5,4},{6,7},{7,6},{8,9},{9,8},{10,11... | collective-permute-start | bytes 245768 | tf_op jit(solution)/shard_map/ppermute | solution.py:583
  43.1 4.5 %collective-permute-start.4 = (f32[160,128]{1,0:T(8,128)S(1)}, f32[160,128]{1,0:T(8,128)S(1)}, u32[]{:S(2)}, u32[]{:S(2)}) collective-permute-start(f32[160,128]{1,0:T(8,128)S(1)} %select_add_fusion), channel_id=1, source_target_pairs={{0,2},{1,9},{2,0},{3,11},{4,6},{5,13},{6,4},{7,15},{8,10},{9,1},{1... | collective-permute-start | bytes 245768 | tf_op jit(solution)/shard_map/ppermute | solution.py:736
  47.6 4.5 %collective-permute-start.5 = (f32[160,128]{1,0:T(8,128)S(1)}, f32[160,128]{1,0:T(8,128)S(1)}, u32[]{:S(2)}, u32[]{:S(2)}) collective-permute-start(f32[160,128]{1,0:T(8,128)S(1)} %add.16), channel_id=1, source_target_pairs={{0,4},{1,17},{2,6},{3,19},{4,0},{5,21},{6,2},{7,23},{8,12},{9,25},... | collective-permute-start | bytes 245768 | tf_op jit(solution)/shard_map/ppermute | solution.py:736
  52.1 4.5 %collective-permute-start.6 = (f32[160,128]{1,0:T(8,128)S(1)}, f32[160,128]{1,0:T(8,128)S(1)}, u32[]{:S(2)}, u32[]{:S(2)}) collective-permute-start(f32[160,128]{1,0:T(8,128)S(1)} %add.17), channel_id=1, source_target_pairs={{0,8},{1,3},{2,10},{3,1},{4,12},{5,7},{6,14},{7,5},{8,0},{9,11},{1... | collective-permute-start | bytes 245768 | tf_op jit(solution)/shard_map/ppermute | solution.py:736
  56.7 5.4 %collective-permute-start.7 = (f32[160,128]{1,0:T(8,128)S(1)}, f32[160,128]{1,0:T(8,128)S(1)}, u32[]{:S(2)}, u32[]{:S(2)}) collective-permute-start(f32[160,128]{1,0:T(8,128)S(1)} %add.18), channel_id=1, source_target_pairs={{0,16},{1,5},{2,18},{3,7},{4,20},{5,1},{6,22},{7,3},{8,24},{9,13},... | collective-permute-start | bytes 245768 | tf_op jit(solution)/shard_map/ppermute | solution.py:736
  62.1 1.3 %collective-permute-start.8 = (f32[160,128]{1,0:T(8,128)S(1)}, f32[160,128]{1,0:T(8,128)S(1)}, u32[]{:S(2)}, u32[]{:S(2)}) collective-permute-start(f32[160,128]{1,0:T(8,128)S(1)} %add.19.mine_ref), channel_id=1, source_target_pairs={{0,1},{1,0},{2,3},{3,2},{4,5},{5,4},{6,7},{7,6},{8,9},{9,8},{10,11... | collective-permute-start | bytes 245768 | tf_op jit(solution)/shard_map/ppermute | solution.py:583

commit v6 on v5

--- a/solution.py
+++ b/solution.py
@@ -9,8 +9,9 @@
 
 LANE = 16
 MIB = 1 << 20
-UNROLL = 5
-ROOM = 41
+UNROLL = 7
+RUN = 4
+ROOM = 40
 KEEP = 36 * MIB
 F32 = jnp.float32
 BF16 = jnp.bfloat16
@@ -95,7 +96,7 @@
     return jnp.sum(col * weight, axis=0, keepdims=True)
 
 
-OFFSET, ADJOINT, DRIVE, FIRST, LAST, DIAGONAL = range(6)
+OFFSET, ADJOINT, DRIVE, FIRST, LAST, MOVED, DIAGONAL = range(7)
 
 
 def triangles(half):
@@ -130,9 +131,9 @@
 def compose_kernel(
     seqs, blocks, total_seqs, keep, steps_in, x_in, guess_in, recur_in, damping_in, in_in, bias_in,
     targets_in,
-    message_ref, maps_ref, before_out, start_ref, hit_out, reach_ref, reach_off_ref, gain_ref,
-    resid_ref, drift_ref,
-    record_ref, record_off_ref, before_ref, off_ref, hit_ref, hit_off_ref, prev_ref,
+    message_ref, maps_ref, before_out, start_ref, lead_ref, lead_off_ref, hit_out, reach_ref,
+    reach_off_ref, gain_out, resid_out, drift_ref,
+    gain_ref, resid_ref, record_ref, record_off_ref, before_ref, off_ref, hit_ref, hit_off_ref, prev_ref,
     steps_ref, x_ref, guess_ref, recur_ref, damping_ref, in_ref, bias_ref, targets_ref, sems,
 ):
     fetches = [
@@ -151,45 +152,53 @@
     chunks = count // LANE
     lanes = seqs * chunks
     block = count // blocks
+    per_block = chunks // blocks
     drift = drift_t(recur_ref, damping_ref)
     drift_ref[...] = drift
     drift_w = right(drift)
-
-    guess = guess_ref[...]
+    for s in range(seqs):
+        last = guess_ref[pl.ds((s + 1) * count - 1, 1), :]
+        message_ref[s, pl.ds(hidden + hidden // 2 + LAST, 1), :] = last
+        message_ref[s, pl.ds(hidden + hidden // 2 + MOVED, 1), :] = mul(eight(last), drift_w)[:1]
     prev_ref[pl.ds(1, rows - 1), :] = guess_ref[pl.ds(0, rows - 1), :]
     for s in range(seqs):
         prev_ref[pl.ds(s * count, 1), :] = jnp.zeros((1, hidden), F32)
-    prev = prev_ref[...]
     for fetch in fetches[3:]:
         fetch.wait()
-    x_high, x_low = split(x_ref[...])
     in_w = jnp.concatenate(split(in_ref[...]), axis=1)
-    drive = bias_ref[...] + halves(
-        jnp.dot(x_high, in_w, preferred_element_type=F32)
-        + jnp.dot(x_low, in_w, preferred_element_type=F32)
-    )
-    activation = jnp.tanh(mul(prev, drift_w) + drive)
-    gain_ref[...] = euler_step * (1.0 - activation * activation)
-    resid_ref[...] = prev + euler_step * activation - guess
-    own = (lax.axis_index("seq") == 0).astype(F32)
-    for s in range(seqs):
-        edge = pl.ds(s * count, 1)
-        gain_ref[edge, :] = gain_ref[edge, :] * own
-        resid_ref[edge, :] = resid_ref[edge, :] * own
-
+
+    for top in range(0, rows, block):
+        part = pl.ds(top, block)
+        x_high, x_low = split(x_ref[part, :])
+        drive = bias_ref[...] + halves(
+            jnp.dot(x_high, in_w, preferred_element_type=F32)
+            + jnp.dot(x_low, in_w, preferred_element_type=F32)
+        )
+        prev = prev_ref[part, :]
+        activation = jnp.tanh(mul(prev, drift_w) + drive)
+        gain_ref[part, :] = euler_step * (1.0 - activation * activation)
+        resid_ref[part, :] = prev + euler_step * activation - guess_ref[part, :]
+        if top % count == 0:
+            own = (lax.axis_index("seq") == 0).astype(F32)
+            edge = pl.ds(top, 1)
+            gain_ref[edge, :] = gain_ref[edge, :] * own
+            resid_ref[edge, :] = resid_ref[edge, :] * own
+            message_ref[top // count, pl.ds(hidden + hidden // 2 + DRIVE, 1), :] = drive[:1]
+
+    sends = [
+        pltpu.make_async_copy(gain_ref, gain_out, sems.at[9]),
+        pltpu.make_async_copy(resid_ref, resid_out, sems.at[10]),
+    ]
+    for send in sends:
+        send.start()
     unit = identity(hidden)
-    for lane in range(lanes):
-        first = unit + drift * gain_ref[pl.ds(lane * LANE, 1), :]
-        maps_ref[lane] = first
-        if keep:
-            record_ref[0, lane] = first
-    off_ref[...] = resid_ref[pl.ds(0, lanes, stride=LANE), :]
-    if keep:
-        record_off_ref[0] = off_ref[...]
 
     def place(j):
         step = (j % blocks) * block + steps_ref[j // blocks, j % blocks]
         return (j // blocks) * chunks + step // LANE, step % LANE, (j // blocks) * count + step
+
+    def opening(lane):
+        return unit + drift * gain_ref[pl.ds(lane * LANE, 1), :]
 
     def capture(now):
         for j in range(seqs * blocks):
@@ -200,7 +209,7 @@
                 hit_ref[j] = maps_ref[lane]
                 hit_off_ref[pl.ds(j, 1), :] = off_ref[pl.ds(lane, 1), :]
 
-    def advance(now, _):
+    def advance(now, _, opened_here=False):
         off = off_ref[...]
         off = (
             off
@@ -211,7 +220,10 @@
         if keep:
             record_off_ref[now] = off
         for lane in range(0, lanes, 2):
-            pair = maps_ref[lane : lane + 2].reshape(2 * hidden, hidden)
+            if opened_here:
+                pair = jnp.concatenate([opening(lane), opening(lane + 1)], axis=0)
+            else:
+                pair = maps_ref[lane : lane + 2].reshape(2 * hidden, hidden)
             moved = mul(pair, drift_w)
             for k in range(2):
                 gain_now = gain_ref[pl.ds((lane + k) * LANE + now, 1), :]
@@ -224,37 +236,49 @@
             capture(now)
         return 0
 
+    off_ref[...] = resid_ref[pl.ds(0, lanes, stride=LANE), :]
     if keep:
-        lax.fori_loop(1, LANE, advance, 0, unroll=UNROLL)
+        record_off_ref[0] = off_ref[...]
+        advance(1, 0, True)
+        lax.fori_loop(2, LANE, advance, 0, unroll=UNROLL)
         for j in range(seqs * blocks):
             lane, at, _ = place(j)
-            hit_ref[j] = record_ref[at, lane]
+            hit_ref[j] = jnp.where(at == 0, opening(lane), record_ref[jnp.maximum(at, 1), lane])
             hit_off_ref[pl.ds(j, 1), :] = record_off_ref[at, pl.ds(lane, 1), :]
     else:
+        for lane in range(lanes):
+            maps_ref[lane] = opening(lane)
         capture(0)
         lax.fori_loop(1, LANE, advance, 0)
-    hit_copy = pltpu.make_async_copy(hit_ref, hit_out, sems.at[9])
+    hit_copy = pltpu.make_async_copy(hit_ref, hit_out, sems.at[8])
     hit_copy.start()
 
-    running = [unit] * seqs
-    offset = [jnp.zeros((8, hidden), F32)] * seqs
-    for chunk in range(chunks):
-        for s in range(seqs):
-            lane = s * chunks + chunk
-            before_ref[lane] = running[s]
-            start_ref[pl.ds(lane, 1), :] = offset[s][:1]
+    hits = seqs * blocks
+    running = [None] * hits
+    offset = [None] * hits
+    for chunk in range(per_block):
+        for j in range(hits):
+            lane = j * per_block + chunk
             this, this_off = maps_ref[lane], off_ref[pl.ds(lane, 1), :]
             if chunk == 0:
-                running[s], offset[s] = this, eight(this_off)
+                before_ref[lane] = unit
+                start_ref[pl.ds(lane, 1), :] = jnp.zeros((1, hidden), F32)
+                running[j], offset[j] = this, eight(this_off)
             else:
+                before_ref[lane] = running[j]
+                start_ref[pl.ds(lane, 1), :] = offset[j][:1]
                 packed = right(this)
-                running[s] = mul(running[s], packed)
-                offset[s] = mul(offset[s], packed) + this_off
-    before_copy = pltpu.make_async_copy(before_ref, before_out, sems.at[8])
-    before_copy.start()
-
-    for s in range(seqs):
-        message_ref[s, pl.ds(0, hidden), :] = running[s]
+                running[j] = mul(running[j], packed)
+                offset[j] = mul(offset[j], packed) + this_off
+            if (chunk + 1) % RUN == 0:
+                run = pl.ds(lane + 1 - RUN, RUN)
+                sends.append(
+                    pltpu.make_async_copy(before_ref.at[run], before_out.at[run], sems.at[9 + len(sends)])
+                )
+                sends[-1].start()
+
+    for s in range(seqs):
+        lead, lead_off = None, None
         total = jnp.zeros((hidden, hidden), F32)
         total_off = jnp.zeros((8, hidden), F32)
         for k in range(blocks):
@@ -263,6 +287,16 @@
             packed = right(hit_ref[j])
             reach = mul(before_ref[lane], packed)
             reach_off = mul(eight(start_ref[pl.ds(lane, 1), :]), packed) + hit_off_ref[pl.ds(j, 1), :]
+            if k:
+                lead_ref[j] = lead
+                lead_off_ref[pl.ds(j, 1), :] = lead_off[:1]
+                reach_w, whole_w = right(reach), right(running[j])
+                reach, reach_off = mul(lead, reach_w), mul(lead_off, reach_w) + reach_off
+                lead, lead_off = mul(lead, whole_w), mul(lead_off, whole_w) + offset[j]
+            else:
+                lead_ref[j] = unit
+                lead_off_ref[pl.ds(j, 1), :] = jnp.zeros((1, hidden), F32)
+                lead, lead_off = running[j], offset[j]
             reach_ref[j] = reach
             miss = reach_off + guess_ref[pl.ds(row, 1), :] - targets_ref[pl.ds(j, 1), :]
             reach_off_ref[pl.ds(j, 1), :] = miss[:1]
@@ -270,20 +304,25 @@
             total = total + mul_t(reach, reach_t)
             total_off = total_off + mul_t(miss, reach_t)
         total = total / total_seqs
+        message_ref[s, pl.ds(0, hidden), :] = lead
         message_ref[s, pl.ds(hidden, hidden // 2), :] = fold(total)
-        message_ref[s, pl.ds(hidden + hidden // 2, 8), :] = vectors(
-            offset[s], total_off / total_seqs, drive[s * count : s * count + 1],
-            guess_ref[pl.ds(s * count, 1), :], guess_ref[pl.ds((s + 1) * count - 1, 1), :],
-            jnp.sum(unit * total, axis=0, keepdims=True),
-        )
-    before_copy.wait()
-    hit_copy.wait()
+        tail = hidden + hidden // 2
+        for at, row in (
+            (OFFSET, lead_off[:1]),
+            (ADJOINT, total_off[:1] / total_seqs),
+            (FIRST, guess_ref[pl.ds(s * count, 1), :]),
+            (DIAGONAL, jnp.sum(unit * total, axis=0, keepdims=True)),
+        ):
+            message_ref[s, pl.ds(tail + at, 1), :] = row
+        message_ref[s, pl.ds(tail + DIAGONAL + 1, 7 - DIAGONAL), :] = jnp.zeros((7 - DIAGONAL, hidden), F32)
+    for send in [*sends, hit_copy]:
+        send.wait()
 
 
 def opened(ref, s, with_map=True):
     hidden = ref.shape[2]
     at = hidden if with_map else 0
-    rows = [eight(ref[s, pl.ds(at + hidden // 2 + k, 1), :]) for k in range(5)]
+    rows = [eight(ref[s, pl.ds(at + hidden // 2 + k, 1), :]) for k in range(6)]
     diagonal = ref[s, pl.ds(at + hidden // 2 + DIAGONAL, 1), :]
     half = unfold(ref[s, pl.ds(at, hidden // 2), :])
     curve = half + half.T + identity(hidden) * diagonal
@@ -294,21 +333,21 @@
     return jax.tree.map(lambda a, b: jnp.where(flag, a, b), one, other)
 
 
-def crossing(last, drive, first, drift_w):
-    activation = jnp.tanh(mul(last, drift_w) + drive)
+def crossing(last, moved, drive, first):
+    activation = jnp.tanh(moved + drive)
     return euler_step * (1.0 - activation * activation), last + euler_step * activation - first
 
 
 def join(one, two, drift_w, with_map=True):
     map_1, curve_1, rows_1 = one
     map_2, curve_2, rows_2 = two
-    gain, resid = crossing(rows_1[LAST], rows_2[DRIVE], rows_2[FIRST], drift_w)
+    gain, resid = crossing(rows_1[LAST], rows_1[MOVED], rows_2[DRIVE], rows_2[FIRST])
     map_1 = map_1 + mul(map_1, drift_w) * gain[:1]
     off_1 = rows_1[OFFSET] + mul(rows_1[OFFSET], drift_w) * gain + resid
     curve_w, map_w, map_1_t = right(curve_2), right(map_2), right_t(map_1)
     curve = curve_1 + mul_t(mul(map_1, curve_w), map_1_t)
     adjoint = rows_1[ADJOINT] + mul_t(mul(off_1, curve_w) + rows_2[ADJOINT], map_1_t)
-    rows = [mul(off_1, map_w) + rows_2[OFFSET], adjoint, rows_1[DRIVE], rows_1[FIRST], rows_2[LAST]]
+    rows = [mul(off_1, map_w) + rows_2[OFFSET], adjoint, rows_1[DRIVE], rows_1[FIRST], rows_2[LAST], rows_2[MOVED]]
     return (mul(map_1, map_w) if with_map else None), curve, rows
 
 
@@ -337,14 +376,14 @@
     for s in range(seqs):
         zero = jnp.zeros((8, hidden), F32)
         lead, lead_off = unit, zero
-        after = (unit, jnp.zeros((hidden, hidden), F32), [zero] * 5)
+        after = (unit, jnp.zeros((hidden, hidden), F32), [zero] * 6)
         edge, edge_gain = zero, zero
         place = lax.axis_index("seq")
         fresh = place >= 0
         for level in range(levels):
             upper = (place >> level) & 1 == 1
             mine, other = opened(mines[level], s), opened(others[level], s)
-            gain, resid = crossing(other[2][LAST], mine[2][DRIVE], mine[2][FIRST], drift_w)
+            gain, resid = crossing(other[2][LAST], other[2][MOVED], mine[2][DRIVE], mine[2][FIRST])
             far = other[0] + mul(other[0], drift_w) * gain[:1]
             far_off = other[2][OFFSET] + mul(other[2][OFFSET], drift_w) * gain + resid
             lead_w = right(lead)
@@ -352,7 +391,7 @@
             known = jnp.logical_and(upper, fresh)
             edge, edge_gain = pick(known, (other[2][LAST], gain), (edge, edge_gain))
             fresh = jnp.logical_and(fresh, jnp.logical_not(upper))
-            after[2][LAST] = mine[2][LAST]
+            after[2][LAST], after[2][MOVED] = mine[2][LAST], mine[2][MOVED]
             extended = join(after, other, drift_w)
             lead, lead_off = pick(upper, longer, (lead, lead_off))
             after = pick(upper, after, extended)
@@ -429,8 +468,8 @@
 ):
     home_refs, pull_refs, refs = refs[:seqs], refs[seqs : 2 * seqs], refs[2 * seqs :]
     (
-        entry_ref, tail_ref, back_ref, sides_ref, before_ref, start_ref, reach_ref, reach_off_ref,
-        gain_ref, mark_ref,
+        before_ref, start_ref, lead_ref, lead_off_ref, entry_ref, tail_ref, back_ref, sides_ref,
+        reach_ref, reach_off_ref, gain_ref, mark_ref,
         state_ref, carry_ref, source_ref, gain_back_ref, edge_ref,
     ) = refs
     rows, hidden = gain_ref.shape
@@ -450,16 +489,24 @@
     entries, tails, sources = [], [], []
     for s in range(seqs):
         mine, other = opened(mine_ref, s, False), opened(other_ref, s, False)
-        last, middle = pick(upper, (other[2][LAST], other[2][OFFSET]), (mine[2][LAST], mine[2][OFFSET]))
+        last, moved, middle = pick(
+            upper,
+            (other[2][LAST], other[2][MOVED], other[2][OFFSET]),
+            (mine[2][LAST], mine[2][MOVED], mine[2][OFFSET]),
+        )
         drive, first = pick(upper, (mine[2][DRIVE], mine[2][FIRST]), (other[2][DRIVE], other[2][FIRST]))
-        gain, resid = crossing(last, drive, first, drift_w)
+        gain, resid = crossing(last, moved, drive, first)
         middle = middle + mul(middle, drift_w) * gain + resid
         middle_col = column(middle[:1], unit)
         row = along(middle_col, jnp.where(upper, entry_ref[s], other[1]))
         lead_off, tail_off, edge, edge_gain = [sides_ref[pl.ds(8 * s + k, 1), :] for k in range(4)]
         beyond = eight(row) + other[2][ADJOINT]
         beyond = beyond + mul_t(beyond * gain, drift_wt)
-        entries.append(column(jnp.where(upper, row, 0.0) + lead_off, unit))
+        entry = column(jnp.where(upper, row, 0.0) + lead_off, unit)
+        entries.append([entry])
+        for k in range(1, blocks):
+            j = s * blocks + k
+            entries[s].append(column(along(entry, lead_ref[j]) + lead_off_ref[pl.ds(j, 1), :], unit))
         tail = jnp.where(
             upper, along(middle_col, tail_ref[s]), along(column(beyond[:1], unit), back_ref[s])
         )
@@ -473,25 +520,39 @@
         here = []
         for k in range(blocks):
             j = s * blocks + k
-            miss = (along(entries[s], reach_ref[j]) + reach_off_ref[pl.ds(j, 1), :]) / total_seqs
+            miss = (along(entries[s][0], reach_ref[j]) + reach_off_ref[pl.ds(j, 1), :]) / total_seqs
             here_rows = pl.ds(j * block, block)
             source_ref[here_rows, :] = mark_ref[here_rows, :] * miss
             here.append(column(miss, unit))
         sources.append(here)
 
+    def starts(part, chunk, _):
+        for s in range(seqs):
+            lane = s * chunks + chunk
+            row = along(entries[s][part], before_ref[lane])
+            state_ref[pl.ds(lane, 1), :] = row + start_ref[pl.ds(lane, 1), :]
+        return 0
+
+    def homes(chunk, _):
+        for s in range(seqs):
+            lane = s * chunks + chunk
+            carry_ref[pl.ds(lane, 1), :] = along(tails[s], home_refs[s][chunk])
+        return 0
+
+    def pulls(s, part, chunk, _):
+        at = pl.ds(s * chunks + chunk, 1)
+        row = sum(sources[s][k] * pull_refs[s][k, chunk] for k in range(part, blocks))
+        carry_ref[at, :] = carry_ref[at, :] + jnp.sum(row, axis=0, keepdims=True)
+        return 0
+
     for part in range(blocks):
-
-        def ends(chunk, _):
-            for s in range(seqs):
-                lane = s * chunks + chunk
-                state_ref[pl.ds(lane, 1), :] = along(entries[s], before_ref[lane]) + start_ref[pl.ds(lane, 1), :]
-                sums = tails[s] * home_refs[s][chunk]
-                for k in range(part, blocks):
-                    sums = sums + sources[s][k] * pull_refs[s][k, chunk]
-                carry_ref[pl.ds(lane, 1), :] = jnp.sum(sums, axis=0, keepdims=True)
-            return 0
-
-        lax.fori_loop(part * per_block, (part + 1) * per_block, ends, 0, unroll=2)
+        starting = functools.partial(starts, part)
+        lax.fori_loop(part * per_block, (part + 1) * per_block, starting, 0, unroll=4)
+    lax.fori_loop(0, chunks, homes, 0, unroll=4)
+    for s in range(seqs):
+        for part in range(blocks):
+            pulling = functools.partial(pulls, s, part)
+            lax.fori_loop(part * per_block, (part + 1) * per_block, pulling, 0, unroll=4)
 
 
 def walk_kernel(
@@ -571,10 +632,11 @@
     )
 
     def pinned(*operands):
-        return run(*[
+        placed = [
             pltpu.with_memory_space_constraint(x, pltpu.HBM) if spec is HBM else x
             for x, spec in zip(operands, in_specs, strict=True)
-        ])
+        ]
+        return run(*placed)
 
     return pinned
 
@@ -603,22 +665,26 @@
     keep = rows * hidden * hidden * 4 <= KEEP
     depth = LANE if keep else 1
 
-    message, maps, before, start, hit, reach, reach_off, gain, resid, drift = call(
+    message, maps, before, start, lead, lead_off, hit, reach, reach_off, gain, resid, drift = call(
         functools.partial(compose_kernel, seqs, blocks, total_seqs, keep),
         [
             near((seqs, hidden + hidden // 2 + 8, hidden)),
             near((lanes, hidden, hidden)),
             far((lanes, hidden, hidden)),
-            (lanes, hidden),
+            near((lanes, hidden)),
+            near((hits, hidden, hidden)),
+            near((hits, hidden)),
             far((hits, hidden, hidden)),
             near((hits, hidden, hidden)),
             (hits, hidden),
-            (rows, hidden),
-            (rows, hidden),
+            far((rows, hidden)),
+            far((rows, hidden)),
             (hidden, hidden),
         ],
         [HBM] * 8,
         [
+            (rows, hidden),
+            (rows, hidden),
             (depth, lanes if keep else 1, hidden, hidden),
             (depth, lanes if keep else 1, hidden),
             (lanes, hidden, hidden),
@@ -634,7 +700,7 @@
             (features, hidden),
             (1, hidden),
             (hits, hidden),
-            pltpu.SemaphoreType.DMA((10,)),
+            pltpu.SemaphoreType.DMA((11 + lanes // RUN,)),
         ],
         room=ROOM,
     )(target_steps, x, guess, recur_weight, damping.reshape(1, hidden), in_weight,
@@ -708,9 +774,8 @@
             near((rows, hidden)),
             near((seqs, hidden)),
         ],
-        [VMEM] * (13 + 2 * seqs),
-    )(drift, groups[-1], other, *[p[0] for p in prepared],
-      *[p[1] for p in prepared], entry, tail, back, sides, before, start, reach, reach_off, gain, mark)
+        [VMEM] * (15 + 2 * seqs),
+    )(drift, groups[-1], other, *[p[0] for p in prepared], *[p[1] for p in prepared], before, start, lead, lead_off, entry, tail, back, sides, reach, reach_off, gain, mark)
     path, pre = call(
         walk_kernel,
         [near((rows, hidden)), near((rows, hidden))],

time: 64.4 us -> 63 us (0.978)
  Pallas kernels: 31.9 us -> 30.1 us
    pallas_call x11, Pallas kernels: 31.9 us -> 30.1 us  [pinned(): return run(*placed)]
where the time goes in v6:
time: 63 us; the launch traced here: 62.8 us
  Pallas kernels  30.1 us (48%)
  waiting for transfers between devices  16.1 us (26%)
  starting transfers between devices  15 us (24%)
  between operations  0.79 us (1%)
  local copies, waits for them, and re-layouts  0.72 us (1%)
    pallas_call x11, Pallas kernels, pinned(): return run(*placed)  30.1 us
    ppermute x4, waiting for transfers between devices, on_device(): kept = kept + lax.ppermute(kept, ('seq', 'batch'), route)  11.5 us
    ppermute x5, starting transfers between devices, swapped(): lax.ppermute(value, axis, [(i, i ^ distance) for i in range(lax.axis_size...  7.63 us
    ppermute x4, starting transfers between devices, on_device(): kept = kept + lax.ppermute(kept, ('seq', 'batch'), route)  7.41 us
    ppermute x5, waiting for transfers between devices, swapped(): lax.ppermute(value, axis, [(i, i ^ distance) for i in range(lax.axis_size...  4.6 us
  transfers between devices with their start and end apart: 9, of which 9 were waited for; matrix products, arithmetic and copies ran while one was open for 1% of the time, Pallas kernels for 15%

profile of v6, /device:TPU:0, one launch (start us, length us, event | category | flops | bytes accessed | tf_op | source)
XLA Modules:
  0.0 62.8 jit_solution(15073881922393973116)
XLA Ops:
  0.6 13.9 %shard_map.103 = (f32[2,200,128]{2,1,0:T(8,128)S(1)}, f32[32,128,128]{2,1,0:T(8,128)S(1)}, f32[32,128,128]{2,1,0:T(8,128)}, f32[32,128]{1,0:T(8,128)S(1)}, f32[4...) custom-call(s32[2,2]{1,0:T(2,128)} %steps_in.7, ...), custom_call_target="tpu_custom_call" | custom-call | bytes 1048576 | tf_op jit(solution)/shard_map/pallas_call | solution.py:639
  14.5 3.0 %collective-permute-start = (f32[2,200,128]{2,1,0:T(8,128)S(1)}, f32[2,200,128]{2,1,0:T(8,128)S(1)}, u32[]{:S(2)}, u32[]{:S(2)}) collective-permute-start(f32[2,200,128]{2,1,0:T(8,128)S(1)} %get-tuple-element.39.mine_ref.refs_0_), channel_id=1, source_target_pairs={{0,4},{4,0},{8,12},{12,8},{16,20},{20,16},{24,28},{28,24},{1,5},{5... | collective-permute-start | bytes 614408 | tf_op jit(solution)/shard_map/ppermute | solution.py:645
  17.5 2.9 %shard_map.104 = (f32[16,128,128]{2,1,0:T(8,128)S(1)}, f32[2,16,128,128]{3,2,1,0:T(8,128)S(1)}, f32[8,128]{1,0:T(8,128)S(1)}) custom-call(s32[2,2]{1,0:T(2,128)} %steps_in.7, f32[4,128,128]{2,1,0:T(8,128)} %get-tuple-element.40.hit_in, f32[32,128,128]{2,1,0:T(8,128)S(1)} %get-tuple-element.41.maps_ref, f32[128,128]{1,0:T(8,128)S(1)} %get-tuple-element.38._.drift_ref), custom_call_target="tpu_custom_call" | custom-call | flops 4294967296 | bytes 1048576 | tf_op jit(solution)/shard_map/pallas_call | solution.py:639
  20.5 2.1 %collective-permute-done.other_ref.refs_2_ = f32[2,200,128]{2,1,0:T(8,128)S(1)} collective-permute-done((f32[2,200,128]{2,1,0:T(8,128)S(1)}, f32[2,200,128]{2,1,0:T(8,128)S(1)}, u32[]{:S(2)}, u32[]{:S(2)}) %collective-permute-start) | collective-permute-done | bytes 204832 | tf_op jit(solution)/shard_map/ppermute | solution.py:645
  22.6 0.9 %shard_map.105._.mine_ref.refs_1_ = f32[2,200,128]{2,1,0:T(8,128)S(1)} custom-call(f32[128,128]{1,0:T(8,128)S(1)} %get-tuple-element.38._.drift_ref, f32[2,200,128]{2,1,0:T(8,128)S(1)} %get-tuple-element.39.mine_ref.refs_0_, f32[2,200,128]{2,1,0:T(8,128)S(1)} %collective-permute-done.other_ref.refs_2_, f32[8,128]{1,0:T(8,128)S(1)} %get-tuple-element.42._), custom_call_target="tpu_custom_call" | custom-call | bytes 1048576 | tf_op jit(solution)/shard_map/pallas_call | solution.py:639
  23.5 1.9 %collective-permute-start.1 = (f32[2,200,128]{2,1,0:T(8,128)S(1)}, f32[2,200,128]{2,1,0:T(8,128)S(1)}, u32[]{:S(2)}, u32[]{:S(2)}) collective-permute-start(f32[2,200,128]{2,1,0:T(8,128)S(1)} %shard_map.105._.mine_ref.refs_1_), channel_id=1, source_target_pairs={{0,8},{4,12},{8,0},{12,4},{16,24},{20,28},{24,16},{28,20},{1,9},{5... | collective-permute-start | bytes 614408 | tf_op jit(solution)/shard_map/ppermute | solution.py:645
  25.4 2.9 %shard_map.106 = (f32[16,128,128]{2,1,0:T(8,128)S(1)}, f32[2,16,128,128]{3,2,1,0:T(8,128)S(1)}, f32[8,128]{1,0:T(8,128)S(1)}) custom-call(s32[2,2]{1,0:T(2,128)} %steps_in.7, f32[4,128,128]{2,1,0:T(8,128)} %get-tuple-element.40.hit_in, f32[32,128,128]{2,1,0:T(8,128)S(1)} %get-tuple-element.41.maps_ref, f32[2,200,128]{2,1,0:T(8,128)S(1)} %shard_map.105._.mine_ref.refs_1_), custom_call_target="tpu_custom_call" | custom-call | flops 4294967296 | bytes 1048576 | tf_op jit(solution)/shard_map/pallas_call | solution.py:639
  28.3 1.4 %shard_map.107 = (bf16[384,512]{1,0:T(8,128)(2,1)S(1)}, bf16[384,512]{1,0:T(8,128)(2,1)S(1)}, f32[512,128]{1,0:T(8,128)S(1)}, f32[8,128]{1,0:T(8,128)S(1)}) custom-call(s32[2,2]{1,0:T(2,128)} %steps_in.7, f32[512,256]{1,0:T(8,128)} %bitcast.11, f32[512,128]{1,0:T(8,128)} %bitcast.8, f32[8,128]{1,0:T(8,128)S(1)} %get-tuple-element.43._), custom_call_target="tpu_custom_call" | custom-call | flops 2147483648 | bytes 1048576 | tf_op jit(solution)/shard_map/pallas_call | solution.py:639
  29.7 0.1 collective-permute-done.1.other_ref.refs_3_
  29.8 0.9 %shard_map.108.mine_ref = f32[2,72,128]{2,1,0:T(8,128)S(1)} custom-call(f32[128,128]{1,0:T(8,128)S(1)} %get-tuple-element.38._.drift_ref, f32[2,200,128]{2,1,0:T(8,128)S(1)} %shard_map.105._.mine_ref.refs_1_, f32[2,200,128]{2,1,0:T(8,128)S(1)} %collective-permute-done.1.other_ref.refs_3_, f32[8,128]{1,0:T(8,128)S(1)} %get-tuple-element.44._), custom_call_target="tpu_custom_call" | custom-call | bytes 1048576 | tf_op jit(solution)/shard_map/pallas_call | solution.py:639
  30.7 0.0 copy-start
  30.7 0.0 copy-start.2
  30.7 2.6 %collective-permute-start.2 = (f32[2,72,128]{2,1,0:T(8,128)S(1)}, f32[2,72,128]{2,1,0:T(8,128)S(1)}, u32[]{:S(2)}, u32[]{:S(2)}) collective-permute-start(f32[2,72,128]{2,1,0:T(8,128)S(1)} %shard_map.108.mine_ref), channel_id=1, source_target_pairs={{0,16},{4,20},{8,24},{12,28},{16,0},{20,4},{24,8},{28,12},{1,17},{... | collective-permute-start | bytes 221192 | tf_op jit(solution)/shard_map/ppermute | solution.py:645
  33.3 2.2 %shard_map.109 = (f32[2,128,128]{2,1,0:T(8,128)S(1)}, f32[2,128,128]{2,1,0:T(8,128)S(1)}, f32[2,128,128]{2,1,0:T(8,128)S(1)}, f32[16,128]{1,0:T(8,128)S(1)}) custom-call(f32[128,128]{1,0:T(8,128)S(1)} %get-tuple-element.38._.drift_ref, f32[2,200,128]{2,1,0:T(8,128)S(1)} %get-tuple-element.39.mine_ref.refs_0_, ...), custom_call_target="tpu_custom_call" | custom-call | flops 1073741824 | bytes 1048576 | tf_op jit(solution)/shard_map/pallas_call | solution.py:639
  35.5 0.5 collective-permute-done.2.other_ref
  36.0 0.0 copy-done
  36.0 0.0 copy-done.2
  36.0 0.0 copy-start.1
  36.0 0.0 copy-start.3
  36.0 1.7 %shard_map.110 = (f32[32,128]{1,0:T(8,128)S(1)}, f32[32,128]{1,0:T(8,128)S(1)}, f32[512,128]{1,0:T(8,128)S(1)}, f32[512,128]{1,0:T(8,128)S(1)}, f32[2,128]{1,0:T(2,128)S(1)}) custom-call(f32[128,128]{1,0:T(8,128)S(1)} %get-tuple-element.38._.drift_ref, f32[2,72,128]{2,1,0:T(8,128)S(1)} %shard_map.108.mine_ref, ...), custom_call_target="tpu_custom_call" | custom-call | bytes 1048576 | tf_op jit(solution)/shard_map/pallas_call | solution.py:639
  37.7 0.0 copy-done.1
  37.7 0.0 copy-done.3
  37.7 2.1 %shard_map.111 = (f32[512,128]{1,0:T(8,128)S(1)}, f32[512,128]{1,0:T(8,128)S(1)}) custom-call(f32[128,128]{1,0:T(8,128)S(1)} %get-tuple-element.38._.drift_ref, f32[32,128]{1,0:T(8,128)S(1)} %get-tuple-element.61.state_ref, f32[32,128]{1,0:T(8,128)S(1)} %get-tuple-element.62.carry_ref, f32[512,128]{1,0:T(8,128)S(1)} %get-tuple-element.63.source_ref, ...), custom_call_target="tpu_custom_call" | custom-call | bytes 1048576 | tf_op jit(solution)/shard_map/pallas_call | solution.py:639
  39.9 0.5 shard_map.112
  40.3 0.1 collective-permute-start.3
  40.4 1.3 %collective-permute-done.3 = f32[160,128]{1,0:T(8,128)S(1)} collective-permute-done((f32[160,128]{1,0:T(8,128)S(1)}, f32[160,128]{1,0:T(8,128)S(1)}, u32[]{:S(2)}, u32[]{:S(2)}) %collective-permute-start.3) | collective-permute-done | bytes 81952 | tf_op jit(solution)/shard_map/ppermute | solution.py:645
  41.7 1.5 %collective-permute-start.4 = (f32[160,128]{1,0:T(8,128)S(1)}, f32[160,128]{1,0:T(8,128)S(1)}, u32[]{:S(2)}, u32[]{:S(2)}) collective-permute-start(f32[160,128]{1,0:T(8,128)S(1)} %select_add_fusion), channel_id=1, source_target_pairs={{0,2},{1,9},{2,0},{3,11},{4,6},{5,13},{6,4},{7,15},{8,10},{9,1},{1... | collective-permute-start | bytes 245768 | tf_op jit(solution)/shard_map/ppermute | solution.py:801
  43.2 3.0 %collective-permute-done.4 = f32[160,128]{1,0:T(8,128)S(1)} collective-permute-done((f32[160,128]{1,0:T(8,128)S(1)}, f32[160,128]{1,0:T(8,128)S(1)}, u32[]{:S(2)}, u32[]{:S(2)}) %collective-permute-start.4) | collective-permute-done | bytes 81952 | tf_op jit(solution)/shard_map/ppermute | solution.py:801
  46.2 1.5 %collective-permute-start.5 = (f32[160,128]{1,0:T(8,128)S(1)}, f32[160,128]{1,0:T(8,128)S(1)}, u32[]{:S(2)}, u32[]{:S(2)}) collective-permute-start(f32[160,128]{1,0:T(8,128)S(1)} %add.16), channel_id=1, source_target_pairs={{0,4},{1,17},{2,6},{3,19},{4,0},{5,21},{6,2},{7,23},{8,12},{9,25},... | collective-permute-start | bytes 245768 | tf_op jit(solution)/shard_map/ppermute | solution.py:801
  47.7 3.0 %collective-permute-done.5 = f32[160,128]{1,0:T(8,128)S(1)} collective-permute-done((f32[160,128]{1,0:T(8,128)S(1)}, f32[160,128]{1,0:T(8,128)S(1)}, u32[]{:S(2)}, u32[]{:S(2)}) %collective-permute-start.5) | collective-permute-done | bytes 81952 | tf_op jit(solution)/shard_map/ppermute | solution.py:801
  50.8 1.6 %collective-permute-start.6 = (f32[160,128]{1,0:T(8,128)S(1)}, f32[160,128]{1,0:T(8,128)S(1)}, u32[]{:S(2)}, u32[]{:S(2)}) collective-permute-start(f32[160,128]{1,0:T(8,128)S(1)} %add.17), channel_id=1, source_target_pairs={{0,8},{1,3},{2,10},{3,1},{4,12},{5,7},{6,14},{7,5},{8,0},{9,11},{1... | collective-permute-start | bytes 245768 | tf_op jit(solution)/shard_map/ppermute | solution.py:801
  52.3 2.9 %collective-permute-done.6 = f32[160,128]{1,0:T(8,128)S(1)} collective-permute-done((f32[160,128]{1,0:T(8,128)S(1)}, f32[160,128]{1,0:T(8,128)S(1)}, u32[]{:S(2)}, u32[]{:S(2)}) %collective-permute-start.6) | collective-permute-done | bytes 81952 | tf_op jit(solution)/shard_map/ppermute | solution.py:801
  55.3 2.8 %collective-permute-start.7 = (f32[160,128]{1,0:T(8,128)S(1)}, f32[160,128]{1,0:T(8,128)S(1)}, u32[]{:S(2)}, u32[]{:S(2)}) collective-permute-start(f32[160,128]{1,0:T(8,128)S(1)} %add.18), channel_id=1, source_target_pairs={{0,16},{1,5},{2,18},{3,7},{4,20},{5,1},{6,22},{7,3},{8,24},{9,13},... | collective-permute-start | bytes 245768 | tf_op jit(solution)/shard_map/ppermute | solution.py:801
  58.1 2.6 %collective-permute-done.7 = f32[160,128]{1,0:T(8,128)S(1)} collective-permute-done((f32[160,128]{1,0:T(8,128)S(1)}, f32[160,128]{1,0:T(8,128)S(1)}, u32[]{:S(2)}, u32[]{:S(2)}) %collective-permute-start.7) | collective-permute-done | bytes 81952 | tf_op jit(solution)/shard_map/ppermute | solution.py:801
  60.7 0.1 collective-permute-start.8
  60.8 0.7 %copy.11 = f32[2,256,128]{2,1,0:T(8,128)} copy(f32[2,256,128]{2,1,0:T(8,128)S(1)} %bitcast.6) | data formatting | bytes 524288
  61.5 0.6 collective-permute-done.8.other_ref
  62.0 0.8 %shard_map.113 = (f32[128,128]{1,0:T(8,128)}, f32[256,128]{1,0:T(8,128)}) custom-call(f32[160,128]{1,0:T(8,128)S(1)} %add.19.mine_ref, f32[160,128]{1,0:T(8,128)S(1)} %collective-permute-done.8.other_ref), custom_call_target="tpu_custom_call" | custom-call | bytes 1048576 | tf_op jit(solution)/shard_map/pallas_call | solution.py:639
  (6 shorter events, 0.1 us)
Async XLA Ops:
  14.5 8.1 %collective-permute-start = (f32[2,200,128]{2,1,0:T(8,128)S(1)}, f32[2,200,128]{2,1,0:T(8,128)S(1)}, u32[]{:S(2)}, u32[]{:S(2)}) collective-permute-start(f32[2,200,128]{2,1,0:T(8,128)S(1)} %get-tuple-element.39.mine_ref.refs_0_), channel_id=1, source_target_pairs={{0,4},{4,0},{8,12},{12,8},{16,20},{20,16},{24,28},{28,24},{1,5},{5... | collective-permute-start | bytes 614408 | tf_op jit(solution)/shard_map/ppermute | solution.py:645
  23.5 6.3 %collective-permute-start.1 = (f32[2,200,128]{2,1,0:T(8,128)S(1)}, f32[2,200,128]{2,1,0:T(8,128)S(1)}, u32[]{:S(2)}, u32[]{:S(2)}) collective-permute-start(f32[2,200,128]{2,1,0:T(8,128)S(1)} %shard_map.105._.mine_ref.refs_1_), channel_id=1, source_target_pairs={{0,8},{4,12},{8,0},{12,4},{16,24},{20,28},{24,16},{28,20},{1,9},{5... | collective-permute-start | bytes 614408 | tf_op jit(solution)/shard_map/ppermute | solution.py:645
  30.7 5.3 %copy-start = (f32[32,128,128]{2,1,0:T(8,128)S(1)}, f32[32,128,128]{2,1,0:T(8,128)}, u32[]{:S(2)}) copy-start(f32[32,128,128]{2,1,0:T(8,128)} %get-tuple-element.49.refs_4_) | copy-start | bytes 6291460
  30.7 5.3 %copy-start.2 = (f32[512,128]{1,0:T(8,128)S(1)}, f32[512,128]{1,0:T(8,128)}, u32[]{:S(2)}) copy-start(f32[512,128]{1,0:T(8,128)} %get-tuple-element.59.refs_14_.gain_ref) | copy-start | bytes 786436
  30.7 5.3 %collective-permute-start.2 = (f32[2,72,128]{2,1,0:T(8,128)S(1)}, f32[2,72,128]{2,1,0:T(8,128)S(1)}, u32[]{:S(2)}, u32[]{:S(2)}) collective-permute-start(f32[2,72,128]{2,1,0:T(8,128)S(1)} %shard_map.108.mine_ref), channel_id=1, source_target_pairs={{0,16},{4,20},{8,24},{12,28},{16,0},{20,4},{24,8},{28,12},{1,17},{... | collective-permute-start | bytes 221192 | tf_op jit(solution)/shard_map/ppermute | solution.py:645
  36.0 1.7 %copy-start.1 = (f32[2,256,128]{2,1,0:T(8,128)S(1)}, f32[2,256,128]{2,1,0:T(8,128)}, u32[]{:S(2)}) copy-start(f32[2,256,128]{2,1,0:T(8,128)} %param.9) | copy-start | bytes 786436
  36.0 1.7 %copy-start.3 = (f32[512,128]{1,0:T(8,128)S(1)}, f32[512,128]{1,0:T(8,128)}, u32[]{:S(2)}) copy-start(f32[512,128]{1,0:T(8,128)} %get-tuple-element.65.resid_ref) | copy-start | bytes 786436
  40.3 1.3 %collective-permute-start.3 = (f32[160,128]{1,0:T(8,128)S(1)}, f32[160,128]{1,0:T(8,128)S(1)}, u32[]{:S(2)}, u32[]{:S(2)}) collective-permute-start(f32[160,128]{1,0:T(8,128)S(1)} %slice_select_fusion), channel_id=1, source_target_pairs={{0,1},{1,0},{2,3},{3,2},{4,5},{5,4},{6,7},{7,6},{8,9},{9,8},{10,11... | collective-permute-start | bytes 245768 | tf_op jit(solution)/shard_map/ppermute | solution.py:645
  41.7 4.5 %collective-permute-start.4 = (f32[160,128]{1,0:T(8,128)S(1)}, f32[160,128]{1,0:T(8,128)S(1)}, u32[]{:S(2)}, u32[]{:S(2)}) collective-permute-start(f32[160,128]{1,0:T(8,128)S(1)} %select_add_fusion), channel_id=1, source_target_pairs={{0,2},{1,9},{2,0},{3,11},{4,6},{5,13},{6,4},{7,15},{8,10},{9,1},{1... | collective-permute-start | bytes 245768 | tf_op jit(solution)/shard_map/ppermute | solution.py:801
  46.2 4.5 %collective-permute-start.5 = (f32[160,128]{1,0:T(8,128)S(1)}, f32[160,128]{1,0:T(8,128)S(1)}, u32[]{:S(2)}, u32[]{:S(2)}) collective-permute-start(f32[160,128]{1,0:T(8,128)S(1)} %add.16), channel_id=1, source_target_pairs={{0,4},{1,17},{2,6},{3,19},{4,0},{5,21},{6,2},{7,23},{8,12},{9,25},... | collective-permute-start | bytes 245768 | tf_op jit(solution)/shard_map/ppermute | solution.py:801
  50.8 4.5 %collective-permute-start.6 = (f32[160,128]{1,0:T(8,128)S(1)}, f32[160,128]{1,0:T(8,128)S(1)}, u32[]{:S(2)}, u32[]{:S(2)}) collective-permute-start(f32[160,128]{1,0:T(8,128)S(1)} %add.17), channel_id=1, source_target_pairs={{0,8},{1,3},{2,10},{3,1},{4,12},{5,7},{6,14},{7,5},{8,0},{9,11},{1... | collective-permute-start | bytes 245768 | tf_op jit(solution)/shard_map/ppermute | solution.py:801
  55.3 5.4 %collective-permute-start.7 = (f32[160,128]{1,0:T(8,128)S(1)}, f32[160,128]{1,0:T(8,128)S(1)}, u32[]{:S(2)}, u32[]{:S(2)}) collective-permute-start(f32[160,128]{1,0:T(8,128)S(1)} %add.18), channel_id=1, source_target_pairs={{0,16},{1,5},{2,18},{3,7},{4,20},{5,1},{6,22},{7,3},{8,24},{9,13},... | collective-permute-start | bytes 245768 | tf_op jit(solution)/shard_map/ppermute | solution.py:801
  60.7 1.3 %collective-permute-start.8 = (f32[160,128]{1,0:T(8,128)S(1)}, f32[160,128]{1,0:T(8,128)S(1)}, u32[]{:S(2)}, u32[]{:S(2)}) collective-permute-start(f32[160,128]{1,0:T(8,128)S(1)} %add.19.mine_ref), channel_id=1, source_target_pairs={{0,1},{1,0},{2,3},{3,2},{4,5},{5,4},{6,7},{7,6},{8,9},{9,8},{10,11... | collective-permute-start | bytes 245768 | tf_op jit(solution)/shard_map/ppermute | solution.py:645

commit v7 on v6

--- a/solution.py
+++ b/solution.py
@@ -9,7 +9,7 @@
 
 LANE = 16
 MIB = 1 << 20
-UNROLL = 7
+UNROLL = 14
 RUN = 4
 ROOM = 40
 KEEP = 36 * MIB
@@ -547,12 +547,12 @@
 
     for part in range(blocks):
         starting = functools.partial(starts, part)
-        lax.fori_loop(part * per_block, (part + 1) * per_block, starting, 0, unroll=4)
-    lax.fori_loop(0, chunks, homes, 0, unroll=4)
+        lax.fori_loop(part * per_block, (part + 1) * per_block, starting, 0, unroll=8)
+    lax.fori_loop(0, chunks, homes, 0, unroll=8)
     for s in range(seqs):
         for part in range(blocks):
             pulling = functools.partial(pulls, s, part)
-            lax.fori_loop(part * per_block, (part + 1) * per_block, pulling, 0, unroll=4)
+            lax.fori_loop(part * per_block, (part + 1) * per_block, pulling, 0, unroll=8)
 
 
 def walk_kernel(
@@ -581,7 +581,8 @@
             return state, adjoint + halves(pltpu.matmul_pop(behind_ref))
 
         both = walk(0, (state_ref[...], carry_ref[...]), 0)
-        lax.fori_loop(1, LANE, walk, both, unroll=3)
+        for now in range(1, LANE):
+            both = walk(now, both)
 
     wide = (lanes, 2 * hidden)
     pl.run_scoped(walks, pltpu.ACC(0)(wide, F32), pltpu.ACC(1)(wide, F32))

time: 63 us -> 61.8 us (0.981)
  Pallas kernels: 30.1 us -> 29.1 us
    pallas_call x11, Pallas kernels: 30.1 us -> 29.1 us  [pinned(): return run(*placed)]
  transfers between devices with their start and end apart: 9 -> 9, of which waited for: 9 -> 9; matrix products, arithmetic and copies ran while one was open for 1% -> 1% of each run, Pallas kernels for 15% -> 16%
where the time goes in v7:
time: 61.8 us; the launch traced here: 61.6 us
  Pallas kernels  29.1 us (47%)
  waiting for transfers between devices  16 us (26%)
  starting transfers between devices  15 us (24%)
  between operations  0.79 us (1%)
  local copies, waits for them, and re-layouts  0.72 us (1%)
    pallas_call x11, Pallas kernels, pinned(): return run(*placed)  29.1 us
    ppermute x4, waiting for transfers between devices, on_device(): kept = kept + lax.ppermute(kept, ('seq', 'batch'), route)  11.5 us
    ppermute x5, starting transfers between devices, swapped(): lax.ppermute(value, axis, [(i, i ^ distance) for i in range(lax.axis_size...  7.62 us
    ppermute x4, starting transfers between devices, on_device(): kept = kept + lax.ppermute(kept, ('seq', 'batch'), route)  7.38 us
    ppermute x5, waiting for transfers between devices, swapped(): lax.ppermute(value, axis, [(i, i ^ distance) for i in range(lax.axis_size...  4.44 us
  transfers between devices with their start and end apart: 9, of which 9 were waited for; matrix products, arithmetic and copies ran while one was open for 1% of the time, Pallas kernels for 16%

profile of v7, /device:TPU:0, one launch (start us, length us, event | category | flops | bytes accessed | tf_op | source)
XLA Modules:
  0.0 61.6 jit_solution(15018419053643126232)
XLA Ops:
  0.6 13.2 %shard_map.103 = (f32[2,200,128]{2,1,0:T(8,128)S(1)}, f32[32,128,128]{2,1,0:T(8,128)S(1)}, f32[32,128,128]{2,1,0:T(8,128)}, f32[32,128]{1,0:T(8,128)S(1)}, f32[4...) custom-call(s32[2,2]{1,0:T(2,128)} %steps_in.7, ...), custom_call_target="tpu_custom_call" | custom-call | bytes 1048576 | tf_op jit(solution)/shard_map/pallas_call | solution.py:640
  13.8 3.0 %collective-permute-start = (f32[2,200,128]{2,1,0:T(8,128)S(1)}, f32[2,200,128]{2,1,0:T(8,128)S(1)}, u32[]{:S(2)}, u32[]{:S(2)}) collective-permute-start(f32[2,200,128]{2,1,0:T(8,128)S(1)} %get-tuple-element.39.mine_ref.refs_0_), channel_id=1, source_target_pairs={{0,4},{4,0},{8,12},{12,8},{16,20},{20,16},{24,28},{28,24},{1,5},{5... | collective-permute-start | bytes 614408 | tf_op jit(solution)/shard_map/ppermute | solution.py:646
  16.8 3.1 %shard_map.104 = (f32[16,128,128]{2,1,0:T(8,128)S(1)}, f32[2,16,128,128]{3,2,1,0:T(8,128)S(1)}, f32[8,128]{1,0:T(8,128)S(1)}) custom-call(s32[2,2]{1,0:T(2,128)} %steps_in.7, f32[4,128,128]{2,1,0:T(8,128)} %get-tuple-element.40.hit_in, f32[32,128,128]{2,1,0:T(8,128)S(1)} %get-tuple-element.41.maps_ref, f32[128,128]{1,0:T(8,128)S(1)} %get-tuple-element.38._.drift_ref), custom_call_target="tpu_custom_call" | custom-call | flops 4294967296 | bytes 1048576 | tf_op jit(solution)/shard_map/pallas_call | solution.py:640
  19.9 2.0 %collective-permute-done.other_ref.refs_2_ = f32[2,200,128]{2,1,0:T(8,128)S(1)} collective-permute-done((f32[2,200,128]{2,1,0:T(8,128)S(1)}, f32[2,200,128]{2,1,0:T(8,128)S(1)}, u32[]{:S(2)}, u32[]{:S(2)}) %collective-permute-start) | collective-permute-done | bytes 204832 | tf_op jit(solution)/shard_map/ppermute | solution.py:646
  21.9 0.9 %shard_map.105._.mine_ref.refs_1_ = f32[2,200,128]{2,1,0:T(8,128)S(1)} custom-call(f32[128,128]{1,0:T(8,128)S(1)} %get-tuple-element.38._.drift_ref, f32[2,200,128]{2,1,0:T(8,128)S(1)} %get-tuple-element.39.mine_ref.refs_0_, f32[2,200,128]{2,1,0:T(8,128)S(1)} %collective-permute-done.other_ref.refs_2_, f32[8,128]{1,0:T(8,128)S(1)} %get-tuple-element.42._), custom_call_target="tpu_custom_call" | custom-call | bytes 1048576 | tf_op jit(solution)/shard_map/pallas_call | solution.py:640
  22.7 1.9 %collective-permute-start.1 = (f32[2,200,128]{2,1,0:T(8,128)S(1)}, f32[2,200,128]{2,1,0:T(8,128)S(1)}, u32[]{:S(2)}, u32[]{:S(2)}) collective-permute-start(f32[2,200,128]{2,1,0:T(8,128)S(1)} %shard_map.105._.mine_ref.refs_1_), channel_id=1, source_target_pairs={{0,8},{4,12},{8,0},{12,4},{16,24},{20,28},{24,16},{28,20},{1,9},{5... | collective-permute-start | bytes 614408 | tf_op jit(solution)/shard_map/ppermute | solution.py:646
  24.6 2.9 %shard_map.106 = (f32[16,128,128]{2,1,0:T(8,128)S(1)}, f32[2,16,128,128]{3,2,1,0:T(8,128)S(1)}, f32[8,128]{1,0:T(8,128)S(1)}) custom-call(s32[2,2]{1,0:T(2,128)} %steps_in.7, f32[4,128,128]{2,1,0:T(8,128)} %get-tuple-element.40.hit_in, f32[32,128,128]{2,1,0:T(8,128)S(1)} %get-tuple-element.41.maps_ref, f32[2,200,128]{2,1,0:T(8,128)S(1)} %shard_map.105._.mine_ref.refs_1_), custom_call_target="tpu_custom_call" | custom-call | flops 4294967296 | bytes 1048576 | tf_op jit(solution)/shard_map/pallas_call | solution.py:640
  27.6 1.4 %shard_map.107 = (bf16[384,512]{1,0:T(8,128)(2,1)S(1)}, bf16[384,512]{1,0:T(8,128)(2,1)S(1)}, f32[512,128]{1,0:T(8,128)S(1)}, f32[8,128]{1,0:T(8,128)S(1)}) custom-call(s32[2,2]{1,0:T(2,128)} %steps_in.7, f32[512,256]{1,0:T(8,128)} %bitcast.11, f32[512,128]{1,0:T(8,128)} %bitcast.8, f32[8,128]{1,0:T(8,128)S(1)} %get-tuple-element.43._), custom_call_target="tpu_custom_call" | custom-call | flops 2147483648 | bytes 1048576 | tf_op jit(solution)/shard_map/pallas_call | solution.py:640
  29.0 0.1 collective-permute-done.1.other_ref.refs_3_
  29.1 0.9 %shard_map.108.mine_ref = f32[2,72,128]{2,1,0:T(8,128)S(1)} custom-call(f32[128,128]{1,0:T(8,128)S(1)} %get-tuple-element.38._.drift_ref, f32[2,200,128]{2,1,0:T(8,128)S(1)} %shard_map.105._.mine_ref.refs_1_, f32[2,200,128]{2,1,0:T(8,128)S(1)} %collective-permute-done.1.other_ref.refs_3_, f32[8,128]{1,0:T(8,128)S(1)} %get-tuple-element.44._), custom_call_target="tpu_custom_call" | custom-call | bytes 1048576 | tf_op jit(solution)/shard_map/pallas_call | solution.py:640
  29.9 0.0 copy-start
  29.9 0.0 copy-start.2
  30.0 2.6 %collective-permute-start.2 = (f32[2,72,128]{2,1,0:T(8,128)S(1)}, f32[2,72,128]{2,1,0:T(8,128)S(1)}, u32[]{:S(2)}, u32[]{:S(2)}) collective-permute-start(f32[2,72,128]{2,1,0:T(8,128)S(1)} %shard_map.108.mine_ref), channel_id=1, source_target_pairs={{0,16},{4,20},{8,24},{12,28},{16,0},{20,4},{24,8},{28,12},{1,17},{... | collective-permute-start | bytes 221192 | tf_op jit(solution)/shard_map/ppermute | solution.py:646
  32.5 2.2 %shard_map.109 = (f32[2,128,128]{2,1,0:T(8,128)S(1)}, f32[2,128,128]{2,1,0:T(8,128)S(1)}, f32[2,128,128]{2,1,0:T(8,128)S(1)}, f32[16,128]{1,0:T(8,128)S(1)}) custom-call(f32[128,128]{1,0:T(8,128)S(1)} %get-tuple-element.38._.drift_ref, f32[2,200,128]{2,1,0:T(8,128)S(1)} %get-tuple-element.39.mine_ref.refs_0_, ...), custom_call_target="tpu_custom_call" | custom-call | flops 1073741824 | bytes 1048576 | tf_op jit(solution)/shard_map/pallas_call | solution.py:640
  34.7 0.5 collective-permute-done.2.other_ref
  35.3 0.0 copy-done
  35.3 0.0 copy-done.2
  35.3 0.0 copy-start.1
  35.3 0.0 copy-start.3
  35.3 1.3 %shard_map.110 = (f32[32,128]{1,0:T(8,128)S(1)}, f32[32,128]{1,0:T(8,128)S(1)}, f32[512,128]{1,0:T(8,128)S(1)}, f32[512,128]{1,0:T(8,128)S(1)}, f32[2,128]{1,0:T(2,128)S(1)}) custom-call(f32[128,128]{1,0:T(8,128)S(1)} %get-tuple-element.38._.drift_ref, f32[2,72,128]{2,1,0:T(8,128)S(1)} %shard_map.108.mine_ref, ...), custom_call_target="tpu_custom_call" | custom-call | bytes 1048576 | tf_op jit(solution)/shard_map/pallas_call | solution.py:640
  36.6 0.0 copy-done.1
  36.6 0.0 copy-done.3
  36.6 2.0 %shard_map.111 = (f32[512,128]{1,0:T(8,128)S(1)}, f32[512,128]{1,0:T(8,128)S(1)}) custom-call(f32[128,128]{1,0:T(8,128)S(1)} %get-tuple-element.38._.drift_ref, f32[32,128]{1,0:T(8,128)S(1)} %get-tuple-element.61.state_ref, f32[32,128]{1,0:T(8,128)S(1)} %get-tuple-element.62.carry_ref, f32[512,128]{1,0:T(8,128)S(1)} %get-tuple-element.63.source_ref, ...), custom_call_target="tpu_custom_call" | custom-call | bytes 1048576 | tf_op jit(solution)/shard_map/pallas_call | solution.py:640
  38.6 0.5 shard_map.112
  39.1 0.1 collective-permute-start.3
  39.2 1.3 %collective-permute-done.3 = f32[160,128]{1,0:T(8,128)S(1)} collective-permute-done((f32[160,128]{1,0:T(8,128)S(1)}, f32[160,128]{1,0:T(8,128)S(1)}, u32[]{:S(2)}, u32[]{:S(2)}) %collective-permute-start.3) | collective-permute-done | bytes 81952 | tf_op jit(solution)/shard_map/ppermute | solution.py:646
  40.5 1.5 %collective-permute-start.4 = (f32[160,128]{1,0:T(8,128)S(1)}, f32[160,128]{1,0:T(8,128)S(1)}, u32[]{:S(2)}, u32[]{:S(2)}) collective-permute-start(f32[160,128]{1,0:T(8,128)S(1)} %select_add_fusion), channel_id=1, source_target_pairs={{0,2},{1,9},{2,0},{3,11},{4,6},{5,13},{6,4},{7,15},{8,10},{9,1},{1... | collective-permute-start | bytes 245768 | tf_op jit(solution)/shard_map/ppermute | solution.py:802
  42.0 3.0 %collective-permute-done.4 = f32[160,128]{1,0:T(8,128)S(1)} collective-permute-done((f32[160,128]{1,0:T(8,128)S(1)}, f32[160,128]{1,0:T(8,128)S(1)}, u32[]{:S(2)}, u32[]{:S(2)}) %collective-permute-start.4) | collective-permute-done | bytes 81952 | tf_op jit(solution)/shard_map/ppermute | solution.py:802
  45.0 1.5 %collective-permute-start.5 = (f32[160,128]{1,0:T(8,128)S(1)}, f32[160,128]{1,0:T(8,128)S(1)}, u32[]{:S(2)}, u32[]{:S(2)}) collective-permute-start(f32[160,128]{1,0:T(8,128)S(1)} %add.16), channel_id=1, source_target_pairs={{0,4},{1,17},{2,6},{3,19},{4,0},{5,21},{6,2},{7,23},{8,12},{9,25},... | collective-permute-start | bytes 245768 | tf_op jit(solution)/shard_map/ppermute | solution.py:802
  46.5 3.0 %collective-permute-done.5 = f32[160,128]{1,0:T(8,128)S(1)} collective-permute-done((f32[160,128]{1,0:T(8,128)S(1)}, f32[160,128]{1,0:T(8,128)S(1)}, u32[]{:S(2)}, u32[]{:S(2)}) %collective-permute-start.5) | collective-permute-done | bytes 81952 | tf_op jit(solution)/shard_map/ppermute | solution.py:802
  49.6 1.6 %collective-permute-start.6 = (f32[160,128]{1,0:T(8,128)S(1)}, f32[160,128]{1,0:T(8,128)S(1)}, u32[]{:S(2)}, u32[]{:S(2)}) collective-permute-start(f32[160,128]{1,0:T(8,128)S(1)} %add.17), channel_id=1, source_target_pairs={{0,8},{1,3},{2,10},{3,1},{4,12},{5,7},{6,14},{7,5},{8,0},{9,11},{1... | collective-permute-start | bytes 245768 | tf_op jit(solution)/shard_map/ppermute | solution.py:802
  51.1 2.9 %collective-permute-done.6 = f32[160,128]{1,0:T(8,128)S(1)} collective-permute-done((f32[160,128]{1,0:T(8,128)S(1)}, f32[160,128]{1,0:T(8,128)S(1)}, u32[]{:S(2)}, u32[]{:S(2)}) %collective-permute-start.6) | collective-permute-done | bytes 81952 | tf_op jit(solution)/shard_map/ppermute | solution.py:802
  54.1 2.8 %collective-permute-start.7 = (f32[160,128]{1,0:T(8,128)S(1)}, f32[160,128]{1,0:T(8,128)S(1)}, u32[]{:S(2)}, u32[]{:S(2)}) collective-permute-start(f32[160,128]{1,0:T(8,128)S(1)} %add.18), channel_id=1, source_target_pairs={{0,16},{1,5},{2,18},{3,7},{4,20},{5,1},{6,22},{7,3},{8,24},{9,13},... | collective-permute-start | bytes 245768 | tf_op jit(solution)/shard_map/ppermute | solution.py:802
  56.9 2.6 %collective-permute-done.7 = f32[160,128]{1,0:T(8,128)S(1)} collective-permute-done((f32[160,128]{1,0:T(8,128)S(1)}, f32[160,128]{1,0:T(8,128)S(1)}, u32[]{:S(2)}, u32[]{:S(2)}) %collective-permute-start.7) | collective-permute-done | bytes 81952 | tf_op jit(solution)/shard_map/ppermute | solution.py:802
  59.5 0.1 collective-permute-start.8
  59.6 0.7 %copy.11 = f32[2,256,128]{2,1,0:T(8,128)} copy(f32[2,256,128]{2,1,0:T(8,128)S(1)} %bitcast.6) | data formatting | bytes 524288
  60.3 0.6 collective-permute-done.8.other_ref
  60.8 0.8 %shard_map.113 = (f32[128,128]{1,0:T(8,128)}, f32[256,128]{1,0:T(8,128)}) custom-call(f32[160,128]{1,0:T(8,128)S(1)} %add.19.mine_ref, f32[160,128]{1,0:T(8,128)S(1)} %collective-permute-done.8.other_ref), custom_call_target="tpu_custom_call" | custom-call | bytes 1048576 | tf_op jit(solution)/shard_map/pallas_call | solution.py:640
  (6 shorter events, 0.1 us)
Async XLA Ops:
  13.8 8.1 %collective-permute-start = (f32[2,200,128]{2,1,0:T(8,128)S(1)}, f32[2,200,128]{2,1,0:T(8,128)S(1)}, u32[]{:S(2)}, u32[]{:S(2)}) collective-permute-start(f32[2,200,128]{2,1,0:T(8,128)S(1)} %get-tuple-element.39.mine_ref.refs_0_), channel_id=1, source_target_pairs={{0,4},{4,0},{8,12},{12,8},{16,20},{20,16},{24,28},{28,24},{1,5},{5... | collective-permute-start | bytes 614408 | tf_op jit(solution)/shard_map/ppermute | solution.py:646
  22.7 6.3 %collective-permute-start.1 = (f32[2,200,128]{2,1,0:T(8,128)S(1)}, f32[2,200,128]{2,1,0:T(8,128)S(1)}, u32[]{:S(2)}, u32[]{:S(2)}) collective-permute-start(f32[2,200,128]{2,1,0:T(8,128)S(1)} %shard_map.105._.mine_ref.refs_1_), channel_id=1, source_target_pairs={{0,8},{4,12},{8,0},{12,4},{16,24},{20,28},{24,16},{28,20},{1,9},{5... | collective-permute-start | bytes 614408 | tf_op jit(solution)/shard_map/ppermute | solution.py:646
  29.9 5.3 %copy-start = (f32[32,128,128]{2,1,0:T(8,128)S(1)}, f32[32,128,128]{2,1,0:T(8,128)}, u32[]{:S(2)}) copy-start(f32[32,128,128]{2,1,0:T(8,128)} %get-tuple-element.49.refs_4_) | copy-start | bytes 6291460
  29.9 5.3 %copy-start.2 = (f32[512,128]{1,0:T(8,128)S(1)}, f32[512,128]{1,0:T(8,128)}, u32[]{:S(2)}) copy-start(f32[512,128]{1,0:T(8,128)} %get-tuple-element.59.refs_14_.gain_ref) | copy-start | bytes 786436
  30.0 5.3 %collective-permute-start.2 = (f32[2,72,128]{2,1,0:T(8,128)S(1)}, f32[2,72,128]{2,1,0:T(8,128)S(1)}, u32[]{:S(2)}, u32[]{:S(2)}) collective-permute-start(f32[2,72,128]{2,1,0:T(8,128)S(1)} %shard_map.108.mine_ref), channel_id=1, source_target_pairs={{0,16},{4,20},{8,24},{12,28},{16,0},{20,4},{24,8},{28,12},{1,17},{... | collective-permute-start | bytes 221192 | tf_op jit(solution)/shard_map/ppermute | solution.py:646
  35.3 1.3 %copy-start.1 = (f32[2,256,128]{2,1,0:T(8,128)S(1)}, f32[2,256,128]{2,1,0:T(8,128)}, u32[]{:S(2)}) copy-start(f32[2,256,128]{2,1,0:T(8,128)} %param.9) | copy-start | bytes 786436
  35.3 1.3 %copy-start.3 = (f32[512,128]{1,0:T(8,128)S(1)}, f32[512,128]{1,0:T(8,128)}, u32[]{:S(2)}) copy-start(f32[512,128]{1,0:T(8,128)} %get-tuple-element.65.resid_ref) | copy-start | bytes 786436
  39.1 1.3 %collective-permute-start.3 = (f32[160,128]{1,0:T(8,128)S(1)}, f32[160,128]{1,0:T(8,128)S(1)}, u32[]{:S(2)}, u32[]{:S(2)}) collective-permute-start(f32[160,128]{1,0:T(8,128)S(1)} %slice_select_fusion), channel_id=1, source_target_pairs={{0,1},{1,0},{2,3},{3,2},{4,5},{5,4},{6,7},{7,6},{8,9},{9,8},{10,11... | collective-permute-start | bytes 245768 | tf_op jit(solution)/shard_map/ppermute | solution.py:646
  40.5 4.5 %collective-permute-start.4 = (f32[160,128]{1,0:T(8,128)S(1)}, f32[160,128]{1,0:T(8,128)S(1)}, u32[]{:S(2)}, u32[]{:S(2)}) collective-permute-start(f32[160,128]{1,0:T(8,128)S(1)} %select_add_fusion), channel_id=1, source_target_pairs={{0,2},{1,9},{2,0},{3,11},{4,6},{5,13},{6,4},{7,15},{8,10},{9,1},{1... | collective-permute-start | bytes 245768 | tf_op jit(solution)/shard_map/ppermute | solution.py:802
  45.0 4.5 %collective-permute-start.5 = (f32[160,128]{1,0:T(8,128)S(1)}, f32[160,128]{1,0:T(8,128)S(1)}, u32[]{:S(2)}, u32[]{:S(2)}) collective-permute-start(f32[160,128]{1,0:T(8,128)S(1)} %add.16), channel_id=1, source_target_pairs={{0,4},{1,17},{2,6},{3,19},{4,0},{5,21},{6,2},{7,23},{8,12},{9,25},... | collective-permute-start | bytes 245768 | tf_op jit(solution)/shard_map/ppermute | solution.py:802
  49.6 4.5 %collective-permute-start.6 = (f32[160,128]{1,0:T(8,128)S(1)}, f32[160,128]{1,0:T(8,128)S(1)}, u32[]{:S(2)}, u32[]{:S(2)}) collective-permute-start(f32[160,128]{1,0:T(8,128)S(1)} %add.17), channel_id=1, source_target_pairs={{0,8},{1,3},{2,10},{3,1},{4,12},{5,7},{6,14},{7,5},{8,0},{9,11},{1... | collective-permute-start | bytes 245768 | tf_op jit(solution)/shard_map/ppermute | solution.py:802
  54.1 5.4 %collective-permute-start.7 = (f32[160,128]{1,0:T(8,128)S(1)}, f32[160,128]{1,0:T(8,128)S(1)}, u32[]{:S(2)}, u32[]{:S(2)}) collective-permute-start(f32[160,128]{1,0:T(8,128)S(1)} %add.18), channel_id=1, source_target_pairs={{0,16},{1,5},{2,18},{3,7},{4,20},{5,1},{6,22},{7,3},{8,24},{9,13},... | collective-permute-start | bytes 245768 | tf_op jit(solution)/shard_map/ppermute | solution.py:802
  59.5 1.3 %collective-permute-start.8 = (f32[160,128]{1,0:T(8,128)S(1)}, f32[160,128]{1,0:T(8,128)S(1)}, u32[]{:S(2)}, u32[]{:S(2)}) collective-permute-start(f32[160,128]{1,0:T(8,128)S(1)} %add.19.mine_ref), channel_id=1, source_target_pairs={{0,1},{1,0},{2,3},{3,2},{4,5},{5,4},{6,7},{7,6},{8,9},{9,8},{10,11... | collective-permute-start | bytes 245768 | tf_op jit(solution)/shard_map/ppermute | solution.py:646

commit v8 on v7

--- a/solution.py
+++ b/solution.py
@@ -793,13 +793,26 @@
     kept = kept + swapped(given, "batch", 1)
     width = lax.axis_size("batch")
     hops = [(0, 1 << k) for k in range(1, levels_of("batch"))] + [(1 << k, 0) for k in range(levels)]
-    for stage in range(len(hops)):
+
+    def moved(value, hop_of):
         route = []
         for i in range(lax.axis_size("seq")):
             for j in range(width):
-                along_seq, along_batch = hops[(stage + (j & 1) * (len(hops) // 2)) % len(hops)]
+                along_seq, along_batch = hop_of(j & 1)
                 route.append((i * width + j, (i ^ along_seq) * width + (j ^ along_batch)))
-        kept = kept + lax.ppermute(kept, ("seq", "batch"), route)
+        return lax.ppermute(value, ("seq", "batch"), route)
+
+    fours = []
+    for one, two in zip(hops[::2], hops[1::2]):
+        fours.append([one, two, (one[0] ^ two[0], one[1] ^ two[1])])
+    for stage in range(len(fours)):
+        parts = []
+        for which in range(3):
+            turn = lambda odd: fours[(stage + odd * (len(fours) // 2)) % len(fours)][which]
+            parts.append(moved(kept, turn))
+        kept = (kept + parts[0]) + (parts[1] + parts[2])
+    if len(hops) % 2:
+        kept = kept + moved(kept, lambda odd: hops[-1])
     grad_recur, grad_in = call(
         finish_kernel,
         [(hidden, hidden), (features, hidden)],

time: 61.8 us -> 62.4 us (level)
  starting transfers between devices: 15 us -> 16.1 us
    ppermute x4 -> x6, starting transfers between devices: 7.38 us -> 8.46 us  [moved(): return lax.ppermute(value, ('seq', 'batch'), route)]
    ppermute x4 -> x6, waiting for transfers between devices: 11.5 us -> 11 us  [moved(): return lax.ppermute(value, ('seq', 'batch'), route)]
  transfers between devices with their start and end apart: 9 -> 11, of which waited for: 9 -> 10; matrix products, arithmetic and copies ran while one was open for 1% -> 1% of each run, Pallas kernels for 16% -> 15%
where the time goes in v8:
time: 62.4 us; the launch traced here: 62.2 us
  Pallas kernels  29.1 us (47%)
  starting transfers between devices  16.1 us (26%)
  waiting for transfers between devices  15.5 us (25%)
  between operations  0.79 us (1%)
  local copies, waits for them, and re-layouts  0.72 us (1%)
    pallas_call x11, Pallas kernels, pinned(): return run(*placed)  29.1 us
    ppermute x6, waiting for transfers between devices, moved(): return lax.ppermute(value, ('seq', 'batch'), route)  11 us
    ppermute x6, starting transfers between devices, moved(): return lax.ppermute(value, ('seq', 'batch'), route)  8.46 us
    ppermute x5, starting transfers between devices, swapped(): lax.ppermute(value, axis, [(i, i ^ distance) for i in range(lax.axis_size...  7.62 us
    ppermute x5, waiting for transfers between devices, swapped(): lax.ppermute(value, axis, [(i, i ^ distance) for i in range(lax.axis_size...  4.43 us
  transfers between devices with their start and end apart: 11, of which 10 were waited for; matrix products, arithmetic and copies ran while one was open for 1% of the time, Pallas kernels for 15%

profile of v8, /device:TPU:0, one launch (start us, length us, event | category | flops | bytes accessed | tf_op | source)
XLA Modules:
  0.0 62.2 jit_solution(16701423333983044385)
XLA Ops:
  0.6 13.1 %shard_map.103 = (f32[2,200,128]{2,1,0:T(8,128)S(1)}, f32[32,128,128]{2,1,0:T(8,128)S(1)}, f32[32,128,128]{2,1,0:T(8,128)}, f32[32,128]{1,0:T(8,128)S(1)}, f32[4...) custom-call(s32[2,2]{1,0:T(2,128)} %steps_in.7, ...), custom_call_target="tpu_custom_call" | custom-call | bytes 1048576 | tf_op jit(solution)/shard_map/pallas_call | solution.py:640
  13.8 3.0 %collective-permute-start = (f32[2,200,128]{2,1,0:T(8,128)S(1)}, f32[2,200,128]{2,1,0:T(8,128)S(1)}, u32[]{:S(2)}, u32[]{:S(2)}) collective-permute-start(f32[2,200,128]{2,1,0:T(8,128)S(1)} %get-tuple-element.39.mine_ref.refs_0_), channel_id=1, source_target_pairs={{0,4},{4,0},{8,12},{12,8},{16,20},{20,16},{24,28},{28,24},{1,5},{5... | collective-permute-start | bytes 614408 | tf_op jit(solution)/shard_map/ppermute | solution.py:646
  16.8 3.1 %shard_map.104 = (f32[16,128,128]{2,1,0:T(8,128)S(1)}, f32[2,16,128,128]{3,2,1,0:T(8,128)S(1)}, f32[8,128]{1,0:T(8,128)S(1)}) custom-call(s32[2,2]{1,0:T(2,128)} %steps_in.7, f32[4,128,128]{2,1,0:T(8,128)} %get-tuple-element.40.hit_in, f32[32,128,128]{2,1,0:T(8,128)S(1)} %get-tuple-element.41.maps_ref, f32[128,128]{1,0:T(8,128)S(1)} %get-tuple-element.38._.drift_ref), custom_call_target="tpu_custom_call" | custom-call | flops 4294967296 | bytes 1048576 | tf_op jit(solution)/shard_map/pallas_call | solution.py:640
  19.9 2.0 %collective-permute-done.other_ref.refs_2_ = f32[2,200,128]{2,1,0:T(8,128)S(1)} collective-permute-done((f32[2,200,128]{2,1,0:T(8,128)S(1)}, f32[2,200,128]{2,1,0:T(8,128)S(1)}, u32[]{:S(2)}, u32[]{:S(2)}) %collective-permute-start) | collective-permute-done | bytes 204832 | tf_op jit(solution)/shard_map/ppermute | solution.py:646
  21.9 0.9 %shard_map.105._.mine_ref.refs_1_ = f32[2,200,128]{2,1,0:T(8,128)S(1)} custom-call(f32[128,128]{1,0:T(8,128)S(1)} %get-tuple-element.38._.drift_ref, f32[2,200,128]{2,1,0:T(8,128)S(1)} %get-tuple-element.39.mine_ref.refs_0_, f32[2,200,128]{2,1,0:T(8,128)S(1)} %collective-permute-done.other_ref.refs_2_, f32[8,128]{1,0:T(8,128)S(1)} %get-tuple-element.42._), custom_call_target="tpu_custom_call" | custom-call | bytes 1048576 | tf_op jit(solution)/shard_map/pallas_call | solution.py:640
  22.7 1.9 %collective-permute-start.1 = (f32[2,200,128]{2,1,0:T(8,128)S(1)}, f32[2,200,128]{2,1,0:T(8,128)S(1)}, u32[]{:S(2)}, u32[]{:S(2)}) collective-permute-start(f32[2,200,128]{2,1,0:T(8,128)S(1)} %shard_map.105._.mine_ref.refs_1_), channel_id=1, source_target_pairs={{0,8},{4,12},{8,0},{12,4},{16,24},{20,28},{24,16},{28,20},{1,9},{5... | collective-permute-start | bytes 614408 | tf_op jit(solution)/shard_map/ppermute | solution.py:646
  24.6 2.9 %shard_map.106 = (f32[16,128,128]{2,1,0:T(8,128)S(1)}, f32[2,16,128,128]{3,2,1,0:T(8,128)S(1)}, f32[8,128]{1,0:T(8,128)S(1)}) custom-call(s32[2,2]{1,0:T(2,128)} %steps_in.7, f32[4,128,128]{2,1,0:T(8,128)} %get-tuple-element.40.hit_in, f32[32,128,128]{2,1,0:T(8,128)S(1)} %get-tuple-element.41.maps_ref, f32[2,200,128]{2,1,0:T(8,128)S(1)} %shard_map.105._.mine_ref.refs_1_), custom_call_target="tpu_custom_call" | custom-call | flops 4294967296 | bytes 1048576 | tf_op jit(solution)/shard_map/pallas_call | solution.py:640
  27.6 1.4 %shard_map.107 = (bf16[384,512]{1,0:T(8,128)(2,1)S(1)}, bf16[384,512]{1,0:T(8,128)(2,1)S(1)}, f32[512,128]{1,0:T(8,128)S(1)}, f32[8,128]{1,0:T(8,128)S(1)}) custom-call(s32[2,2]{1,0:T(2,128)} %steps_in.7, f32[512,256]{1,0:T(8,128)} %bitcast.11, f32[512,128]{1,0:T(8,128)} %bitcast.8, f32[8,128]{1,0:T(8,128)S(1)} %get-tuple-element.43._), custom_call_target="tpu_custom_call" | custom-call | flops 2147483648 | bytes 1048576 | tf_op jit(solution)/shard_map/pallas_call | solution.py:640
  29.0 0.1 collective-permute-done.1.other_ref.refs_3_
  29.1 0.9 %shard_map.108.mine_ref = f32[2,72,128]{2,1,0:T(8,128)S(1)} custom-call(f32[128,128]{1,0:T(8,128)S(1)} %get-tuple-element.38._.drift_ref, f32[2,200,128]{2,1,0:T(8,128)S(1)} %shard_map.105._.mine_ref.refs_1_, f32[2,200,128]{2,1,0:T(8,128)S(1)} %collective-permute-done.1.other_ref.refs_3_, f32[8,128]{1,0:T(8,128)S(1)} %get-tuple-element.44._), custom_call_target="tpu_custom_call" | custom-call | bytes 1048576 | tf_op jit(solution)/shard_map/pallas_call | solution.py:640
  29.9 0.0 copy-start
  29.9 0.0 copy-start.2
  29.9 2.6 %collective-permute-start.2 = (f32[2,72,128]{2,1,0:T(8,128)S(1)}, f32[2,72,128]{2,1,0:T(8,128)S(1)}, u32[]{:S(2)}, u32[]{:S(2)}) collective-permute-start(f32[2,72,128]{2,1,0:T(8,128)S(1)} %shard_map.108.mine_ref), channel_id=1, source_target_pairs={{0,16},{4,20},{8,24},{12,28},{16,0},{20,4},{24,8},{28,12},{1,17},{... | collective-permute-start | bytes 221192 | tf_op jit(solution)/shard_map/ppermute | solution.py:646
  32.5 2.2 %shard_map.109 = (f32[2,128,128]{2,1,0:T(8,128)S(1)}, f32[2,128,128]{2,1,0:T(8,128)S(1)}, f32[2,128,128]{2,1,0:T(8,128)S(1)}, f32[16,128]{1,0:T(8,128)S(1)}) custom-call(f32[128,128]{1,0:T(8,128)S(1)} %get-tuple-element.38._.drift_ref, f32[2,200,128]{2,1,0:T(8,128)S(1)} %get-tuple-element.39.mine_ref.refs_0_, ...), custom_call_target="tpu_custom_call" | custom-call | flops 1073741824 | bytes 1048576 | tf_op jit(solution)/shard_map/pallas_call | solution.py:640
  34.7 0.5 collective-permute-done.2.other_ref
  35.3 0.0 copy-done
  35.3 0.0 copy-done.2
  35.3 0.0 copy-start.1
  35.3 0.0 copy-start.3
  35.3 1.3 %shard_map.110 = (f32[32,128]{1,0:T(8,128)S(1)}, f32[32,128]{1,0:T(8,128)S(1)}, f32[512,128]{1,0:T(8,128)S(1)}, f32[512,128]{1,0:T(8,128)S(1)}, f32[2,128]{1,0:T(2,128)S(1)}) custom-call(f32[128,128]{1,0:T(8,128)S(1)} %get-tuple-element.38._.drift_ref, f32[2,72,128]{2,1,0:T(8,128)S(1)} %shard_map.108.mine_ref, ...), custom_call_target="tpu_custom_call" | custom-call | bytes 1048576 | tf_op jit(solution)/shard_map/pallas_call | solution.py:640
  36.6 0.0 copy-done.1
  36.6 0.0 copy-done.3
  36.6 2.0 %shard_map.111 = (f32[512,128]{1,0:T(8,128)S(1)}, f32[512,128]{1,0:T(8,128)S(1)}) custom-call(f32[128,128]{1,0:T(8,128)S(1)} %get-tuple-element.38._.drift_ref, f32[32,128]{1,0:T(8,128)S(1)} %get-tuple-element.61.state_ref, f32[32,128]{1,0:T(8,128)S(1)} %get-tuple-element.62.carry_ref, f32[512,128]{1,0:T(8,128)S(1)} %get-tuple-element.63.source_ref, ...), custom_call_target="tpu_custom_call" | custom-call | bytes 1048576 | tf_op jit(solution)/shard_map/pallas_call | solution.py:640
  38.6 0.5 shard_map.112
  39.1 0.1 collective-permute-start.3
  39.2 1.3 %collective-permute-done.3 = f32[160,128]{1,0:T(8,128)S(1)} collective-permute-done((f32[160,128]{1,0:T(8,128)S(1)}, f32[160,128]{1,0:T(8,128)S(1)}, u32[]{:S(2)}, u32[]{:S(2)}) %collective-permute-start.3) | collective-permute-done | bytes 81952 | tf_op jit(solution)/shard_map/ppermute | solution.py:646
  40.5 1.5 %collective-permute-start.4 = (f32[160,128]{1,0:T(8,128)S(1)}, f32[160,128]{1,0:T(8,128)S(1)}, u32[]{:S(2)}, u32[]{:S(2)}) collective-permute-start(f32[160,128]{1,0:T(8,128)S(1)} %select_add_fusion), channel_id=1, source_target_pairs={{0,2},{1,9},{2,0},{3,11},{4,6},{5,13},{6,4},{7,15},{8,10},{9,1},{1... | collective-permute-start | bytes 245768 | tf_op jit(solution)/shard_map/ppermute | solution.py:803
  42.0 1.5 %collective-permute-start.5 = (f32[160,128]{1,0:T(8,128)S(1)}, f32[160,128]{1,0:T(8,128)S(1)}, u32[]{:S(2)}, u32[]{:S(2)}) collective-permute-start(f32[160,128]{1,0:T(8,128)S(1)} %select_add_fusion), channel_id=1, source_target_pairs={{0,4},{1,17},{2,6},{3,19},{4,0},{5,21},{6,2},{7,23},{8,12},{9,25},... | collective-permute-start | bytes 245768 | tf_op jit(solution)/shard_map/ppermute | solution.py:803
  43.5 0.5 collective-permute-start.6
  44.1 1.0 %collective-permute-done.4 = f32[160,128]{1,0:T(8,128)S(1)} collective-permute-done((f32[160,128]{1,0:T(8,128)S(1)}, f32[160,128]{1,0:T(8,128)S(1)}, u32[]{:S(2)}, u32[]{:S(2)}) %collective-permute-start.4) | collective-permute-done | bytes 81952 | tf_op jit(solution)/shard_map/ppermute | solution.py:803
  45.0 1.5 %collective-permute-done.5 = f32[160,128]{1,0:T(8,128)S(1)} collective-permute-done((f32[160,128]{1,0:T(8,128)S(1)}, f32[160,128]{1,0:T(8,128)S(1)}, u32[]{:S(2)}, u32[]{:S(2)}) %collective-permute-start.5) | collective-permute-done | bytes 81952 | tf_op jit(solution)/shard_map/ppermute | solution.py:803
  46.5 2.4 %collective-permute-done.6 = f32[160,128]{1,0:T(8,128)S(1)} collective-permute-done((f32[160,128]{1,0:T(8,128)S(1)}, f32[160,128]{1,0:T(8,128)S(1)}, u32[]{:S(2)}, u32[]{:S(2)}) %collective-permute-start.6) | collective-permute-done | bytes 81952 | tf_op jit(solution)/shard_map/ppermute | solution.py:803
  48.9 1.6 %collective-permute-start.7 = (f32[160,128]{1,0:T(8,128)S(1)}, f32[160,128]{1,0:T(8,128)S(1)}, u32[]{:S(2)}, u32[]{:S(2)}) collective-permute-start(f32[160,128]{1,0:T(8,128)S(1)} %add_add_fusion.1), channel_id=1, source_target_pairs={{0,8},{1,3},{2,10},{3,1},{4,12},{5,7},{6,14},{7,5},{8,0},{9,11},{1... | collective-permute-start | bytes 245768 | tf_op jit(solution)/shard_map/ppermute | solution.py:803
  50.5 3.3 %collective-permute-start.8 = (f32[160,128]{1,0:T(8,128)S(1)}, f32[160,128]{1,0:T(8,128)S(1)}, u32[]{:S(2)}, u32[]{:S(2)}) collective-permute-start(f32[160,128]{1,0:T(8,128)S(1)} %add_add_fusion.1), channel_id=1, source_target_pairs={{0,16},{1,5},{2,18},{3,7},{4,20},{5,1},{6,22},{7,3},{8,24},{9,13},... | collective-permute-start | bytes 245768 | tf_op jit(solution)/shard_map/ppermute | solution.py:803
  53.8 0.0 collective-permute-start.9
  53.8 0.0 collective-permute-done.7
  53.8 3.3 %collective-permute-done.8 = f32[160,128]{1,0:T(8,128)S(1)} collective-permute-done((f32[160,128]{1,0:T(8,128)S(1)}, f32[160,128]{1,0:T(8,128)S(1)}, u32[]{:S(2)}, u32[]{:S(2)}) %collective-permute-start.8) | collective-permute-done | bytes 81952 | tf_op jit(solution)/shard_map/ppermute | solution.py:803
  57.1 2.9 %collective-permute-done.9 = f32[160,128]{1,0:T(8,128)S(1)} collective-permute-done((f32[160,128]{1,0:T(8,128)S(1)}, f32[160,128]{1,0:T(8,128)S(1)}, u32[]{:S(2)}, u32[]{:S(2)}) %collective-permute-start.9) | collective-permute-done | bytes 81952 | tf_op jit(solution)/shard_map/ppermute | solution.py:803
  60.0 0.1 collective-permute-start.10
  60.1 0.7 %copy.11 = f32[2,256,128]{2,1,0:T(8,128)} copy(f32[2,256,128]{2,1,0:T(8,128)S(1)} %bitcast.6) | data formatting | bytes 524288
  60.8 0.6 collective-permute-done.10.other_ref
  61.4 0.8 %shard_map.113 = (f32[128,128]{1,0:T(8,128)}, f32[256,128]{1,0:T(8,128)}) custom-call(f32[160,128]{1,0:T(8,128)S(1)} %add_add_fusion.mine_ref, f32[160,128]{1,0:T(8,128)S(1)} %collective-permute-done.10.other_ref), custom_call_target="tpu_custom_call" | custom-call | bytes 1048576 | tf_op jit(solution)/shard_map/pallas_call | solution.py:640
  (4 shorter events, 0.1 us)
Async XLA Ops:
  13.8 8.1 %collective-permute-start = (f32[2,200,128]{2,1,0:T(8,128)S(1)}, f32[2,200,128]{2,1,0:T(8,128)S(1)}, u32[]{:S(2)}, u32[]{:S(2)}) collective-permute-start(f32[2,200,128]{2,1,0:T(8,128)S(1)} %get-tuple-element.39.mine_ref.refs_0_), channel_id=1, source_target_pairs={{0,4},{4,0},{8,12},{12,8},{16,20},{20,16},{24,28},{28,24},{1,5},{5... | collective-permute-start | bytes 614408 | tf_op jit(solution)/shard_map/ppermute | solution.py:646
  22.7 6.3 %collective-permute-start.1 = (f32[2,200,128]{2,1,0:T(8,128)S(1)}, f32[2,200,128]{2,1,0:T(8,128)S(1)}, u32[]{:S(2)}, u32[]{:S(2)}) collective-permute-start(f32[2,200,128]{2,1,0:T(8,128)S(1)} %shard_map.105._.mine_ref.refs_1_), channel_id=1, source_target_pairs={{0,8},{4,12},{8,0},{12,4},{16,24},{20,28},{24,16},{28,20},{1,9},{5... | collective-permute-start | bytes 614408 | tf_op jit(solution)/shard_map/ppermute | solution.py:646
  29.9 5.3 %copy-start = (f32[32,128,128]{2,1,0:T(8,128)S(1)}, f32[32,128,128]{2,1,0:T(8,128)}, u32[]{:S(2)}) copy-start(f32[32,128,128]{2,1,0:T(8,128)} %get-tuple-element.49.refs_4_) | copy-start | bytes 6291460
  29.9 5.3 %copy-start.2 = (f32[512,128]{1,0:T(8,128)S(1)}, f32[512,128]{1,0:T(8,128)}, u32[]{:S(2)}) copy-start(f32[512,128]{1,0:T(8,128)} %get-tuple-element.59.refs_14_.gain_ref) | copy-start | bytes 786436
  29.9 5.3 %collective-permute-start.2 = (f32[2,72,128]{2,1,0:T(8,128)S(1)}, f32[2,72,128]{2,1,0:T(8,128)S(1)}, u32[]{:S(2)}, u32[]{:S(2)}) collective-permute-start(f32[2,72,128]{2,1,0:T(8,128)S(1)} %shard_map.108.mine_ref), channel_id=1, source_target_pairs={{0,16},{4,20},{8,24},{12,28},{16,0},{20,4},{24,8},{28,12},{1,17},{... | collective-permute-start | bytes 221192 | tf_op jit(solution)/shard_map/ppermute | solution.py:646
  35.3 1.3 %copy-start.1 = (f32[2,256,128]{2,1,0:T(8,128)S(1)}, f32[2,256,128]{2,1,0:T(8,128)}, u32[]{:S(2)}) copy-start(f32[2,256,128]{2,1,0:T(8,128)} %param.9) | copy-start | bytes 786436
  35.3 1.3 %copy-start.3 = (f32[512,128]{1,0:T(8,128)S(1)}, f32[512,128]{1,0:T(8,128)}, u32[]{:S(2)}) copy-start(f32[512,128]{1,0:T(8,128)} %get-tuple-element.65.resid_ref) | copy-start | bytes 786436
  39.1 1.3 %collective-permute-start.3 = (f32[160,128]{1,0:T(8,128)S(1)}, f32[160,128]{1,0:T(8,128)S(1)}, u32[]{:S(2)}, u32[]{:S(2)}) collective-permute-start(f32[160,128]{1,0:T(8,128)S(1)} %slice_select_fusion), channel_id=1, source_target_pairs={{0,1},{1,0},{2,3},{3,2},{4,5},{5,4},{6,7},{7,6},{8,9},{9,8},{10,11... | collective-permute-start | bytes 245768 | tf_op jit(solution)/shard_map/ppermute | solution.py:646
  40.5 4.5 %collective-permute-start.4 = (f32[160,128]{1,0:T(8,128)S(1)}, f32[160,128]{1,0:T(8,128)S(1)}, u32[]{:S(2)}, u32[]{:S(2)}) collective-permute-start(f32[160,128]{1,0:T(8,128)S(1)} %select_add_fusion), channel_id=1, source_target_pairs={{0,2},{1,9},{2,0},{3,11},{4,6},{5,13},{6,4},{7,15},{8,10},{9,1},{1... | collective-permute-start | bytes 245768 | tf_op jit(solution)/shard_map/ppermute | solution.py:803
  42.0 4.4 %collective-permute-start.5 = (f32[160,128]{1,0:T(8,128)S(1)}, f32[160,128]{1,0:T(8,128)S(1)}, u32[]{:S(2)}, u32[]{:S(2)}) collective-permute-start(f32[160,128]{1,0:T(8,128)S(1)} %select_add_fusion), channel_id=1, source_target_pairs={{0,4},{1,17},{2,6},{3,19},{4,0},{5,21},{6,2},{7,23},{8,12},{9,25},... | collective-permute-start | bytes 245768 | tf_op jit(solution)/shard_map/ppermute | solution.py:803
  43.5 5.3 %collective-permute-start.6 = (f32[160,128]{1,0:T(8,128)S(1)}, f32[160,128]{1,0:T(8,128)S(1)}, u32[]{:S(2)}, u32[]{:S(2)}) collective-permute-start(f32[160,128]{1,0:T(8,128)S(1)} %select_add_fusion), channel_id=1, source_target_pairs={{0,6},{1,25},{2,4},{3,27},{4,2},{5,29},{6,0},{7,31},{8,14},{9,17},... | collective-permute-start | bytes 245768 | tf_op jit(solution)/shard_map/ppermute | solution.py:803
  48.9 4.9 %collective-permute-start.7 = (f32[160,128]{1,0:T(8,128)S(1)}, f32[160,128]{1,0:T(8,128)S(1)}, u32[]{:S(2)}, u32[]{:S(2)}) collective-permute-start(f32[160,128]{1,0:T(8,128)S(1)} %add_add_fusion.1), channel_id=1, source_target_pairs={{0,8},{1,3},{2,10},{3,1},{4,12},{5,7},{6,14},{7,5},{8,0},{9,11},{1... | collective-permute-start | bytes 245768 | tf_op jit(solution)/shard_map/ppermute | solution.py:803
  50.5 6.6 %collective-permute-start.8 = (f32[160,128]{1,0:T(8,128)S(1)}, f32[160,128]{1,0:T(8,128)S(1)}, u32[]{:S(2)}, u32[]{:S(2)}) collective-permute-start(f32[160,128]{1,0:T(8,128)S(1)} %add_add_fusion.1), channel_id=1, source_target_pairs={{0,16},{1,5},{2,18},{3,7},{4,20},{5,1},{6,22},{7,3},{8,24},{9,13},... | collective-permute-start | bytes 245768 | tf_op jit(solution)/shard_map/ppermute | solution.py:803
  53.8 6.2 %collective-permute-start.9 = (f32[160,128]{1,0:T(8,128)S(1)}, f32[160,128]{1,0:T(8,128)S(1)}, u32[]{:S(2)}, u32[]{:S(2)}) collective-permute-start(f32[160,128]{1,0:T(8,128)S(1)} %add_add_fusion.1), channel_id=1, source_target_pairs={{0,24},{1,7},{2,26},{3,5},{4,28},{5,3},{6,30},{7,1},{8,16},{9,15},... | collective-permute-start | bytes 245768 | tf_op jit(solution)/shard_map/ppermute | solution.py:803
  60.0 1.3 %collective-permute-start.10 = (f32[160,128]{1,0:T(8,128)S(1)}, f32[160,128]{1,0:T(8,128)S(1)}, u32[]{:S(2)}, u32[]{:S(2)}) collective-permute-start(f32[160,128]{1,0:T(8,128)S(1)} %add_add_fusion.mine_ref), channel_id=1, source_target_pairs={{0,1},{1,0},{2,3},{3,2},{4,5},{5,4},{6,7},{7,6},{8,9},{9,8},{10,11... | collective-permute-start | bytes 245768 | tf_op jit(solution)/shard_map/ppermute | solution.py:646

commit v9 on v7

--- a/solution.py
+++ b/solution.py
@@ -793,13 +793,23 @@
     kept = kept + swapped(given, "batch", 1)
     width = lax.axis_size("batch")
     hops = [(0, 1 << k) for k in range(1, levels_of("batch"))] + [(1 << k, 0) for k in range(levels)]
-    for stage in range(len(hops)):
+
+    def moved(value, hop_of):
         route = []
         for i in range(lax.axis_size("seq")):
             for j in range(width):
-                along_seq, along_batch = hops[(stage + (j & 1) * (len(hops) // 2)) % len(hops)]
+                along_seq, along_batch = hop_of(j & 1)
                 route.append((i * width + j, (i ^ along_seq) * width + (j ^ along_batch)))
-        kept = kept + lax.ppermute(kept, ("seq", "batch"), route)
+        return lax.ppermute(value, ("seq", "batch"), route)
+
+    one, two = hops[:2]
+    near_by = [one, two, (one[0] ^ two[0], one[1] ^ two[1])]
+    parts = [moved(kept, lambda odd: hop) for hop in near_by]
+    kept = (kept + parts[0]) + (parts[1] + parts[2])
+    rest = hops[2:]
+    for stage in range(len(rest)):
+        turn = lambda odd: rest[(stage + odd * (len(rest) // 2)) % len(rest)]
+        kept = kept + moved(kept, turn)
     grad_recur, grad_in = call(
         finish_kernel,
         [(hidden, hidden), (features, hidden)],

time: 61.8 us -> 61.1 us (0.989)
  waiting for transfers between devices: 16 us -> 14.6 us
  starting transfers between devices: 15 us -> 15.7 us
    ppermute x4 -> x5, waiting for transfers between devices: 11.5 us -> 10.2 us  [moved(): return lax.ppermute(value, ('seq', 'batch'), route)]
    ppermute x4 -> x5, starting transfers between devices: 7.38 us -> 8.08 us  [moved(): return lax.ppermute(value, ('seq', 'batch'), route)]
  transfers between devices with their start and end apart: 9 -> 10, of which waited for: 9 -> 10; matrix products, arithmetic and copies ran while one was open for 1% -> 1% of each run, Pallas kernels for 16% -> 16%
where the time goes in v9:
time: 61.1 us; the launch traced here: 61 us
  Pallas kernels  29.1 us (48%)
  starting transfers between devices  15.7 us (26%)
  waiting for transfers between devices  14.6 us (24%)
  between operations  0.79 us (1%)
  local copies, waits for them, and re-layouts  0.72 us (1%)
    pallas_call x11, Pallas kernels, pinned(): return run(*placed)  29.1 us
    ppermute x5, waiting for transfers between devices, moved(): return lax.ppermute(value, ('seq', 'batch'), route)  10.2 us
    ppermute x5, starting transfers between devices, moved(): return lax.ppermute(value, ('seq', 'batch'), route)  8.08 us
    ppermute x5, starting transfers between devices, swapped(): lax.ppermute(value, axis, [(i, i ^ distance) for i in range(lax.axis_size...  7.62 us
    ppermute x5, waiting for transfers between devices, swapped(): lax.ppermute(value, axis, [(i, i ^ distance) for i in range(lax.axis_size...  4.43 us
  transfers between devices with their start and end apart: 10, of which 10 were waited for; matrix products, arithmetic and copies ran while one was open for 1% of the time, Pallas kernels for 16%

profile of v9, /device:TPU:0, one launch (start us, length us, event | category | flops | bytes accessed | tf_op | source)
XLA Modules:
  0.0 61.0 jit_solution(8615366169017405324)
XLA Ops:
  0.6 13.2 %shard_map.103 = (f32[2,200,128]{2,1,0:T(8,128)S(1)}, f32[32,128,128]{2,1,0:T(8,128)S(1)}, f32[32,128,128]{2,1,0:T(8,128)}, f32[32,128]{1,0:T(8,128)S(1)}, f32[4...) custom-call(s32[2,2]{1,0:T(2,128)} %steps_in.7, ...), custom_call_target="tpu_custom_call" | custom-call | bytes 1048576 | tf_op jit(solution)/shard_map/pallas_call | solution.py:640
  13.8 3.0 %collective-permute-start = (f32[2,200,128]{2,1,0:T(8,128)S(1)}, f32[2,200,128]{2,1,0:T(8,128)S(1)}, u32[]{:S(2)}, u32[]{:S(2)}) collective-permute-start(f32[2,200,128]{2,1,0:T(8,128)S(1)} %get-tuple-element.39.mine_ref.refs_0_), channel_id=1, source_target_pairs={{0,4},{4,0},{8,12},{12,8},{16,20},{20,16},{24,28},{28,24},{1,5},{5... | collective-permute-start | bytes 614408 | tf_op jit(solution)/shard_map/ppermute | solution.py:646
  16.8 3.1 %shard_map.104 = (f32[16,128,128]{2,1,0:T(8,128)S(1)}, f32[2,16,128,128]{3,2,1,0:T(8,128)S(1)}, f32[8,128]{1,0:T(8,128)S(1)}) custom-call(s32[2,2]{1,0:T(2,128)} %steps_in.7, f32[4,128,128]{2,1,0:T(8,128)} %get-tuple-element.40.hit_in, f32[32,128,128]{2,1,0:T(8,128)S(1)} %get-tuple-element.41.maps_ref, f32[128,128]{1,0:T(8,128)S(1)} %get-tuple-element.38._.drift_ref), custom_call_target="tpu_custom_call" | custom-call | flops 4294967296 | bytes 1048576 | tf_op jit(solution)/shard_map/pallas_call | solution.py:640
  19.9 2.0 %collective-permute-done.other_ref.refs_2_ = f32[2,200,128]{2,1,0:T(8,128)S(1)} collective-permute-done((f32[2,200,128]{2,1,0:T(8,128)S(1)}, f32[2,200,128]{2,1,0:T(8,128)S(1)}, u32[]{:S(2)}, u32[]{:S(2)}) %collective-permute-start) | collective-permute-done | bytes 204832 | tf_op jit(solution)/shard_map/ppermute | solution.py:646
  21.9 0.9 %shard_map.105._.mine_ref.refs_1_ = f32[2,200,128]{2,1,0:T(8,128)S(1)} custom-call(f32[128,128]{1,0:T(8,128)S(1)} %get-tuple-element.38._.drift_ref, f32[2,200,128]{2,1,0:T(8,128)S(1)} %get-tuple-element.39.mine_ref.refs_0_, f32[2,200,128]{2,1,0:T(8,128)S(1)} %collective-permute-done.other_ref.refs_2_, f32[8,128]{1,0:T(8,128)S(1)} %get-tuple-element.42._), custom_call_target="tpu_custom_call" | custom-call | bytes 1048576 | tf_op jit(solution)/shard_map/pallas_call | solution.py:640
  22.7 1.9 %collective-permute-start.1 = (f32[2,200,128]{2,1,0:T(8,128)S(1)}, f32[2,200,128]{2,1,0:T(8,128)S(1)}, u32[]{:S(2)}, u32[]{:S(2)}) collective-permute-start(f32[2,200,128]{2,1,0:T(8,128)S(1)} %shard_map.105._.mine_ref.refs_1_), channel_id=1, source_target_pairs={{0,8},{4,12},{8,0},{12,4},{16,24},{20,28},{24,16},{28,20},{1,9},{5... | collective-permute-start | bytes 614408 | tf_op jit(solution)/shard_map/ppermute | solution.py:646
  24.6 2.9 %shard_map.106 = (f32[16,128,128]{2,1,0:T(8,128)S(1)}, f32[2,16,128,128]{3,2,1,0:T(8,128)S(1)}, f32[8,128]{1,0:T(8,128)S(1)}) custom-call(s32[2,2]{1,0:T(2,128)} %steps_in.7, f32[4,128,128]{2,1,0:T(8,128)} %get-tuple-element.40.hit_in, f32[32,128,128]{2,1,0:T(8,128)S(1)} %get-tuple-element.41.maps_ref, f32[2,200,128]{2,1,0:T(8,128)S(1)} %shard_map.105._.mine_ref.refs_1_), custom_call_target="tpu_custom_call" | custom-call | flops 4294967296 | bytes 1048576 | tf_op jit(solution)/shard_map/pallas_call | solution.py:640
  27.6 1.4 %shard_map.107 = (bf16[384,512]{1,0:T(8,128)(2,1)S(1)}, bf16[384,512]{1,0:T(8,128)(2,1)S(1)}, f32[512,128]{1,0:T(8,128)S(1)}, f32[8,128]{1,0:T(8,128)S(1)}) custom-call(s32[2,2]{1,0:T(2,128)} %steps_in.7, f32[512,256]{1,0:T(8,128)} %bitcast.11, f32[512,128]{1,0:T(8,128)} %bitcast.8, f32[8,128]{1,0:T(8,128)S(1)} %get-tuple-element.43._), custom_call_target="tpu_custom_call" | custom-call | flops 2147483648 | bytes 1048576 | tf_op jit(solution)/shard_map/pallas_call | solution.py:640
  29.0 0.1 collective-permute-done.1.other_ref.refs_3_
  29.1 0.9 %shard_map.108.mine_ref = f32[2,72,128]{2,1,0:T(8,128)S(1)} custom-call(f32[128,128]{1,0:T(8,128)S(1)} %get-tuple-element.38._.drift_ref, f32[2,200,128]{2,1,0:T(8,128)S(1)} %shard_map.105._.mine_ref.refs_1_, f32[2,200,128]{2,1,0:T(8,128)S(1)} %collective-permute-done.1.other_ref.refs_3_, f32[8,128]{1,0:T(8,128)S(1)} %get-tuple-element.44._), custom_call_target="tpu_custom_call" | custom-call | bytes 1048576 | tf_op jit(solution)/shard_map/pallas_call | solution.py:640
  29.9 0.0 copy-start
  29.9 0.0 copy-start.2
  30.0 2.6 %collective-permute-start.2 = (f32[2,72,128]{2,1,0:T(8,128)S(1)}, f32[2,72,128]{2,1,0:T(8,128)S(1)}, u32[]{:S(2)}, u32[]{:S(2)}) collective-permute-start(f32[2,72,128]{2,1,0:T(8,128)S(1)} %shard_map.108.mine_ref), channel_id=1, source_target_pairs={{0,16},{4,20},{8,24},{12,28},{16,0},{20,4},{24,8},{28,12},{1,17},{... | collective-permute-start | bytes 221192 | tf_op jit(solution)/shard_map/ppermute | solution.py:646
  32.5 2.2 %shard_map.109 = (f32[2,128,128]{2,1,0:T(8,128)S(1)}, f32[2,128,128]{2,1,0:T(8,128)S(1)}, f32[2,128,128]{2,1,0:T(8,128)S(1)}, f32[16,128]{1,0:T(8,128)S(1)}) custom-call(f32[128,128]{1,0:T(8,128)S(1)} %get-tuple-element.38._.drift_ref, f32[2,200,128]{2,1,0:T(8,128)S(1)} %get-tuple-element.39.mine_ref.refs_0_, ...), custom_call_target="tpu_custom_call" | custom-call | flops 1073741824 | bytes 1048576 | tf_op jit(solution)/shard_map/pallas_call | solution.py:640
  34.7 0.5 collective-permute-done.2.other_ref
  35.3 0.0 copy-done
  35.3 0.0 copy-done.2
  35.3 0.0 copy-start.1
  35.3 0.0 copy-start.3
  35.3 1.3 %shard_map.110 = (f32[32,128]{1,0:T(8,128)S(1)}, f32[32,128]{1,0:T(8,128)S(1)}, f32[512,128]{1,0:T(8,128)S(1)}, f32[512,128]{1,0:T(8,128)S(1)}, f32[2,128]{1,0:T(2,128)S(1)}) custom-call(f32[128,128]{1,0:T(8,128)S(1)} %get-tuple-element.38._.drift_ref, f32[2,72,128]{2,1,0:T(8,128)S(1)} %shard_map.108.mine_ref, ...), custom_call_target="tpu_custom_call" | custom-call | bytes 1048576 | tf_op jit(solution)/shard_map/pallas_call | solution.py:640
  36.6 0.0 copy-done.1
  36.6 0.0 copy-done.3
  36.6 2.0 %shard_map.111 = (f32[512,128]{1,0:T(8,128)S(1)}, f32[512,128]{1,0:T(8,128)S(1)}) custom-call(f32[128,128]{1,0:T(8,128)S(1)} %get-tuple-element.38._.drift_ref, f32[32,128]{1,0:T(8,128)S(1)} %get-tuple-element.61.state_ref, f32[32,128]{1,0:T(8,128)S(1)} %get-tuple-element.62.carry_ref, f32[512,128]{1,0:T(8,128)S(1)} %get-tuple-element.63.source_ref, ...), custom_call_target="tpu_custom_call" | custom-call | bytes 1048576 | tf_op jit(solution)/shard_map/pallas_call | solution.py:640
  38.6 0.5 shard_map.112
  39.1 0.1 collective-permute-start.3
  39.2 1.3 %collective-permute-done.3 = f32[160,128]{1,0:T(8,128)S(1)} collective-permute-done((f32[160,128]{1,0:T(8,128)S(1)}, f32[160,128]{1,0:T(8,128)S(1)}, u32[]{:S(2)}, u32[]{:S(2)}) %collective-permute-start.3) | collective-permute-done | bytes 81952 | tf_op jit(solution)/shard_map/ppermute | solution.py:646
  40.5 1.5 %collective-permute-start.4 = (f32[160,128]{1,0:T(8,128)S(1)}, f32[160,128]{1,0:T(8,128)S(1)}, u32[]{:S(2)}, u32[]{:S(2)}) collective-permute-start(f32[160,128]{1,0:T(8,128)S(1)} %select_add_fusion), channel_id=1, source_target_pairs={{0,2},{1,3},{2,0},{3,1},{4,6},{5,7},{6,4},{7,5},{8,10},{9,11},{10,... | collective-permute-start | bytes 245768 | tf_op jit(solution)/shard_map/ppermute | solution.py:803
  42.0 1.5 %collective-permute-start.5 = (f32[160,128]{1,0:T(8,128)S(1)}, f32[160,128]{1,0:T(8,128)S(1)}, u32[]{:S(2)}, u32[]{:S(2)}) collective-permute-start(f32[160,128]{1,0:T(8,128)S(1)} %select_add_fusion), channel_id=1, source_target_pairs={{0,4},{1,5},{2,6},{3,7},{4,0},{5,1},{6,2},{7,3},{8,12},{9,13},{10,... | collective-permute-start | bytes 245768 | tf_op jit(solution)/shard_map/ppermute | solution.py:803
  43.5 0.5 collective-permute-start.6
  44.1 1.0 %collective-permute-done.4 = f32[160,128]{1,0:T(8,128)S(1)} collective-permute-done((f32[160,128]{1,0:T(8,128)S(1)}, f32[160,128]{1,0:T(8,128)S(1)}, u32[]{:S(2)}, u32[]{:S(2)}) %collective-permute-start.4) | collective-permute-done | bytes 81952 | tf_op jit(solution)/shard_map/ppermute | solution.py:803
  45.1 2.2 %collective-permute-done.5 = f32[160,128]{1,0:T(8,128)S(1)} collective-permute-done((f32[160,128]{1,0:T(8,128)S(1)}, f32[160,128]{1,0:T(8,128)S(1)}, u32[]{:S(2)}, u32[]{:S(2)}) %collective-permute-start.5) | collective-permute-done | bytes 81952 | tf_op jit(solution)/shard_map/ppermute | solution.py:803
  47.3 1.6 %collective-permute-done.6 = f32[160,128]{1,0:T(8,128)S(1)} collective-permute-done((f32[160,128]{1,0:T(8,128)S(1)}, f32[160,128]{1,0:T(8,128)S(1)}, u32[]{:S(2)}, u32[]{:S(2)}) %collective-permute-start.6) | collective-permute-done | bytes 81952 | tf_op jit(solution)/shard_map/ppermute | solution.py:803
  48.9 1.6 %collective-permute-start.7 = (f32[160,128]{1,0:T(8,128)S(1)}, f32[160,128]{1,0:T(8,128)S(1)}, u32[]{:S(2)}, u32[]{:S(2)}) collective-permute-start(f32[160,128]{1,0:T(8,128)S(1)} %add_add_fusion), channel_id=1, source_target_pairs={{0,8},{1,17},{2,10},{3,19},{4,12},{5,21},{6,14},{7,23},{8,0},{9,25... | collective-permute-start | bytes 245768 | tf_op jit(solution)/shard_map/ppermute | solution.py:803
  50.5 2.9 %collective-permute-done.7 = f32[160,128]{1,0:T(8,128)S(1)} collective-permute-done((f32[160,128]{1,0:T(8,128)S(1)}, f32[160,128]{1,0:T(8,128)S(1)}, u32[]{:S(2)}, u32[]{:S(2)}) %collective-permute-start.7) | collective-permute-done | bytes 81952 | tf_op jit(solution)/shard_map/ppermute | solution.py:803
  53.4 2.9 %collective-permute-start.8 = (f32[160,128]{1,0:T(8,128)S(1)}, f32[160,128]{1,0:T(8,128)S(1)}, u32[]{:S(2)}, u32[]{:S(2)}) collective-permute-start(f32[160,128]{1,0:T(8,128)S(1)} %add.22), channel_id=1, source_target_pairs={{0,16},{1,9},{2,18},{3,11},{4,20},{5,13},{6,22},{7,15},{8,24},{9,1... | collective-permute-start | bytes 245768 | tf_op jit(solution)/shard_map/ppermute | solution.py:803
  56.3 2.5 %collective-permute-done.8 = f32[160,128]{1,0:T(8,128)S(1)} collective-permute-done((f32[160,128]{1,0:T(8,128)S(1)}, f32[160,128]{1,0:T(8,128)S(1)}, u32[]{:S(2)}, u32[]{:S(2)}) %collective-permute-start.8) | collective-permute-done | bytes 81952 | tf_op jit(solution)/shard_map/ppermute | solution.py:803
  58.8 0.1 collective-permute-start.9
  58.9 0.7 %copy.11 = f32[2,256,128]{2,1,0:T(8,128)} copy(f32[2,256,128]{2,1,0:T(8,128)S(1)} %bitcast.6) | data formatting | bytes 524288
  59.6 0.6 collective-permute-done.9.other_ref
  60.2 0.8 %shard_map.113 = (f32[128,128]{1,0:T(8,128)}, f32[256,128]{1,0:T(8,128)}) custom-call(f32[160,128]{1,0:T(8,128)S(1)} %add.23.mine_ref, f32[160,128]{1,0:T(8,128)S(1)} %collective-permute-done.9.other_ref), custom_call_target="tpu_custom_call" | custom-call | bytes 1048576 | tf_op jit(solution)/shard_map/pallas_call | solution.py:640
  (5 shorter events, 0.1 us)
Async XLA Ops:
  13.8 8.1 %collective-permute-start = (f32[2,200,128]{2,1,0:T(8,128)S(1)}, f32[2,200,128]{2,1,0:T(8,128)S(1)}, u32[]{:S(2)}, u32[]{:S(2)}) collective-permute-start(f32[2,200,128]{2,1,0:T(8,128)S(1)} %get-tuple-element.39.mine_ref.refs_0_), channel_id=1, source_target_pairs={{0,4},{4,0},{8,12},{12,8},{16,20},{20,16},{24,28},{28,24},{1,5},{5... | collective-permute-start | bytes 614408 | tf_op jit(solution)/shard_map/ppermute | solution.py:646
  22.7 6.3 %collective-permute-start.1 = (f32[2,200,128]{2,1,0:T(8,128)S(1)}, f32[2,200,128]{2,1,0:T(8,128)S(1)}, u32[]{:S(2)}, u32[]{:S(2)}) collective-permute-start(f32[2,200,128]{2,1,0:T(8,128)S(1)} %shard_map.105._.mine_ref.refs_1_), channel_id=1, source_target_pairs={{0,8},{4,12},{8,0},{12,4},{16,24},{20,28},{24,16},{28,20},{1,9},{5... | collective-permute-start | bytes 614408 | tf_op jit(solution)/shard_map/ppermute | solution.py:646
  29.9 5.3 %copy-start = (f32[32,128,128]{2,1,0:T(8,128)S(1)}, f32[32,128,128]{2,1,0:T(8,128)}, u32[]{:S(2)}) copy-start(f32[32,128,128]{2,1,0:T(8,128)} %get-tuple-element.49.refs_4_) | copy-start | bytes 6291460
  29.9 5.3 %copy-start.2 = (f32[512,128]{1,0:T(8,128)S(1)}, f32[512,128]{1,0:T(8,128)}, u32[]{:S(2)}) copy-start(f32[512,128]{1,0:T(8,128)} %get-tuple-element.59.refs_14_.gain_ref) | copy-start | bytes 786436
  30.0 5.3 %collective-permute-start.2 = (f32[2,72,128]{2,1,0:T(8,128)S(1)}, f32[2,72,128]{2,1,0:T(8,128)S(1)}, u32[]{:S(2)}, u32[]{:S(2)}) collective-permute-start(f32[2,72,128]{2,1,0:T(8,128)S(1)} %shard_map.108.mine_ref), channel_id=1, source_target_pairs={{0,16},{4,20},{8,24},{12,28},{16,0},{20,4},{24,8},{28,12},{1,17},{... | collective-permute-start | bytes 221192 | tf_op jit(solution)/shard_map/ppermute | solution.py:646
  35.3 1.3 %copy-start.1 = (f32[2,256,128]{2,1,0:T(8,128)S(1)}, f32[2,256,128]{2,1,0:T(8,128)}, u32[]{:S(2)}) copy-start(f32[2,256,128]{2,1,0:T(8,128)} %param.9) | copy-start | bytes 786436
  35.3 1.3 %copy-start.3 = (f32[512,128]{1,0:T(8,128)S(1)}, f32[512,128]{1,0:T(8,128)}, u32[]{:S(2)}) copy-start(f32[512,128]{1,0:T(8,128)} %get-tuple-element.65.resid_ref) | copy-start | bytes 786436
  39.1 1.3 %collective-permute-start.3 = (f32[160,128]{1,0:T(8,128)S(1)}, f32[160,128]{1,0:T(8,128)S(1)}, u32[]{:S(2)}, u32[]{:S(2)}) collective-permute-start(f32[160,128]{1,0:T(8,128)S(1)} %slice_select_fusion), channel_id=1, source_target_pairs={{0,1},{1,0},{2,3},{3,2},{4,5},{5,4},{6,7},{7,6},{8,9},{9,8},{10,11... | collective-permute-start | bytes 245768 | tf_op jit(solution)/shard_map/ppermute | solution.py:646
  40.5 4.6 %collective-permute-start.4 = (f32[160,128]{1,0:T(8,128)S(1)}, f32[160,128]{1,0:T(8,128)S(1)}, u32[]{:S(2)}, u32[]{:S(2)}) collective-permute-start(f32[160,128]{1,0:T(8,128)S(1)} %select_add_fusion), channel_id=1, source_target_pairs={{0,2},{1,3},{2,0},{3,1},{4,6},{5,7},{6,4},{7,5},{8,10},{9,11},{10,... | collective-permute-start | bytes 245768 | tf_op jit(solution)/shard_map/ppermute | solution.py:803
  42.0 5.3 %collective-permute-start.5 = (f32[160,128]{1,0:T(8,128)S(1)}, f32[160,128]{1,0:T(8,128)S(1)}, u32[]{:S(2)}, u32[]{:S(2)}) collective-permute-start(f32[160,128]{1,0:T(8,128)S(1)} %select_add_fusion), channel_id=1, source_target_pairs={{0,4},{1,5},{2,6},{3,7},{4,0},{5,1},{6,2},{7,3},{8,12},{9,13},{10,... | collective-permute-start | bytes 245768 | tf_op jit(solution)/shard_map/ppermute | solution.py:803
  43.5 5.3 %collective-permute-start.6 = (f32[160,128]{1,0:T(8,128)S(1)}, f32[160,128]{1,0:T(8,128)S(1)}, u32[]{:S(2)}, u32[]{:S(2)}) collective-permute-start(f32[160,128]{1,0:T(8,128)S(1)} %select_add_fusion), channel_id=1, source_target_pairs={{0,6},{1,7},{2,4},{3,5},{4,2},{5,3},{6,0},{7,1},{8,14},{9,15},{10,... | collective-permute-start | bytes 245768 | tf_op jit(solution)/shard_map/ppermute | solution.py:803
  48.9 4.5 %collective-permute-start.7 = (f32[160,128]{1,0:T(8,128)S(1)}, f32[160,128]{1,0:T(8,128)S(1)}, u32[]{:S(2)}, u32[]{:S(2)}) collective-permute-start(f32[160,128]{1,0:T(8,128)S(1)} %add_add_fusion), channel_id=1, source_target_pairs={{0,8},{1,17},{2,10},{3,19},{4,12},{5,21},{6,14},{7,23},{8,0},{9,25... | collective-permute-start | bytes 245768 | tf_op jit(solution)/shard_map/ppermute | solution.py:803
  53.4 5.4 %collective-permute-start.8 = (f32[160,128]{1,0:T(8,128)S(1)}, f32[160,128]{1,0:T(8,128)S(1)}, u32[]{:S(2)}, u32[]{:S(2)}) collective-permute-start(f32[160,128]{1,0:T(8,128)S(1)} %add.22), channel_id=1, source_target_pairs={{0,16},{1,9},{2,18},{3,11},{4,20},{5,13},{6,22},{7,15},{8,24},{9,1... | collective-permute-start | bytes 245768 | tf_op jit(solution)/shard_map/ppermute | solution.py:803
  58.8 1.3 %collective-permute-start.9 = (f32[160,128]{1,0:T(8,128)S(1)}, f32[160,128]{1,0:T(8,128)S(1)}, u32[]{:S(2)}, u32[]{:S(2)}) collective-permute-start(f32[160,128]{1,0:T(8,128)S(1)} %add.23.mine_ref), channel_id=1, source_target_pairs={{0,1},{1,0},{2,3},{3,2},{4,5},{5,4},{6,7},{7,6},{8,9},{9,8},{10,11... | collective-permute-start | bytes 245768 | tf_op jit(solution)/shard_map/ppermute | solution.py:646

commit v10 on v9

--- a/solution.py
+++ b/solution.py
@@ -324,9 +324,13 @@
     at = hidden if with_map else 0
     rows = [eight(ref[s, pl.ds(at + hidden // 2 + k, 1), :]) for k in range(6)]
     diagonal = ref[s, pl.ds(at + hidden // 2 + DIAGONAL, 1), :]
-    half = unfold(ref[s, pl.ds(at, hidden // 2), :])
-    curve = half + half.T + identity(hidden) * diagonal
+    curve = (unfold(ref[s, pl.ds(at, hidden // 2), :]), diagonal)
     return (ref[s, pl.ds(0, hidden), :] if with_map else None, curve, rows)
+
+
+def entire(curve):
+    half, diagonal = curve
+    return half + half.T + identity(half.shape[0]) * diagonal
 
 
 def pick(flag, one, other):
@@ -344,9 +348,19 @@
     gain, resid = crossing(rows_1[LAST], rows_1[MOVED], rows_2[DRIVE], rows_2[FIRST])
     map_1 = map_1 + mul(map_1, drift_w) * gain[:1]
     off_1 = rows_1[OFFSET] + mul(rows_1[OFFSET], drift_w) * gain + resid
-    curve_w, map_w, map_1_t = right(curve_2), right(map_2), right_t(map_1)
-    curve = curve_1 + mul_t(mul(map_1, curve_w), map_1_t)
-    adjoint = rows_1[ADJOINT] + mul_t(mul(off_1, curve_w) + rows_2[ADJOINT], map_1_t)
+    half_2, diagonal_2 = curve_2
+    half_w, half_wt, map_w, map_1_t = right(half_2), right_t(half_2), right(map_2), right_t(map_1)
+
+    def bent(value):
+        return mul(value, half_w) + mul_t(value, half_wt) + value * diagonal_2
+
+    square = mul_t(bent(map_1), map_1_t)
+    unit = identity(square.shape[0])
+    curve = (
+        curve_1[0] + unfold(fold(square)),
+        curve_1[1] + jnp.sum(unit * square, axis=0, keepdims=True),
+    )
+    adjoint = rows_1[ADJOINT] + mul_t(bent(off_1) + rows_2[ADJOINT], map_1_t)
     rows = [mul(off_1, map_w) + rows_2[OFFSET], adjoint, rows_1[DRIVE], rows_1[FIRST], rows_2[LAST], rows_2[MOVED]]
     return (mul(map_1, map_w) if with_map else None), curve, rows
 
@@ -362,8 +376,8 @@
         if with_map:
             out_ref[s, pl.ds(0, hidden), :] = whole
             at = hidden
-        out_ref[s, pl.ds(at, hidden // 2), :] = fold(curve)
-        diagonal = jnp.sum(identity(hidden) * curve, axis=0, keepdims=True)
+        out_ref[s, pl.ds(at, hidden // 2), :] = fold(curve[0])
+        diagonal = curve[1]
         out_ref[s, pl.ds(at + hidden // 2, 8), :] = vectors(*rows, diagonal)
 
 
@@ -376,7 +390,7 @@
     for s in range(seqs):
         zero = jnp.zeros((8, hidden), F32)
         lead, lead_off = unit, zero
-        after = (unit, jnp.zeros((hidden, hidden), F32), [zero] * 6)
+        after = (unit, (jnp.zeros((hidden, hidden), F32), zero[:1]), [zero] * 6)
         edge, edge_gain = zero, zero
         place = lax.axis_index("seq")
         fresh = place >= 0
@@ -396,7 +410,7 @@
             lead, lead_off = pick(upper, longer, (lead, lead_off))
             after = pick(upper, after, extended)
         own_map, _, own_rows = opened(mines[0], s)
-        own_w, curve_w = right(own_map), right(after[1])
+        own_w, curve_w = right(own_map), right(entire(after[1]))
         entry_ref[s] = lead
         tail_ref[s] = mul(mul(lead, own_w), curve_w)
         back_ref[s] = after[0].T
@@ -498,7 +512,7 @@
         gain, resid = crossing(last, moved, drive, first)
         middle = middle + mul(middle, drift_w) * gain + resid
         middle_col = column(middle[:1], unit)
-        row = along(middle_col, jnp.where(upper, entry_ref[s], other[1]))
+        row = along(middle_col, jnp.where(upper, entry_ref[s], entire(other[1])))
         lead_off, tail_off, edge, edge_gain = [sides_ref[pl.ds(8 * s + k, 1), :] for k in range(4)]
         beyond = eight(row) + other[2][ADJOINT]
         beyond = beyond + mul_t(beyond * gain, drift_wt)

time: 61.1 us -> 62.1 us (1.016)
  Pallas kernels: 29.1 us -> 30.5 us
    pallas_call x11, Pallas kernels: 29.1 us -> 30.5 us  [pinned(): return run(*placed)]
  transfers between devices with their start and end apart: 10 -> 10, of which waited for: 10 -> 9; matrix products, arithmetic and copies ran while one was open for 1% -> 1% of each run, Pallas kernels for 16% -> 17%
where the time goes in v10:
time: 62.1 us; the launch traced here: 61.9 us
  Pallas kernels  30.5 us (49%)
  starting transfers between devices  15.3 us (25%)
  waiting for transfers between devices  14.6 us (24%)
  between operations  0.81 us (1%)
  local copies, waits for them, and re-layouts  0.72 us (1%)
    pallas_call x11, Pallas kernels, pinned(): return run(*placed)  30.5 us
    ppermute x5, waiting for transfers between devices, moved(): return lax.ppermute(value, ('seq', 'batch'), route)  10.7 us
    ppermute x5, starting transfers between devices, moved(): return lax.ppermute(value, ('seq', 'batch'), route)  7.65 us
    ppermute x5, starting transfers between devices, swapped(): lax.ppermute(value, axis, [(i, i ^ distance) for i in range(lax.axis_size...  7.62 us
    ppermute x5, waiting for transfers between devices, swapped(): lax.ppermute(value, axis, [(i, i ^ distance) for i in range(lax.axis_size...  3.92 us
  transfers between devices with their start and end apart: 10, of which 9 were waited for; matrix products, arithmetic and copies ran while one was open for 1% of the time, Pallas kernels for 17%

profile of v10, /device:TPU:0, one launch (start us, length us, event | category | flops | bytes accessed | tf_op | source)
XLA Modules:
  0.0 61.9 jit_solution(18157165255918551370)
XLA Ops:
  0.6 13.2 %shard_map.103 = (f32[2,200,128]{2,1,0:T(8,128)S(1)}, f32[32,128,128]{2,1,0:T(8,128)S(1)}, f32[32,128,128]{2,1,0:T(8,128)}, f32[32,128]{1,0:T(8,128)S(1)}, f32[4...) custom-call(s32[2,2]{1,0:T(2,128)} %steps_in.7, ...), custom_call_target="tpu_custom_call" | custom-call | bytes 1048576 | tf_op jit(solution)/shard_map/pallas_call | solution.py:654
  13.8 3.0 %collective-permute-start = (f32[2,200,128]{2,1,0:T(8,128)S(1)}, f32[2,200,128]{2,1,0:T(8,128)S(1)}, u32[]{:S(2)}, u32[]{:S(2)}) collective-permute-start(f32[2,200,128]{2,1,0:T(8,128)S(1)} %get-tuple-element.39.mine_ref.refs_0_), channel_id=1, source_target_pairs={{0,4},{4,0},{8,12},{12,8},{16,20},{20,16},{24,28},{28,24},{1,5},{5... | collective-permute-start | bytes 614408 | tf_op jit(solution)/shard_map/ppermute | solution.py:660
  16.8 3.1 %shard_map.104 = (f32[16,128,128]{2,1,0:T(8,128)S(1)}, f32[2,16,128,128]{3,2,1,0:T(8,128)S(1)}, f32[8,128]{1,0:T(8,128)S(1)}) custom-call(s32[2,2]{1,0:T(2,128)} %steps_in.7, f32[4,128,128]{2,1,0:T(8,128)} %get-tuple-element.40.hit_in, f32[32,128,128]{2,1,0:T(8,128)S(1)} %get-tuple-element.41.maps_ref, f32[128,128]{1,0:T(8,128)S(1)} %get-tuple-element.38._.drift_ref), custom_call_target="tpu_custom_call" | custom-call | flops 4294967296 | bytes 1048576 | tf_op jit(solution)/shard_map/pallas_call | solution.py:654
  19.9 2.0 %collective-permute-done.other_ref.refs_2_ = f32[2,200,128]{2,1,0:T(8,128)S(1)} collective-permute-done((f32[2,200,128]{2,1,0:T(8,128)S(1)}, f32[2,200,128]{2,1,0:T(8,128)S(1)}, u32[]{:S(2)}, u32[]{:S(2)}) %collective-permute-start) | collective-permute-done | bytes 204832 | tf_op jit(solution)/shard_map/ppermute | solution.py:660
  21.9 1.1 %shard_map.105._.mine_ref.refs_1_ = f32[2,200,128]{2,1,0:T(8,128)S(1)} custom-call(f32[128,128]{1,0:T(8,128)S(1)} %get-tuple-element.38._.drift_ref, f32[2,200,128]{2,1,0:T(8,128)S(1)} %get-tuple-element.39.mine_ref.refs_0_, f32[2,200,128]{2,1,0:T(8,128)S(1)} %collective-permute-done.other_ref.refs_2_, f32[8,128]{1,0:T(8,128)S(1)} %get-tuple-element.42._), custom_call_target="tpu_custom_call" | custom-call | bytes 1048576 | tf_op jit(solution)/shard_map/pallas_call | solution.py:654
  23.0 1.9 %collective-permute-start.1 = (f32[2,200,128]{2,1,0:T(8,128)S(1)}, f32[2,200,128]{2,1,0:T(8,128)S(1)}, u32[]{:S(2)}, u32[]{:S(2)}) collective-permute-start(f32[2,200,128]{2,1,0:T(8,128)S(1)} %shard_map.105._.mine_ref.refs_1_), channel_id=1, source_target_pairs={{0,8},{4,12},{8,0},{12,4},{16,24},{20,28},{24,16},{28,20},{1,9},{5... | collective-permute-start | bytes 614408 | tf_op jit(solution)/shard_map/ppermute | solution.py:660
  24.9 2.9 %shard_map.106 = (f32[16,128,128]{2,1,0:T(8,128)S(1)}, f32[2,16,128,128]{3,2,1,0:T(8,128)S(1)}, f32[8,128]{1,0:T(8,128)S(1)}) custom-call(s32[2,2]{1,0:T(2,128)} %steps_in.7, f32[4,128,128]{2,1,0:T(8,128)} %get-tuple-element.40.hit_in, f32[32,128,128]{2,1,0:T(8,128)S(1)} %get-tuple-element.41.maps_ref, f32[2,200,128]{2,1,0:T(8,128)S(1)} %shard_map.105._.mine_ref.refs_1_), custom_call_target="tpu_custom_call" | custom-call | flops 4294967296 | bytes 1048576 | tf_op jit(solution)/shard_map/pallas_call | solution.py:654
  27.8 1.4 %shard_map.107 = (bf16[384,512]{1,0:T(8,128)(2,1)S(1)}, bf16[384,512]{1,0:T(8,128)(2,1)S(1)}, f32[512,128]{1,0:T(8,128)S(1)}, f32[8,128]{1,0:T(8,128)S(1)}) custom-call(s32[2,2]{1,0:T(2,128)} %steps_in.7, f32[512,256]{1,0:T(8,128)} %bitcast.11, f32[512,128]{1,0:T(8,128)} %bitcast.8, f32[8,128]{1,0:T(8,128)S(1)} %get-tuple-element.43._), custom_call_target="tpu_custom_call" | custom-call | flops 2147483648 | bytes 1048576 | tf_op jit(solution)/shard_map/pallas_call | solution.py:654
  29.2 0.1 collective-permute-done.1.other_ref.refs_3_
  29.4 1.2 %shard_map.108.mine_ref = f32[2,72,128]{2,1,0:T(8,128)S(1)} custom-call(f32[128,128]{1,0:T(8,128)S(1)} %get-tuple-element.38._.drift_ref, f32[2,200,128]{2,1,0:T(8,128)S(1)} %shard_map.105._.mine_ref.refs_1_, f32[2,200,128]{2,1,0:T(8,128)S(1)} %collective-permute-done.1.other_ref.refs_3_, f32[8,128]{1,0:T(8,128)S(1)} %get-tuple-element.44._), custom_call_target="tpu_custom_call" | custom-call | bytes 1048576 | tf_op jit(solution)/shard_map/pallas_call | solution.py:654
  30.5 0.0 copy-start
  30.5 0.0 copy-start.2
  30.5 2.6 %collective-permute-start.2 = (f32[2,72,128]{2,1,0:T(8,128)S(1)}, f32[2,72,128]{2,1,0:T(8,128)S(1)}, u32[]{:S(2)}, u32[]{:S(2)}) collective-permute-start(f32[2,72,128]{2,1,0:T(8,128)S(1)} %shard_map.108.mine_ref), channel_id=1, source_target_pairs={{0,16},{4,20},{8,24},{12,28},{16,0},{20,4},{24,8},{28,12},{1,17},{... | collective-permute-start | bytes 221192 | tf_op jit(solution)/shard_map/ppermute | solution.py:660
  33.1 3.0 %shard_map.109 = (f32[2,128,128]{2,1,0:T(8,128)S(1)}, f32[2,128,128]{2,1,0:T(8,128)S(1)}, f32[2,128,128]{2,1,0:T(8,128)S(1)}, f32[16,128]{1,0:T(8,128)S(1)}) custom-call(f32[128,128]{1,0:T(8,128)S(1)} %get-tuple-element.38._.drift_ref, f32[2,200,128]{2,1,0:T(8,128)S(1)} %get-tuple-element.39.mine_ref.refs_0_, ...), custom_call_target="tpu_custom_call" | custom-call | flops 1073741824 | bytes 1048576 | tf_op jit(solution)/shard_map/pallas_call | solution.py:654
  36.1 0.0 collective-permute-done.2.other_ref
  36.2 0.0 copy-done
  36.2 0.0 copy-done.2
  36.2 0.0 copy-start.1
  36.2 0.0 copy-start.3
  36.2 1.3 %shard_map.110 = (f32[32,128]{1,0:T(8,128)S(1)}, f32[32,128]{1,0:T(8,128)S(1)}, f32[512,128]{1,0:T(8,128)S(1)}, f32[512,128]{1,0:T(8,128)S(1)}, f32[2,128]{1,0:T(2,128)S(1)}) custom-call(f32[128,128]{1,0:T(8,128)S(1)} %get-tuple-element.38._.drift_ref, f32[2,72,128]{2,1,0:T(8,128)S(1)} %shard_map.108.mine_ref, ...), custom_call_target="tpu_custom_call" | custom-call | bytes 1048576 | tf_op jit(solution)/shard_map/pallas_call | solution.py:654
  37.5 0.0 copy-done.1
  37.5 0.0 copy-done.3
  37.5 2.0 %shard_map.111 = (f32[512,128]{1,0:T(8,128)S(1)}, f32[512,128]{1,0:T(8,128)S(1)}) custom-call(f32[128,128]{1,0:T(8,128)S(1)} %get-tuple-element.38._.drift_ref, f32[32,128]{1,0:T(8,128)S(1)} %get-tuple-element.61.state_ref, f32[32,128]{1,0:T(8,128)S(1)} %get-tuple-element.62.carry_ref, f32[512,128]{1,0:T(8,128)S(1)} %get-tuple-element.63.source_ref, ...), custom_call_target="tpu_custom_call" | custom-call | bytes 1048576 | tf_op jit(solution)/shard_map/pallas_call | solution.py:654
  39.5 0.5 shard_map.112
  40.1 0.1 collective-permute-start.3
  40.1 1.3 %collective-permute-done.3 = f32[160,128]{1,0:T(8,128)S(1)} collective-permute-done((f32[160,128]{1,0:T(8,128)S(1)}, f32[160,128]{1,0:T(8,128)S(1)}, u32[]{:S(2)}, u32[]{:S(2)}) %collective-permute-start.3) | collective-permute-done | bytes 81952 | tf_op jit(solution)/shard_map/ppermute | solution.py:660
  41.4 1.6 %collective-permute-start.4 = (f32[160,128]{1,0:T(8,128)S(1)}, f32[160,128]{1,0:T(8,128)S(1)}, u32[]{:S(2)}, u32[]{:S(2)}) collective-permute-start(f32[160,128]{1,0:T(8,128)S(1)} %select_add_fusion), channel_id=1, source_target_pairs={{0,2},{1,3},{2,0},{3,1},{4,6},{5,7},{6,4},{7,5},{8,10},{9,11},{10,... | collective-permute-start | bytes 245768 | tf_op jit(solution)/shard_map/ppermute | solution.py:817
  43.0 1.5 %collective-permute-start.5 = (f32[160,128]{1,0:T(8,128)S(1)}, f32[160,128]{1,0:T(8,128)S(1)}, u32[]{:S(2)}, u32[]{:S(2)}) collective-permute-start(f32[160,128]{1,0:T(8,128)S(1)} %select_add_fusion), channel_id=1, source_target_pairs={{0,4},{1,5},{2,6},{3,7},{4,0},{5,1},{6,2},{7,3},{8,12},{9,13},{10,... | collective-permute-start | bytes 245768 | tf_op jit(solution)/shard_map/ppermute | solution.py:817
  44.5 0.5 collective-permute-start.6
  45.0 1.0 %collective-permute-done.4 = f32[160,128]{1,0:T(8,128)S(1)} collective-permute-done((f32[160,128]{1,0:T(8,128)S(1)}, f32[160,128]{1,0:T(8,128)S(1)}, u32[]{:S(2)}, u32[]{:S(2)}) %collective-permute-start.4) | collective-permute-done | bytes 81952 | tf_op jit(solution)/shard_map/ppermute | solution.py:817
  46.0 2.3 %collective-permute-done.5 = f32[160,128]{1,0:T(8,128)S(1)} collective-permute-done((f32[160,128]{1,0:T(8,128)S(1)}, f32[160,128]{1,0:T(8,128)S(1)}, u32[]{:S(2)}, u32[]{:S(2)}) %collective-permute-start.5) | collective-permute-done | bytes 81952 | tf_op jit(solution)/shard_map/ppermute | solution.py:817
  48.3 1.6 %collective-permute-done.6 = f32[160,128]{1,0:T(8,128)S(1)} collective-permute-done((f32[160,128]{1,0:T(8,128)S(1)}, f32[160,128]{1,0:T(8,128)S(1)}, u32[]{:S(2)}, u32[]{:S(2)}) %collective-permute-start.6) | collective-permute-done | bytes 81952 | tf_op jit(solution)/shard_map/ppermute | solution.py:817
  49.9 1.6 %collective-permute-start.7 = (f32[160,128]{1,0:T(8,128)S(1)}, f32[160,128]{1,0:T(8,128)S(1)}, u32[]{:S(2)}, u32[]{:S(2)}) collective-permute-start(f32[160,128]{1,0:T(8,128)S(1)} %add_add_fusion), channel_id=1, source_target_pairs={{0,8},{1,17},{2,10},{3,19},{4,12},{5,21},{6,14},{7,23},{8,0},{9,25... | collective-permute-start | bytes 245768 | tf_op jit(solution)/shard_map/ppermute | solution.py:817
  51.5 2.9 %collective-permute-done.7 = f32[160,128]{1,0:T(8,128)S(1)} collective-permute-done((f32[160,128]{1,0:T(8,128)S(1)}, f32[160,128]{1,0:T(8,128)S(1)}, u32[]{:S(2)}, u32[]{:S(2)}) %collective-permute-start.7) | collective-permute-done | bytes 81952 | tf_op jit(solution)/shard_map/ppermute | solution.py:817
  54.4 2.5 %collective-permute-start.8 = (f32[160,128]{1,0:T(8,128)S(1)}, f32[160,128]{1,0:T(8,128)S(1)}, u32[]{:S(2)}, u32[]{:S(2)}) collective-permute-start(f32[160,128]{1,0:T(8,128)S(1)} %add.22), channel_id=1, source_target_pairs={{0,16},{1,9},{2,18},{3,11},{4,20},{5,13},{6,22},{7,15},{8,24},{9,1... | collective-permute-start | bytes 245768 | tf_op jit(solution)/shard_map/ppermute | solution.py:817
  56.9 2.9 %collective-permute-done.8 = f32[160,128]{1,0:T(8,128)S(1)} collective-permute-done((f32[160,128]{1,0:T(8,128)S(1)}, f32[160,128]{1,0:T(8,128)S(1)}, u32[]{:S(2)}, u32[]{:S(2)}) %collective-permute-start.8) | collective-permute-done | bytes 81952 | tf_op jit(solution)/shard_map/ppermute | solution.py:817
  59.8 0.1 collective-permute-start.9
  59.9 0.7 %copy.11 = f32[2,256,128]{2,1,0:T(8,128)} copy(f32[2,256,128]{2,1,0:T(8,128)S(1)} %bitcast.6) | data formatting | bytes 524288
  60.6 0.6 collective-permute-done.9.other_ref
  61.1 0.8 %shard_map.113 = (f32[128,128]{1,0:T(8,128)}, f32[256,128]{1,0:T(8,128)}) custom-call(f32[160,128]{1,0:T(8,128)S(1)} %add.23.mine_ref, f32[160,128]{1,0:T(8,128)S(1)} %collective-permute-done.9.other_ref), custom_call_target="tpu_custom_call" | custom-call | bytes 1048576 | tf_op jit(solution)/shard_map/pallas_call | solution.py:654
  (5 shorter events, 0.1 us)
Async XLA Ops:
  13.8 8.1 %collective-permute-start = (f32[2,200,128]{2,1,0:T(8,128)S(1)}, f32[2,200,128]{2,1,0:T(8,128)S(1)}, u32[]{:S(2)}, u32[]{:S(2)}) collective-permute-start(f32[2,200,128]{2,1,0:T(8,128)S(1)} %get-tuple-element.39.mine_ref.refs_0_), channel_id=1, source_target_pairs={{0,4},{4,0},{8,12},{12,8},{16,20},{20,16},{24,28},{28,24},{1,5},{5... | collective-permute-start | bytes 614408 | tf_op jit(solution)/shard_map/ppermute | solution.py:660
  23.0 6.3 %collective-permute-start.1 = (f32[2,200,128]{2,1,0:T(8,128)S(1)}, f32[2,200,128]{2,1,0:T(8,128)S(1)}, u32[]{:S(2)}, u32[]{:S(2)}) collective-permute-start(f32[2,200,128]{2,1,0:T(8,128)S(1)} %shard_map.105._.mine_ref.refs_1_), channel_id=1, source_target_pairs={{0,8},{4,12},{8,0},{12,4},{16,24},{20,28},{24,16},{28,20},{1,9},{5... | collective-permute-start | bytes 614408 | tf_op jit(solution)/shard_map/ppermute | solution.py:660
  30.5 5.7 %copy-start = (f32[32,128,128]{2,1,0:T(8,128)S(1)}, f32[32,128,128]{2,1,0:T(8,128)}, u32[]{:S(2)}) copy-start(f32[32,128,128]{2,1,0:T(8,128)} %get-tuple-element.49.refs_4_) | copy-start | bytes 6291460
  30.5 5.7 %copy-start.2 = (f32[512,128]{1,0:T(8,128)S(1)}, f32[512,128]{1,0:T(8,128)}, u32[]{:S(2)}) copy-start(f32[512,128]{1,0:T(8,128)} %get-tuple-element.59.refs_14_.gain_ref) | copy-start | bytes 786436
  30.5 5.6 %collective-permute-start.2 = (f32[2,72,128]{2,1,0:T(8,128)S(1)}, f32[2,72,128]{2,1,0:T(8,128)S(1)}, u32[]{:S(2)}, u32[]{:S(2)}) collective-permute-start(f32[2,72,128]{2,1,0:T(8,128)S(1)} %shard_map.108.mine_ref), channel_id=1, source_target_pairs={{0,16},{4,20},{8,24},{12,28},{16,0},{20,4},{24,8},{28,12},{1,17},{... | collective-permute-start | bytes 221192 | tf_op jit(solution)/shard_map/ppermute | solution.py:660
  36.2 1.3 %copy-start.1 = (f32[2,256,128]{2,1,0:T(8,128)S(1)}, f32[2,256,128]{2,1,0:T(8,128)}, u32[]{:S(2)}) copy-start(f32[2,256,128]{2,1,0:T(8,128)} %param.9) | copy-start | bytes 786436
  36.2 1.3 %copy-start.3 = (f32[512,128]{1,0:T(8,128)S(1)}, f32[512,128]{1,0:T(8,128)}, u32[]{:S(2)}) copy-start(f32[512,128]{1,0:T(8,128)} %get-tuple-element.65.resid_ref) | copy-start | bytes 786436
  40.1 1.3 %collective-permute-start.3 = (f32[160,128]{1,0:T(8,128)S(1)}, f32[160,128]{1,0:T(8,128)S(1)}, u32[]{:S(2)}, u32[]{:S(2)}) collective-permute-start(f32[160,128]{1,0:T(8,128)S(1)} %slice_select_fusion), channel_id=1, source_target_pairs={{0,1},{1,0},{2,3},{3,2},{4,5},{5,4},{6,7},{7,6},{8,9},{9,8},{10,11... | collective-permute-start | bytes 245768 | tf_op jit(solution)/shard_map/ppermute | solution.py:660
  41.4 4.6 %collective-permute-start.4 = (f32[160,128]{1,0:T(8,128)S(1)}, f32[160,128]{1,0:T(8,128)S(1)}, u32[]{:S(2)}, u32[]{:S(2)}) collective-permute-start(f32[160,128]{1,0:T(8,128)S(1)} %select_add_fusion), channel_id=1, source_target_pairs={{0,2},{1,3},{2,0},{3,1},{4,6},{5,7},{6,4},{7,5},{8,10},{9,11},{10,... | collective-permute-start | bytes 245768 | tf_op jit(solution)/shard_map/ppermute | solution.py:817
  43.0 5.3 %collective-permute-start.5 = (f32[160,128]{1,0:T(8,128)S(1)}, f32[160,128]{1,0:T(8,128)S(1)}, u32[]{:S(2)}, u32[]{:S(2)}) collective-permute-start(f32[160,128]{1,0:T(8,128)S(1)} %select_add_fusion), channel_id=1, source_target_pairs={{0,4},{1,5},{2,6},{3,7},{4,0},{5,1},{6,2},{7,3},{8,12},{9,13},{10,... | collective-permute-start | bytes 245768 | tf_op jit(solution)/shard_map/ppermute | solution.py:817
  44.5 5.3 %collective-permute-start.6 = (f32[160,128]{1,0:T(8,128)S(1)}, f32[160,128]{1,0:T(8,128)S(1)}, u32[]{:S(2)}, u32[]{:S(2)}) collective-permute-start(f32[160,128]{1,0:T(8,128)S(1)} %select_add_fusion), channel_id=1, source_target_pairs={{0,6},{1,7},{2,4},{3,5},{4,2},{5,3},{6,0},{7,1},{8,14},{9,15},{10,... | collective-permute-start | bytes 245768 | tf_op jit(solution)/shard_map/ppermute | solution.py:817
  49.9 4.5 %collective-permute-start.7 = (f32[160,128]{1,0:T(8,128)S(1)}, f32[160,128]{1,0:T(8,128)S(1)}, u32[]{:S(2)}, u32[]{:S(2)}) collective-permute-start(f32[160,128]{1,0:T(8,128)S(1)} %add_add_fusion), channel_id=1, source_target_pairs={{0,8},{1,17},{2,10},{3,19},{4,12},{5,21},{6,14},{7,23},{8,0},{9,25... | collective-permute-start | bytes 245768 | tf_op jit(solution)/shard_map/ppermute | solution.py:817
  54.4 5.4 %collective-permute-start.8 = (f32[160,128]{1,0:T(8,128)S(1)}, f32[160,128]{1,0:T(8,128)S(1)}, u32[]{:S(2)}, u32[]{:S(2)}) collective-permute-start(f32[160,128]{1,0:T(8,128)S(1)} %add.22), channel_id=1, source_target_pairs={{0,16},{1,9},{2,18},{3,11},{4,20},{5,13},{6,22},{7,15},{8,24},{9,1... | collective-permute-start | bytes 245768 | tf_op jit(solution)/shard_map/ppermute | solution.py:817
  59.8 1.3 %collective-permute-start.9 = (f32[160,128]{1,0:T(8,128)S(1)}, f32[160,128]{1,0:T(8,128)S(1)}, u32[]{:S(2)}, u32[]{:S(2)}) collective-permute-start(f32[160,128]{1,0:T(8,128)S(1)} %add.23.mine_ref), channel_id=1, source_target_pairs={{0,1},{1,0},{2,3},{3,2},{4,5},{5,4},{6,7},{7,6},{8,9},{9,8},{10,11... | collective-permute-start | bytes 245768 | tf_op jit(solution)/shard_map/ppermute | solution.py:660
